TPU v7x, 128 devices: a whole 4x4x4 slice. The times are simulated.
128 devices in a mesh: dp: 16 (over x, z_hi, core), tensor: 8 (over z_lo, y).
Axes of the slice: x: 4, y: 4, z: 4 (z_hi: 2, z_lo: 2; z = z_hi * 2 + z_lo), core: 2. Of those that a mesh axis runs over, the one named last changes fastest.
Arguments:
- resid: bfloat16 [8192, 4096], P('dp', 'tensor'), may hold values from -32 to 32
- hidden: bfloat16 [8192, 14336], P('dp', 'tensor'), may hold values from -6 to 6
- down_weight: bfloat16 [14336, 4096], P('tensor'), may hold values from -1 to 1
- gain: float32 [4096], replicated, may hold values from 0.1 to 1.9
- domain_ids: int32 [16], replicated, may hold values from 0 to 3
Outputs:
- grad_hidden: bfloat16 [8192, 14336], P('dp', 'tensor')
- grad_resid: bfloat16 [8192, 4096], P('dp', 'tensor')
- grad_down: float32 [14336, 4096], P('tensor', 'dp')
- grad_gain: float32 [4096], P('tensor')
All inputs are finite; a program needn't handle non-finite values.
Results may differ from a plain program's by a relative error of at most 0.0034.
Values may be sent and summed in bfloat16 or wider, within the bound.
No kernel may reach another device: no remote copies, remote signals or barrier semaphores. Data moves between devices by JAX's collectives and lax.ppermute only.
A program may use at most 128 MiB of HBM per device.

v0:
```python
import jax
import jax.numpy as jnp
from jax import lax
from jax.sharding import PartitionSpec as P

SEQ = 128


score_scale = 20.0
loss_scale = 8192.0
eps_norm = 1e-05
eps_embed = 1e-06
highest = lax.Precision.HIGHEST


def score_gradient(scores, allowed, target):
    weights = jnp.where(allowed, jnp.exp(scores), 0.0)
    soft_weights = weights / jnp.sum(weights, axis=1, keepdims=True)
    return loss_scale * (soft_weights - target.astype(jnp.float32))


def per_device(resid, hidden, down_weight, gain, domain_ids):
    tok_rows = hidden.shape[0]
    model_width = down_weight.shape[1]
    slab_width = model_width // lax.axis_size("tensor")
    tensor_rank = lax.axis_index("tensor")
    shard_rank = lax.axis_index("dp")
    pairs_here = tok_rows // (2 * SEQ)
    offset = tensor_rank * slab_width
    partial_out = jnp.dot(hidden, down_weight, preferred_element_type=jnp.float32)
    own_cols = lax.dynamic_slice_in_dim(partial_out, offset, slab_width, 1) + resid.astype(
        jnp.float32
    )
    partial_out = lax.dynamic_update_slice_in_dim(partial_out, own_cols, offset, 1)
    layer = lax.psum(partial_out, "tensor")
    squares = jnp.sum(layer * layer, axis=1)
    inverse = lax.rsqrt(squares / model_width + eps_norm)
    normed = layer * inverse[:, None] * gain[None, :]
    pooled = jnp.mean(normed.reshape(pairs_here, 2, SEQ, -1), axis=2)
    queries = pooled[:, 0]
    passages = pooled[:, 1]
    total_pairs = pairs_here * lax.axis_size("dp")
    owners = jnp.repeat(domain_ids, pairs_here)
    my_domain = lax.dynamic_slice_in_dim(domain_ids, shard_rank, 1, 0)
    first_own = shard_rank * pairs_here
    own_index = first_own + jnp.arange(pairs_here)
    pair_index = jnp.arange(total_pairs)
    passage_all = lax.all_gather(passages, "dp", axis=0, tiled=True)
    raw_dots = jnp.dot(queries, passage_all.T, precision=highest)
    query_sq = jnp.sum(queries * queries, axis=1)
    passage_sq = jnp.sum(passage_all * passage_all, axis=1)
    query_norm = jnp.sqrt(query_sq + eps_embed)
    passage_norm = jnp.sqrt(passage_sq + eps_embed)
    scores = score_scale * raw_dots / (query_norm[:, None] * passage_norm[None, :])
    allowed = jnp.broadcast_to((owners == my_domain)[None, :], scores.shape)
    target = own_index[:, None] == pair_index[None, :]
    d_score = score_gradient(scores, allowed, target)
    query_unit = queries / query_norm[:, None]
    passage_unit = passage_all / passage_norm[:, None]
    query_coef = jnp.sum(d_score * scores, axis=1)
    d_query = (
        score_scale * jnp.dot(d_score, passage_unit, precision=highest)
        - query_unit * query_coef[:, None]
    ) / query_norm[:, None]
    passage_terms = score_scale * jnp.dot(d_score.T, query_unit, precision=highest)
    passage_coef = jnp.sum(d_score * scores, axis=0)
    passage_sum, coef_sum = (
        lax.psum_scatter(passage_terms, "dp", scatter_dimension=0, tiled=True),
        lax.psum_scatter(passage_coef, "dp", scatter_dimension=0, tiled=True),
    )
    own_unit = lax.dynamic_slice_in_dim(passage_unit, first_own, pairs_here, 0)
    own_norm = lax.dynamic_slice_in_dim(passage_norm, first_own, pairs_here, 0)
    d_passage = (passage_sum - own_unit * coef_sum[:, None]) / own_norm[:, None]
    d_pooled = jnp.stack((d_query, d_passage), axis=1) / SEQ
    d_normed = jnp.broadcast_to(
        d_pooled[:, :, None, :], (pairs_here, 2, SEQ, d_pooled.shape[2])
    ).reshape(tok_rows, -1)
    scaled = d_normed * gain[None, :]
    along = jnp.sum(scaled * layer, axis=1)
    gain_terms = jnp.sum(d_normed * layer * inverse[:, None], axis=0)
    gain_terms = lax.dynamic_slice_in_dim(gain_terms, offset, slab_width, 0)
    grad_gain = lax.psum(gain_terms, "dp")
    d_layer = (
        inverse[:, None] * scaled
        - layer * (inverse * inverse * inverse * along / model_width)[:, None]
    )
    d_low = d_layer.astype(jnp.bfloat16)
    hidden_grad32 = lax.dot_general(
        d_low, down_weight, (((1,), (1,)), ((), ())), preferred_element_type=jnp.float32
    )
    down_part = lax.dot_general(
        hidden, d_low, (((0,), (0,)), ((), ())), preferred_element_type=jnp.float32
    )
    grad_resid = lax.dynamic_slice_in_dim(d_low, offset, slab_width, 1)
    grad_down = lax.psum_scatter(down_part, "dp", scatter_dimension=1, tiled=True)
    return (hidden_grad32.astype(jnp.bfloat16), grad_resid, grad_down, grad_gain)


def solution(mesh):
    return jax.shard_map(
        per_device,
        mesh=mesh,
        in_specs=(P("dp", "tensor"), P("dp", "tensor"), P("tensor", None), P(), P()),
        out_specs=(P("dp", "tensor"), P("dp", "tensor"), P("tensor", "dp"), P("tensor")),
        check_vma=False,
    )
```

profile of v0, /device:TPU:0, one launch (start us, length us, event | category | flops | bytes accessed | tf_op | source)
XLA Modules:
  0.0 630.3 jit_solution(15986077360968587242)
XLA Ops:
  7.2 0.0 copy-start
  7.2 0.0 all-reduce.5.cloned.1.call-start
  7.2 1.4 copy-done
  8.7 13.0 %fusion.23 = f32[512,4096]{1,0:T(8,128)} fusion(bf16[512,1792]{1,0:T(8,128)(2,1)S(1)} %copy-done, bf16[1792,4096]{1,0:T(8,128)(2,1)} %param.7), kind=kOutput, calls=%fused_computation.51 | convolution fusion | flops 7516192768 | bytes 24903680 | tf_op jit(solution)/shard_map/dot_general | solution.py:30
  21.7 0.0 copy-done.4
  21.7 2.5 add_dynamic-update-slice_fusion
  24.1 0.0 all-reduce.5.cloned.1.call-update
  24.2 0.0 all-reduce.7.cloned.1.call-start
  24.2 0.0 copy-done.6
  24.2 0.6 dynamic_slice.19
  24.8 0.6 broadcast_compare_fusion
  25.5 0.1 broadcast_in_dim.9
  25.5 0.1 eq.34
  25.7 0.0 copy-done.7
  25.7 0.6 dynamic-slice
  26.9 184.2 %all-reduce.5.cloned.1.call-done = f32[512,4096]{1,0:T(8,128)} async-done(((f32[512,4096]{1,0:T(8,128)}), f32[512,4096]{1,0:T(8,128)}) %all-reduce.5.cloned.1.call-update) | async-done | bytes 8388624 | tf_op jit(solution)/shard_map/psum | solution.py:35
  211.2 4.2 multiply_reduce_fusion
  215.3 0.0 copy-done.5
  215.3 1.6 copy-done.2
  216.9 1.3 bitcast_reduce_fusion
  218.3 0.1 copy_multiply_fusion
  218.4 0.1 multiply_reduce_fusion.1
  218.5 25.3 %all-gather = f32[32,1,4096]{2,1,0:T(1,128)S(1)} all-gather(f32[2,1,4096]{2,1,0:T(1,128)S(1)} %copy.14), channel_id=2, replica_groups=mesh['dp'=16,'tensor'=8] {'dp'}, dimensions={0}, use_global_device_ids=true | all-gather | bytes 557056 | tf_op jit(solution)/shard_map/all_gather | solution.py:48
  243.9 0.4 fusion.12
  244.3 0.9 fusion.20
  245.1 0.2 multiply_reduce_fusion.3
  245.3 1.4 convolution_multiply_fusion
  246.8 0.0 all-reduce.7.cloned.1.call-update
  246.8 0.0 reduce-scatter.2.cloned.1.call-start
  246.9 0.3 bitcast_divide_fusion
  247.2 0.1 dynamic_slice.21
  247.3 33.7 %all-reduce.1 = f32[32]{0:T(128)S(1)} all-reduce(f32[32]{0:T(128)S(1)} %get-tuple-element.19), channel_id=4, replica_groups=mesh['dp'=16,'tensor'=8] {'dp'}, use_global_device_ids=true, to_apply=%region_9.10.clone | all-reduce | flops 32 | bytes 256
  280.9 0.1 dynamic-slice.3
  281.0 0.4 fusion.9
  281.4 98.5 %all-reduce.7.cloned.1.call-done = f32[32,4096]{1,0:T(8,128)} async-done(((f32[32,4096]{1,0:T(8,128)}), f32[32,4096]{1,0:T(8,128)}) %all-reduce.7.cloned.1.call-update) | async-done | bytes 524304
  379.9 1.0 fusion.15
  381.0 0.1 copy.15
  381.0 5.0 fusion.6
  386.1 4.3 fusion.3
  390.4 1.9 copy-done.3
  392.4 13.6 %convolution_bitcast_fusion = f32[1792,4096]{0,1:T(8,128)} fusion(bf16[512,4096]{1,0:T(8,128)(2,1)S(1)} %fusion.3, bf16[512,1792]{1,0:T(8,128)(2,1)S(1)} %copy-done), kind=kOutput, calls=%fused_computation | convolution fusion | flops 7516192768 | bytes 35389440 | tf_op jit(solution)/shard_map/dot_general | solution.py:91
  406.0 0.0 reduce-scatter.2.cloned.1.call-update
  406.0 0.1 dynamic_slice.23
  406.1 38.9 %psum.15 = f32[512]{0:T(512)} all-reduce(f32[512]{0:T(512)S(1)} %dynamic_slice.23), channel_id=1, replica_groups=mesh['dp'=16,'tensor'=8] {'dp'}, use_global_device_ids=true, to_apply=%region_13.14 | all-reduce | flops 512 | bytes 4096 | tf_op jit(solution)/shard_map/psum | solution.py:82
  445.0 2.0 constant_dynamic-slice_fusion
  447.1 14.7 %convolution_convert_fusion = bf16[512,1792]{1,0:T(8,128)(2,1)} fusion(bf16[512,4096]{1,0:T(8,128)(2,1)} %copy-done.3, bf16[1792,4096]{1,0:T(8,128)(2,1)} %param.7), kind=kOutput, calls=%fused_computation.18 | convolution fusion | flops 7517110272 | bytes 20709376 | tf_op jit(solution)/shard_map/dot_general | solution.py:88
  461.8 159.2 %reduce-scatter.2.cloned.1.call-done = f32[1792,256]{0,1:T(8,128)} async-done(((f32[1792,4096]{0,1:T(8,128)}), f32[1792,256]{0,1:T(8,128)}) %reduce-scatter.2.cloned.1.call-update) | async-done | bytes 1835024 | tf_op jit(solution)/shard_map/reduce_scatter | solution.py:95
  621.0 2.7 copy.16
  (16 shorter events, 0.1 us)
Async XLA Ops:
  7.2 1.5 copy-start
  7.2 204.0 %all-reduce.5.cloned.1.call-start = ((), (), s32[]{:S(2)}) async-start(), calls=%async_computation.1 | async-start | bytes 16777216 | tf_op jit(solution)/shard_map/psum | solution.py:35
  8.7 13.0 %copy-start.4 = (bf16[512,512]{1,0:T(8,128)(2,1)S(1)}, bf16[512,512]{1,0:T(8,128)(2,1)}, u32[]{:S(2)}) copy-start(bf16[512,512]{1,0:T(8,128)(2,1)} %param.5) | copy-start | bytes 1572868
  21.7 2.6 copy-start.6
  21.7 4.0 copy-start.7
  24.1 191.2 %copy-start.5 = (f32[4096]{0:T(1024)S(1)}, f32[4096]{0:T(1024)}, u32[]{:S(2)}) copy-start(f32[4096]{0:T(1024)} %param.8) | copy-start | bytes 49156
  24.2 355.8 %all-reduce.7.cloned.1.call-start = ((), (), s32[]{:S(2)}) async-start(), calls=%async_computation.3 | async-start | bytes 1048576
  211.2 5.8 copy-start.2
  246.8 374.2 %reduce-scatter.2.cloned.1.call-start = ((), (), s32[]{:S(2)}) async-start(), calls=%async_computation.2 | async-start | bytes 31195136 | tf_op jit(solution)/shard_map/reduce_scatter | solution.py:95
  390.4 1.9 copy-start.3
  447.0 176.7 %copy-start.1 = (bf16[512,1792]{1,0:T(8,128)(2,1)S(1)}, bf16[512,1792]{1,0:T(8,128)(2,1)}, u32[]{:S(2)}) copy-start(bf16[512,1792]{1,0:T(8,128)(2,1)} %param.6) | copy-start | bytes 5505028
Sparse Core Ops, SparseCore 0:
  24.3 186.8 all-reduce.4
  246.9 132.9 all-reduce.6
  406.2 214.8 reduce-scatter.1
where the time goes:
time: 631 us; the launch traced here: 630 us
  waiting for transfers between devices  442 us (70%)
  blocking collectives  97.9 us (16%)
  matrix products  44 us (7%)
  other arithmetic  20.1 us (3%)
  between operations  14.6 us (2%)
  local copies, waits for them, and re-layouts  11.4 us (2%)
    psum x1, waiting for transfers between devices, per_device(): layer = lax.psum(partial_out, 'tensor')  184 us
    reduce_scatter x1, waiting for transfers between devices, per_device(): lax.psum_scatter(down_part, 'dp', scatter_dimension=1, tiled=True)  159 us
    unnamed x4, waiting for transfers between devices  98.6 us
    psum x1, blocking collectives, per_device(): grad_gain = lax.psum(gain_terms, 'dp')  38.9 us
    unnamed x1, blocking collectives  33.7 us
    all_gather x1, blocking collectives, per_device(): passage_all = lax.all_gather(passages, 'dp', axis=0, tiled=True)  25.3 us
    dot_general x1, matrix products, per_device(): lax.dot_general(d_low, down_weight, (((1,), (1,)), ((), ())), preferred_e...  14.7 us
    dot_general x1, matrix products, per_device(): lax.dot_general(hidden, d_low, (((0,), (0,)), ((), ())), preferred_elemen...  13.6 us
  transfers between devices with their start and end apart: 3, of which 3 were waited for; matrix products, arithmetic and copies ran while one was open for 3% of the time, Pallas kernels for 0%

commit v1 on v0

v1 whole, which is shorter than its diff:
```python
import functools
import jax
import jax.numpy as jnp
from jax import lax
from jax.experimental import pallas as pl
from jax.experimental.pallas import tpu as pltpu
from jax.sharding import PartitionSpec as P

SEQ = 128
NX, NZH, NCORE, NZL, NY = 4, 2, 2, 2, 4

score_scale = 20.0
loss_scale = 8192.0
eps_norm = 1e-05
eps_embed = 1e-06
highest = lax.Precision.HIGHEST
f32 = jnp.float32
bf16 = jnp.bfloat16
MIB = 1024 * 1024


def dp_route(dx, dz, dc):
    pairs = []
    for x in range(NX):
        for z in range(NZH):
            for c in range(NCORE):
                to = (((x + dx) % NX) * NZH + (z + dz) % NZH) * NCORE + (c + dc) % NCORE
                pairs.append(((x * NZH + z) * NCORE + c, to))
    return pairs


def tensor_route(dz, dy):
    pairs = []
    for z in range(NZL):
        for y in range(NY):
            pairs.append((z * NY + y, ((z + dz) % NZL) * NY + (y + dy) % NY))
    return pairs


def over_x(value, step):
    return lax.ppermute(value, "dp", dp_route(step, 0, 0))


def over_zh(value):
    return lax.ppermute(value, "dp", dp_route(0, 1, 0))


def over_core(value):
    return lax.ppermute(value, "dp", dp_route(0, 0, 1))


def over_y(value, step):
    return lax.ppermute(value, "tensor", tensor_route(0, step))


def over_zl(value):
    return lax.ppermute(value, "tensor", tensor_route(1, 0))


def gather_small(value, axis):
    n = lax.axis_size(axis)
    copies = jnp.broadcast_to(value[None], (n,) + value.shape)
    return lax.all_to_all(copies, axis, 0, 0)


def slab_dot_kernel(slab_ref, hidden_ref, weight_ref, out_ref):
    out_ref[0] = jnp.dot(
        hidden_ref[...], weight_ref[...], preferred_element_type=f32
    ).astype(out_ref.dtype)


def slab_dot(hidden, weight, slabs, width, out_dtype):
    tokens, units = hidden.shape
    count = slabs.shape[0]
    return pl.pallas_call(
        slab_dot_kernel,
        grid_spec=pltpu.PrefetchScalarGridSpec(
            num_scalar_prefetch=1,
            grid=(count,),
            in_specs=[
                pl.BlockSpec((tokens, units), lambda i, s: (0, 0)),
                pl.BlockSpec((units, width), lambda i, s: (0, s[i])),
            ],
            out_specs=pl.BlockSpec((1, tokens, width), lambda i, s: (i, 0, 0)),
        ),
        out_shape=jax.ShapeDtypeStruct((count, tokens, width), out_dtype),
        compiler_params=pltpu.CompilerParams(vmem_limit_bytes=24 * MIB),
        cost_estimate=pl.CostEstimate(
            flops=2 * count * tokens * units * width,
            bytes_accessed=2 * (tokens * units + count * units * width + count * tokens * width),
            transcendentals=0,
        ),
    )(slabs, hidden, weight)


def contrast_kernel(mean_ref, gain_ref, same_ref, scaled_ref, gain_grad_ref):
    slabs, seqs, _ = mean_ref.shape
    rows = lax.broadcasted_iota(jnp.int32, (seqs, seqs), 0)
    cols = lax.broadcasted_iota(jnp.int32, (seqs, seqs), 1)
    across = (((1,), (1,)), ((), ()))
    gram = jnp.zeros((seqs, seqs), f32)
    for b in range(slabs):
        pooled = mean_ref[b] * gain_ref[b]
        gram += lax.dot_general(pooled, pooled, across, precision=highest, preferred_element_type=f32)
    diagonal = jnp.where(rows == cols, gram, 0.0)
    norm_col = jnp.sqrt(jnp.sum(diagonal, axis=1, keepdims=True) + eps_embed)
    norm_row = jnp.sqrt(jnp.sum(diagonal, axis=0, keepdims=True) + eps_embed)
    norms = norm_col * norm_row
    scores = score_scale * gram / norms
    query = rows % 2 == 0
    valid = query & (cols % 2 == 1) & (same_ref[...] > 0.5)
    weights = jnp.where(valid, jnp.exp(scores), 0.0)
    totals = jnp.sum(weights, axis=1, keepdims=True)
    soft = weights / jnp.where(totals > 0.0, totals, 1.0)
    target = jnp.where(query & (cols == rows + 1), 1.0, 0.0)
    d_score = loss_scale * (soft - target)
    both = d_score + d_score.T
    coef = jnp.sum(both * scores, axis=1, keepdims=True)
    mix = score_scale * both / norms - jnp.where(rows == cols, coef / (norm_col * norm_col), 0.0)
    for b in range(slabs):
        gain = gain_ref[b]
        mean = mean_ref[b]
        d_pooled = jnp.dot(mix, mean * gain, precision=highest, preferred_element_type=f32)
        gain_grad_ref[b] = jnp.sum(d_pooled * mean, axis=0, keepdims=True)
        scaled_ref[b] = d_pooled * gain * (1.0 / SEQ)


def contrast(means, gain, same):
    slabs, seqs, width = means.shape
    return pl.pallas_call(
        contrast_kernel,
        out_shape=(
            jax.ShapeDtypeStruct((slabs, seqs, width), f32),
            jax.ShapeDtypeStruct((slabs, 1, width), f32),
        ),
        compiler_params=pltpu.CompilerParams(vmem_limit_bytes=24 * MIB),
        cost_estimate=pl.CostEstimate(
            flops=24 * seqs * seqs * slabs * width, bytes_accessed=8 * slabs * seqs * width, transcendentals=seqs * seqs
        ),
    )(means, gain.reshape(slabs, 1, width), same)


def layer_grad_kernel(first_ref, layer_ref, scaled_ref, inverse_ref, low_ref, coef_ref):
    slabs, _, width = layer_ref.shape
    seq = first_ref[0] + pl.program_id(0)
    along = None
    for b in range(slabs):
        term = layer_ref[b].astype(f32) * scaled_ref[b, pl.ds(seq, 1), :]
        along = term if along is None else along + term
    inverse = inverse_ref[...]
    model_width = slabs * width
    coef = inverse * inverse * inverse * jnp.sum(along, axis=1, keepdims=True) / model_width
    coef_ref[...] = coef
    for b in range(slabs):
        low_ref[b] = (
            inverse * scaled_ref[b, pl.ds(seq, 1), :] - layer_ref[b].astype(f32) * coef
        ).astype(bf16)


def layer_grad(layer, scaled, inverse, first):
    slabs, tokens, width = layer.shape
    whole = pl.BlockSpec(scaled.shape, lambda i, s: (0, 0, 0))
    rows = pl.BlockSpec((slabs, SEQ, width), lambda i, s: (0, i, 0))
    column = pl.BlockSpec((SEQ, 1), lambda i, s: (i, 0))
    return pl.pallas_call(
        layer_grad_kernel,
        grid_spec=pltpu.PrefetchScalarGridSpec(
            num_scalar_prefetch=1,
            grid=(tokens // SEQ,),
            in_specs=[rows, whole, column],
            out_specs=[rows, column],
        ),
        out_shape=(
            jax.ShapeDtypeStruct((slabs, tokens, width), bf16),
            jax.ShapeDtypeStruct((tokens, 1), f32),
        ),
        compiler_params=pltpu.CompilerParams(vmem_limit_bytes=24 * MIB),
        cost_estimate=pl.CostEstimate(
            flops=6 * slabs * tokens * width, bytes_accessed=4 * slabs * tokens * width, transcendentals=0
        ),
    )(first, layer, scaled, inverse)


def hidden_grad_kernel(low_ref, weight_ref, out_ref, total_ref):
    step = pl.program_id(0)
    part = lax.dot_general(
        low_ref[0], weight_ref[...], (((1,), (1,)), ((), ())), preferred_element_type=f32
    )

    @pl.when(step == 0)
    def _():
        total_ref[...] = part

    @pl.when(step > 0)
    def _():
        total_ref[...] += part

    @pl.when(step == pl.num_programs(0) - 1)
    def _():
        out_ref[...] = total_ref[...].astype(out_ref.dtype)


def hidden_grad(low, weight):
    slabs, tokens, width = low.shape
    units = weight.shape[0]
    return pl.pallas_call(
        hidden_grad_kernel,
        grid=(slabs,),
        in_specs=[
            pl.BlockSpec((1, tokens, width), lambda i: (i, 0, 0)),
            pl.BlockSpec((units, width), lambda i: (0, i)),
        ],
        out_specs=pl.BlockSpec((tokens, units), lambda i: (0, 0)),
        out_shape=jax.ShapeDtypeStruct((tokens, units), bf16),
        scratch_shapes=[pltpu.VMEM((tokens, units), f32)],
        compiler_params=pltpu.CompilerParams(vmem_limit_bytes=32 * MIB),
        cost_estimate=pl.CostEstimate(
            flops=2 * slabs * tokens * units * width,
            bytes_accessed=2 * (slabs * tokens * width + slabs * units * width + tokens * units),
            transcendentals=0,
        ),
    )(low, weight)


def per_device(resid, hidden, down_weight, gain, domain_ids):
    tokens, units = hidden.shape
    model_width = down_weight.shape[1]
    group = lax.axis_size("tensor")
    shards = lax.axis_size("dp")
    width = model_width // group
    seqs_here = tokens // SEQ
    seqs = seqs_here * shards
    rank = lax.axis_index("tensor")
    zl, y = rank // NY, rank % NY
    shard = lax.axis_index("dp")
    x, zh, core = shard // (NZH * NCORE), (shard // NCORE) % NZH, shard % NCORE

    def slab_pair(step):
        column = (y + step) % NY
        return jnp.stack([zl * NY + column, (1 - zl) * NY + column]).astype(jnp.int32)

    with jax.named_scope("hidden_exchange"):
        hidden_x = [hidden] + [over_x(hidden, step) for step in (1, -1, 2)]

    with jax.named_scope("layer_sum"):
        far = slab_dot(hidden, down_weight, slab_pair(2), width, bf16)
        from_left = over_y(far[0], 1)
        from_right = over_y(far[1], -1)
        right = slab_dot(hidden, down_weight, slab_pair(1), width, bf16)
        left = slab_dot(hidden, down_weight, slab_pair(3), width, bf16)
        got_right1 = over_y(right[1], 1)
        got_left0 = over_y(left[0], -1)
        right0 = (right[0].astype(f32) + from_left.astype(f32)).astype(bf16)
        left1 = (left[1].astype(f32) + from_right.astype(f32)).astype(bf16)
        got_right0 = over_y(right0, 1)
        got_left1 = over_y(left1, -1)
        own = slab_dot(hidden, down_weight, slab_pair(0), width, f32)
        other_sum = own[1] + got_right1.astype(f32) + got_left1.astype(f32)
        from_zl = over_zl(other_sum.astype(bf16))
        layer = (
            own[0]
            + resid.astype(f32)
            + got_right0.astype(f32)
            + got_left0.astype(f32)
            + from_zl.astype(f32)
        )

    with jax.named_scope("layer_gather"):
        low_layer = layer.astype(bf16)
        zl_slab = over_zl(low_layer)
        y_slabs = {(0, 0): low_layer, (1, 0): zl_slab}
        for part in (0, 1):
            y_slabs[part, 1] = over_y(y_slabs[part, 0], -1)
            y_slabs[part, 3] = over_y(y_slabs[part, 0], 1)
        y_slabs[0, 2] = over_y(y_slabs[0, 3], 1)
        y_slabs[1, 2] = over_y(y_slabs[1, 1], -1)
        layer_all = jnp.zeros((group, tokens, width), bf16)
        for (part, step), slab in y_slabs.items():
            index = ((zl + part) % NZL) * NY + (y + step) % NY
            layer_all = lax.dynamic_update_slice(layer_all, slab[None], (index, 0, 0))

    with jax.named_scope("layer_exchange"):
        per_x = group // NX
        layer_x = []
        for step in (0, 1, -1, 2):
            first = ((x + step) % NX) * per_x
            block = lax.dynamic_slice_in_dim(layer_all, first, per_x, 0)
            layer_x.append(block if step == 0 else over_x(block, step))

    with jax.named_scope("norm"):
        squares = jnp.sum(layer * layer, axis=1)
        squares = jnp.sum(gather_small(squares, "tensor"), axis=0)
        inverse = lax.rsqrt(squares / model_width + eps_norm)
        means = jnp.mean((layer * inverse[:, None]).reshape(seqs_here, SEQ, width), axis=1)

    with jax.named_scope("contrast"):
        means_all = gather_small(means, "dp").reshape(seqs, width)
        means_full = gather_small(means_all, "tensor")
        owners = jnp.repeat(domain_ids, seqs_here)
        same = (owners[:, None] == owners[None, :]).astype(f32)
        scaled, gain_grad = contrast(means_full, gain, same)
        grad_gain = lax.dynamic_slice_in_dim(gain_grad, rank, 1, 0).reshape(width)

    with jax.named_scope("layer_grad"):
        first_seq = shard * seqs_here
        inverse_col = inverse[:, None]
        low, coef = layer_grad(
            layer_all, scaled, inverse_col, first_seq.astype(jnp.int32).reshape(1)
        )
        grad_resid = lax.dynamic_slice_in_dim(low, rank, 1, 0)[0]

    with jax.named_scope("down_grad"):
        factors = jnp.stack([inverse, coef[:, 0]])
        factors_x = [factors] + [over_x(factors, step) for step in (1, -1, 2)]
        half = width // NCORE
        hidden_rows = jnp.concatenate(hidden_x, axis=0)

        def low_block(part, side):
            slab = (zh + part) % NZH
            column = ((core + side) % NCORE) * half
            blocks = []
            for i, step in enumerate((0, -1, 1, 2)):
                peer = ((x + step) % NX) * (NZH * NCORE) + zh * NCORE + core
                layer_block = lax.dynamic_slice(layer_x[i], (slab, 0, column), (1, tokens, half))[0]
                scaled_block = lax.dynamic_slice(
                    scaled, (x * per_x + slab, peer * seqs_here, column), (1, seqs_here, half)
                )[0]
                wide = jnp.broadcast_to(scaled_block[:, None], (seqs_here, SEQ, half)).reshape(tokens, half)
                blocks.append(
                    (
                        factors_x[i][0][:, None] * wide
                        - layer_block.astype(f32) * factors_x[i][1][:, None]
                    ).astype(bf16)
                )
            return jnp.concatenate(blocks, axis=0)

        def down(part, side):
            return lax.dot_general(
                hidden_rows,
                low_block(part, side),
                (((0,), (0,)), ((), ())),
                preferred_element_type=f32,
            )

        sent = over_core(down(1, 1).astype(bf16))
        across = over_zh((down(1, 0) + sent.astype(f32)).astype(bf16))
        near = over_core(down(0, 1).astype(bf16))
        grad_down = down(0, 0) + near.astype(f32) + across.astype(f32)

    with jax.named_scope("hidden_grad"):
        grad_hidden = hidden_grad(low, down_weight)

    return (grad_hidden, grad_resid, grad_down, grad_gain)


def solution(mesh):
    return jax.shard_map(
        per_device,
        mesh=mesh,
        in_specs=(P("dp", "tensor"), P("dp", "tensor"), P("tensor", None), P(), P()),
        out_specs=(P("dp", "tensor"), P("dp", "tensor"), P("tensor", "dp"), P("tensor")),
        check_vma=False,
    )
```

time: 631 us -> 316 us (0.50)
  waiting for transfers between devices: 442 us -> 126 us
  blocking collectives: 97.9 us -> 0 us
  starting transfers between devices: 0.12 us -> 55.5 us
  local copies, waits for them, and re-layouts: 11.4 us -> 58.2 us
  Pallas kernels: 0 us -> 35.5 us
  matrix products: 44 us -> 23.4 us
  between operations: 14.6 us -> 1.25 us
    psum x1 -> x0, waiting for transfers between devices: 184 us -> none  [per_device(): layer = lax.psum(partial_out, 'tensor')]
    reduce_scatter x1 -> x0, waiting for transfers between devices: 159 us -> none  [per_device(): lax.psum_scatter(down_part, 'dp', scatter_dimension=1, tiled=True)]
    unnamed x4 -> x0, waiting for transfers between devices: 98.6 us -> none
    ppermute x0 -> x26, waiting for transfers between devices: none -> 74.9 us  [the longest x12 37.2 us: over_y(): return lax.ppermute(value, 'tensor', tensor_route(0, step))]
    all_to_all x0 -> x3, waiting for transfers between devices: none -> 51 us  [gather_small(): return lax.all_to_all(copies, axis, 0, 0)]
    psum x1 -> x0, blocking collectives: 38.9 us -> none  [per_device(): grad_gain = lax.psum(gain_terms, 'dp')]
    ppermute x0 -> x26, starting transfers between devices: none -> 37.2 us  [the longest x12 18 us: over_y(): return lax.ppermute(value, 'tensor', tensor_route(0, step))]
    pallas_call x0 -> x7, Pallas kernels: none -> 35.5 us  [the longest x1 14.5 us: hidden_grad(): pl.pallas_call(hidden_grad_kernel, grid=(slabs,), in_specs=[pl.BlockSpec(...]
  transfers between devices with their start and end apart: 3 -> 29, of which waited for: 3 -> 11; matrix products, arithmetic and copies ran while one was open for 3% -> 17% of each run, Pallas kernels for 0% -> 11%
where the time goes in v1:
time: 316 us; the launch traced here: 315 us
  waiting for transfers between devices  126 us (40%)
  local copies, waits for them, and re-layouts  58.2 us (18%)
  starting transfers between devices  55.5 us (18%)
  Pallas kernels  35.5 us (11%)
  matrix products  23.4 us (7%)
  other arithmetic  14.8 us (5%)
    all_to_all x3, waiting for transfers between devices, gather_small(): return lax.all_to_all(copies, axis, 0, 0)  51 us
    ppermute x12, waiting for transfers between devices, over_y(): return lax.ppermute(value, 'tensor', tensor_route(0, step))  37.2 us
    unnamed x41, local copies, waits for them, and re-layouts  34.5 us
    ppermute x9, waiting for transfers between devices, over_x(): return lax.ppermute(value, 'dp', dp_route(step, 0, 0))  25.3 us
    dot_general x4, matrix products, down(): lax.dot_general(hidden_rows, low_block(part, side), (((0,), (0,)), ((), (...  23.4 us
    all_to_all x3, starting transfers between devices, gather_small(): return lax.all_to_all(copies, axis, 0, 0)  18.2 us
    ppermute x12, starting transfers between devices, over_y(): return lax.ppermute(value, 'tensor', tensor_route(0, step))  18 us
    ppermute x9, starting transfers between devices, over_x(): return lax.ppermute(value, 'dp', dp_route(step, 0, 0))  15.9 us
  transfers between devices with their start and end apart: 29, of which 11 were waited for; matrix products, arithmetic and copies ran while one was open for 17% of the time, Pallas kernels for 11%

profile of v1, /device:TPU:0, one launch (start us, length us, event | category | flops | bytes accessed | tf_op | source)
XLA Modules:
  0.0 314.5 jit_solution(1111653867513207678)
XLA Ops:
  2.4 5.2 %copy-done = bf16[1792,4096]{1,0:T(8,128)(2,1)S(1)} copy-done((bf16[1792,4096]{1,0:T(8,128)(2,1)S(1)}, bf16[1792,4096]{1,0:T(8,128)(2,1)}, u32[]{:S(2)}) %copy-start) | copy-done | bytes 14680088
  9.0 3.1 layer_sum.6
  13.2 3.0 collective-permute-start.4
  16.3 5.2 %copy-done.1 = bf16[1792,4096]{1,0:T(8,128)(2,1)S(1)} copy-done((bf16[1792,4096]{1,0:T(8,128)(2,1)S(1)}, bf16[1792,4096]{1,0:T(8,128)(2,1)}, u32[]{:S(2)}) %copy-start.1) | copy-done | bytes 14680088
  21.4 3.1 layer_sum.5
  25.5 5.2 %copy-done.2 = bf16[1792,4096]{1,0:T(8,128)(2,1)S(1)} copy-done((bf16[1792,4096]{1,0:T(8,128)(2,1)S(1)}, bf16[1792,4096]{1,0:T(8,128)(2,1)}, u32[]{:S(2)}) %copy-start.2) | copy-done | bytes 14680088
  30.6 3.1 layer_sum.7
  35.6 3.2 %collective-permute-start.2 = (bf16[512,512]{1,0:T(8,128)(2,1)}, bf16[512,512]{1,0:T(8,128)(2,1)}, u32[]{:S(2)}, u32[]{:S(2)}) collective-permute-start(bf16[512,512]{1,0:T(8,128)(2,1)} %slice_bitcast_fusion.5), channel_id=1, source_target_pairs={{0,3},{1,0},{2,1},{3,2},{4,7},{5,4},{6,5},{7,6},{8,11},{9,8},{10,9... | collective-permute-start | bytes 1572872 | tf_op jit(solution)/shard_map/layer_sum/ppermute | solution.py:53
  40.0 3.3 %collective-permute-start.5 = (bf16[512,512]{1,0:T(8,128)(2,1)S(1)}, bf16[512,512]{1,0:T(8,128)(2,1)S(1)}, u32[]{:S(2)}, u32[]{:S(2)}) collective-permute-start(bf16[512,512]{1,0:T(8,128)(2,1)S(1)} %fusion.37), channel_id=1, source_target_pairs={{0,3},{1,0},{2,1},{3,2},{4,7},{5,4},{6,5},{7,6},{8,11},{9,8},{10,9... | collective-permute-start | bytes 1572872 | tf_op jit(solution)/shard_map/layer_sum/ppermute | solution.py:53
  43.4 5.2 %copy-done.3 = bf16[1792,4096]{1,0:T(8,128)(2,1)S(1)} copy-done((bf16[1792,4096]{1,0:T(8,128)(2,1)S(1)}, bf16[1792,4096]{1,0:T(8,128)(2,1)}, u32[]{:S(2)}) %copy-start.3) | copy-done | bytes 14680088
  48.5 3.1 layer_sum.4
  54.2 6.4 %collective-permute-done.5 = bf16[512,512]{1,0:T(8,128)(2,1)S(1)} collective-permute-done((bf16[512,512]{1,0:T(8,128)(2,1)S(1)}, bf16[512,512]{1,0:T(8,128)(2,1)S(1)}, u32[]{:S(2)}, u32[]{:S(2)}) %collective-permute-start.5) | collective-permute-done | bytes 524320 | tf_op jit(solution)/shard_map/layer_sum/ppermute | solution.py:53
  61.9 2.0 collective-permute-start.6
  69.0 5.1 %collective-permute-done.6 = bf16[512,512]{1,0:T(8,128)(2,1)} collective-permute-done((bf16[512,512]{1,0:T(8,128)(2,1)S(1)}, bf16[512,512]{1,0:T(8,128)(2,1)}, u32[]{:S(2)}, u32[]{:S(2)}) %collective-permute-start.6) | collective-permute-done | bytes 524320 | tf_op jit(solution)/shard_map/layer_sum/ppermute | solution.py:57
  74.2 2.0 multiply_reduce_fusion
  76.8 6.1 %all-to-all-start = ((f32[8,1,512]{2,1,0:T(1,128)}), f32[8,1,512]{2,1,0:T(1,128)S(1)}, u32[]{:S(2)}, u32[]{:S(2)}) async-start(f32[8,1,512]{2,1,0:T(1,128)} %broadcast_in_dim.172), calls=%async_computation | async-start | bytes 32768 | tf_op jit(solution)/shard_map/norm/all_to_all | solution.py:63
  83.3 5.8 %all-to-all-done = f32[8,1,512]{2,1,0:T(1,128)S(1)} async-done(((f32[8,1,512]{2,1,0:T(1,128)}), f32[8,1,512]{2,1,0:T(1,128)S(1)}, u32[]{:S(2)}, u32[]{:S(2)}) %all-to-all-start) | async-done | bytes 16416 | tf_op jit(solution)/shard_map/norm/all_to_all | solution.py:63
  90.0 7.1 %all-to-all-start.1 = ((f32[16,4,512]{2,1,0:T(4,128)}), f32[16,4,512]{2,1,0:T(4,128)S(1)}, u32[]{:S(2)}, u32[]{:S(2)}) async-start(f32[16,4,512]{2,1,0:T(4,128)} %broadcast_in_dim.173), calls=%async_computation.1 | async-start | bytes 262144 | tf_op jit(solution)/shard_map/contrast/all_to_all | solution.py:63
  97.1 2.3 broadcast_in_dim.163
  101.8 45.1 %all-to-all-done.1 = f32[16,4,512]{2,1,0:T(4,128)S(1)} async-done(((f32[16,4,512]{2,1,0:T(4,128)}), f32[16,4,512]{2,1,0:T(4,128)S(1)}, u32[]{:S(2)}, u32[]{:S(2)}) %all-to-all-start.1) | async-done | bytes 131104 | tf_op jit(solution)/shard_map/contrast/all_to_all | solution.py:63
  148.1 5.0 %all-to-all-start.2 = ((f32[8,64,512]{2,1,0:T(8,128)}), f32[8,64,512]{2,1,0:T(8,128)S(1)}, u32[]{:S(2)}, u32[]{:S(2)}) async-start(f32[8,64,512]{2,1,0:T(8,128)} %broadcast_in_dim.175), calls=%async_computation.2 | async-start | bytes 2097152 | tf_op jit(solution)/shard_map/contrast/all_to_all | solution.py:63
  153.1 2.0 collective-permute-start.9
  155.1 2.8 constant_dynamic-update-slice_fusion.2
  157.9 2.9 constant_dynamic-update-slice_fusion.1
  162.8 17.0 %collective-permute-done.9 = bf16[512,512]{1,0:T(8,128)(2,1)S(1)} collective-permute-done((bf16[512,512]{1,0:T(8,128)(2,1)}, bf16[512,512]{1,0:T(8,128)(2,1)S(1)}, u32[]{:S(2)}, u32[]{:S(2)}) %collective-permute-start.9) | collective-permute-done | bytes 524320 | tf_op jit(solution)/shard_map/layer_gather/ppermute | solution.py:53
  181.9 1.9 bitcast_dynamic-update-slice_fusion.5
  184.7 3.0 collective-permute-start.13
  188.5 2.6 collective-permute-done.11
  191.9 10.0 %collective-permute-done.12 = bf16[512,512]{1,0:T(8,128)(2,1)S(1)} collective-permute-done((bf16[512,512]{1,0:T(8,128)(2,1)S(1)}, bf16[512,512]{1,0:T(8,128)(2,1)S(1)}, u32[]{:S(2)}, u32[]{:S(2)}) %collective-permute-start.12) | collective-permute-done | bytes 524320 | tf_op jit(solution)/shard_map/layer_gather/ppermute | solution.py:53
  203.6 3.6 %constant_dynamic-slice_fusion.3 = (bf16[2,512,512]{2,1,0:T(8,128)(2,1)}, bf16[2,512,512]{2,1,0:T(8,128)(2,1)}, bf16[2,512,512]{2,1,0:T(8,128)(2,1)}) fusion(bf16[8,512,512]{2,1,0:T(8,128)(2,1)} %bitcast_dynamic-update-slice_fusion.layer_ref, s32[]{:T(128)S(6)} %select_n.334, s32[]{:T(128)S(6)} %select_n.339, s32[]{:T(128)S(6)} %select_n.336), kind=kLoop, calls=%fused_computation.137 | loop fusion | bytes 6291468 | tf_op jit(solution)/shard_map/layer_exchange/dynamic_slice | solution.py:287
  207.2 2.7 collective-permute-start.22
  209.9 1.9 collective-permute-start.20
  211.9 2.9 constant_dynamic-update-slice_fusion
  217.0 3.8 %contrast.1 = (f32[8,64,512]{2,1,0:T(8,128)S(1)}, f32[8,1,512]{2,1,0:T(1,128)S(1)}) custom-call(f32[8,64,512]{2,1,0:T(8,128)S(1)} %copy-done.10, f32[8,1,512]{2,1,0:T(1,128)S(1)} %bitcast.227, f32[64,64]{1,0:T(8,128)S(1)} %compare_convert_fusion.same_ref), custom_call_target="tpu_custom_call" | custom-call | flops 402653184 | bytes 2097152 | tf_op jit(solution)/shard_map/contrast/pallas_call | solution.py:130
  220.8 4.7 %layer_grad.1 = (bf16[8,512,512]{2,1,0:T(8,128)(2,1)S(1)}, f32[512,1]{1,0:T(8,128)S(1)}) custom-call(s32[1]{0:T(128)} %bitcast.first_ref, bf16[8,512,512]{2,1,0:T(8,128)(2,1)} %bitcast_dynamic-update-slice_fusion.layer_ref, f32[8,64,512]{2,1,0:T(8,128)S(1)} %get-tuple-element.8.scaled_ref, f32[512,1]{1,0:T(8,128)S(1)} %copy.12.inverse_ref), custom_call_target="tpu_custom_call" | custom-call | flops 12582912 | bytes 8388608 | tf_op jit(solution)/shard_map/layer_grad/pallas_call | solution.py:165
  225.6 2.0 copy-done.11
  229.2 2.6 collective-permute-start.19
  231.8 2.0 fusion.70
  233.9 22.4 %collective-permute-done.21 = f32[2,512]{1,0:T(2,128)S(1)} collective-permute-done((f32[2,512]{1,0:T(2,128)S(1)}, f32[2,512]{1,0:T(2,128)S(1)}, u32[]{:S(2)}, u32[]{:S(2)}) %collective-permute-start.21) | collective-permute-done | bytes 4128 | tf_op jit(solution)/shard_map/down_grad/ppermute | solution.py:41
  256.3 2.0 collective-permute-start.17
  258.3 2.8 collective-permute-done.17
  264.3 2.3 fusion.68
  266.6 6.1 %convolution_convert_fusion = bf16[1792,256]{1,0:T(8,128)(2,1)} fusion(bf16[2048,1792]{1,0:T(8,128)(2,1)} %constant_dynamic-update-slice_fusion, bf16[512,256]{1,0:T(8,128)(2,1)S(1)} %get-tuple-element.34, bf16[512,256]{1,0:T(8,128)(2,1)S(1)} %get-tuple-element.30, bf16[512,256]{1,0:T(8,128)(2,1)S(1)} %get-tuple-element.26, ...), kind=kOutput, calls=%fused_computation.3 | convolution fusion | flops 1883701248 | bytes 9306112 | tf_op jit(solution)/shard_map/down_grad/dot_general | solution.py:338
  272.7 5.3 %convolution_convert_fusion.1 = bf16[1792,256]{1,0:T(8,128)(2,1)S(1)} fusion(bf16[2048,1792]{1,0:T(8,128)(2,1)} %constant_dynamic-update-slice_fusion, bf16[512,256]{1,0:T(8,128)(2,1)S(1)} %get-tuple-element.32, bf16[512,256]{1,0:T(8,128)(2,1)S(1)} %get-tuple-element.28, bf16[512,256]{1,0:T(8,128)(2,1)} %get-tuple-element.24, ...), kind=kOutput, calls=%fused_computation.4 | convolution fusion | flops 1883701248 | bytes 9306112 | tf_op jit(solution)/shard_map/down_grad/dot_general | solution.py:338
  278.7 5.5 %fusion.1 = bf16[1792,256]{1,0:T(8,128)(2,1)S(1)} fusion(bf16[2048,1792]{1,0:T(8,128)(2,1)} %constant_dynamic-update-slice_fusion, bf16[1792,256]{1,0:T(8,128)(2,1)} %collective-permute-done.24, bf16[512,256]{1,0:T(8,128)(2,1)S(1)} %get-tuple-element.33, bf16[512,256]{1,0:T(8,128)(2,1)S(1)} %get-tuple-element.29, ...), kind=kOutput, calls=%fused_computation.5 | convolution fusion | flops 1884618752 | bytes 10223616 | tf_op jit(solution)/shard_map/down_grad/dot_general | solution.py:338
  286.4 14.5 %hidden_grad.1 = bf16[512,1792]{1,0:T(8,128)(2,1)} custom-call(bf16[8,512,512]{2,1,0:T(8,128)(2,1)S(1)} %copy-done.12, bf16[1792,4096]{1,0:T(8,128)(2,1)S(1)} %bitcast.226), custom_call_target="tpu_custom_call" | custom-call | flops 7516192768 | bytes 20709376 | tf_op jit(solution)/shard_map/hidden_grad/pallas_call | solution.py:206
  300.9 7.2 %collective-permute-done.25 = bf16[1792,256]{1,0:T(8,128)(2,1)S(1)} collective-permute-done((bf16[1792,256]{1,0:T(8,128)(2,1)S(1)}, bf16[1792,256]{1,0:T(8,128)(2,1)S(1)}, u32[]{:S(2)}, u32[]{:S(2)}) %collective-permute-start.25) | collective-permute-done | bytes 917536 | tf_op jit(solution)/shard_map/down_grad/ppermute | solution.py:45
  308.1 6.4 %fusion = f32[1792,256]{1,0:T(8,128)} fusion(bf16[2048,1792]{1,0:T(8,128)(2,1)} %constant_dynamic-update-slice_fusion, bf16[1792,256]{1,0:T(8,128)(2,1)S(1)} %collective-permute-done.25, bf16[1792,256]{1,0:T(8,128)(2,1)S(1)} %collective-permute-done.23, bf16[512,256]{1,0:T(8,128)(2,1)S(1)} %get-tuple-element.31, bf16[512,256]{1,0:T(8,128)(2,1)S(1)} %get-tuple-element.27, ...), kind=kOutput, calls=%fused_computation.2 | convolution fusion | flops 1885077504 | bytes 12058624 | tf_op jit(solution)/shard_map/down_grad/dot_general | solution.py:338
  (109 shorter events, 40.5 us)
Async XLA Ops:
  0.6 152.5 %collective-permute-start.14 = (bf16[512,1792]{1,0:T(8,128)(2,1)}, bf16[512,1792]{1,0:T(8,128)(2,1)}, u32[]{:S(2)}, u32[]{:S(2)}) collective-permute-start(bf16[512,1792]{1,0:T(8,128)(2,1)} %hidden_ref.7), channel_id=1, source_target_pairs={{0,32},{8,40},{16,48},{24,56},{32,64},{40,72},{48,80},{56,88},{64,... | collective-permute-start | bytes 5505032 | tf_op jit(solution)/shard_map/hidden_exchange/ppermute | solution.py:41
  2.3 5.2 %copy-start = (bf16[1792,4096]{1,0:T(8,128)(2,1)S(1)}, bf16[1792,4096]{1,0:T(8,128)(2,1)}, u32[]{:S(2)}) copy-start(bf16[1792,4096]{1,0:T(8,128)(2,1)} %weight_ref.9) | copy-start | bytes 44040196
  7.5 1.5 copy-start.4
  9.0 7.2 %copy-start.5 = (bf16[512,1792]{1,0:T(8,128)(2,1)S(1)}, bf16[512,1792]{1,0:T(8,128)(2,1)}, u32[]{:S(2)}) copy-start(bf16[512,1792]{1,0:T(8,128)(2,1)} %hidden_ref.7) | copy-start | bytes 5505028
  13.2 25.6 %collective-permute-start.4 = (bf16[512,512]{1,0:T(8,128)(2,1)}, bf16[512,512]{1,0:T(8,128)(2,1)S(1)}, u32[]{:S(2)}, u32[]{:S(2)}) collective-permute-start(bf16[512,512]{1,0:T(8,128)(2,1)} %get-tuple-element.52), channel_id=1, source_target_pairs={{0,3},{1,0},{2,1},{3,2},{4,7},{5,4},{6,5},{7,6},{8,11},{9,8},{10,9... | collective-permute-start | bytes 1572872 | tf_op jit(solution)/shard_map/layer_sum/ppermute | solution.py:53
  16.3 5.2 %copy-start.1 = (bf16[1792,4096]{1,0:T(8,128)(2,1)S(1)}, bf16[1792,4096]{1,0:T(8,128)(2,1)}, u32[]{:S(2)}) copy-start(bf16[1792,4096]{1,0:T(8,128)(2,1)} %weight_ref.9) | copy-start | bytes 44040196
  25.4 28.8 %collective-permute-start.3 = (bf16[512,512]{1,0:T(8,128)(2,1)}, bf16[512,512]{1,0:T(8,128)(2,1)}, u32[]{:S(2)}, u32[]{:S(2)}) collective-permute-start(bf16[512,512]{1,0:T(8,128)(2,1)} %slice_bitcast_fusion.4), channel_id=1, source_target_pairs={{0,1},{1,2},{2,3},{3,0},{4,5},{5,6},{6,7},{7,4},{8,9},{9,10},{10,1... | collective-permute-start | bytes 1572872 | tf_op jit(solution)/shard_map/layer_sum/ppermute | solution.py:53
  25.5 5.2 %copy-start.2 = (bf16[1792,4096]{1,0:T(8,128)(2,1)S(1)}, bf16[1792,4096]{1,0:T(8,128)(2,1)}, u32[]{:S(2)}) copy-start(bf16[1792,4096]{1,0:T(8,128)(2,1)} %weight_ref.9) | copy-start | bytes 44040196
  33.8 1.0 copy-start.8
  35.6 31.6 %collective-permute-start.2 = (bf16[512,512]{1,0:T(8,128)(2,1)}, bf16[512,512]{1,0:T(8,128)(2,1)}, u32[]{:S(2)}, u32[]{:S(2)}) collective-permute-start(bf16[512,512]{1,0:T(8,128)(2,1)} %slice_bitcast_fusion.5), channel_id=1, source_target_pairs={{0,3},{1,0},{2,1},{3,2},{4,7},{5,4},{6,5},{7,6},{8,11},{9,8},{10,9... | collective-permute-start | bytes 1572872 | tf_op jit(solution)/shard_map/layer_sum/ppermute | solution.py:53
  38.8 14.1 %collective-permute-start = (bf16[512,512]{1,0:T(8,128)(2,1)}, bf16[512,512]{1,0:T(8,128)(2,1)}, u32[]{:S(2)}, u32[]{:S(2)}) collective-permute-start(bf16[512,512]{1,0:T(8,128)(2,1)} %get-tuple-element.51), channel_id=1, source_target_pairs={{0,1},{1,2},{2,3},{3,0},{4,5},{5,6},{6,7},{7,4},{8,9},{9,10},{10,1... | collective-permute-start | bytes 1572872 | tf_op jit(solution)/shard_map/layer_sum/ppermute | solution.py:53
  40.0 20.6 %collective-permute-start.5 = (bf16[512,512]{1,0:T(8,128)(2,1)S(1)}, bf16[512,512]{1,0:T(8,128)(2,1)S(1)}, u32[]{:S(2)}, u32[]{:S(2)}) collective-permute-start(bf16[512,512]{1,0:T(8,128)(2,1)S(1)} %fusion.37), channel_id=1, source_target_pairs={{0,3},{1,0},{2,1},{3,2},{4,7},{5,4},{6,5},{7,6},{8,11},{9,8},{10,9... | collective-permute-start | bytes 1572872 | tf_op jit(solution)/shard_map/layer_sum/ppermute | solution.py:53
  43.4 5.2 %copy-start.3 = (bf16[1792,4096]{1,0:T(8,128)(2,1)S(1)}, bf16[1792,4096]{1,0:T(8,128)(2,1)}, u32[]{:S(2)}) copy-start(bf16[1792,4096]{1,0:T(8,128)(2,1)} %weight_ref.9) | copy-start | bytes 44040196
  51.7 10.2 %copy-start.6 = (f32[2,512,512]{2,1,0:T(8,128)}, f32[2,512,512]{2,1,0:T(8,128)S(1)}, u32[]{:S(2)}) copy-start(f32[2,512,512]{2,1,0:T(8,128)S(1)} %layer_sum.4) | copy-start | bytes 6291460
  51.7 14.0 %copy-start.14 = (s32[16]{0:T(128)S(1)}, s32[16]{0:T(128)}, u32[]{:S(2)}) copy-start(s32[16]{0:T(128)} %param.9) | copy-start | bytes 196
  54.1 15.0 %collective-permute-start.1 = (bf16[512,512]{1,0:T(8,128)(2,1)S(1)}, bf16[512,512]{1,0:T(8,128)(2,1)}, u32[]{:S(2)}, u32[]{:S(2)}) collective-permute-start(bf16[512,512]{1,0:T(8,128)(2,1)S(1)} %fusion.38), channel_id=1, source_target_pairs={{0,1},{1,2},{2,3},{3,0},{4,5},{5,6},{6,7},{7,4},{8,9},{9,10},{10,1... | collective-permute-start | bytes 1572872 | tf_op jit(solution)/shard_map/layer_sum/ppermute | solution.py:53
  61.9 12.3 %collective-permute-start.6 = (bf16[512,512]{1,0:T(8,128)(2,1)S(1)}, bf16[512,512]{1,0:T(8,128)(2,1)}, u32[]{:S(2)}, u32[]{:S(2)}) collective-permute-start(bf16[512,512]{1,0:T(8,128)(2,1)S(1)} %fusion.4), channel_id=1, source_target_pairs={{0,4},{1,5},{2,6},{3,7},{4,0},{5,1},{6,2},{7,3},{8,12},{9,13},{10,... | collective-permute-start | bytes 1572872 | tf_op jit(solution)/shard_map/layer_sum/ppermute | solution.py:57
  63.9 94.1 %collective-permute-start.15 = (bf16[512,1792]{1,0:T(8,128)(2,1)S(1)}, bf16[512,1792]{1,0:T(8,128)(2,1)}, u32[]{:S(2)}, u32[]{:S(2)}) collective-permute-start(bf16[512,1792]{1,0:T(8,128)(2,1)S(1)} %copy-done.5), channel_id=1, source_target_pairs={{0,96},{8,104},{16,112},{24,120},{32,0},{40,8},{48,16},{56,24},{64... | collective-permute-start | bytes 5505032 | tf_op jit(solution)/shard_map/hidden_exchange/ppermute | solution.py:41
  65.8 8.4 %copy-start.7 = (f32[2,512,512]{2,1,0:T(8,128)S(1)}, f32[2,512,512]{2,1,0:T(8,128)}, u32[]{:S(2)}) copy-start(f32[2,512,512]{2,1,0:T(8,128)} %copy-done.6) | copy-start | bytes 6291460
  67.2 144.7 %collective-permute-start.16 = (bf16[512,1792]{1,0:T(8,128)(2,1)S(1)}, bf16[512,1792]{1,0:T(8,128)(2,1)}, u32[]{:S(2)}, u32[]{:S(2)}) collective-permute-start(bf16[512,1792]{1,0:T(8,128)(2,1)S(1)} %copy-done.5), channel_id=1, source_target_pairs={{0,64},{8,72},{16,80},{24,88},{32,96},{40,104},{48,112},{56,120},{... | collective-permute-start | bytes 5505032 | tf_op jit(solution)/shard_map/hidden_exchange/ppermute | solution.py:41
  76.8 12.4 %all-to-all-start = ((f32[8,1,512]{2,1,0:T(1,128)}), f32[8,1,512]{2,1,0:T(1,128)S(1)}, u32[]{:S(2)}, u32[]{:S(2)}) async-start(f32[8,1,512]{2,1,0:T(1,128)} %broadcast_in_dim.172), calls=%async_computation | async-start | bytes 32768 | tf_op jit(solution)/shard_map/norm/all_to_all | solution.py:63
  90.0 57.0 %all-to-all-start.1 = ((f32[16,4,512]{2,1,0:T(4,128)}), f32[16,4,512]{2,1,0:T(4,128)S(1)}, u32[]{:S(2)}, u32[]{:S(2)}) async-start(f32[16,4,512]{2,1,0:T(4,128)} %broadcast_in_dim.173), calls=%async_computation.1 | async-start | bytes 262144 | tf_op jit(solution)/shard_map/contrast/all_to_all | solution.py:63
  100.5 60.3 %collective-permute-start.7 = (bf16[512,512]{1,0:T(8,128)(2,1)}, bf16[512,512]{1,0:T(8,128)(2,1)}, u32[]{:S(2)}, u32[]{:S(2)}) collective-permute-start(bf16[512,512]{1,0:T(8,128)(2,1)} %get-tuple-element.15), channel_id=1, source_target_pairs={{0,4},{1,5},{2,6},{3,7},{4,0},{5,1},{6,2},{7,3},{8,12},{9,13},{10,... | collective-permute-start | bytes 1572872 | tf_op jit(solution)/shard_map/layer_gather/ppermute | solution.py:57
  100.5 81.4 %collective-permute-start.8 = (bf16[512,512]{1,0:T(8,128)(2,1)}, bf16[512,512]{1,0:T(8,128)(2,1)}, u32[]{:S(2)}, u32[]{:S(2)}) collective-permute-start(bf16[512,512]{1,0:T(8,128)(2,1)} %get-tuple-element.15), channel_id=1, source_target_pairs={{0,3},{1,0},{2,1},{3,2},{4,7},{5,4},{6,5},{7,6},{8,11},{9,8},{10,9... | collective-permute-start | bytes 1572872 | tf_op jit(solution)/shard_map/layer_gather/ppermute | solution.py:53
  148.1 66.7 %all-to-all-start.2 = ((f32[8,64,512]{2,1,0:T(8,128)}), f32[8,64,512]{2,1,0:T(8,128)S(1)}, u32[]{:S(2)}, u32[]{:S(2)}) async-start(f32[8,64,512]{2,1,0:T(8,128)} %broadcast_in_dim.175), calls=%async_computation.2 | async-start | bytes 2097152 | tf_op jit(solution)/shard_map/contrast/all_to_all | solution.py:63
  153.1 26.8 %collective-permute-start.9 = (bf16[512,512]{1,0:T(8,128)(2,1)}, bf16[512,512]{1,0:T(8,128)(2,1)S(1)}, u32[]{:S(2)}, u32[]{:S(2)}) collective-permute-start(bf16[512,512]{1,0:T(8,128)(2,1)} %get-tuple-element.15), channel_id=1, source_target_pairs={{0,1},{1,2},{2,3},{3,0},{4,5},{5,6},{6,7},{7,4},{8,9},{9,10},{10,1... | collective-permute-start | bytes 1572872 | tf_op jit(solution)/shard_map/layer_gather/ppermute | solution.py:53
  160.8 23.9 %collective-permute-start.10 = (bf16[512,512]{1,0:T(8,128)(2,1)}, bf16[512,512]{1,0:T(8,128)(2,1)S(1)}, u32[]{:S(2)}, u32[]{:S(2)}) collective-permute-start(bf16[512,512]{1,0:T(8,128)(2,1)} %collective-permute-done.7), channel_id=1, source_target_pairs={{0,3},{1,0},{2,1},{3,2},{4,7},{5,4},{6,5},{7,6},{8,11},{9,8},{10,9... | collective-permute-start | bytes 1572872 | tf_op jit(solution)/shard_map/layer_gather/ppermute | solution.py:53
  162.1 29.0 %collective-permute-start.11 = (bf16[512,512]{1,0:T(8,128)(2,1)}, bf16[512,512]{1,0:T(8,128)(2,1)S(1)}, u32[]{:S(2)}, u32[]{:S(2)}) collective-permute-start(bf16[512,512]{1,0:T(8,128)(2,1)} %collective-permute-done.7), channel_id=1, source_target_pairs={{0,1},{1,2},{2,3},{3,0},{4,5},{5,6},{6,7},{7,4},{8,9},{9,10},{10,1... | collective-permute-start | bytes 1572872 | tf_op jit(solution)/shard_map/layer_gather/ppermute | solution.py:53
  179.9 22.1 %collective-permute-start.12 = (bf16[512,512]{1,0:T(8,128)(2,1)S(1)}, bf16[512,512]{1,0:T(8,128)(2,1)S(1)}, u32[]{:S(2)}, u32[]{:S(2)}) collective-permute-start(bf16[512,512]{1,0:T(8,128)(2,1)S(1)} %collective-permute-done.9), channel_id=1, source_target_pairs={{0,1},{1,2},{2,3},{3,0},{4,5},{5,6},{6,7},{7,4},{8,9},{9,10},{10,1... | collective-permute-start | bytes 1572872 | tf_op jit(solution)/shard_map/layer_gather/ppermute | solution.py:53
  184.7 18.1 %collective-permute-start.13 = (bf16[512,512]{1,0:T(8,128)(2,1)S(1)}, bf16[512,512]{1,0:T(8,128)(2,1)S(1)}, u32[]{:S(2)}, u32[]{:S(2)}) collective-permute-start(bf16[512,512]{1,0:T(8,128)(2,1)S(1)} %collective-permute-done.10), channel_id=1, source_target_pairs={{0,3},{1,0},{2,1},{3,2},{4,7},{5,4},{6,5},{7,6},{8,11},{9,8},{10,9... | collective-permute-start | bytes 1572872 | tf_op jit(solution)/shard_map/layer_gather/ppermute | solution.py:53
  203.6 12.2 %copy-start.13 = (f32[4096]{0:T(1024)S(1)}, f32[4096]{0:T(1024)}, u32[]{:S(2)}) copy-start(f32[4096]{0:T(1024)} %param.8) | copy-start | bytes 49156
  207.2 53.9 %collective-permute-start.22 = (bf16[2,512,512]{2,1,0:T(8,128)(2,1)}, bf16[2,512,512]{2,1,0:T(8,128)(2,1)}, u32[]{:S(2)}, u32[]{:S(2)}) collective-permute-start(bf16[2,512,512]{2,1,0:T(8,128)(2,1)} %get-tuple-element.21), channel_id=1, source_target_pairs={{0,64},{8,72},{16,80},{24,88},{32,96},{40,104},{48,112},{56,120},{... | collective-permute-start | bytes 3145736 | tf_op jit(solution)/shard_map/layer_exchange/ppermute | solution.py:41
  209.9 52.8 %collective-permute-start.20 = (bf16[2,512,512]{2,1,0:T(8,128)(2,1)}, bf16[2,512,512]{2,1,0:T(8,128)(2,1)}, u32[]{:S(2)}, u32[]{:S(2)}) collective-permute-start(bf16[2,512,512]{2,1,0:T(8,128)(2,1)} %get-tuple-element.22), channel_id=1, source_target_pairs={{0,96},{8,104},{16,112},{24,120},{32,0},{40,8},{48,16},{56,24},{64... | collective-permute-start | bytes 3145736 | tf_op jit(solution)/shard_map/layer_exchange/ppermute | solution.py:41
  211.8 52.5 %collective-permute-start.18 = (bf16[2,512,512]{2,1,0:T(8,128)(2,1)}, bf16[2,512,512]{2,1,0:T(8,128)(2,1)}, u32[]{:S(2)}, u32[]{:S(2)}) collective-permute-start(bf16[2,512,512]{2,1,0:T(8,128)(2,1)} %get-tuple-element.20), channel_id=1, source_target_pairs={{0,32},{8,40},{16,48},{24,56},{32,64},{40,72},{48,80},{56,88},{64,... | collective-permute-start | bytes 3145736 | tf_op jit(solution)/shard_map/layer_exchange/ppermute | solution.py:41
  214.8 1.0 copy-start.9
  215.8 1.2 copy-start.10
  225.6 2.0 copy-start.11
  227.7 28.6 %collective-permute-start.21 = (f32[2,512]{1,0:T(2,128)S(1)}, f32[2,512]{1,0:T(2,128)S(1)}, u32[]{:S(2)}, u32[]{:S(2)}) collective-permute-start(f32[2,512]{1,0:T(2,128)S(1)} %pad_maximum_fusion), channel_id=1, source_target_pairs={{0,64},{8,72},{16,80},{24,88},{32,96},{40,104},{48,112},{56,120},{... | collective-permute-start | bytes 12296 | tf_op jit(solution)/shard_map/down_grad/ppermute | solution.py:41
  229.2 29.0 %collective-permute-start.19 = (f32[2,512]{1,0:T(2,128)S(1)}, f32[2,512]{1,0:T(2,128)S(1)}, u32[]{:S(2)}, u32[]{:S(2)}) collective-permute-start(f32[2,512]{1,0:T(2,128)S(1)} %pad_maximum_fusion), channel_id=1, source_target_pairs={{0,96},{8,104},{16,112},{24,120},{32,0},{40,8},{48,16},{56,24},{64... | collective-permute-start | bytes 12296 | tf_op jit(solution)/shard_map/down_grad/ppermute | solution.py:41
  256.3 4.8 %collective-permute-start.17 = (f32[2,512]{1,0:T(2,128)S(1)}, f32[2,512]{1,0:T(2,128)S(1)}, u32[]{:S(2)}, u32[]{:S(2)}) collective-permute-start(f32[2,512]{1,0:T(2,128)S(1)} %pad_maximum_fusion), channel_id=1, source_target_pairs={{0,32},{8,40},{16,48},{24,56},{32,64},{40,72},{48,80},{56,88},{64,... | collective-permute-start | bytes 12296 | tf_op jit(solution)/shard_map/down_grad/ppermute | solution.py:41
  272.7 5.9 %collective-permute-start.24 = (bf16[1792,256]{1,0:T(8,128)(2,1)}, bf16[1792,256]{1,0:T(8,128)(2,1)}, u32[]{:S(2)}, u32[]{:S(2)}) collective-permute-start(bf16[1792,256]{1,0:T(8,128)(2,1)} %convolution_convert_fusion), channel_id=1, source_target_pairs={{0,8},{8,0},{16,24},{24,16},{32,40},{40,32},{48,56},{56,48},{64,72... | collective-permute-start | bytes 2752520 | tf_op jit(solution)/shard_map/down_grad/ppermute | solution.py:49
  272.7 13.6 %slice-start = ((s8[14680064]{0:T(1024)(128)(4,1)}), s8[4194304]{0:T(1024)(128)(4,1)S(1)}, s32[]{:S(2)}) async-start(s8[14680064]{0:T(1024)(128)(4,1)} %bitcast.225), calls=%async_computation.3 | async-start | bytes 8388608
  272.7 13.6 %slice-start.1 = ((s8[14680064]{0:T(1024)(128)(4,1)}), s8[4194304]{0:T(1024)(128)(4,1)S(1)}, s32[]{:S(2)}) async-start(s8[14680064]{0:T(1024)(128)(4,1)} %bitcast.225), calls=%async_computation.4 | async-start | bytes 8388608
  278.1 22.8 %collective-permute-start.23 = (bf16[1792,256]{1,0:T(8,128)(2,1)S(1)}, bf16[1792,256]{1,0:T(8,128)(2,1)S(1)}, u32[]{:S(2)}, u32[]{:S(2)}) collective-permute-start(bf16[1792,256]{1,0:T(8,128)(2,1)S(1)} %convolution_convert_fusion.1), channel_id=1, source_target_pairs={{0,8},{8,0},{16,24},{24,16},{32,40},{40,32},{48,56},{56,48},{64,72... | collective-permute-start | bytes 2752520 | tf_op jit(solution)/shard_map/down_grad/ppermute | solution.py:49
  278.7 6.9 %copy-start.12 = (bf16[8,512,512]{2,1,0:T(8,128)(2,1)S(1)}, bf16[8,512,512]{2,1,0:T(8,128)(2,1)}, u32[]{:S(2)}) copy-start(bf16[8,512,512]{2,1,0:T(8,128)(2,1)} %copy-done.11) | copy-start | bytes 12582916
  278.7 7.7 %slice-start.2 = ((s8[14680064]{0:T(1024)(128)(4,1)}), s8[4194304]{0:T(1024)(128)(4,1)S(1)}, s32[]{:S(2)}) async-start(s8[14680064]{0:T(1024)(128)(4,1)} %bitcast.225), calls=%async_computation.5 | async-start | bytes 8388608
  278.7 7.7 %slice-start.3 = ((s8[14680064]{0:T(1024)(128)(4,1)}), s8[2097152]{0:T(1024)(128)(4,1)S(1)}, s32[]{:S(2)}) async-start(s8[14680064]{0:T(1024)(128)(4,1)} %bitcast.225), calls=%async_computation.6 | async-start | bytes 4194304
  284.2 23.9 %collective-permute-start.25 = (bf16[1792,256]{1,0:T(8,128)(2,1)S(1)}, bf16[1792,256]{1,0:T(8,128)(2,1)S(1)}, u32[]{:S(2)}, u32[]{:S(2)}) collective-permute-start(bf16[1792,256]{1,0:T(8,128)(2,1)S(1)} %fusion.1), channel_id=1, source_target_pairs={{0,16},{8,24},{16,0},{24,8},{32,48},{40,56},{48,32},{56,40},{64,80... | collective-permute-start | bytes 2752520 | tf_op jit(solution)/shard_map/down_grad/ppermute | solution.py:45

commit v2 on v1

v2 whole, which is shorter than its diff:
```python
import functools
import jax
import jax.numpy as jnp
from jax import lax
from jax.experimental import pallas as pl
from jax.experimental.pallas import tpu as pltpu
from jax.sharding import PartitionSpec as P

SEQ = 128
NX, NZH, NCORE, NZL, NY = 4, 2, 2, 2, 4

score_scale = 20.0
loss_scale = 8192.0
eps_norm = 1e-05
eps_embed = 1e-06
highest = lax.Precision.HIGHEST
f32 = jnp.float32
bf16 = jnp.bfloat16
MIB = 1024 * 1024


def dp_route(dx, dz, dc):
    pairs = []
    for x in range(NX):
        for z in range(NZH):
            for c in range(NCORE):
                to = (((x + dx) % NX) * NZH + (z + dz) % NZH) * NCORE + (c + dc) % NCORE
                pairs.append(((x * NZH + z) * NCORE + c, to))
    return pairs


def tensor_route(dz, dy):
    pairs = []
    for z in range(NZL):
        for y in range(NY):
            pairs.append((z * NY + y, ((z + dz) % NZL) * NY + (y + dy) % NY))
    return pairs


def resid_route(step):
    return [(r, (r % NY % 2) * NY + (r // 2 + step) % NY) for r in range(NZL * NY)]


def over_x(value, step):
    return lax.ppermute(value, "dp", dp_route(step, 0, 0))


def over_zh(value):
    return lax.ppermute(value, "dp", dp_route(0, 1, 0))


def over_core(value):
    return lax.ppermute(value, "dp", dp_route(0, 0, 1))


def over_y(value, step):
    return lax.ppermute(value, "tensor", tensor_route(0, step))


def over_zl(value):
    return lax.ppermute(value, "tensor", tensor_route(1, 0))


def gather_small(value, axis):
    n = lax.axis_size(axis)
    copies = jnp.broadcast_to(value[None], (n,) + value.shape)
    return lax.all_to_all(copies, axis, 0, 0)


def strip_dot_kernel(owner_ref, hidden_ref, *refs):
    *weight_refs, out_ref = refs
    weight = jnp.concatenate([ref[...] for ref in weight_refs], axis=1)
    total = jnp.dot(hidden_ref[...], weight, preferred_element_type=f32)
    lanes = out_ref.shape[-1]
    for b in range(len(weight_refs)):
        out_ref[0, b] = total[:, b * lanes : (b + 1) * lanes].astype(out_ref.dtype)


def strip_dot(hidden, weight, owners, group, out_dtype):
    tokens, units = hidden.shape
    count = owners.shape[0]
    lanes = weight.shape[1] // (NX * group)
    strips = [
        pl.BlockSpec((units, lanes), functools.partial(lambda b, i, s: (0, b * group + s[i]), b))
        for b in range(NX)
    ]
    return pl.pallas_call(
        strip_dot_kernel,
        grid_spec=pltpu.PrefetchScalarGridSpec(
            num_scalar_prefetch=1,
            grid=(count,),
            in_specs=[pl.BlockSpec((tokens, units), lambda i, s: (0, 0))] + strips,
            out_specs=pl.BlockSpec((1, NX, tokens, lanes), lambda i, s: (i, 0, 0, 0)),
        ),
        out_shape=jax.ShapeDtypeStruct((count, NX, tokens, lanes), out_dtype),
        compiler_params=pltpu.CompilerParams(vmem_limit_bytes=56 * MIB),
        cost_estimate=pl.CostEstimate(
            flops=2 * count * tokens * units * NX * lanes,
            bytes_accessed=2 * (tokens * units + count * (units + tokens) * NX * lanes),
            transcendentals=0,
        ),
    )(owners, hidden, *([weight] * NX))


def contrast_kernel(mean_ref, gain_ref, same_ref, scaled_ref, gain_grad_ref):
    slabs, seqs, _ = mean_ref.shape
    rows = lax.broadcasted_iota(jnp.int32, (seqs, seqs), 0)
    cols = lax.broadcasted_iota(jnp.int32, (seqs, seqs), 1)
    across = (((1,), (1,)), ((), ()))
    gram = jnp.zeros((seqs, seqs), f32)
    for b in range(slabs):
        pooled = mean_ref[b] * gain_ref[b]
        gram += lax.dot_general(pooled, pooled, across, precision=highest, preferred_element_type=f32)
    diagonal = jnp.where(rows == cols, gram, 0.0)
    norm_col = jnp.sqrt(jnp.sum(diagonal, axis=1, keepdims=True) + eps_embed)
    norm_row = jnp.sqrt(jnp.sum(diagonal, axis=0, keepdims=True) + eps_embed)
    norms = norm_col * norm_row
    scores = score_scale * gram / norms
    query = rows % 2 == 0
    valid = query & (cols % 2 == 1) & (same_ref[...] > 0.5)
    weights = jnp.where(valid, jnp.exp(scores), 0.0)
    totals = jnp.sum(weights, axis=1, keepdims=True)
    soft = weights / jnp.where(totals > 0.0, totals, 1.0)
    target = jnp.where(query & (cols == rows + 1), 1.0, 0.0)
    d_score = loss_scale * (soft - target)
    both = d_score + d_score.T
    coef = jnp.sum(both * scores, axis=1, keepdims=True)
    mix = score_scale * both / norms - jnp.where(rows == cols, coef / (norm_col * norm_col), 0.0)
    for b in range(slabs):
        gain = gain_ref[b]
        mean = mean_ref[b]
        d_pooled = jnp.dot(mix, mean * gain, precision=highest, preferred_element_type=f32)
        gain_grad_ref[b] = jnp.sum(d_pooled * mean, axis=0, keepdims=True)
        scaled_ref[b] = d_pooled * gain * (1.0 / SEQ)


def contrast(means, gain, same):
    slabs, seqs, width = means.shape
    return pl.pallas_call(
        contrast_kernel,
        out_shape=(
            jax.ShapeDtypeStruct((slabs, seqs, width), f32),
            jax.ShapeDtypeStruct((slabs, 1, width), f32),
        ),
        compiler_params=pltpu.CompilerParams(vmem_limit_bytes=24 * MIB),
        cost_estimate=pl.CostEstimate(
            flops=24 * seqs * seqs * slabs * width, bytes_accessed=8 * slabs * seqs * width, transcendentals=seqs * seqs
        ),
    )(means, gain, same)


def row_to_column(row):
    n = row.shape[1]
    eye = lax.broadcasted_iota(jnp.int32, (n, n), 0) == lax.broadcasted_iota(jnp.int32, (n, n), 1)
    return jnp.sum(jnp.where(eye, jnp.broadcast_to(row, (n, n)), 0.0), axis=1, keepdims=True)


def column_to_row(column):
    n = column.shape[0]
    eye = lax.broadcasted_iota(jnp.int32, (n, n), 0) == lax.broadcasted_iota(jnp.int32, (n, n), 1)
    return jnp.sum(jnp.where(eye, jnp.broadcast_to(column, (n, n)), 0.0), axis=0, keepdims=True)


def layer_grad_kernel(first_ref, layer_ref, scaled_ref, inverse_ref, low_ref, coef_ref):
    group, blocks, _, lanes = layer_ref.shape
    here = pl.program_id(0)
    seq = first_ref[0] + here
    along = None
    for r in range(group):
        scaled = scaled_ref[r, pl.ds(seq, 1), :]
        for b in range(blocks):
            term = layer_ref[r, b].astype(f32) * scaled[:, b * lanes : (b + 1) * lanes]
            along = term if along is None else along + term
    inverse = row_to_column(inverse_ref[pl.ds(here, 1), :])
    model_width = group * blocks * lanes
    coef = inverse * inverse * inverse * jnp.sum(along, axis=1, keepdims=True) / model_width
    coef_ref[pl.ds(here, 1), :] = column_to_row(coef)
    for r in range(group):
        scaled = scaled_ref[r, pl.ds(seq, 1), :]
        for b in range(blocks):
            column = (b * group + r) * lanes
            low_ref[:, column : column + lanes] = (
                inverse * scaled[:, b * lanes : (b + 1) * lanes] - layer_ref[r, b].astype(f32) * coef
            ).astype(bf16)


def layer_grad(strips, scaled, inverse, first):
    group, _, tokens, lanes = strips.shape
    seqs_here = tokens // SEQ
    model_width = group * NX * lanes
    return pl.pallas_call(
        layer_grad_kernel,
        grid_spec=pltpu.PrefetchScalarGridSpec(
            num_scalar_prefetch=1,
            grid=(seqs_here,),
            in_specs=[
                pl.BlockSpec((group, NX, SEQ, lanes), lambda i, s: (0, 0, i, 0)),
                pl.BlockSpec(scaled.shape, lambda i, s: (0, 0, 0)),
                pl.BlockSpec((seqs_here, SEQ), lambda i, s: (0, 0)),
            ],
            out_specs=[
                pl.BlockSpec((SEQ, model_width), lambda i, s: (i, 0)),
                pl.BlockSpec((seqs_here, SEQ), lambda i, s: (0, 0)),
            ],
        ),
        out_shape=(
            jax.ShapeDtypeStruct((tokens, model_width), bf16),
            jax.ShapeDtypeStruct((seqs_here, SEQ), f32),
        ),
        compiler_params=pltpu.CompilerParams(vmem_limit_bytes=24 * MIB),
        cost_estimate=pl.CostEstimate(
            flops=6 * tokens * model_width, bytes_accessed=4 * tokens * model_width, transcendentals=0
        ),
    )(first, strips, scaled, inverse)


def group_grad_kernel(plan_ref, layer_ref, scaled_ref, factor_ref, low_ref):
    group, _, tokens, lanes = layer_ref.shape
    here = pl.program_id(0)
    first, me = plan_ref[4 + here], plan_ref[9]
    seqs_here = tokens // SEQ
    for s in range(seqs_here):
        rows = slice(s * SEQ, (s + 1) * SEQ)
        inverse = row_to_column(factor_ref[here, s : s + 1, :])
        coef = row_to_column(factor_ref[here, seqs_here + s : seqs_here + s + 1, :])
        for r in range(group):
            scaled = scaled_ref[r, pl.ds(first + s, 1), :]
            low = inverse * scaled - layer_ref[r, 0, rows, :].astype(f32) * coef
            side = r % 2 * lanes
            low_ref[(r // 2) ^ me, rows, side : side + lanes] = low.astype(bf16)


def group_grad(strips, scaled, factors, plan):
    group, _, tokens, lanes = strips.shape
    quarter = group * lanes // 4
    return pl.pallas_call(
        group_grad_kernel,
        grid_spec=pltpu.PrefetchScalarGridSpec(
            num_scalar_prefetch=1,
            grid=(NX,),
            in_specs=[
                pl.BlockSpec((group, 1, tokens, lanes), lambda i, s: (0, s[i], 0, 0)),
                pl.BlockSpec(scaled.shape[:2] + (lanes,), lambda i, s: (0, 0, s[8])),
                pl.BlockSpec(factors.shape, lambda i, s: (0, 0, 0)),
            ],
            out_specs=pl.BlockSpec((4, tokens, quarter), lambda i, s: (0, i, 0)),
        ),
        out_shape=jax.ShapeDtypeStruct((4, NX * tokens, quarter), bf16),
        compiler_params=pltpu.CompilerParams(vmem_limit_bytes=24 * MIB),
        cost_estimate=pl.CostEstimate(
            flops=3 * NX * tokens * group * lanes, bytes_accessed=4 * NX * tokens * group * lanes, transcendentals=0
        ),
    )(plan, strips, scaled, factors)


def hidden_grad_kernel(low_ref, weight_ref, out_ref, total_ref):
    step = pl.program_id(0)
    part = lax.dot_general(
        low_ref[...], weight_ref[...], (((1,), (1,)), ((), ())), preferred_element_type=f32
    )

    @pl.when(step == 0)
    def _():
        total_ref[...] = part

    @pl.when(step > 0)
    def _():
        total_ref[...] += part

    @pl.when(step == pl.num_programs(0) - 1)
    def _():
        out_ref[...] = total_ref[...].astype(out_ref.dtype)


def hidden_grad(low, weight, steps):
    tokens, model_width = low.shape
    units = weight.shape[0]
    width = model_width // steps
    return pl.pallas_call(
        hidden_grad_kernel,
        grid=(steps,),
        in_specs=[
            pl.BlockSpec((tokens, width), lambda i: (0, i)),
            pl.BlockSpec((units, width), lambda i: (0, i)),
        ],
        out_specs=pl.BlockSpec((tokens, units), lambda i: (0, 0)),
        out_shape=jax.ShapeDtypeStruct((tokens, units), bf16),
        scratch_shapes=[pltpu.VMEM((tokens, units), f32)],
        compiler_params=pltpu.CompilerParams(vmem_limit_bytes=56 * MIB),
        cost_estimate=pl.CostEstimate(
            flops=2 * tokens * units * model_width,
            bytes_accessed=2 * (tokens * model_width + units * model_width + tokens * units),
            transcendentals=0,
        ),
    )(low, weight)


def per_device(resid, hidden, down_weight, gain, domain_ids):
    tokens, units = hidden.shape
    model_width = down_weight.shape[1]
    group = lax.axis_size("tensor")
    shards = lax.axis_size("dp")
    width = model_width // group
    lanes = width // NX
    seqs_here = tokens // SEQ
    seqs = seqs_here * shards
    rank = lax.axis_index("tensor")
    zl, y = rank // NY, rank % NY
    shard = lax.axis_index("dp")
    x, zh, core = shard // (NZH * NCORE), (shard // NCORE) % NZH, shard % NCORE

    def owners(step):
        column = (y + step) % NY
        return jnp.stack([zl * NY + column, (1 - zl) * NY + column]).astype(jnp.int32)

    with jax.named_scope("hidden_exchange"):
        hidden_left = over_x(hidden, 1)
        hidden_right = over_x(hidden, -1)
        hidden_far = (
            over_x(hidden_left[: tokens // 2], 1),
            over_x(hidden_right[tokens // 2 :], -1),
        )
        hidden_rows = jnp.concatenate((hidden, hidden_left, hidden_right) + hidden_far, axis=0)

    with jax.named_scope("resid_exchange"):
        block = rank // 2
        pieces = []
        for step in range(NY):
            first = ((block + step) % NY) * lanes
            piece = lax.dynamic_slice_in_dim(resid, first, lanes, 1)
            pieces.append(lax.ppermute(piece, "tensor", resid_route(step)))
        pieces = jnp.stack(pieces)
        resid_strips = jnp.concatenate(
            [lax.dynamic_slice_in_dim(pieces, (y - b) % NY, 1, 0) for b in range(NX)], axis=0
        )

    with jax.named_scope("layer_sum"):
        far = strip_dot(hidden, down_weight, owners(2), group, bf16)
        from_left = over_y(far[0], 1)
        from_right = over_y(far[1], -1)
        right = strip_dot(hidden, down_weight, owners(1), group, bf16)
        left = strip_dot(hidden, down_weight, owners(3), group, bf16)
        got_right1 = over_y(right[1], 1)
        got_left0 = over_y(left[0], -1)
        right0 = (right[0].astype(f32) + from_left.astype(f32)).astype(bf16)
        left1 = (left[1].astype(f32) + from_right.astype(f32)).astype(bf16)
        got_right0 = over_y(right0, 1)
        got_left1 = over_y(left1, -1)
        own = strip_dot(hidden, down_weight, owners(0), group, f32)
        other_sum = own[1] + got_right1.astype(f32) + got_left1.astype(f32)
        from_zl = over_zl(other_sum.astype(bf16))
        layer = (
            own[0]
            + resid_strips.astype(f32)
            + got_right0.astype(f32)
            + got_left0.astype(f32)
            + from_zl.astype(f32)
        )

    with jax.named_scope("strip_exchange"):
        low_layer = layer.astype(bf16)
        strips_x = [low_layer]
        for step in (1, -1, 2):
            strip = lax.dynamic_slice_in_dim(low_layer, (x + step) % NX, 1, 0)
            strips_x.append(over_x(strip, step))
        message = jnp.concatenate(strips_x, axis=0)

    with jax.named_scope("norm"):
        squares = jnp.sum(layer * layer, axis=(0, 2))
        squares = jnp.sum(gather_small(squares.reshape(seqs_here, SEQ), "tensor"), axis=0)
        squares, message, hidden_rows = lax.optimization_barrier((squares, message, hidden_rows))
        inverse = lax.rsqrt(squares / model_width + eps_norm)
        weighted = layer.reshape(NX, seqs_here, SEQ, lanes) * inverse[None, :, :, None]
        means = jnp.mean(weighted, axis=2).transpose(1, 0, 2)

    with jax.named_scope("strip_gather"):
        got = {(0, 0): message}
        got[1, 0] = over_zl(message)
        got[0, 1] = over_y(message, -1)
        got[0, 3] = over_y(message, 1)
        means_all = gather_small(means, "dp")
        means_all, got[1, 0], got[0, 1], got[0, 3] = lax.optimization_barrier(
            (means_all, got[1, 0], got[0, 1], got[0, 3])
        )
        means_all = means_all.reshape(seqs, width)
        got[1, 1] = over_y(got[1, 0], -1)
        got[1, 3] = over_y(got[1, 0], 1)
        got[0, 2] = over_y(got[0, 3], 1)
        means_full = gather_small(means_all, "tensor")
        got[1, 2] = over_y(got[1, 1], -1)
        strips = jnp.zeros((group,) + message.shape, bf16)
        for (part, step), value in got.items():
            index = ((zl + part) % NZL) * NY + (y + step) % NY
            strips = lax.dynamic_update_slice(strips, value[None], (index, 0, 0, 0))

    with jax.named_scope("contrast"):
        owner = jnp.repeat(domain_ids, seqs_here)
        same = (owner[:, None] == owner[None, :]).astype(f32)
        gain_strips = gain.reshape(NX, group, lanes).transpose(1, 0, 2).reshape(group, 1, width)
        scaled, gain_grad = contrast(means_full, gain_strips, same)
        gain_grad = gain_grad.reshape(group, NX, lanes)
        grad_gain = lax.dynamic_slice(
            gain_grad, ((rank % 2) * NX, rank // 2, 0), (NX, 1, lanes)
        ).reshape(width)

    with jax.named_scope("layer_grad"):
        first_seq = (shard * seqs_here).astype(jnp.int32)
        low, coef = layer_grad(strips, scaled, inverse, first_seq.reshape(1))
        grad_resid = lax.dynamic_slice_in_dim(low, rank * width, width, 1)

    with jax.named_scope("down_grad"):
        factors = jnp.concatenate([inverse, coef], axis=0)
        factors_x = jnp.stack([factors] + [over_x(factors, step) for step in (1, -1, 2)])
        peers = [((x + step) % NX) * (NZH * NCORE) + zh * NCORE + core for step in (0, -1, 1, 2)]
        plan = [x, NX, NX + 1, NX + 2] + [p * seqs_here for p in peers] + [x, zh * NCORE + core]
        plan = jnp.stack([jnp.asarray(v, jnp.int32) for v in plan])
        low_x = group_grad(strips, scaled, factors_x, plan)

        def down(block):
            return lax.dot_general(
                hidden_rows, low_x[block], (((0,), (0,)), ((), ())), preferred_element_type=f32
            )

        from_core = over_core(down(3))
        across = over_zh((down(2) + from_core).astype(bf16))
        near = down(0) + over_core(down(1))
        near, across = lax.optimization_barrier((near, across))
        grad_down = near + across.astype(f32)

    with jax.named_scope("hidden_grad"):
        grad_hidden = hidden_grad(low, down_weight, group)

    return (grad_hidden, grad_resid, grad_down, grad_gain)


def solution(mesh):
    return jax.shard_map(
        per_device,
        mesh=mesh,
        in_specs=(P("dp", "tensor"), P("dp", "tensor"), P("tensor", None), P(), P()),
        out_specs=(P("dp", "tensor"), P("dp", "tensor"), P("tensor", "dp"), P("tensor")),
        check_vma=False,
    )
```

time: 316 us -> 287 us (0.908)
  waiting for transfers between devices: 126 us -> 77.6 us
  Pallas kernels: 35.5 us -> 54.3 us
  starting transfers between devices: 55.5 us -> 71.1 us
  local copies, waits for them, and re-layouts: 58.2 us -> 47.3 us
  other arithmetic: 14.8 us -> 11.2 us
    all_to_all x3, waiting for transfers between devices: 51 us -> 15.3 us  [gather_small(): return lax.all_to_all(copies, axis, 0, 0)]
    unnamed x41 -> x33, local copies, waits for them, and re-layouts: 34.5 us -> 12 us
    pallas_call x5 -> x6, Pallas kernels: 26.9 us -> 45.7 us  [the longest x4 24.8 us: strip_dot(): pl.pallas_call(strip_dot_kernel, grid_spec=pltpu.PrefetchScalarGridSpec(n...]
    ppermute x0 -> x4, starting transfers between devices: none -> 16.7 us  [per_device(): pieces.append(lax.ppermute(piece, 'tensor', resid_route(step)))]
    ppermute x9 -> x10, waiting for transfers between devices: 25.3 us -> 10.6 us  [over_x(): return lax.ppermute(value, 'dp', dp_route(step, 0, 0))]
    ppermute x1, waiting for transfers between devices: 7.21 us -> 15.9 us  [over_zh(): return lax.ppermute(value, 'dp', dp_route(0, 1, 0))]
    dynamic_update_slice x7 -> x8, local copies, waits for them, and re-layouts: 7.99 us -> 15.2 us  [per_device(): strips = lax.dynamic_update_slice(strips, value[None], (index, 0, 0, 0))]
    convert_element_type x5 -> x2, other arithmetic: 7.52 us -> 2.11 us  [the longest x1 2.03 us: per_device(): low_layer = layer.astype(bf16)]
  transfers between devices with their start and end apart: 29 -> 34, of which waited for: 11 -> 16; matrix products, arithmetic and copies ran while one was open for 17% -> 23% of each run, Pallas kernels for 11% -> 16%
where the time goes in v2:
time: 287 us; the launch traced here: 285 us
  waiting for transfers between devices  77.6 us (27%)
  starting transfers between devices  71.1 us (25%)
  Pallas kernels  54.3 us (19%)
  local copies, waits for them, and re-layouts  47.3 us (16%)
  matrix products  22.4 us (8%)
  other arithmetic  11.2 us (4%)
    ppermute x12, waiting for transfers between devices, over_y(): return lax.ppermute(value, 'tensor', tensor_route(0, step))  34.5 us
    pallas_call x4, Pallas kernels, strip_dot(): pl.pallas_call(strip_dot_kernel, grid_spec=pltpu.PrefetchScalarGridSpec(n...  24.8 us
    dot_general x4, matrix products, down(): lax.dot_general(hidden_rows, low_x[block], (((0,), (0,)), ((), ())), pref...  22.4 us
    ppermute x12, starting transfers between devices, over_y(): return lax.ppermute(value, 'tensor', tensor_route(0, step))  22.2 us
    ppermute x4, starting transfers between devices, per_device(): pieces.append(lax.ppermute(piece, 'tensor', resid_route(step)))  16.7 us
    all_to_all x3, starting transfers between devices, gather_small(): return lax.all_to_all(copies, axis, 0, 0)  16.2 us
    ppermute x1, waiting for transfers between devices, over_zh(): return lax.ppermute(value, 'dp', dp_route(0, 1, 0))  15.9 us
    pallas_call x1, Pallas kernels, hidden_grad(): pl.pallas_call(hidden_grad_kernel, grid=(steps,), in_specs=[pl.BlockSpec(...  15.7 us
  transfers between devices with their start and end apart: 34, of which 16 were waited for; matrix products, arithmetic and copies ran while one was open for 23% of the time, Pallas kernels for 16%

profile of v2, /device:TPU:0, one launch (start us, length us, event | category | flops | bytes accessed | tf_op | source)
XLA Modules:
  0.0 285.0 jit_solution(11528139753539973751)
XLA Ops:
  4.5 6.1 %layer_sum.6 = bf16[2,4,512,128]{3,2,1,0:T(8,128)(2,1)} custom-call(s32[2]{0:T(128)} %pad_add_fusion.2.owner_ref, bf16[512,1792]{1,0:T(8,128)(2,1)} %hidden_ref.7, bf16[1792,4096]{1,0:T(8,128)(2,1)} %weight_ref.1, bf16[1792,4096]{1,0:T(8,128)(2,1)} %weight_ref.1, bf16[1792,4096]{1,0:T(8,128)(2,1)} %weight_ref.1, bf16[1792,4096]{1,0:T(8,128)(2,1)} %weight_ref.1), custom_call_target="tpu_custom_call" | custom-call | flops 1879048192 | bytes 6553600 | tf_op jit(solution)/shard_map/layer_sum/pallas_call | solution.py:87
  11.9 3.2 %collective-permute-start.8 = (bf16[4,512,128]{2,1,0:T(8,128)(2,1)S(1)}, bf16[4,512,128]{2,1,0:T(8,128)(2,1)S(1)}, u32[]{:S(2)}, u32[]{:S(2)}) collective-permute-start(bf16[4,512,128]{2,1,0:T(8,128)(2,1)S(1)} %get-tuple-element.33), channel_id=1, source_target_pairs={{0,3},{1,0},{2,1},{3,2},{4,7},{5,4},{6,5},{7,6},{8,11},{9,8},{10,9... | collective-permute-start | bytes 1572872 | tf_op jit(solution)/shard_map/layer_sum/ppermute | solution.py:57
  15.6 6.2 %layer_sum.5 = bf16[2,4,512,128]{3,2,1,0:T(8,128)(2,1)} custom-call(s32[2]{0:T(128)} %pad_add_fusion.1.owner_ref, bf16[512,1792]{1,0:T(8,128)(2,1)} %hidden_ref.7, bf16[1792,4096]{1,0:T(8,128)(2,1)} %weight_ref.1, bf16[1792,4096]{1,0:T(8,128)(2,1)} %weight_ref.1, bf16[1792,4096]{1,0:T(8,128)(2,1)} %weight_ref.1, bf16[1792,4096]{1,0:T(8,128)(2,1)} %weight_ref.1), custom_call_target="tpu_custom_call" | custom-call | flops 1879048192 | bytes 6553600 | tf_op jit(solution)/shard_map/layer_sum/pallas_call | solution.py:87
  25.1 6.1 %layer_sum.7 = bf16[2,4,512,128]{3,2,1,0:T(8,128)(2,1)} custom-call(s32[2]{0:T(128)} %pad_add_fusion.3.owner_ref, bf16[512,1792]{1,0:T(8,128)(2,1)} %hidden_ref.7, bf16[1792,4096]{1,0:T(8,128)(2,1)} %weight_ref.1, bf16[1792,4096]{1,0:T(8,128)(2,1)} %weight_ref.1, bf16[1792,4096]{1,0:T(8,128)(2,1)} %weight_ref.1, bf16[1792,4096]{1,0:T(8,128)(2,1)} %weight_ref.1), custom_call_target="tpu_custom_call" | custom-call | flops 1879048192 | bytes 6553600 | tf_op jit(solution)/shard_map/layer_sum/pallas_call | solution.py:87
  34.2 2.8 collective-permute-start.9
  37.5 6.4 %layer_sum.4 = f32[2,4,512,128]{3,2,1,0:T(8,128)} custom-call(s32[2]{0:T(128)} %pad_add_fusion.owner_ref, bf16[512,1792]{1,0:T(8,128)(2,1)} %hidden_ref.7, bf16[1792,4096]{1,0:T(8,128)(2,1)} %weight_ref.1, bf16[1792,4096]{1,0:T(8,128)(2,1)} %weight_ref.1, bf16[1792,4096]{1,0:T(8,128)(2,1)} %weight_ref.1, bf16[1792,4096]{1,0:T(8,128)(2,1)} %weight_ref.1), custom_call_target="tpu_custom_call" | custom-call | flops 1879048192 | bytes 6553600 | tf_op jit(solution)/shard_map/layer_sum/pallas_call | solution.py:87
  44.0 5.3 %collective-permute-done.4 = bf16[4,512,128]{2,1,0:T(8,128)(2,1)S(1)} collective-permute-done((bf16[4,512,128]{2,1,0:T(8,128)(2,1)S(1)}, bf16[4,512,128]{2,1,0:T(8,128)(2,1)S(1)}, u32[]{:S(2)}, u32[]{:S(2)}) %collective-permute-start.4) | collective-permute-done | bytes 524320 | tf_op jit(solution)/shard_map/layer_sum/ppermute | solution.py:57
  50.2 8.8 %collective-permute-start.1 = (bf16[512,128]{1,0:T(8,128)(2,1)S(1)}, bf16[512,128]{1,0:T(8,128)(2,1)S(1)}, u32[]{:S(2)}, u32[]{:S(2)}) collective-permute-start(bf16[512,128]{1,0:T(8,128)(2,1)S(1)} %get-tuple-element.42), channel_id=1, source_target_pairs={{0,1},{1,5},{2,2},{3,6},{4,3},{5,7},{6,0},{7,4},{8,9},{9,13},{10,1... | collective-permute-start | bytes 393224 | tf_op jit(solution)/shard_map/resid_exchange/ppermute | solution.py:331
  59.9 6.2 %collective-permute-start.3 = (bf16[512,128]{1,0:T(8,128)(2,1)S(1)}, bf16[512,128]{1,0:T(8,128)(2,1)S(1)}, u32[]{:S(2)}, u32[]{:S(2)}) collective-permute-start(bf16[512,128]{1,0:T(8,128)(2,1)S(1)} %get-tuple-element.43), channel_id=1, source_target_pairs={{0,3},{1,7},{2,0},{3,4},{4,1},{5,5},{6,2},{7,6},{8,11},{9,15},{10,... | collective-permute-start | bytes 393224 | tf_op jit(solution)/shard_map/resid_exchange/ppermute | solution.py:331
  67.9 2.4 collective-permute-start.5
  74.5 5.0 %collective-permute-done.6 = bf16[4,512,128]{2,1,0:T(8,128)(2,1)S(1)} collective-permute-done((bf16[4,512,128]{2,1,0:T(8,128)(2,1)}, bf16[4,512,128]{2,1,0:T(8,128)(2,1)S(1)}, u32[]{:S(2)}, u32[]{:S(2)}) %collective-permute-start.6) | collective-permute-done | bytes 524320 | tf_op jit(solution)/shard_map/layer_sum/ppermute | solution.py:57
  81.4 2.0 fusion.13
  84.4 3.0 %collective-permute-start.12 = (bf16[1,512,128]{2,1,0:T(8,128)(2,1)}, bf16[1,512,128]{2,1,0:T(8,128)(2,1)}, u32[]{:S(2)}, u32[]{:S(2)}) collective-permute-start(bf16[1,512,128]{2,1,0:T(8,128)(2,1)} %get-tuple-element.36), channel_id=1, source_target_pairs={{0,96},{8,104},{16,112},{24,120},{32,0},{40,8},{48,16},{56,24},{64... | collective-permute-start | bytes 393224 | tf_op jit(solution)/shard_map/strip_exchange/ppermute | solution.py:45
  88.7 5.0 %all-to-all-start = ((f32[8,4,128]{2,1,0:T(4,128)}), f32[8,4,128]{2,1,0:T(4,128)S(1)}, u32[]{:S(2)}, u32[]{:S(2)}) async-start(f32[8,4,128]{2,1,0:T(4,128)} %broadcast_in_dim.53), calls=%async_computation | async-start | bytes 32768 | tf_op jit(solution)/shard_map/norm/all_to_all | solution.py:67
  93.7 2.2 slice.64
  97.8 2.1 all-to-all-done
  103.5 2.9 %constant_dynamic-update-slice_fusion.3 = bf16[2048,1792]{1,0:T(8,128)(2,1)} fusion(bf16[2048,1792]{1,0:T(8,128)(2,1)} %constant_dynamic-update-slice_fusion.4, bf16[512,1792]{1,0:T(8,128)(2,1)} %collective-permute-done.14), kind=kLoop, calls=%fused_computation.47 | loop fusion | bytes 3670016
  106.4 2.9 %constant_dynamic-update-slice_fusion.2 = bf16[2048,1792]{1,0:T(8,128)(2,1)} fusion(bf16[2048,1792]{1,0:T(8,128)(2,1)} %constant_dynamic-update-slice_fusion.3, bf16[512,1792]{1,0:T(8,128)(2,1)} %collective-permute-done.15), kind=kLoop, calls=%fused_computation.46 | loop fusion | bytes 3670016
  109.2 5.1 %collective-permute-done.16 = bf16[256,1792]{1,0:T(8,128)(2,1)} collective-permute-done((bf16[256,1792]{1,0:T(8,128)(2,1)}, bf16[256,1792]{1,0:T(8,128)(2,1)}, u32[]{:S(2)}, u32[]{:S(2)}) %collective-permute-start.16) | collective-permute-done | bytes 917536 | tf_op jit(solution)/shard_map/hidden_exchange/ppermute | solution.py:45
  114.3 2.2 constant_dynamic-update-slice_fusion.1
  119.3 2.7 collective-permute-start.19
  122.8 7.7 %all-to-all-start.1 = ((f32[16,4,4,128]{3,2,1,0:T(4,128)}), f32[16,4,4,128]{3,2,1,0:T(4,128)S(1)}, u32[]{:S(2)}, u32[]{:S(2)}) async-start(f32[16,4,4,128]{3,2,1,0:T(4,128)} %broadcast_in_dim.55), calls=%async_computation.1 | async-start | bytes 262144 | tf_op jit(solution)/shard_map/strip_gather/all_to_all | solution.py:67
  130.7 7.8 %all-to-all-done.1 = f32[16,4,4,128]{3,2,1,0:T(4,128)S(1)} async-done(((f32[16,4,4,128]{3,2,1,0:T(4,128)}), f32[16,4,4,128]{3,2,1,0:T(4,128)S(1)}, u32[]{:S(2)}, u32[]{:S(2)}) %all-to-all-start.1) | async-done | bytes 131104 | tf_op jit(solution)/shard_map/strip_gather/all_to_all | solution.py:67
  138.5 3.3 %collective-permute-start.21 = (bf16[7,512,128]{2,1,0:T(8,128)(2,1)}, bf16[7,512,128]{2,1,0:T(8,128)(2,1)S(1)}, u32[]{:S(2)}, u32[]{:S(2)}) collective-permute-start(bf16[7,512,128]{2,1,0:T(8,128)(2,1)} %collective-permute-done.18), channel_id=1, source_target_pairs={{0,3},{1,0},{2,1},{3,2},{4,7},{5,4},{6,5},{7,6},{8,11},{9,8},{10,9... | collective-permute-start | bytes 2752520 | tf_op jit(solution)/shard_map/strip_gather/ppermute | solution.py:57
  143.1 3.6 %all-to-all-start.2 = ((f32[8,64,512]{2,1,0:T(8,128)}), f32[8,64,512]{2,1,0:T(8,128)S(1)}, u32[]{:S(2)}, u32[]{:S(2)}) async-start(f32[8,64,512]{2,1,0:T(8,128)} %broadcast_in_dim.64), calls=%async_computation.2 | async-start | bytes 2097152 | tf_op jit(solution)/shard_map/strip_gather/all_to_all | solution.py:67
  146.7 4.8 %broadcast_in_dim.51 = bf16[8,7,512,128]{3,2,1,0:T(8,128)(2,1)} broadcast(bf16[]{:T(256)} %constant.194.clone.1), dimensions={} | broadcast | bytes 7340034 | tf_op jit(solution)/shard_map/strip_gather/broadcast_in_dim | solution.py:391
  155.9 2.2 bitcast_dynamic-update-slice_fusion.6
  158.1 2.2 bitcast_dynamic-update-slice_fusion.5
  160.2 2.6 collective-permute-done.21
  162.9 3.6 %collective-permute-start.24 = (bf16[7,512,128]{2,1,0:T(8,128)(2,1)S(1)}, bf16[7,512,128]{2,1,0:T(8,128)(2,1)}, u32[]{:S(2)}, u32[]{:S(2)}) collective-permute-start(bf16[7,512,128]{2,1,0:T(8,128)(2,1)S(1)} %collective-permute-done.21), channel_id=1, source_target_pairs={{0,3},{1,0},{2,1},{3,2},{4,7},{5,4},{6,5},{7,6},{8,11},{9,8},{10,9... | collective-permute-start | bytes 2752520 | tf_op jit(solution)/shard_map/strip_gather/ppermute | solution.py:57
  166.4 2.2 bitcast_dynamic-update-slice_fusion.4
  168.6 5.5 %all-to-all-done.2.mean_ref = f32[8,64,512]{2,1,0:T(8,128)S(1)} async-done(((f32[8,64,512]{2,1,0:T(8,128)}), f32[8,64,512]{2,1,0:T(8,128)S(1)}, u32[]{:S(2)}, u32[]{:S(2)}) %all-to-all-start.2) | async-done | bytes 1048608 | tf_op jit(solution)/shard_map/strip_gather/all_to_all | solution.py:67
  174.1 3.8 %contrast.1 = (f32[8,64,512]{2,1,0:T(8,128)S(1)}, f32[8,1,512]{2,1,0:T(1,128)S(1)}) custom-call(f32[8,64,512]{2,1,0:T(8,128)S(1)} %all-to-all-done.2.mean_ref, f32[8,1,512]{2,1,0:T(1,128)S(1)} %bitcast.109, f32[64,64]{1,0:T(8,128)S(1)} %compare_convert_fusion.same_ref), custom_call_target="tpu_custom_call" | custom-call | flops 402653184 | bytes 2097152 | tf_op jit(solution)/shard_map/contrast/pallas_call | solution.py:139
  179.0 2.9 %collective-permute-done.22 = bf16[7,512,128]{2,1,0:T(8,128)(2,1)} collective-permute-done((bf16[7,512,128]{2,1,0:T(8,128)(2,1)}, bf16[7,512,128]{2,1,0:T(8,128)(2,1)}, u32[]{:S(2)}, u32[]{:S(2)}) %collective-permute-start.22) | collective-permute-done | bytes 917536 | tf_op jit(solution)/shard_map/strip_gather/ppermute | solution.py:57
  181.8 2.2 bitcast_dynamic-update-slice_fusion.2
  184.0 17.1 %collective-permute-done.23 = bf16[7,512,128]{2,1,0:T(8,128)(2,1)} collective-permute-done((bf16[7,512,128]{2,1,0:T(8,128)(2,1)}, bf16[7,512,128]{2,1,0:T(8,128)(2,1)}, u32[]{:S(2)}, u32[]{:S(2)}) %collective-permute-start.23) | collective-permute-done | bytes 917536 | tf_op jit(solution)/shard_map/strip_gather/ppermute | solution.py:57
  201.1 2.2 bitcast_dynamic-update-slice_fusion.1
  203.3 2.2 bitcast_dynamic-update-slice_fusion.layer_ref
  205.5 4.8 %layer_grad.1 = (bf16[512,4096]{1,0:T(8,128)(2,1)S(1)}, f32[4,128]{1,0:T(4,128)S(1)}) custom-call(s32[1]{0:T(128)} %bitcast.first_ref, bf16[8,7,512,128]{3,2,1,0:T(8,128)(2,1)} %bitcast_dynamic-update-slice_fusion.layer_ref, f32[8,64,512]{2,1,0:T(8,128)S(1)} %get-tuple-element.23.scaled_ref, f32[4,128]{1,0:T(4,128)S(1)} %add_rsqrt_fusion.inverse_ref), custom_call_target="tpu_custom_call" | custom-call | flops 12582912 | bytes 8388608 | tf_op jit(solution)/shard_map/layer_grad/pallas_call | solution.py:191
  212.8 2.8 collective-permute-start.26
  217.1 3.5 %collective-permute-done.27 = f32[8,128]{1,0:T(8,128)S(1)} collective-permute-done((f32[8,128]{1,0:T(8,128)S(1)}, f32[8,128]{1,0:T(8,128)S(1)}, u32[]{:S(2)}, u32[]{:S(2)}) %collective-permute-start.27) | collective-permute-done | bytes 4128 | tf_op jit(solution)/shard_map/down_grad/ppermute | solution.py:45
  220.6 5.2 %down_grad.1 = bf16[4,2048,256]{2,1,0:T(8,128)(2,1)S(1)} custom-call(s32[10]{0:T(128)S(1)} %stack.111.plan_ref, bf16[8,7,512,128]{3,2,1,0:T(8,128)(2,1)} %bitcast_dynamic-update-slice_fusion.layer_ref, f32[8,64,512]{2,1,0:T(8,128)S(1)} %get-tuple-element.23.scaled_ref, f32[4,8,128]{2,1,0:T(8,128)S(1)} %pad_maximum_fusion.2.factor_ref), custom_call_target="tpu_custom_call" | custom-call | flops 6291456 | bytes 8388608 | tf_op jit(solution)/shard_map/down_grad/pallas_call | solution.py:236
  225.9 8.0 %fusion.1 = f32[1792,256]{1,0:T(8,128)} fusion(bf16[2048,1792]{1,0:T(8,128)(2,1)} %constant_dynamic-update-slice_fusion, bf16[4,2048,256]{2,1,0:T(8,128)(2,1)S(1)} %down_grad.1), kind=kOutput, calls=%fused_computation.5 | convolution fusion | flops 1879048192 | bytes 10223616 | tf_op jit(solution)/shard_map/down_grad/dot_general | solution.py:420
  233.9 3.3 %fusion.2 = f32[1792,256]{1,0:T(8,128)} fusion(bf16[2048,1792]{1,0:T(8,128)(2,1)S(1)} %bitcast.114, bf16[4,2048,256]{2,1,0:T(8,128)(2,1)S(1)} %down_grad.1), kind=kOutput, calls=%fused_computation.8 | convolution fusion | flops 1879048192 | bytes 10223616 | tf_op jit(solution)/shard_map/down_grad/dot_general | solution.py:420
  238.3 15.7 %hidden_grad.1 = bf16[512,1792]{1,0:T(8,128)(2,1)} custom-call(bf16[512,4096]{1,0:T(8,128)(2,1)} %copy-done.2, bf16[1792,4096]{1,0:T(8,128)(2,1)} %weight_ref.1), custom_call_target="tpu_custom_call" | custom-call | flops 7516192768 | bytes 20709376 | tf_op jit(solution)/shard_map/hidden_grad/pallas_call | solution.py:279
  254.0 5.7 %fusion = bf16[1792,256]{1,0:T(8,128)(2,1)S(1)} fusion(f32[1792,256]{1,0:T(8,128)} %collective-permute-done.29, bf16[2048,1792]{1,0:T(8,128)(2,1)} %constant_dynamic-update-slice_fusion, bf16[4,2048,256]{2,1,0:T(8,128)(2,1)S(1)} %copy-done.1), kind=kOutput, calls=%fused_computation.2 | convolution fusion | flops 1879965696 | bytes 11141120 | tf_op jit(solution)/shard_map/down_grad/dot_general | solution.py:420
  262.4 5.3 %convolution_add_fusion.1 = f32[1792,256]{1,0:T(8,128)S(1)} fusion(f32[1792,256]{1,0:T(8,128)S(1)} %collective-permute-done.28, bf16[2048,1792]{1,0:T(8,128)(2,1)} %constant_dynamic-update-slice_fusion, bf16[4,2048,256]{2,1,0:T(8,128)(2,1)S(1)} %copy-done.1), kind=kOutput, calls=%fused_computation.1 | convolution fusion | flops 1879506944 | bytes 12058624 | tf_op jit(solution)/shard_map/down_grad/dot_general | solution.py:420
  267.7 15.9 %collective-permute-done.30 = bf16[1792,256]{1,0:T(8,128)(2,1)S(1)} collective-permute-done((bf16[1792,256]{1,0:T(8,128)(2,1)S(1)}, bf16[1792,256]{1,0:T(8,128)(2,1)S(1)}, u32[]{:S(2)}, u32[]{:S(2)}) %collective-permute-start.30) | collective-permute-done | bytes 917536 | tf_op jit(solution)/shard_map/down_grad/ppermute | solution.py:49
  (113 shorter events, 49.8 us)
Async XLA Ops:
  0.6 93.1 %collective-permute-start.14 = (bf16[512,1792]{1,0:T(8,128)(2,1)}, bf16[512,1792]{1,0:T(8,128)(2,1)}, u32[]{:S(2)}, u32[]{:S(2)}) collective-permute-start(bf16[512,1792]{1,0:T(8,128)(2,1)} %hidden_ref.7), channel_id=1, source_target_pairs={{0,32},{8,40},{16,48},{24,56},{32,64},{40,72},{48,80},{56,88},{64,... | collective-permute-start | bytes 5505032 | tf_op jit(solution)/shard_map/hidden_exchange/ppermute | solution.py:45
  2.3 97.7 %collective-permute-start.15 = (bf16[512,1792]{1,0:T(8,128)(2,1)}, bf16[512,1792]{1,0:T(8,128)(2,1)}, u32[]{:S(2)}, u32[]{:S(2)}) collective-permute-start(bf16[512,1792]{1,0:T(8,128)(2,1)} %hidden_ref.7), channel_id=1, source_target_pairs={{0,96},{8,104},{16,112},{24,120},{32,0},{40,8},{48,16},{56,24},{64... | collective-permute-start | bytes 5505032 | tf_op jit(solution)/shard_map/hidden_exchange/ppermute | solution.py:45
  11.9 21.1 %collective-permute-start.8 = (bf16[4,512,128]{2,1,0:T(8,128)(2,1)S(1)}, bf16[4,512,128]{2,1,0:T(8,128)(2,1)S(1)}, u32[]{:S(2)}, u32[]{:S(2)}) collective-permute-start(bf16[4,512,128]{2,1,0:T(8,128)(2,1)S(1)} %get-tuple-element.33), channel_id=1, source_target_pairs={{0,3},{1,0},{2,1},{3,2},{4,7},{5,4},{6,5},{7,6},{8,11},{9,8},{10,9... | collective-permute-start | bytes 1572872 | tf_op jit(solution)/shard_map/layer_sum/ppermute | solution.py:57
  15.6 8.7 %copy-start.6 = (bf16[512,512]{1,0:T(8,128)(2,1)S(1)}, bf16[512,512]{1,0:T(8,128)(2,1)}, u32[]{:S(2)}) copy-start(bf16[512,512]{1,0:T(8,128)(2,1)} %param.5) | copy-start | bytes 1572868
  23.7 35.3 %collective-permute-start.7 = (bf16[4,512,128]{2,1,0:T(8,128)(2,1)}, bf16[4,512,128]{2,1,0:T(8,128)(2,1)S(1)}, u32[]{:S(2)}, u32[]{:S(2)}) collective-permute-start(bf16[4,512,128]{2,1,0:T(8,128)(2,1)} %slice_bitcast_fusion.12), channel_id=1, source_target_pairs={{0,1},{1,2},{2,3},{3,0},{4,5},{5,6},{6,7},{7,4},{8,9},{9,10},{10,1... | collective-permute-start | bytes 1572872 | tf_op jit(solution)/shard_map/layer_sum/ppermute | solution.py:57
  23.7 25.5 %collective-permute-start.4 = (bf16[4,512,128]{2,1,0:T(8,128)(2,1)S(1)}, bf16[4,512,128]{2,1,0:T(8,128)(2,1)S(1)}, u32[]{:S(2)}, u32[]{:S(2)}) collective-permute-start(bf16[4,512,128]{2,1,0:T(8,128)(2,1)S(1)} %get-tuple-element.32), channel_id=1, source_target_pairs={{0,1},{1,2},{2,3},{3,0},{4,5},{5,6},{6,7},{7,4},{8,9},{9,10},{10,1... | collective-permute-start | bytes 1572872 | tf_op jit(solution)/shard_map/layer_sum/ppermute | solution.py:57
  34.2 25.7 %collective-permute-start.9 = (bf16[4,512,128]{2,1,0:T(8,128)(2,1)S(1)}, bf16[4,512,128]{2,1,0:T(8,128)(2,1)S(1)}, u32[]{:S(2)}, u32[]{:S(2)}) collective-permute-start(bf16[4,512,128]{2,1,0:T(8,128)(2,1)S(1)} %fusion.10), channel_id=1, source_target_pairs={{0,3},{1,0},{2,1},{3,2},{4,7},{5,4},{6,5},{7,6},{8,11},{9,8},{10,9... | collective-permute-start | bytes 1572872 | tf_op jit(solution)/shard_map/layer_sum/ppermute | solution.py:57
  37.5 12.5 %copy-start.4 = (bf16[2,4,512,128]{3,2,1,0:T(8,128)(2,1)S(1)}, bf16[2,4,512,128]{3,2,1,0:T(8,128)(2,1)}, u32[]{:S(2)}) copy-start(bf16[2,4,512,128]{3,2,1,0:T(8,128)(2,1)} %layer_sum.5) | copy-start | bytes 3145732
  49.2 47.3 %copy-start.3 = (bf16[512,1792]{1,0:T(8,128)(2,1)S(1)}, bf16[512,1792]{1,0:T(8,128)(2,1)}, u32[]{:S(2)}) copy-start(bf16[512,1792]{1,0:T(8,128)(2,1)} %hidden_ref.7) | copy-start | bytes 5505028
  49.2 1.0 collective-permute-start
  50.2 17.4 %collective-permute-start.1 = (bf16[512,128]{1,0:T(8,128)(2,1)S(1)}, bf16[512,128]{1,0:T(8,128)(2,1)S(1)}, u32[]{:S(2)}, u32[]{:S(2)}) collective-permute-start(bf16[512,128]{1,0:T(8,128)(2,1)S(1)} %get-tuple-element.42), channel_id=1, source_target_pairs={{0,1},{1,5},{2,2},{3,6},{4,3},{5,7},{6,0},{7,4},{8,9},{9,13},{10,1... | collective-permute-start | bytes 393224 | tf_op jit(solution)/shard_map/resid_exchange/ppermute | solution.py:331
  59.0 8.9 %collective-permute-start.2 = (bf16[512,128]{1,0:T(8,128)(2,1)S(1)}, bf16[512,128]{1,0:T(8,128)(2,1)S(1)}, u32[]{:S(2)}, u32[]{:S(2)}) collective-permute-start(bf16[512,128]{1,0:T(8,128)(2,1)S(1)} %get-tuple-element.44), channel_id=1, source_target_pairs={{0,2},{1,6},{2,3},{3,7},{4,0},{5,4},{6,1},{7,5},{8,10},{9,14},{10,... | collective-permute-start | bytes 393224 | tf_op jit(solution)/shard_map/resid_exchange/ppermute | solution.py:331
  59.9 11.5 %collective-permute-start.3 = (bf16[512,128]{1,0:T(8,128)(2,1)S(1)}, bf16[512,128]{1,0:T(8,128)(2,1)S(1)}, u32[]{:S(2)}, u32[]{:S(2)}) collective-permute-start(bf16[512,128]{1,0:T(8,128)(2,1)S(1)} %get-tuple-element.43), channel_id=1, source_target_pairs={{0,3},{1,7},{2,0},{3,4},{4,1},{5,5},{6,2},{7,6},{8,11},{9,15},{10,... | collective-permute-start | bytes 393224 | tf_op jit(solution)/shard_map/resid_exchange/ppermute | solution.py:331
  67.5 2.7 copy-start.7
  67.6 12.0 %collective-permute-start.6 = (bf16[4,512,128]{2,1,0:T(8,128)(2,1)}, bf16[4,512,128]{2,1,0:T(8,128)(2,1)S(1)}, u32[]{:S(2)}, u32[]{:S(2)}) collective-permute-start(bf16[4,512,128]{2,1,0:T(8,128)(2,1)} %slice_bitcast_fusion.13), channel_id=1, source_target_pairs={{0,3},{1,0},{2,1},{3,2},{4,7},{5,4},{6,5},{7,6},{8,11},{9,8},{10,9... | collective-permute-start | bytes 1572872 | tf_op jit(solution)/shard_map/layer_sum/ppermute | solution.py:57
  67.9 3.5 %copy-start.8 = (bf16[512,128]{1,0:T(8,128)(2,1)}, bf16[512,128]{1,0:T(8,128)(2,1)S(1)}, u32[]{:S(2)}) copy-start(bf16[512,128]{1,0:T(8,128)(2,1)S(1)} %collective-permute-done.2) | copy-start | bytes 393220
  67.9 13.3 %collective-permute-start.5 = (bf16[4,512,128]{2,1,0:T(8,128)(2,1)S(1)}, bf16[4,512,128]{2,1,0:T(8,128)(2,1)}, u32[]{:S(2)}, u32[]{:S(2)}) collective-permute-start(bf16[4,512,128]{2,1,0:T(8,128)(2,1)S(1)} %fusion.11), channel_id=1, source_target_pairs={{0,1},{1,2},{2,3},{3,0},{4,5},{5,6},{6,7},{7,4},{8,9},{9,10},{10,1... | collective-permute-start | bytes 1572872 | tf_op jit(solution)/shard_map/layer_sum/ppermute | solution.py:57
  71.4 0.7 copy-start.9
  72.1 9.3 %collective-permute-start.10 = (bf16[4,512,128]{2,1,0:T(8,128)(2,1)S(1)}, bf16[4,512,128]{2,1,0:T(8,128)(2,1)}, u32[]{:S(2)}, u32[]{:S(2)}) collective-permute-start(bf16[4,512,128]{2,1,0:T(8,128)(2,1)S(1)} %fusion.5), channel_id=1, source_target_pairs={{0,4},{1,5},{2,6},{3,7},{4,0},{5,1},{6,2},{7,3},{8,12},{9,13},{10,... | collective-permute-start | bytes 1572872 | tf_op jit(solution)/shard_map/layer_sum/ppermute | solution.py:61
  79.5 1.8 copy-start.5
  84.2 18.3 %collective-permute-start.11 = (bf16[1,512,128]{2,1,0:T(8,128)(2,1)}, bf16[1,512,128]{2,1,0:T(8,128)(2,1)S(1)}, u32[]{:S(2)}, u32[]{:S(2)}) collective-permute-start(bf16[1,512,128]{2,1,0:T(8,128)(2,1)} %get-tuple-element.34), channel_id=1, source_target_pairs={{0,32},{8,40},{16,48},{24,56},{32,64},{40,72},{48,80},{56,88},{64,... | collective-permute-start | bytes 393224 | tf_op jit(solution)/shard_map/strip_exchange/ppermute | solution.py:45
  84.4 18.0 %collective-permute-start.12 = (bf16[1,512,128]{2,1,0:T(8,128)(2,1)}, bf16[1,512,128]{2,1,0:T(8,128)(2,1)}, u32[]{:S(2)}, u32[]{:S(2)}) collective-permute-start(bf16[1,512,128]{2,1,0:T(8,128)(2,1)} %get-tuple-element.36), channel_id=1, source_target_pairs={{0,96},{8,104},{16,112},{24,120},{32,0},{40,8},{48,16},{56,24},{64... | collective-permute-start | bytes 393224 | tf_op jit(solution)/shard_map/strip_exchange/ppermute | solution.py:45
  87.4 15.0 %collective-permute-start.13 = (bf16[1,512,128]{2,1,0:T(8,128)(2,1)}, bf16[1,512,128]{2,1,0:T(8,128)(2,1)}, u32[]{:S(2)}, u32[]{:S(2)}) collective-permute-start(bf16[1,512,128]{2,1,0:T(8,128)(2,1)} %get-tuple-element.35), channel_id=1, source_target_pairs={{0,64},{8,72},{16,80},{24,88},{32,96},{40,104},{48,112},{56,120},{... | collective-permute-start | bytes 393224 | tf_op jit(solution)/shard_map/strip_exchange/ppermute | solution.py:45
  88.7 11.2 %all-to-all-start = ((f32[8,4,128]{2,1,0:T(4,128)}), f32[8,4,128]{2,1,0:T(4,128)S(1)}, u32[]{:S(2)}, u32[]{:S(2)}) async-start(f32[8,4,128]{2,1,0:T(4,128)} %broadcast_in_dim.53), calls=%async_computation | async-start | bytes 32768 | tf_op jit(solution)/shard_map/norm/all_to_all | solution.py:67
  95.9 18.5 %collective-permute-start.16 = (bf16[256,1792]{1,0:T(8,128)(2,1)}, bf16[256,1792]{1,0:T(8,128)(2,1)}, u32[]{:S(2)}, u32[]{:S(2)}) collective-permute-start(bf16[256,1792]{1,0:T(8,128)(2,1)} %slice.64), channel_id=1, source_target_pairs={{0,32},{8,40},{16,48},{24,56},{32,64},{40,72},{48,80},{56,88},{64,... | collective-permute-start | bytes 2752520 | tf_op jit(solution)/shard_map/hidden_exchange/ppermute | solution.py:45
  101.2 29.4 %copy-start.11 = (s32[16]{0:T(128)S(1)}, s32[16]{0:T(128)}, u32[]{:S(2)}) copy-start(s32[16]{0:T(128)} %param.9) | copy-start | bytes 196
  101.2 40.7 %copy-start.10 = (f32[4096]{0:T(1024)S(1)}, f32[4096]{0:T(1024)}, u32[]{:S(2)}) copy-start(f32[4096]{0:T(1024)} %param.8) | copy-start | bytes 49156
  101.2 16.0 %collective-permute-start.17 = (bf16[256,1792]{1,0:T(8,128)(2,1)S(1)}, bf16[256,1792]{1,0:T(8,128)(2,1)S(1)}, u32[]{:S(2)}, u32[]{:S(2)}) collective-permute-start(bf16[256,1792]{1,0:T(8,128)(2,1)S(1)} %slice.65), channel_id=1, source_target_pairs={{0,96},{8,104},{16,112},{24,120},{32,0},{40,8},{48,16},{56,24},{64... | collective-permute-start | bytes 2752520 | tf_op jit(solution)/shard_map/hidden_exchange/ppermute | solution.py:45
  118.2 20.3 %collective-permute-start.18 = (bf16[7,512,128]{2,1,0:T(8,128)(2,1)S(1)}, bf16[7,512,128]{2,1,0:T(8,128)(2,1)}, u32[]{:S(2)}, u32[]{:S(2)}) collective-permute-start(bf16[7,512,128]{2,1,0:T(8,128)(2,1)S(1)} %pad_maximum_fusion), channel_id=1, source_target_pairs={{0,4},{1,5},{2,6},{3,7},{4,0},{5,1},{6,2},{7,3},{8,12},{9,13},{10,... | collective-permute-start | bytes 2752520 | tf_op jit(solution)/shard_map/strip_gather/ppermute | solution.py:61
  119.3 19.2 %collective-permute-start.19 = (bf16[7,512,128]{2,1,0:T(8,128)(2,1)S(1)}, bf16[7,512,128]{2,1,0:T(8,128)(2,1)}, u32[]{:S(2)}, u32[]{:S(2)}) collective-permute-start(bf16[7,512,128]{2,1,0:T(8,128)(2,1)S(1)} %pad_maximum_fusion), channel_id=1, source_target_pairs={{0,3},{1,0},{2,1},{3,2},{4,7},{5,4},{6,5},{7,6},{8,11},{9,8},{10,9... | collective-permute-start | bytes 2752520 | tf_op jit(solution)/shard_map/strip_gather/ppermute | solution.py:57
  122.0 16.6 %collective-permute-start.20 = (bf16[7,512,128]{2,1,0:T(8,128)(2,1)S(1)}, bf16[7,512,128]{2,1,0:T(8,128)(2,1)}, u32[]{:S(2)}, u32[]{:S(2)}) collective-permute-start(bf16[7,512,128]{2,1,0:T(8,128)(2,1)S(1)} %pad_maximum_fusion), channel_id=1, source_target_pairs={{0,1},{1,2},{2,3},{3,0},{4,5},{5,6},{6,7},{7,4},{8,9},{9,10},{10,1... | collective-permute-start | bytes 2752520 | tf_op jit(solution)/shard_map/strip_gather/ppermute | solution.py:57
  122.8 15.7 %all-to-all-start.1 = ((f32[16,4,4,128]{3,2,1,0:T(4,128)}), f32[16,4,4,128]{3,2,1,0:T(4,128)S(1)}, u32[]{:S(2)}, u32[]{:S(2)}) async-start(f32[16,4,4,128]{3,2,1,0:T(4,128)} %broadcast_in_dim.55), calls=%async_computation.1 | async-start | bytes 262144 | tf_op jit(solution)/shard_map/strip_gather/all_to_all | solution.py:67
  138.5 24.3 %collective-permute-start.21 = (bf16[7,512,128]{2,1,0:T(8,128)(2,1)}, bf16[7,512,128]{2,1,0:T(8,128)(2,1)S(1)}, u32[]{:S(2)}, u32[]{:S(2)}) collective-permute-start(bf16[7,512,128]{2,1,0:T(8,128)(2,1)} %collective-permute-done.18), channel_id=1, source_target_pairs={{0,3},{1,0},{2,1},{3,2},{4,7},{5,4},{6,5},{7,6},{8,11},{9,8},{10,9... | collective-permute-start | bytes 2752520 | tf_op jit(solution)/shard_map/strip_gather/ppermute | solution.py:57
  143.1 31.0 %all-to-all-start.2 = ((f32[8,64,512]{2,1,0:T(8,128)}), f32[8,64,512]{2,1,0:T(8,128)S(1)}, u32[]{:S(2)}, u32[]{:S(2)}) async-start(f32[8,64,512]{2,1,0:T(8,128)} %broadcast_in_dim.64), calls=%async_computation.2 | async-start | bytes 2097152 | tf_op jit(solution)/shard_map/strip_gather/all_to_all | solution.py:67
  152.5 29.3 %collective-permute-start.22 = (bf16[7,512,128]{2,1,0:T(8,128)(2,1)}, bf16[7,512,128]{2,1,0:T(8,128)(2,1)}, u32[]{:S(2)}, u32[]{:S(2)}) collective-permute-start(bf16[7,512,128]{2,1,0:T(8,128)(2,1)} %collective-permute-done.18), channel_id=1, source_target_pairs={{0,1},{1,2},{2,3},{3,0},{4,5},{5,6},{6,7},{7,4},{8,9},{9,10},{10,1... | collective-permute-start | bytes 2752520 | tf_op jit(solution)/shard_map/strip_gather/ppermute | solution.py:57
  154.4 46.7 %collective-permute-start.23 = (bf16[7,512,128]{2,1,0:T(8,128)(2,1)}, bf16[7,512,128]{2,1,0:T(8,128)(2,1)}, u32[]{:S(2)}, u32[]{:S(2)}) collective-permute-start(bf16[7,512,128]{2,1,0:T(8,128)(2,1)} %collective-permute-done.20), channel_id=1, source_target_pairs={{0,1},{1,2},{2,3},{3,0},{4,5},{5,6},{6,7},{7,4},{8,9},{9,10},{10,1... | collective-permute-start | bytes 2752520 | tf_op jit(solution)/shard_map/strip_gather/ppermute | solution.py:57
  162.9 40.5 %collective-permute-start.24 = (bf16[7,512,128]{2,1,0:T(8,128)(2,1)S(1)}, bf16[7,512,128]{2,1,0:T(8,128)(2,1)}, u32[]{:S(2)}, u32[]{:S(2)}) collective-permute-start(bf16[7,512,128]{2,1,0:T(8,128)(2,1)S(1)} %collective-permute-done.21), channel_id=1, source_target_pairs={{0,3},{1,0},{2,1},{3,2},{4,7},{5,4},{6,5},{7,6},{8,11},{9,8},{10,9... | collective-permute-start | bytes 2752520 | tf_op jit(solution)/shard_map/strip_gather/ppermute | solution.py:57
  210.3 2.0 copy-start.2
  212.3 4.8 %collective-permute-start.25 = (f32[8,128]{1,0:T(8,128)S(1)}, f32[8,128]{1,0:T(8,128)S(1)}, u32[]{:S(2)}, u32[]{:S(2)}) collective-permute-start(f32[8,128]{1,0:T(8,128)S(1)} %get-tuple-element.46), channel_id=1, source_target_pairs={{0,32},{8,40},{16,48},{24,56},{32,64},{40,72},{48,80},{56,88},{64,... | collective-permute-start | bytes 12296 | tf_op jit(solution)/shard_map/down_grad/ppermute | solution.py:45
  212.8 4.3 %collective-permute-start.26 = (f32[8,128]{1,0:T(8,128)S(1)}, f32[8,128]{1,0:T(8,128)S(1)}, u32[]{:S(2)}, u32[]{:S(2)}) collective-permute-start(f32[8,128]{1,0:T(8,128)S(1)} %get-tuple-element.46), channel_id=1, source_target_pairs={{0,96},{8,104},{16,112},{24,120},{32,0},{40,8},{48,16},{56,24},{64... | collective-permute-start | bytes 12296 | tf_op jit(solution)/shard_map/down_grad/ppermute | solution.py:45
  215.5 5.1 %collective-permute-start.27 = (f32[8,128]{1,0:T(8,128)S(1)}, f32[8,128]{1,0:T(8,128)S(1)}, u32[]{:S(2)}, u32[]{:S(2)}) collective-permute-start(f32[8,128]{1,0:T(8,128)S(1)} %get-tuple-element.46), channel_id=1, source_target_pairs={{0,64},{8,72},{16,80},{24,88},{32,96},{40,104},{48,112},{56,120},{... | collective-permute-start | bytes 12296 | tf_op jit(solution)/shard_map/down_grad/ppermute | solution.py:45
  220.6 13.3 %slice-start = ((s8[7340032]{0:T(1024)(128)(4,1)}), s8[3145728]{0:T(1024)(128)(4,1)S(1)}, s32[]{:S(2)}) async-start(s8[7340032]{0:T(1024)(128)(4,1)} %bitcast.113), calls=%async_computation.3 | async-start | bytes 6291456
  225.9 8.0 %copy-start = (bf16[4,2048,256]{2,1,0:T(8,128)(2,1)}, bf16[4,2048,256]{2,1,0:T(8,128)(2,1)S(1)}, u32[]{:S(2)}) copy-start(bf16[4,2048,256]{2,1,0:T(8,128)(2,1)S(1)} %down_grad.1) | copy-start | bytes 12582916
  225.9 8.0 %slice-start.1 = ((s8[7340032]{0:T(1024)(128)(4,1)}), s8[4194304]{0:T(1024)(128)(4,1)S(1)}, s32[]{:S(2)}) async-start(s8[7340032]{0:T(1024)(128)(4,1)} %bitcast.113), calls=%async_computation.4 | async-start | bytes 8388608
  233.9 20.2 %collective-permute-start.29 = (f32[1792,256]{1,0:T(8,128)}, f32[1792,256]{1,0:T(8,128)}, u32[]{:S(2)}, u32[]{:S(2)}) collective-permute-start(f32[1792,256]{1,0:T(8,128)} %fusion.1), channel_id=1, source_target_pairs={{0,8},{8,0},{16,24},{24,16},{32,40},{40,32},{48,56},{56,48},{64,72... | collective-permute-start | bytes 5505032 | tf_op jit(solution)/shard_map/down_grad/ppermute | solution.py:53
  237.3 25.2 %collective-permute-start.28 = (f32[1792,256]{1,0:T(8,128)}, f32[1792,256]{1,0:T(8,128)S(1)}, u32[]{:S(2)}, u32[]{:S(2)}) collective-permute-start(f32[1792,256]{1,0:T(8,128)} %fusion.2), channel_id=1, source_target_pairs={{0,8},{8,0},{16,24},{24,16},{32,40},{40,32},{48,56},{56,48},{64,72... | collective-permute-start | bytes 5505032 | tf_op jit(solution)/shard_map/down_grad/ppermute | solution.py:53
  238.3 15.7 %copy-start.1 = (bf16[4,2048,256]{2,1,0:T(8,128)(2,1)S(1)}, bf16[4,2048,256]{2,1,0:T(8,128)(2,1)}, u32[]{:S(2)}) copy-start(bf16[4,2048,256]{2,1,0:T(8,128)(2,1)} %copy-done) | copy-start | bytes 12582916
  259.7 23.9 %collective-permute-start.30 = (bf16[1792,256]{1,0:T(8,128)(2,1)S(1)}, bf16[1792,256]{1,0:T(8,128)(2,1)S(1)}, u32[]{:S(2)}, u32[]{:S(2)}) collective-permute-start(bf16[1792,256]{1,0:T(8,128)(2,1)S(1)} %fusion), channel_id=1, source_target_pairs={{0,16},{8,24},{16,0},{24,8},{32,48},{40,56},{48,32},{56,40},{64,80... | collective-permute-start | bytes 2752520 | tf_op jit(solution)/shard_map/down_grad/ppermute | solution.py:49

commit v3 on v2

v3 whole, which is shorter than its diff:
```python
import functools
import jax
import jax.numpy as jnp
from jax import lax
from jax.experimental import pallas as pl
from jax.experimental.pallas import tpu as pltpu
from jax.sharding import PartitionSpec as P

SEQ = 128
NX, NZH, NCORE, NZL, NY = 4, 2, 2, 2, 4

score_scale = 20.0
loss_scale = 8192.0
eps_norm = 1e-05
eps_embed = 1e-06
highest = lax.Precision.HIGHEST
f32 = jnp.float32
bf16 = jnp.bfloat16
MIB = 1024 * 1024


def dp_route(dx, dz, dc):
    pairs = []
    for x in range(NX):
        for z in range(NZH):
            for c in range(NCORE):
                to = (((x + dx) % NX) * NZH + (z + dz) % NZH) * NCORE + (c + dc) % NCORE
                pairs.append(((x * NZH + z) * NCORE + c, to))
    return pairs


def tensor_route(dz, dy):
    pairs = []
    for z in range(NZL):
        for y in range(NY):
            pairs.append((z * NY + y, ((z + dz) % NZL) * NY + (y + dy) % NY))
    return pairs


def resid_route(step):
    pairs = []
    for r in range(NZL * NY):
        j = (r // 2 + step) % NY
        pairs.append((r, (j % 2) * NY + (r % 2) * 2 + j // 2))
    return pairs


def over_x(value, step):
    return lax.ppermute(value, "dp", dp_route(step, 0, 0))


def over_zh(value):
    return lax.ppermute(value, "dp", dp_route(0, 1, 0))


def over_core(value):
    return lax.ppermute(value, "dp", dp_route(0, 0, 1))


def over_y(value, step):
    return lax.ppermute(value, "tensor", tensor_route(0, step))


def over_zl(value):
    return lax.ppermute(value, "tensor", tensor_route(1, 0))


def gather_small(value, axis):
    n = lax.axis_size(axis)
    copies = jnp.broadcast_to(value[None], (n,) + value.shape)
    return lax.all_to_all(copies, axis, 0, 0)


def pair_dot_kernel(plan_ref, hidden_ref, weight_ref, same_ref, other_ref):
    total = jnp.dot(hidden_ref[...], weight_ref[...], preferred_element_type=f32)
    lanes = same_ref.shape[-1]
    first, second = total[:, :lanes], total[:, lanes:]
    flip = plan_ref[1] == 1
    same_ref[0] = jnp.where(flip, second, first).astype(same_ref.dtype)
    other_ref[0] = jnp.where(flip, first, second).astype(other_ref.dtype)


def pair_dot(hidden, weight, column, zl, group, out_dtype):
    tokens, units = hidden.shape
    lanes = weight.shape[1] // (NX * group)
    strips = jax.ShapeDtypeStruct((NX, tokens, lanes), out_dtype)
    out = pl.BlockSpec((1, tokens, lanes), lambda b, s: (b, 0, 0))
    return pl.pallas_call(
        pair_dot_kernel,
        grid_spec=pltpu.PrefetchScalarGridSpec(
            num_scalar_prefetch=1,
            grid=(NX,),
            in_specs=[
                pl.BlockSpec((tokens, units), lambda b, s: (0, 0)),
                pl.BlockSpec((units, 2 * lanes), lambda b, s: (0, b * NY + s[0])),
            ],
            out_specs=[out, out],
        ),
        out_shape=(strips, strips),
        compiler_params=pltpu.CompilerParams(vmem_limit_bytes=56 * MIB),
        cost_estimate=pl.CostEstimate(
            flops=4 * tokens * units * NX * lanes,
            bytes_accessed=2 * (tokens * units + 2 * (units + tokens) * NX * lanes),
            transcendentals=0,
        ),
    )(jnp.stack([column, zl]).astype(jnp.int32), hidden, weight)


def gram_kernel(plan_ref, mean_ref, gain_ref, strip_ref, out_ref):
    pooled = mean_ref[...] * gain_ref[...]
    gram = lax.dot_general(
        pooled, pooled, (((1,), (1,)), ((), ())), precision=highest, preferred_element_type=f32
    )
    out_ref[0] = jnp.concatenate([gram, jnp.zeros_like(gram)], axis=1)
    out_ref[1] = strip_ref[...]


def gram_part(means, gain, x):
    seqs, width = means.shape
    lanes = 2 * seqs
    return pl.pallas_call(
        gram_kernel,
        grid_spec=pltpu.PrefetchScalarGridSpec(
            num_scalar_prefetch=1,
            grid=(1,),
            in_specs=[
                pl.BlockSpec((seqs, width), lambda i, s: (0, 0)),
                pl.BlockSpec((1, width), lambda i, s: (0, 0)),
                pl.BlockSpec((seqs, lanes), lambda i, s: (0, s[0])),
            ],
            out_specs=pl.BlockSpec((2, seqs, lanes), lambda i, s: (0, 0, 0)),
        ),
        out_shape=jax.ShapeDtypeStruct((2, seqs, lanes), f32),
        compiler_params=pltpu.CompilerParams(vmem_limit_bytes=16 * MIB),
        cost_estimate=pl.CostEstimate(
            flops=12 * seqs * seqs * width, bytes_accessed=4 * seqs * (width + 3 * lanes), transcendentals=0
        ),
    )(x.astype(jnp.int32).reshape(1), means, gain, means)


def contrast_kernel(
    plan_ref, part_ref, same_ref, gain_block_ref, mean_ref, gain_ref, block_ref, own_ref, gain_grad_ref
):
    group = part_ref.shape[0]
    seqs = mean_ref.shape[0]
    rows = lax.broadcasted_iota(jnp.int32, (seqs, seqs), 0)
    cols = lax.broadcasted_iota(jnp.int32, (seqs, seqs), 1)
    gram = part_ref[0, 0]
    for r in range(1, group):
        gram += part_ref[r, 0]
    gram = gram[:, :seqs]
    diagonal = jnp.where(rows == cols, gram, 0.0)
    norm_col = jnp.sqrt(jnp.sum(diagonal, axis=1, keepdims=True) + eps_embed)
    norm_row = jnp.sqrt(jnp.sum(diagonal, axis=0, keepdims=True) + eps_embed)
    norms = norm_col * norm_row
    scores = score_scale * gram / norms
    query = rows % 2 == 0
    valid = query & (cols % 2 == 1) & (same_ref[...] > 0.5)
    weights = jnp.where(valid, jnp.exp(scores), 0.0)
    totals = jnp.sum(weights, axis=1, keepdims=True)
    soft = weights / jnp.where(totals > 0.0, totals, 1.0)
    target = jnp.where(query & (cols == rows + 1), 1.0, 0.0)
    d_score = loss_scale * (soft - target)
    both = d_score + d_score.T
    coef = jnp.sum(both * scores, axis=1, keepdims=True)
    mix = score_scale * both / norms - jnp.where(rows == cols, coef / (norm_col * norm_col), 0.0)
    mean, gain = mean_ref[...], gain_ref[...]
    d_pooled = jnp.dot(mix, mean * gain, precision=highest, preferred_element_type=f32)
    gain_grad_ref[...] = jnp.sum(d_pooled * mean, axis=0, keepdims=True)
    own_ref[...] = d_pooled * gain * (1.0 / SEQ)
    for place in range(group):
        part = part_ref[(place % NZL) * NY + place // NZL, 1]
        gain = gain_block_ref[0, place : place + 1, :]
        d_pooled = jnp.dot(mix, part * gain, precision=highest, preferred_element_type=f32)
        block_ref[place] = d_pooled * gain * (1.0 / SEQ)


def contrast(parts, same, gain_blocks, means, gain, x):
    group, _, seqs, lanes = parts.shape
    width = means.shape[1]
    whole = lambda shape: pl.BlockSpec(shape, lambda i, s: (0,) * len(shape))
    return pl.pallas_call(
        contrast_kernel,
        grid_spec=pltpu.PrefetchScalarGridSpec(
            num_scalar_prefetch=1,
            grid=(1,),
            in_specs=[
                whole(parts.shape),
                whole(same.shape),
                pl.BlockSpec((1, group, lanes), lambda i, s: (s[0], 0, 0)),
                whole(means.shape),
                whole(gain.shape),
            ],
            out_specs=[whole((group, seqs, lanes)), whole((seqs, width)), whole((1, width))],
        ),
        out_shape=(
            jax.ShapeDtypeStruct((group, seqs, lanes), f32),
            jax.ShapeDtypeStruct((seqs, width), f32),
            jax.ShapeDtypeStruct((1, width), f32),
        ),
        compiler_params=pltpu.CompilerParams(vmem_limit_bytes=16 * MIB),
        cost_estimate=pl.CostEstimate(
            flops=12 * seqs * seqs * (group * lanes + width), bytes_accessed=16 * group * seqs * lanes, transcendentals=seqs * seqs
        ),
    )(x.astype(jnp.int32).reshape(1), parts, same, gain_blocks, means, gain)


def row_to_column(row):
    n = row.shape[1]
    eye = lax.broadcasted_iota(jnp.int32, (n, n), 0) == lax.broadcasted_iota(jnp.int32, (n, n), 1)
    return jnp.sum(jnp.where(eye, jnp.broadcast_to(row, (n, n)), 0.0), axis=1, keepdims=True)


def column_to_row(column):
    n = column.shape[0]
    eye = lax.broadcasted_iota(jnp.int32, (n, n), 0) == lax.broadcasted_iota(jnp.int32, (n, n), 1)
    return jnp.sum(jnp.where(eye, jnp.broadcast_to(column, (n, n)), 0.0), axis=0, keepdims=True)


def along_kernel(plan_ref, layer_ref, scaled_ref, out_ref):
    group, _, tokens, _ = layer_ref.shape
    first = plan_ref[pl.program_id(0)]
    for s in range(tokens // SEQ):
        rows = slice(s * SEQ, (s + 1) * SEQ)
        along = None
        for p in range(group):
            term = layer_ref[p, 0, rows, :].astype(f32) * scaled_ref[p, pl.ds(first + s, 1), :]
            along = term if along is None else along + term
        out_ref[0, s : s + 1, :] = column_to_row(jnp.sum(along, axis=1, keepdims=True))


def along_part(strips, scaled, plan):
    group, _, tokens, lanes = strips.shape
    seqs_here = tokens // SEQ
    return pl.pallas_call(
        along_kernel,
        grid_spec=pltpu.PrefetchScalarGridSpec(
            num_scalar_prefetch=1,
            grid=(NX,),
            in_specs=[
                pl.BlockSpec((group, 1, tokens, lanes), lambda i, s: (0, i, 0, 0)),
                pl.BlockSpec(scaled.shape, lambda i, s: (0, 0, 0)),
            ],
            out_specs=pl.BlockSpec((1, seqs_here, SEQ), lambda i, s: (i, 0, 0)),
        ),
        out_shape=jax.ShapeDtypeStruct((NX, seqs_here, SEQ), f32),
        compiler_params=pltpu.CompilerParams(vmem_limit_bytes=16 * MIB),
        cost_estimate=pl.CostEstimate(
            flops=2 * NX * tokens * group * lanes, bytes_accessed=2 * NX * tokens * group * lanes, transcendentals=0
        ),
    )(plan, strips, scaled)


ORDERS = ((0, 1, 2, 3), (2, 0, 3, 1), (1, 3, 0, 2), (3, 2, 1, 0))


def group_grad_kernel(plan_ref, layer_ref, scaled_ref, *refs):
    *part_refs, low_ref, coef_ref, factor_ref = refs
    group, _, tokens, lanes = layer_ref.shape
    seqs_here = tokens // SEQ
    here = pl.program_id(0)
    first, me = plan_ref[here], plan_ref[4]

    @pl.when(here == 0)
    def _():
        for i in range(NX):
            inverse = part_refs[i][NX]
            along = part_refs[0][i]
            for ref, order in zip(part_refs[1:], ORDERS[1:]):
                along += ref[order[i]]
            coef = inverse * inverse * inverse * along / (NX * group * lanes)
            factor_ref[i, :seqs_here] = inverse
            factor_ref[i, seqs_here:] = coef
            if i == 0:
                coef_ref[...] = coef

    for s in range(seqs_here):
        rows = slice(s * SEQ, (s + 1) * SEQ)
        inverse = row_to_column(factor_ref[here, s : s + 1, :])
        coef = row_to_column(factor_ref[here, seqs_here + s : seqs_here + s + 1, :])
        for p in range(group):
            scaled = scaled_ref[p, pl.ds(first + s, 1), :]
            low = inverse * scaled - layer_ref[p, 0, rows, :].astype(f32) * coef
            side = p % 2 * lanes
            low_ref[(p // 2) ^ me, rows, side : side + lanes] = low.astype(bf16)


def group_grad(strips, scaled, parts, plan):
    group, _, tokens, lanes = strips.shape
    quarter = group * lanes // 4
    seqs_here = tokens // SEQ
    return pl.pallas_call(
        group_grad_kernel,
        grid_spec=pltpu.PrefetchScalarGridSpec(
            num_scalar_prefetch=1,
            grid=(NX,),
            in_specs=[
                pl.BlockSpec((group, 1, tokens, lanes), lambda i, s: (0, i, 0, 0)),
                pl.BlockSpec(scaled.shape, lambda i, s: (0, 0, 0)),
            ]
            + [pl.BlockSpec(parts[0].shape, lambda i, s: (0, 0, 0))] * NX,
            out_specs=[
                pl.BlockSpec((4, tokens, quarter), lambda i, s: (0, i, 0)),
                pl.BlockSpec((seqs_here, SEQ), lambda i, s: (0, 0)),
            ],
            scratch_shapes=[pltpu.VMEM((NX, 2 * seqs_here, SEQ), f32)],
        ),
        out_shape=(
            jax.ShapeDtypeStruct((4, NX * tokens, quarter), bf16),
            jax.ShapeDtypeStruct((seqs_here, SEQ), f32),
        ),
        compiler_params=pltpu.CompilerParams(vmem_limit_bytes=24 * MIB),
        cost_estimate=pl.CostEstimate(
            flops=3 * NX * tokens * group * lanes, bytes_accessed=4 * NX * tokens * group * lanes, transcendentals=0
        ),
    )(plan, strips, scaled, *parts)


def hidden_grad_kernel(low_ref, weight_ref, out_ref, total_ref):
    step = pl.program_id(0)
    low = jnp.concatenate([low_ref[j, 0] for j in range(low_ref.shape[0])], axis=1)
    part = lax.dot_general(
        low, weight_ref[...], (((1,), (1,)), ((), ())), preferred_element_type=f32
    )

    @pl.when(step == 0)
    def _():
        total_ref[...] = part

    @pl.when(step > 0)
    def _():
        total_ref[...] += part

    @pl.when(step == pl.num_programs(0) - 1)
    def _():
        out_ref[...] = total_ref[...].astype(out_ref.dtype)


def hidden_grad(low, weight):
    group, blocks, tokens, lanes = low.shape
    units = weight.shape[0]
    model_width = group * blocks * lanes
    steps = 2 * blocks
    return pl.pallas_call(
        hidden_grad_kernel,
        grid=(steps,),
        in_specs=[
            pl.BlockSpec((group // 2, 1, tokens, lanes), lambda i: (i % 2, i // 2, 0, 0)),
            pl.BlockSpec((units, model_width // steps), lambda i: (0, i)),
        ],
        out_specs=pl.BlockSpec((tokens, units), lambda i: (0, 0)),
        out_shape=jax.ShapeDtypeStruct((tokens, units), bf16),
        scratch_shapes=[pltpu.VMEM((tokens, units), f32)],
        compiler_params=pltpu.CompilerParams(vmem_limit_bytes=56 * MIB),
        cost_estimate=pl.CostEstimate(
            flops=2 * tokens * units * model_width,
            bytes_accessed=2 * (tokens * model_width + units * model_width + tokens * units),
            transcendentals=0,
        ),
    )(low, weight)


def tie(*values):
    return lax.optimization_barrier(values)


def gather_start(value):
    return {
        (0, 0): value,
        (1, 0): over_zl(value),
        (0, 1): over_y(value, -1),
        (0, 3): over_y(value, 1),
    }


def gather_next(got):
    got = dict(got)
    got[1, 1] = over_y(got[1, 0], -1)
    got[1, 3] = over_y(got[1, 0], 1)
    got[0, 2] = over_y(got[0, 3], 1)
    return got


def gather_end(got, zl, y):
    got = dict(got)
    got[1, 2] = over_y(got[1, 1], -1)
    shape = got[0, 0].shape
    out = jnp.zeros((NZL * NY,) + shape, got[0, 0].dtype)
    for (part, step), value in got.items():
        place = ((y + step) % NY) * NZL + (zl + part) % NZL
        out = lax.dynamic_update_slice(out, value[None], (place,) + (0,) * len(shape))
    return out


def per_device(resid, hidden, down_weight, gain, domain_ids):
    tokens, units = hidden.shape
    model_width = down_weight.shape[1]
    group = lax.axis_size("tensor")
    shards = lax.axis_size("dp")
    width = model_width // group
    lanes = width // NX
    seqs_here = tokens // SEQ
    seqs = seqs_here * shards
    rank = lax.axis_index("tensor")
    zl, y = rank // NY, rank % NY
    place = y * NZL + zl
    shard = lax.axis_index("dp")
    x, zh, core = shard // (NZH * NCORE), (shard // NCORE) % NZH, shard % NCORE

    with jax.named_scope("tables"):
        owner = jnp.repeat(domain_ids, seqs_here)
        same = (owner[:, None] == owner[None, :]).astype(f32)
        gain_blocks = gain.reshape(NX, group, lanes)
        gain_own = lax.dynamic_slice_in_dim(gain_blocks, place, 1, 1).reshape(1, width)
        peers = [((x + step) % NX) * (NZH * NCORE) + zh * NCORE + core for step in (0, -1, 1, 2)]
        plan = [p * seqs_here for p in peers] + [zh * NCORE + core]
        plan = jnp.stack([jnp.asarray(v, jnp.int32) for v in plan])

    with jax.named_scope("hidden_exchange"):
        hidden_left = over_x(hidden, 1)
        hidden_right = over_x(hidden, -1)

    with jax.named_scope("resid_exchange"):
        block = rank // 2
        pieces = []
        for step in range(NY):
            first = ((block + step) % NY) * lanes
            piece = lax.dynamic_slice_in_dim(resid, first, lanes, 1)
            pieces.append(lax.ppermute(piece, "tensor", resid_route(step)))

    with jax.named_scope("layer_sum"):
        def dot_for(step, dtype):
            return pair_dot(hidden, down_weight, (y + step) % NY, zl, group, dtype)

        far = dot_for(2, bf16)
        from_left = over_y(far[0], 1)
        from_right = over_y(far[1], -1)
        right = dot_for(1, bf16)
        left = dot_for(3, bf16)
        got_right1 = over_y(right[1], 1)
        got_left0 = over_y(left[0], -1)
        from_left, from_right, *pieces = tie(from_left, from_right, *pieces)
        right0 = (right[0].astype(f32) + from_left.astype(f32)).astype(bf16)
        left1 = (left[1].astype(f32) + from_right.astype(f32)).astype(bf16)
        got_right0 = over_y(right0, 1)
        got_left1 = over_y(left1, -1)
        own = dot_for(0, f32)
        got_right1, got_left0, hidden_left, hidden_right = tie(
            got_right1, got_left0, hidden_left, hidden_right
        )
        other_sum = own[1] + got_right1.astype(f32) + got_left1.astype(f32)
        from_zl = over_zl(other_sum.astype(bf16))
        at = (y % 2) * NZL + zl
        pieces = jnp.stack(pieces)
        resid_strips = jnp.concatenate(
            [lax.dynamic_slice_in_dim(pieces, (at - b) % NY, 1, 0) for b in range(NX)], axis=0
        )
        layer = (
            own[0]
            + resid_strips.astype(f32)
            + got_right0.astype(f32)
            + got_left0.astype(f32)
            + from_zl.astype(f32)
        )

    with jax.named_scope("hidden_exchange"):
        hidden_far = (
            over_x(hidden_left[: tokens // 2], 1),
            over_x(hidden_right[tokens // 2 :], -1),
        )
        hidden_rows = jnp.concatenate((hidden, hidden_left, hidden_right) + hidden_far, axis=0)

    with jax.named_scope("strip_exchange"):
        low_layer = layer.astype(bf16)
        strips_x = [lax.dynamic_slice_in_dim(low_layer, x, 1, 0)]
        for step in (1, -1, 2):
            strip = lax.dynamic_slice_in_dim(low_layer, (x + step) % NX, 1, 0)
            strips_x.append(over_x(strip, step))
        got = gather_start(jnp.concatenate(strips_x, axis=0))

    with jax.named_scope("norm"):
        squares = jnp.sum(layer * layer, axis=(0, 2)).reshape(seqs_here, SEQ)
        squares = jnp.sum(gather_small(squares, "tensor"), axis=0)
        inverse = lax.rsqrt(squares / model_width + eps_norm)
        weighted = layer.reshape(NX, seqs_here, SEQ, lanes) * inverse[None, :, :, None]
        means = jnp.mean(weighted, axis=2).transpose(1, 0, 2).reshape(seqs_here, width)

    with jax.named_scope("contrast"):
        means_all = gather_small(means, "dp")
        keys = list(got)
        means_all, hidden_rows, *values = tie(means_all, hidden_rows, *got.values())
        got = gather_next(dict(zip(keys, values)))
        means_all = means_all.reshape(seqs, width)
        parts = gather_small(gram_part(means_all, gain_own, x), "tensor")
        keys = list(got)
        parts, *values = tie(parts, *got.values())
        strips = gather_end(dict(zip(keys, values)), zl, y)
        scaled, scaled_own, gain_grad = contrast(parts, same, gain_blocks, means_all, gain_own, x)

    with jax.named_scope("along"):
        part = jnp.concatenate([along_part(strips, scaled, plan), inverse[None]], axis=0)
        parts_x = [part] + [over_x(part, step) for step in (1, -1, 2)]

    with jax.named_scope("down_grad"):
        low_x, coef = group_grad(strips, scaled, parts_x, plan)

        def down(low):
            return lax.dot_general(
                hidden_rows, low, (((0,), (0,)), ((), ())), preferred_element_type=f32
            )

        from_core = over_core(down(low_x[3]))
        summed = (down(low_x[2]) + from_core).astype(bf16)

    with jax.named_scope("layer_grad"):
        own_rows = lax.dynamic_slice_in_dim(scaled_own, shard * seqs_here, seqs_here, 0)
        own_rows = own_rows.reshape(seqs_here, NX, lanes).transpose(1, 0, 2)
        low_own = (
            inverse[None, :, :, None] * own_rows[:, :, None, :]
            - layer.reshape(NX, seqs_here, SEQ, lanes) * coef[None, :, :, None]
        ).astype(bf16)
        got = gather_start(low_own.reshape(NX, tokens, lanes))
        keys = list(got)
        summed, low0, low1, *values = tie(summed, low_x[0], low_x[1], *got.values())
        low_rows = gather_end(gather_next(dict(zip(keys, values))), zl, y)
        grad_resid = lax.dynamic_slice(
            low_rows, ((rank % 2) * 4, rank // 2, 0, 0), (4, 1, tokens, lanes)
        )
        grad_resid = grad_resid[:, 0].transpose(1, 0, 2).reshape(tokens, width)
        places = [(p % NZL) * NY + p // NZL for p in range(group)]
        gain_grad = gather_small(gain_grad.reshape(NX, lanes), "tensor")
        gain_grad = jnp.stack([gain_grad[p] for p in places])
        grad_gain = lax.dynamic_slice(
            gain_grad, ((rank % 2) * 4, rank // 2, 0), (4, 1, lanes)
        ).reshape(width)

    with jax.named_scope("down_grad"):
        across = over_zh(summed)
        near = down(low0) + over_core(down(low1))
        near, across = tie(near, across)
        grad_down = near + across.astype(f32)

    with jax.named_scope("hidden_grad"):
        grad_hidden = hidden_grad(low_rows, down_weight)

    return (grad_hidden, grad_resid, grad_down, grad_gain)


def solution(mesh):
    return jax.shard_map(
        per_device,
        mesh=mesh,
        in_specs=(P("dp", "tensor"), P("dp", "tensor"), P("tensor", None), P(), P()),
        out_specs=(P("dp", "tensor"), P("dp", "tensor"), P("tensor", "dp"), P("tensor")),
        check_vma=False,
    )
```

time: 287 us -> 275 us (0.958)
  local copies, waits for them, and re-layouts: 47.3 us -> 38.9 us
  starting transfers between devices: 71.1 us -> 77.9 us
  matrix products: 22.4 us -> 17.8 us
    ppermute x1, waiting for transfers between devices: 15.9 us -> 0.01 us  [over_zh(): return lax.ppermute(value, 'dp', dp_route(0, 1, 0))]
    all_to_all x3 -> x4, waiting for transfers between devices: 15.3 us -> 29.9 us  [gather_small(): return lax.all_to_all(copies, axis, 0, 0)]
    ppermute x12 -> x18, waiting for transfers between devices: 34.5 us -> 26.1 us  [over_y(): return lax.ppermute(value, 'tensor', tensor_route(0, step))]
    ppermute x2 -> x3, waiting for transfers between devices: 0.17 us -> 7.43 us  [over_zl(): return lax.ppermute(value, 'tensor', tensor_route(1, 0))]
    all_to_all x3 -> x4, starting transfers between devices: 16.2 us -> 22.4 us  [gather_small(): return lax.all_to_all(copies, axis, 0, 0)]
    squeeze x3 -> x1, local copies, waits for them, and re-layouts: 5.01 us -> 0.14 us  [per_device(): summed, low0, low1, *values = tie(summed, low_x[0], low_x[1], *got.values())]
    broadcast_in_dim x1 -> x0, local copies, waits for them, and re-layouts: 4.78 us -> none  [per_device(): strips = jnp.zeros((group,) + message.shape, bf16)]
    dot_general x4, matrix products: 22.4 us -> 17.8 us  [down(): lax.dot_general(hidden_rows, low, (((0,), (0,)), ((), ())), preferred_ele...]
  transfers between devices with their start and end apart: 34 -> 42, of which waited for: 16 -> 16; matrix products, arithmetic and copies ran while one was open for 23% -> 20% of each run, Pallas kernels for 16% -> 15%
where the time goes in v3:
time: 275 us; the launch traced here: 273 us
  starting transfers between devices  77.9 us (28%)
  waiting for transfers between devices  75.1 us (27%)
  Pallas kernels  52.1 us (19%)
  local copies, waits for them, and re-layouts  38.9 us (14%)
  matrix products  17.8 us (6%)
  other arithmetic  10.4 us (4%)
    all_to_all x4, waiting for transfers between devices, gather_small(): return lax.all_to_all(copies, axis, 0, 0)  29.9 us
    pallas_call x4, Pallas kernels, pair_dot(): pl.pallas_call(pair_dot_kernel, grid_spec=pltpu.PrefetchScalarGridSpec(nu...  26.4 us
    ppermute x18, waiting for transfers between devices, over_y(): return lax.ppermute(value, 'tensor', tensor_route(0, step))  26.1 us
    ppermute x18, starting transfers between devices, over_y(): return lax.ppermute(value, 'tensor', tensor_route(0, step))  24.1 us
    all_to_all x4, starting transfers between devices, gather_small(): return lax.all_to_all(copies, axis, 0, 0)  22.4 us
    dot_general x4, matrix products, down(): lax.dot_general(hidden_rows, low, (((0,), (0,)), ((), ())), preferred_ele...  17.8 us
    pallas_call x1, Pallas kernels, hidden_grad(): pl.pallas_call(hidden_grad_kernel, grid=(steps,), in_specs=[pl.BlockSpec(...  15.6 us
    ppermute x4, starting transfers between devices, per_device(): pieces.append(lax.ppermute(piece, 'tensor', resid_route(step)))  12.9 us
  transfers between devices with their start and end apart: 42, of which 16 were waited for; matrix products, arithmetic and copies ran while one was open for 20% of the time, Pallas kernels for 15%

profile of v3, /device:TPU:0, one launch (start us, length us, event | category | flops | bytes accessed | tf_op | source)
XLA Modules:
  0.0 273.4 jit_solution(11256584574387211229)
XLA Ops:
  0.6 2.9 %collective-permute-start.10 = (bf16[512,1792]{1,0:T(8,128)(2,1)}, bf16[512,1792]{1,0:T(8,128)(2,1)S(1)}, u32[]{:S(2)}, u32[]{:S(2)}) collective-permute-start(bf16[512,1792]{1,0:T(8,128)(2,1)} %hidden_ref.7), channel_id=1, source_target_pairs={{0,96},{8,104},{16,112},{24,120},{32,0},{40,8},{48,16},{56,24},{64... | collective-permute-start | bytes 5505032 | tf_op jit(solution)/shard_map/hidden_exchange/ppermute | solution.py:49
  5.4 6.2 %collective-permute-start.3 = (bf16[512,128]{1,0:T(8,128)(2,1)S(1)}, bf16[512,128]{1,0:T(8,128)(2,1)S(1)}, u32[]{:S(2)}, u32[]{:S(2)}) collective-permute-start(bf16[512,128]{1,0:T(8,128)(2,1)S(1)} %get-tuple-element.125), channel_id=1, source_target_pairs={{0,4},{1,6},{2,1},{3,3},{4,5},{5,7},{6,0},{7,2},{8,12},{9,14},{10,... | collective-permute-start | bytes 393224 | tf_op jit(solution)/shard_map/resid_exchange/ppermute | solution.py:429
  12.2 6.7 %layer_sum.5 = (bf16[4,512,128]{2,1,0:T(8,128)(2,1)}, bf16[4,512,128]{2,1,0:T(8,128)(2,1)}) custom-call(s32[2]{0:T(128)} %get-tuple-element.132.plan_ref, bf16[512,1792]{1,0:T(8,128)(2,1)} %hidden_ref.7, bf16[1792,4096]{1,0:T(8,128)(2,1)} %weight_ref.9), custom_call_target="tpu_custom_call" | custom-call | flops 1879048192 | bytes 6553600 | tf_op jit(solution)/shard_map/layer_sum/pallas_call | solution.py:88
  18.9 1.9 collective-permute-start
  24.9 6.5 %layer_sum.6 = (bf16[4,512,128]{2,1,0:T(8,128)(2,1)}, bf16[4,512,128]{2,1,0:T(8,128)(2,1)}) custom-call(s32[2]{0:T(128)} %get-tuple-element.133.plan_ref, bf16[512,1792]{1,0:T(8,128)(2,1)} %hidden_ref.7, bf16[1792,4096]{1,0:T(8,128)(2,1)} %weight_ref.9), custom_call_target="tpu_custom_call" | custom-call | flops 1879048192 | bytes 6553600 | tf_op jit(solution)/shard_map/layer_sum/pallas_call | solution.py:88
  31.4 2.8 %collective-permute-done.4 = bf16[512,128]{1,0:T(8,128)(2,1)S(1)} collective-permute-done((bf16[512,128]{1,0:T(8,128)(2,1)S(1)}, bf16[512,128]{1,0:T(8,128)(2,1)S(1)}, u32[]{:S(2)}, u32[]{:S(2)}) %collective-permute-start.4) | collective-permute-done | bytes 131104 | tf_op jit(solution)/shard_map/resid_exchange/ppermute | solution.py:429
  34.2 5.4 %collective-permute-start.5 = (bf16[512,128]{1,0:T(8,128)(2,1)S(1)}, bf16[512,128]{1,0:T(8,128)(2,1)S(1)}, u32[]{:S(2)}, u32[]{:S(2)}) collective-permute-start(bf16[512,128]{1,0:T(8,128)(2,1)S(1)} %get-tuple-element.124), channel_id=1, source_target_pairs={{0,5},{1,7},{2,0},{3,2},{4,4},{5,6},{6,1},{7,3},{8,13},{9,15},{10,... | collective-permute-start | bytes 393224 | tf_op jit(solution)/shard_map/resid_exchange/ppermute | solution.py:429
  39.6 6.5 %layer_sum.7 = (bf16[4,512,128]{2,1,0:T(8,128)(2,1)}, bf16[4,512,128]{2,1,0:T(8,128)(2,1)}) custom-call(s32[2]{0:T(128)} %get-tuple-element.134.plan_ref, bf16[512,1792]{1,0:T(8,128)(2,1)} %hidden_ref.7, bf16[1792,4096]{1,0:T(8,128)(2,1)} %weight_ref.9), custom_call_target="tpu_custom_call" | custom-call | flops 1879048192 | bytes 6553600 | tf_op jit(solution)/shard_map/layer_sum/pallas_call | solution.py:88
  46.7 2.7 collective-permute-start.8
  49.4 2.0 add_convert_fusion.1
  51.6 6.7 %layer_sum.4 = (f32[4,512,128]{2,1,0:T(8,128)}, f32[4,512,128]{2,1,0:T(8,128)}) custom-call(s32[2]{0:T(128)} %get-tuple-element.131.plan_ref, bf16[512,1792]{1,0:T(8,128)(2,1)} %hidden_ref.7, bf16[1792,4096]{1,0:T(8,128)(2,1)} %weight_ref.9), custom_call_target="tpu_custom_call" | custom-call | flops 1879048192 | bytes 6553600 | tf_op jit(solution)/shard_map/layer_sum/pallas_call | solution.py:88
  60.7 1.9 collective-permute-start.6
  62.6 7.2 %collective-permute-done.11 = bf16[4,512,128]{2,1,0:T(8,128)(2,1)} collective-permute-done((bf16[4,512,128]{2,1,0:T(8,128)(2,1)}, bf16[4,512,128]{2,1,0:T(8,128)(2,1)}, u32[]{:S(2)}, u32[]{:S(2)}) %collective-permute-start.11) | collective-permute-done | bytes 524320 | tf_op jit(solution)/shard_map/layer_sum/ppermute | solution.py:61
  72.4 2.2 slice.42
  75.8 3.0 %collective-permute-start.14 = (bf16[256,1792]{1,0:T(8,128)(2,1)}, bf16[256,1792]{1,0:T(8,128)(2,1)}, u32[]{:S(2)}, u32[]{:S(2)}) collective-permute-start(bf16[256,1792]{1,0:T(8,128)(2,1)} %slice.43), channel_id=1, source_target_pairs={{0,96},{8,104},{16,112},{24,120},{32,0},{40,8},{48,16},{56,24},{64... | collective-permute-start | bytes 2752520 | tf_op jit(solution)/shard_map/hidden_exchange/ppermute | solution.py:49
  78.8 2.9 %constant_dynamic-update-slice_fusion.3 = bf16[2048,1792]{1,0:T(8,128)(2,1)} fusion(bf16[2048,1792]{1,0:T(8,128)(2,1)} %constant_dynamic-update-slice_fusion.4, bf16[512,1792]{1,0:T(8,128)(2,1)} %collective-permute-done.9), kind=kLoop, calls=%fused_computation.43 | loop fusion | bytes 3670016
  85.3 5.3 %all-to-all-start = ((f32[8,4,128]{2,1,0:T(4,128)}), f32[8,4,128]{2,1,0:T(4,128)S(1)}, u32[]{:S(2)}, u32[]{:S(2)}) async-start(f32[8,4,128]{2,1,0:T(4,128)} %broadcast_in_dim.84), calls=%async_computation | async-start | bytes 32768 | tf_op jit(solution)/shard_map/norm/all_to_all | solution.py:71
  90.6 3.2 %collective-permute-start.16 = (bf16[1,512,128]{2,1,0:T(8,128)(2,1)S(1)}, bf16[1,512,128]{2,1,0:T(8,128)(2,1)S(1)}, u32[]{:S(2)}, u32[]{:S(2)}) collective-permute-start(bf16[1,512,128]{2,1,0:T(8,128)(2,1)S(1)} %get-tuple-element.118), channel_id=1, source_target_pairs={{0,96},{8,104},{16,112},{24,120},{32,0},{40,8},{48,16},{56,24},{64... | collective-permute-start | bytes 393224 | tf_op jit(solution)/shard_map/strip_exchange/ppermute | solution.py:49
  93.9 2.9 %all-to-all-done = f32[8,4,128]{2,1,0:T(4,128)S(1)} async-done(((f32[8,4,128]{2,1,0:T(4,128)}), f32[8,4,128]{2,1,0:T(4,128)S(1)}, u32[]{:S(2)}, u32[]{:S(2)}) %all-to-all-start) | async-done | bytes 16416 | tf_op jit(solution)/shard_map/norm/all_to_all | solution.py:71
  102.5 2.8 %collective-permute-start.19 = (bf16[4,512,128]{2,1,0:T(8,128)(2,1)S(1)}, bf16[4,512,128]{2,1,0:T(8,128)(2,1)S(1)}, u32[]{:S(2)}, u32[]{:S(2)}) collective-permute-start(bf16[4,512,128]{2,1,0:T(8,128)(2,1)S(1)} %pad_maximum_fusion.1), channel_id=1, source_target_pairs={{0,3},{1,0},{2,1},{3,2},{4,7},{5,4},{6,5},{7,6},{8,11},{9,8},{10,9... | collective-permute-start | bytes 1572872 | tf_op jit(solution)/shard_map/strip_exchange/ppermute | solution.py:61
  106.0 7.7 %all-to-all-start.1 = ((f32[16,4,512]{2,1,0:T(4,128)}), f32[16,4,512]{2,1,0:T(4,128)S(1)}, u32[]{:S(2)}, u32[]{:S(2)}) async-start(f32[16,4,512]{2,1,0:T(4,128)} %broadcast_in_dim.86), calls=%async_computation.1 | async-start | bytes 262144 | tf_op jit(solution)/shard_map/contrast/all_to_all | solution.py:71
  113.8 2.2 constant_dynamic-update-slice_fusion.1
  115.9 2.2 constant_dynamic-update-slice_fusion
  118.1 3.6 %all-to-all-done.1 = f32[16,4,512]{2,1,0:T(4,128)S(1)} async-done(((f32[16,4,512]{2,1,0:T(4,128)}), f32[16,4,512]{2,1,0:T(4,128)S(1)}, u32[]{:S(2)}, u32[]{:S(2)}) %all-to-all-start.1) | async-done | bytes 131104 | tf_op jit(solution)/shard_map/contrast/all_to_all | solution.py:71
  121.7 3.5 %collective-permute-start.21 = (bf16[4,512,128]{2,1,0:T(8,128)(2,1)S(1)}, bf16[4,512,128]{2,1,0:T(8,128)(2,1)}, u32[]{:S(2)}, u32[]{:S(2)}) collective-permute-start(bf16[4,512,128]{2,1,0:T(8,128)(2,1)S(1)} %collective-permute-done.18), channel_id=1, source_target_pairs={{0,3},{1,0},{2,1},{3,2},{4,7},{5,4},{6,5},{7,6},{8,11},{9,8},{10,9... | collective-permute-start | bytes 1572872 | tf_op jit(solution)/shard_map/contrast/ppermute | solution.py:61
  126.4 6.0 %all-to-all-start.2 = ((f32[8,2,64,128]{3,2,1,0:T(8,128)}), f32[8,2,64,128]{3,2,1,0:T(8,128)S(1)}, u32[]{:S(2)}, u32[]{:S(2)}) async-start(f32[8,2,64,128]{3,2,1,0:T(8,128)} %broadcast_in_dim.87), calls=%async_computation.2 | async-start | bytes 1048576 | tf_op jit(solution)/shard_map/contrast/all_to_all | solution.py:71
  132.8 23.4 %all-to-all-done.2.part_ref = f32[8,2,64,128]{3,2,1,0:T(8,128)S(1)} async-done(((f32[8,2,64,128]{3,2,1,0:T(8,128)}), f32[8,2,64,128]{3,2,1,0:T(8,128)S(1)}, u32[]{:S(2)}, u32[]{:S(2)}) %all-to-all-start.2) | async-done | bytes 524320 | tf_op jit(solution)/shard_map/contrast/all_to_all | solution.py:71
  157.7 3.4 %all-to-all-start.3 = ((f32[8,4,128]{2,1,0:T(4,128)}), f32[8,4,128]{2,1,0:T(4,128)S(1)}, u32[]{:S(2)}, u32[]{:S(2)}) async-start(f32[8,4,128]{2,1,0:T(4,128)} %broadcast_in_dim.106), calls=%async_computation.3 | async-start | bytes 32768 | tf_op jit(solution)/shard_map/layer_grad/all_to_all | solution.py:71
  161.1 3.2 %collective-permute-start.24 = (bf16[4,512,128]{2,1,0:T(8,128)(2,1)}, bf16[4,512,128]{2,1,0:T(8,128)(2,1)}, u32[]{:S(2)}, u32[]{:S(2)}) collective-permute-start(bf16[4,512,128]{2,1,0:T(8,128)(2,1)} %collective-permute-done.21), channel_id=1, source_target_pairs={{0,3},{1,0},{2,1},{3,2},{4,7},{5,4},{6,5},{7,6},{8,11},{9,8},{10,9... | collective-permute-start | bytes 1572872 | tf_op jit(solution)/shard_map/contrast/ppermute | solution.py:61
  164.4 2.9 %broadcast.72.clone = bf16[8,4,512,128]{3,2,1,0:T(8,128)(2,1)} broadcast(bf16[]{:T(256)} %constant.230.clone.1), dimensions={} | broadcast | bytes 4194306 | tf_op jit(solution)/shard_map/broadcast.1
  169.9 1.9 bitcast_dynamic-update-slice_fusion.12
  171.7 1.9 bitcast_dynamic-update-slice_fusion.11
  173.6 1.9 bitcast_dynamic-update-slice_fusion.10
  175.5 1.9 bitcast_dynamic-update-slice_fusion.9
  177.4 1.9 bitcast_dynamic-update-slice_fusion.8.layer_ref
  179.3 4.0 %along.1 = f32[4,4,128]{2,1,0:T(4,128)S(1)} custom-call(s32[5]{0:T(128)S(1)} %stack.85.plan_ref, bf16[8,4,512,128]{3,2,1,0:T(8,128)(2,1)} %bitcast_dynamic-update-slice_fusion.8.layer_ref, f32[8,64,128]{2,1,0:T(8,128)S(1)} %get-tuple-element.82.scaled_ref), custom_call_target="tpu_custom_call" | custom-call | flops 4194304 | bytes 4194304 | tf_op jit(solution)/shard_map/along/pallas_call | solution.py:235
  183.9 2.8 %collective-permute-start.26 = (f32[5,4,128]{2,1,0:T(4,128)S(1)}, f32[5,4,128]{2,1,0:T(4,128)S(1)}, u32[]{:S(2)}, u32[]{:S(2)}) collective-permute-start(f32[5,4,128]{2,1,0:T(4,128)S(1)} %pad_maximum_fusion.2.refs_0_), channel_id=1, source_target_pairs={{0,96},{8,104},{16,112},{24,120},{32,0},{40,8},{48,16},{56,24},{64... | collective-permute-start | bytes 30728 | tf_op jit(solution)/shard_map/along/ppermute | solution.py:49
  188.3 3.5 %collective-permute-done.27.refs_3_ = f32[5,4,128]{2,1,0:T(4,128)S(1)} collective-permute-done((f32[5,4,128]{2,1,0:T(4,128)S(1)}, f32[5,4,128]{2,1,0:T(4,128)S(1)}, u32[]{:S(2)}, u32[]{:S(2)}) %collective-permute-start.27) | collective-permute-done | bytes 10272 | tf_op jit(solution)/shard_map/along/ppermute | solution.py:49
  191.8 4.9 %down_grad.1 = (bf16[4,2048,256]{2,1,0:T(8,128)(2,1)S(1)}, f32[4,128]{1,0:T(4,128)S(1)}) custom-call(s32[5]{0:T(128)S(1)} %stack.85.plan_ref, bf16[8,4,512,128]{3,2,1,0:T(8,128)(2,1)} %bitcast_dynamic-update-slice_fusion.8.layer_ref, f32[8,64,128]{2,1,0:T(8,128)S(1)} %get-tuple-element.82.scaled_ref, f32[5,4,128]{2,1,0:T(4,128)S(1)} %pad_maximum_fusion.2.refs_0_, ...), custom_call_target="tpu_custom_call" | custom-call | flops 6291456 | bytes 8388608 | tf_op jit(solution)/shard_map/down_grad/pallas_call | solution.py:292
  196.7 5.4 %fusion.3 = f32[1792,256]{1,0:T(8,128)S(1)} fusion(bf16[2048,1792]{1,0:T(8,128)(2,1)} %constant_dynamic-update-slice_fusion, bf16[4,2048,256]{2,1,0:T(8,128)(2,1)S(1)} %get-tuple-element.83), kind=kOutput, calls=%fused_computation.7 | convolution fusion | flops 1879048192 | bytes 10223616 | tf_op jit(solution)/shard_map/down_grad/dot_general | solution.py:508
  206.9 3.2 %fusion = bf16[1792,256]{1,0:T(8,128)(2,1)} fusion(f32[1792,256]{1,0:T(8,128)S(1)} %collective-permute-done.28, bf16[2048,1792]{1,0:T(8,128)(2,1)S(1)} %bitcast.101, bf16[4,2048,256]{2,1,0:T(8,128)(2,1)S(1)} %get-tuple-element.83), kind=kOutput, calls=%fused_computation.2 | convolution fusion | flops 1879965696 | bytes 11141120 | tf_op jit(solution)/shard_map/down_grad/dot_general | solution.py:508
  210.1 7.4 %collective-permute-done.29 = bf16[4,512,128]{2,1,0:T(8,128)(2,1)S(1)} collective-permute-done((bf16[4,512,128]{2,1,0:T(8,128)(2,1)S(1)}, bf16[4,512,128]{2,1,0:T(8,128)(2,1)S(1)}, u32[]{:S(2)}, u32[]{:S(2)}) %collective-permute-start.29) | collective-permute-done | bytes 524320 | tf_op jit(solution)/shard_map/layer_grad/ppermute | solution.py:65
  222.5 3.4 %fusion.12 = f32[1792,256]{1,0:T(8,128)} fusion(bf16[2048,1792]{1,0:T(8,128)(2,1)S(1)} %bitcast.101, bf16[2048,256]{1,0:T(8,128)(2,1)S(1)} %get-tuple-element.91), kind=kOutput, calls=%fused_computation.79 | convolution fusion | flops 1879048192 | bytes 10223616 | tf_op jit(solution)/shard_map/down_grad/dot_general | solution.py:508
  228.3 5.1 %collective-permute-done.32 = bf16[4,512,128]{2,1,0:T(8,128)(2,1)S(1)} collective-permute-done((bf16[4,512,128]{2,1,0:T(8,128)(2,1)S(1)}, bf16[4,512,128]{2,1,0:T(8,128)(2,1)S(1)}, u32[]{:S(2)}, u32[]{:S(2)}) %collective-permute-start.32) | collective-permute-done | bytes 524320 | tf_op jit(solution)/shard_map/layer_grad/ppermute | solution.py:61
  236.9 9.2 %collective-permute-done.34 = bf16[4,512,128]{2,1,0:T(8,128)(2,1)S(1)} collective-permute-done((bf16[4,512,128]{2,1,0:T(8,128)(2,1)S(1)}, bf16[4,512,128]{2,1,0:T(8,128)(2,1)S(1)}, u32[]{:S(2)}, u32[]{:S(2)}) %collective-permute-start.34) | collective-permute-done | bytes 524320 | tf_op jit(solution)/shard_map/layer_grad/ppermute | solution.py:61
  246.3 1.9 copy-done.2
  248.3 15.6 %hidden_grad.1 = bf16[512,1792]{1,0:T(8,128)(2,1)} custom-call(bf16[8,4,512,128]{3,2,1,0:T(8,128)(2,1)} %copy-done.2, bf16[1792,4096]{1,0:T(8,128)(2,1)} %weight_ref.9), custom_call_target="tpu_custom_call" | custom-call | flops 7516192768 | bytes 20709376 | tf_op jit(solution)/shard_map/hidden_grad/pallas_call | solution.py:344
  266.2 5.8 %convolution_add_fusion = f32[1792,256]{1,0:T(8,128)S(1)} fusion(f32[1792,256]{1,0:T(8,128)} %collective-permute-done.36, bf16[2048,1792]{1,0:T(8,128)(2,1)} %constant_dynamic-update-slice_fusion, bf16[2048,256]{1,0:T(8,128)(2,1)S(1)} %get-tuple-element.90), kind=kOutput, calls=%fused_computation | convolution fusion | flops 1879506944 | bytes 12058624 | tf_op jit(solution)/shard_map/down_grad/dot_general | solution.py:508
  (144 shorter events, 50.7 us)
Async XLA Ops:
  0.6 62.0 %collective-permute-start.10 = (bf16[512,1792]{1,0:T(8,128)(2,1)}, bf16[512,1792]{1,0:T(8,128)(2,1)S(1)}, u32[]{:S(2)}, u32[]{:S(2)}) collective-permute-start(bf16[512,1792]{1,0:T(8,128)(2,1)} %hidden_ref.7), channel_id=1, source_target_pairs={{0,96},{8,104},{16,112},{24,120},{32,0},{40,8},{48,16},{56,24},{64... | collective-permute-start | bytes 5505032 | tf_op jit(solution)/shard_map/hidden_exchange/ppermute | solution.py:49
  3.5 59.1 %collective-permute-start.9 = (bf16[512,1792]{1,0:T(8,128)(2,1)}, bf16[512,1792]{1,0:T(8,128)(2,1)}, u32[]{:S(2)}, u32[]{:S(2)}) collective-permute-start(bf16[512,1792]{1,0:T(8,128)(2,1)} %hidden_ref.7), channel_id=1, source_target_pairs={{0,32},{8,40},{16,48},{24,56},{32,64},{40,72},{48,80},{56,88},{64,... | collective-permute-start | bytes 5505032 | tf_op jit(solution)/shard_map/hidden_exchange/ppermute | solution.py:49
  4.7 16.2 %collective-permute-start.2 = (bf16[512,128]{1,0:T(8,128)(2,1)S(1)}, bf16[512,128]{1,0:T(8,128)(2,1)S(1)}, u32[]{:S(2)}, u32[]{:S(2)}) collective-permute-start(bf16[512,128]{1,0:T(8,128)(2,1)S(1)} %get-tuple-element.126), channel_id=1, source_target_pairs={{0,0},{1,2},{2,4},{3,6},{4,1},{5,3},{6,5},{7,7},{8,8},{9,10},{10,1... | collective-permute-start | bytes 393224 | tf_op jit(solution)/shard_map/resid_exchange/ppermute | solution.py:429
  5.4 18.8 %collective-permute-start.3 = (bf16[512,128]{1,0:T(8,128)(2,1)S(1)}, bf16[512,128]{1,0:T(8,128)(2,1)S(1)}, u32[]{:S(2)}, u32[]{:S(2)}) collective-permute-start(bf16[512,128]{1,0:T(8,128)(2,1)S(1)} %get-tuple-element.125), channel_id=1, source_target_pairs={{0,4},{1,6},{2,1},{3,3},{4,5},{5,7},{6,0},{7,2},{8,12},{9,14},{10,... | collective-permute-start | bytes 393224 | tf_op jit(solution)/shard_map/resid_exchange/ppermute | solution.py:429
  18.9 27.8 %collective-permute-start = (bf16[4,512,128]{2,1,0:T(8,128)(2,1)}, bf16[4,512,128]{2,1,0:T(8,128)(2,1)S(1)}, u32[]{:S(2)}, u32[]{:S(2)}) collective-permute-start(bf16[4,512,128]{2,1,0:T(8,128)(2,1)} %get-tuple-element.51), channel_id=1, source_target_pairs={{0,1},{1,2},{2,3},{3,0},{4,5},{5,6},{6,7},{7,4},{8,9},{9,10},{10,1... | collective-permute-start | bytes 1572872 | tf_op jit(solution)/shard_map/layer_sum/ppermute | solution.py:61
  20.8 28.6 %collective-permute-start.1 = (bf16[4,512,128]{2,1,0:T(8,128)(2,1)}, bf16[4,512,128]{2,1,0:T(8,128)(2,1)S(1)}, u32[]{:S(2)}, u32[]{:S(2)}) collective-permute-start(bf16[4,512,128]{2,1,0:T(8,128)(2,1)} %get-tuple-element.52), channel_id=1, source_target_pairs={{0,3},{1,0},{2,1},{3,2},{4,7},{5,4},{6,5},{7,6},{8,11},{9,8},{10,9... | collective-permute-start | bytes 1572872 | tf_op jit(solution)/shard_map/layer_sum/ppermute | solution.py:61
  24.2 10.0 %collective-permute-start.4 = (bf16[512,128]{1,0:T(8,128)(2,1)S(1)}, bf16[512,128]{1,0:T(8,128)(2,1)S(1)}, u32[]{:S(2)}, u32[]{:S(2)}) collective-permute-start(bf16[512,128]{1,0:T(8,128)(2,1)S(1)} %get-tuple-element.127), channel_id=1, source_target_pairs={{0,1},{1,3},{2,5},{3,7},{4,0},{5,2},{6,4},{7,6},{8,9},{9,11},{10,1... | collective-permute-start | bytes 393224 | tf_op jit(solution)/shard_map/resid_exchange/ppermute | solution.py:429
  34.2 11.9 %copy-start.8 = (bf16[512,128]{1,0:T(8,128)(2,1)}, bf16[512,128]{1,0:T(8,128)(2,1)S(1)}, u32[]{:S(2)}) copy-start(bf16[512,128]{1,0:T(8,128)(2,1)S(1)} %collective-permute-done.4) | copy-start | bytes 393220
  34.2 11.9 %collective-permute-start.5 = (bf16[512,128]{1,0:T(8,128)(2,1)S(1)}, bf16[512,128]{1,0:T(8,128)(2,1)S(1)}, u32[]{:S(2)}, u32[]{:S(2)}) collective-permute-start(bf16[512,128]{1,0:T(8,128)(2,1)S(1)} %get-tuple-element.124), channel_id=1, source_target_pairs={{0,5},{1,7},{2,0},{3,2},{4,4},{5,6},{6,1},{7,3},{8,13},{9,15},{10,... | collective-permute-start | bytes 393224 | tf_op jit(solution)/shard_map/resid_exchange/ppermute | solution.py:429
  46.1 14.6 %collective-permute-start.7 = (bf16[4,512,128]{2,1,0:T(8,128)(2,1)}, bf16[4,512,128]{2,1,0:T(8,128)(2,1)}, u32[]{:S(2)}, u32[]{:S(2)}) collective-permute-start(bf16[4,512,128]{2,1,0:T(8,128)(2,1)} %get-tuple-element.59), channel_id=1, source_target_pairs={{0,1},{1,2},{2,3},{3,0},{4,5},{5,6},{6,7},{7,4},{8,9},{9,10},{10,1... | collective-permute-start | bytes 1572872 | tf_op jit(solution)/shard_map/layer_sum/ppermute | solution.py:61
  46.7 15.9 %collective-permute-start.8 = (bf16[4,512,128]{2,1,0:T(8,128)(2,1)}, bf16[4,512,128]{2,1,0:T(8,128)(2,1)}, u32[]{:S(2)}, u32[]{:S(2)}) collective-permute-start(bf16[4,512,128]{2,1,0:T(8,128)(2,1)} %get-tuple-element.60), channel_id=1, source_target_pairs={{0,3},{1,0},{2,1},{3,2},{4,7},{5,4},{6,5},{7,6},{8,11},{9,8},{10,9... | collective-permute-start | bytes 1572872 | tf_op jit(solution)/shard_map/layer_sum/ppermute | solution.py:61
  51.4 18.4 %collective-permute-start.11 = (bf16[4,512,128]{2,1,0:T(8,128)(2,1)}, bf16[4,512,128]{2,1,0:T(8,128)(2,1)}, u32[]{:S(2)}, u32[]{:S(2)}) collective-permute-start(bf16[4,512,128]{2,1,0:T(8,128)(2,1)} %add_convert_fusion.1), channel_id=1, source_target_pairs={{0,3},{1,0},{2,1},{3,2},{4,7},{5,4},{6,5},{7,6},{8,11},{9,8},{10,9... | collective-permute-start | bytes 1572872 | tf_op jit(solution)/shard_map/layer_sum/ppermute | solution.py:61
  58.3 11.5 %copy-start.3 = (f32[4,512,128]{2,1,0:T(8,128)S(1)}, f32[4,512,128]{2,1,0:T(8,128)}, u32[]{:S(2)}) copy-start(f32[4,512,128]{2,1,0:T(8,128)} %get-tuple-element.62) | copy-start | bytes 3145732
  60.7 22.4 %collective-permute-start.6 = (bf16[4,512,128]{2,1,0:T(8,128)(2,1)S(1)}, bf16[4,512,128]{2,1,0:T(8,128)(2,1)S(1)}, u32[]{:S(2)}, u32[]{:S(2)}) collective-permute-start(bf16[4,512,128]{2,1,0:T(8,128)(2,1)S(1)} %add_convert_fusion.2), channel_id=1, source_target_pairs={{0,1},{1,2},{2,3},{3,0},{4,5},{5,6},{6,7},{7,4},{8,9},{9,10},{10,1... | collective-permute-start | bytes 1572872 | tf_op jit(solution)/shard_map/layer_sum/ppermute | solution.py:61
  71.2 11.9 %collective-permute-start.12 = (bf16[4,512,128]{2,1,0:T(8,128)(2,1)S(1)}, bf16[4,512,128]{2,1,0:T(8,128)(2,1)S(1)}, u32[]{:S(2)}, u32[]{:S(2)}) collective-permute-start(bf16[4,512,128]{2,1,0:T(8,128)(2,1)S(1)} %add_convert_fusion), channel_id=1, source_target_pairs={{0,4},{1,5},{2,6},{3,7},{4,0},{5,1},{6,2},{7,3},{8,12},{9,13},{10,... | collective-permute-start | bytes 1572872 | tf_op jit(solution)/shard_map/layer_sum/ppermute | solution.py:65
  74.6 39.1 %collective-permute-start.13 = (bf16[256,1792]{1,0:T(8,128)(2,1)}, bf16[256,1792]{1,0:T(8,128)(2,1)}, u32[]{:S(2)}, u32[]{:S(2)}) collective-permute-start(bf16[256,1792]{1,0:T(8,128)(2,1)} %slice.42), channel_id=1, source_target_pairs={{0,32},{8,40},{16,48},{24,56},{32,64},{40,72},{48,80},{56,88},{64,... | collective-permute-start | bytes 2752520 | tf_op jit(solution)/shard_map/hidden_exchange/ppermute | solution.py:49
  75.8 40.2 %collective-permute-start.14 = (bf16[256,1792]{1,0:T(8,128)(2,1)}, bf16[256,1792]{1,0:T(8,128)(2,1)}, u32[]{:S(2)}, u32[]{:S(2)}) collective-permute-start(bf16[256,1792]{1,0:T(8,128)(2,1)} %slice.43), channel_id=1, source_target_pairs={{0,96},{8,104},{16,112},{24,120},{32,0},{40,8},{48,16},{56,24},{64... | collective-permute-start | bytes 2752520 | tf_op jit(solution)/shard_map/hidden_exchange/ppermute | solution.py:49
  84.5 40.7 %copy-start = (f32[4096]{0:T(1024)S(1)}, f32[4096]{0:T(1024)}, u32[]{:S(2)}) copy-start(f32[4096]{0:T(1024)} %param.8) | copy-start | bytes 49156
  85.3 11.5 %all-to-all-start = ((f32[8,4,128]{2,1,0:T(4,128)}), f32[8,4,128]{2,1,0:T(4,128)S(1)}, u32[]{:S(2)}, u32[]{:S(2)}) async-start(f32[8,4,128]{2,1,0:T(4,128)} %broadcast_in_dim.84), calls=%async_computation | async-start | bytes 32768 | tf_op jit(solution)/shard_map/norm/all_to_all | solution.py:71
  90.6 8.1 %collective-permute-start.15 = (bf16[1,512,128]{2,1,0:T(8,128)(2,1)S(1)}, bf16[1,512,128]{2,1,0:T(8,128)(2,1)S(1)}, u32[]{:S(2)}, u32[]{:S(2)}) collective-permute-start(bf16[1,512,128]{2,1,0:T(8,128)(2,1)S(1)} %get-tuple-element.119), channel_id=1, source_target_pairs={{0,32},{8,40},{16,48},{24,56},{32,64},{40,72},{48,80},{56,88},{64,... | collective-permute-start | bytes 393224 | tf_op jit(solution)/shard_map/strip_exchange/ppermute | solution.py:49
  90.6 9.6 %collective-permute-start.16 = (bf16[1,512,128]{2,1,0:T(8,128)(2,1)S(1)}, bf16[1,512,128]{2,1,0:T(8,128)(2,1)S(1)}, u32[]{:S(2)}, u32[]{:S(2)}) collective-permute-start(bf16[1,512,128]{2,1,0:T(8,128)(2,1)S(1)} %get-tuple-element.118), channel_id=1, source_target_pairs={{0,96},{8,104},{16,112},{24,120},{32,0},{40,8},{48,16},{56,24},{64... | collective-permute-start | bytes 393224 | tf_op jit(solution)/shard_map/strip_exchange/ppermute | solution.py:49
  93.9 6.8 %collective-permute-start.17 = (bf16[1,512,128]{2,1,0:T(8,128)(2,1)S(1)}, bf16[1,512,128]{2,1,0:T(8,128)(2,1)S(1)}, u32[]{:S(2)}, u32[]{:S(2)}) collective-permute-start(bf16[1,512,128]{2,1,0:T(8,128)(2,1)S(1)} %get-tuple-element.117), channel_id=1, source_target_pairs={{0,64},{8,72},{16,80},{24,88},{32,96},{40,104},{48,112},{56,120},{... | collective-permute-start | bytes 393224 | tf_op jit(solution)/shard_map/strip_exchange/ppermute | solution.py:49
  96.8 35.6 %copy-start.10 = (s32[16]{0:T(128)S(1)}, s32[16]{0:T(128)}, u32[]{:S(2)}) copy-start(s32[16]{0:T(128)} %param.9) | copy-start | bytes 196
  100.7 21.0 %collective-permute-start.18 = (bf16[4,512,128]{2,1,0:T(8,128)(2,1)S(1)}, bf16[4,512,128]{2,1,0:T(8,128)(2,1)S(1)}, u32[]{:S(2)}, u32[]{:S(2)}) collective-permute-start(bf16[4,512,128]{2,1,0:T(8,128)(2,1)S(1)} %pad_maximum_fusion.1), channel_id=1, source_target_pairs={{0,4},{1,5},{2,6},{3,7},{4,0},{5,1},{6,2},{7,3},{8,12},{9,13},{10,... | collective-permute-start | bytes 1572872 | tf_op jit(solution)/shard_map/strip_exchange/ppermute | solution.py:65
  102.5 19.2 %collective-permute-start.19 = (bf16[4,512,128]{2,1,0:T(8,128)(2,1)S(1)}, bf16[4,512,128]{2,1,0:T(8,128)(2,1)S(1)}, u32[]{:S(2)}, u32[]{:S(2)}) collective-permute-start(bf16[4,512,128]{2,1,0:T(8,128)(2,1)S(1)} %pad_maximum_fusion.1), channel_id=1, source_target_pairs={{0,3},{1,0},{2,1},{3,2},{4,7},{5,4},{6,5},{7,6},{8,11},{9,8},{10,9... | collective-permute-start | bytes 1572872 | tf_op jit(solution)/shard_map/strip_exchange/ppermute | solution.py:61
  105.3 16.4 %collective-permute-start.20 = (bf16[4,512,128]{2,1,0:T(8,128)(2,1)S(1)}, bf16[4,512,128]{2,1,0:T(8,128)(2,1)}, u32[]{:S(2)}, u32[]{:S(2)}) collective-permute-start(bf16[4,512,128]{2,1,0:T(8,128)(2,1)S(1)} %pad_maximum_fusion.1), channel_id=1, source_target_pairs={{0,1},{1,2},{2,3},{3,0},{4,5},{5,6},{6,7},{7,4},{8,9},{9,10},{10,1... | collective-permute-start | bytes 1572872 | tf_op jit(solution)/shard_map/strip_exchange/ppermute | solution.py:61
  106.0 15.7 %all-to-all-start.1 = ((f32[16,4,512]{2,1,0:T(4,128)}), f32[16,4,512]{2,1,0:T(4,128)S(1)}, u32[]{:S(2)}, u32[]{:S(2)}) async-start(f32[16,4,512]{2,1,0:T(4,128)} %broadcast_in_dim.86), calls=%async_computation.1 | async-start | bytes 262144 | tf_op jit(solution)/shard_map/contrast/all_to_all | solution.py:71
  121.7 34.5 %collective-permute-start.21 = (bf16[4,512,128]{2,1,0:T(8,128)(2,1)S(1)}, bf16[4,512,128]{2,1,0:T(8,128)(2,1)}, u32[]{:S(2)}, u32[]{:S(2)}) collective-permute-start(bf16[4,512,128]{2,1,0:T(8,128)(2,1)S(1)} %collective-permute-done.18), channel_id=1, source_target_pairs={{0,3},{1,0},{2,1},{3,2},{4,7},{5,4},{6,5},{7,6},{8,11},{9,8},{10,9... | collective-permute-start | bytes 1572872 | tf_op jit(solution)/shard_map/contrast/ppermute | solution.py:61
  125.2 31.0 %collective-permute-start.22 = (bf16[4,512,128]{2,1,0:T(8,128)(2,1)S(1)}, bf16[4,512,128]{2,1,0:T(8,128)(2,1)}, u32[]{:S(2)}, u32[]{:S(2)}) collective-permute-start(bf16[4,512,128]{2,1,0:T(8,128)(2,1)S(1)} %collective-permute-done.18), channel_id=1, source_target_pairs={{0,1},{1,2},{2,3},{3,0},{4,5},{5,6},{6,7},{7,4},{8,9},{9,10},{10,1... | collective-permute-start | bytes 1572872 | tf_op jit(solution)/shard_map/contrast/ppermute | solution.py:61
  125.2 31.0 %collective-permute-start.23 = (bf16[4,512,128]{2,1,0:T(8,128)(2,1)}, bf16[4,512,128]{2,1,0:T(8,128)(2,1)}, u32[]{:S(2)}, u32[]{:S(2)}) collective-permute-start(bf16[4,512,128]{2,1,0:T(8,128)(2,1)} %collective-permute-done.20), channel_id=1, source_target_pairs={{0,1},{1,2},{2,3},{3,0},{4,5},{5,6},{6,7},{7,4},{8,9},{9,10},{10,1... | collective-permute-start | bytes 1572872 | tf_op jit(solution)/shard_map/contrast/ppermute | solution.py:61
  126.4 29.8 %all-to-all-start.2 = ((f32[8,2,64,128]{3,2,1,0:T(8,128)}), f32[8,2,64,128]{3,2,1,0:T(8,128)S(1)}, u32[]{:S(2)}, u32[]{:S(2)}) async-start(f32[8,2,64,128]{3,2,1,0:T(8,128)} %broadcast_in_dim.87), calls=%async_computation.2 | async-start | bytes 1048576 | tf_op jit(solution)/shard_map/contrast/all_to_all | solution.py:71
  157.1 12.0 %copy-start.6 = (bf16[4,512,128]{2,1,0:T(8,128)(2,1)S(1)}, bf16[4,512,128]{2,1,0:T(8,128)(2,1)}, u32[]{:S(2)}) copy-start(bf16[4,512,128]{2,1,0:T(8,128)(2,1)} %copy-done.5) | copy-start | bytes 1572868
  157.7 19.7 %all-to-all-start.3 = ((f32[8,4,128]{2,1,0:T(4,128)}), f32[8,4,128]{2,1,0:T(4,128)S(1)}, u32[]{:S(2)}, u32[]{:S(2)}) async-start(f32[8,4,128]{2,1,0:T(4,128)} %broadcast_in_dim.106), calls=%async_computation.3 | async-start | bytes 32768 | tf_op jit(solution)/shard_map/layer_grad/all_to_all | solution.py:71
  161.1 16.2 %collective-permute-start.24 = (bf16[4,512,128]{2,1,0:T(8,128)(2,1)}, bf16[4,512,128]{2,1,0:T(8,128)(2,1)}, u32[]{:S(2)}, u32[]{:S(2)}) collective-permute-start(bf16[4,512,128]{2,1,0:T(8,128)(2,1)} %collective-permute-done.21), channel_id=1, source_target_pairs={{0,3},{1,0},{2,1},{3,2},{4,7},{5,4},{6,5},{7,6},{8,11},{9,8},{10,9... | collective-permute-start | bytes 1572872 | tf_op jit(solution)/shard_map/contrast/ppermute | solution.py:61
  183.3 5.0 %collective-permute-start.25 = (f32[5,4,128]{2,1,0:T(4,128)S(1)}, f32[5,4,128]{2,1,0:T(4,128)S(1)}, u32[]{:S(2)}, u32[]{:S(2)}) collective-permute-start(f32[5,4,128]{2,1,0:T(4,128)S(1)} %pad_maximum_fusion.2.refs_0_), channel_id=1, source_target_pairs={{0,32},{8,40},{16,48},{24,56},{32,64},{40,72},{48,80},{56,88},{64,... | collective-permute-start | bytes 30728 | tf_op jit(solution)/shard_map/along/ppermute | solution.py:49
  183.9 4.4 %collective-permute-start.26 = (f32[5,4,128]{2,1,0:T(4,128)S(1)}, f32[5,4,128]{2,1,0:T(4,128)S(1)}, u32[]{:S(2)}, u32[]{:S(2)}) collective-permute-start(f32[5,4,128]{2,1,0:T(4,128)S(1)} %pad_maximum_fusion.2.refs_0_), channel_id=1, source_target_pairs={{0,96},{8,104},{16,112},{24,120},{32,0},{40,8},{48,16},{56,24},{64... | collective-permute-start | bytes 30728 | tf_op jit(solution)/shard_map/along/ppermute | solution.py:49
  186.6 5.2 %collective-permute-start.27 = (f32[5,4,128]{2,1,0:T(4,128)S(1)}, f32[5,4,128]{2,1,0:T(4,128)S(1)}, u32[]{:S(2)}, u32[]{:S(2)}) collective-permute-start(f32[5,4,128]{2,1,0:T(4,128)S(1)} %pad_maximum_fusion.2.refs_0_), channel_id=1, source_target_pairs={{0,64},{8,72},{16,80},{24,88},{32,96},{40,104},{48,112},{56,120},{... | collective-permute-start | bytes 30728 | tf_op jit(solution)/shard_map/along/ppermute | solution.py:49
  196.7 10.1 %slice-start = ((s8[7340032]{0:T(1024)(128)(4,1)}), s8[4194304]{0:T(1024)(128)(4,1)S(1)}, s32[]{:S(2)}) async-start(s8[7340032]{0:T(1024)(128)(4,1)} %bitcast.100), calls=%async_computation.4 | async-start | bytes 8388608
  202.2 4.7 %collective-permute-start.28 = (f32[1792,256]{1,0:T(8,128)S(1)}, f32[1792,256]{1,0:T(8,128)S(1)}, u32[]{:S(2)}, u32[]{:S(2)}) collective-permute-start(f32[1792,256]{1,0:T(8,128)S(1)} %fusion.3), channel_id=1, source_target_pairs={{0,8},{8,0},{16,24},{24,16},{32,40},{40,32},{48,56},{56,48},{64,72... | collective-permute-start | bytes 5505032 | tf_op jit(solution)/shard_map/down_grad/ppermute | solution.py:57
  203.1 14.4 %collective-permute-start.29 = (bf16[4,512,128]{2,1,0:T(8,128)(2,1)S(1)}, bf16[4,512,128]{2,1,0:T(8,128)(2,1)S(1)}, u32[]{:S(2)}, u32[]{:S(2)}) collective-permute-start(bf16[4,512,128]{2,1,0:T(8,128)(2,1)S(1)} %fusion.2), channel_id=1, source_target_pairs={{0,4},{1,5},{2,6},{3,7},{4,0},{5,1},{6,2},{7,3},{8,12},{9,13},{10,... | collective-permute-start | bytes 1572872 | tf_op jit(solution)/shard_map/layer_grad/ppermute | solution.py:65
  204.7 14.0 %collective-permute-start.30 = (bf16[4,512,128]{2,1,0:T(8,128)(2,1)S(1)}, bf16[4,512,128]{2,1,0:T(8,128)(2,1)S(1)}, u32[]{:S(2)}, u32[]{:S(2)}) collective-permute-start(bf16[4,512,128]{2,1,0:T(8,128)(2,1)S(1)} %fusion.2), channel_id=1, source_target_pairs={{0,3},{1,0},{2,1},{3,2},{4,7},{5,4},{6,5},{7,6},{8,11},{9,8},{10,9... | collective-permute-start | bytes 1572872 | tf_op jit(solution)/shard_map/layer_grad/ppermute | solution.py:61
  205.5 15.0 %collective-permute-start.31 = (bf16[4,512,128]{2,1,0:T(8,128)(2,1)S(1)}, bf16[4,512,128]{2,1,0:T(8,128)(2,1)S(1)}, u32[]{:S(2)}, u32[]{:S(2)}) collective-permute-start(bf16[4,512,128]{2,1,0:T(8,128)(2,1)S(1)} %fusion.2), channel_id=1, source_target_pairs={{0,1},{1,2},{2,3},{3,0},{4,5},{5,6},{6,7},{7,4},{8,9},{9,10},{10,1... | collective-permute-start | bytes 1572872 | tf_op jit(solution)/shard_map/layer_grad/ppermute | solution.py:61
  220.5 12.9 %collective-permute-start.32 = (bf16[4,512,128]{2,1,0:T(8,128)(2,1)S(1)}, bf16[4,512,128]{2,1,0:T(8,128)(2,1)S(1)}, u32[]{:S(2)}, u32[]{:S(2)}) collective-permute-start(bf16[4,512,128]{2,1,0:T(8,128)(2,1)S(1)} %collective-permute-done.29), channel_id=1, source_target_pairs={{0,3},{1,0},{2,1},{3,2},{4,7},{5,4},{6,5},{7,6},{8,11},{9,8},{10,9... | collective-permute-start | bytes 1572872 | tf_op jit(solution)/shard_map/layer_grad/ppermute | solution.py:61
  220.8 16.1 %collective-permute-start.33 = (bf16[4,512,128]{2,1,0:T(8,128)(2,1)S(1)}, bf16[4,512,128]{2,1,0:T(8,128)(2,1)S(1)}, u32[]{:S(2)}, u32[]{:S(2)}) collective-permute-start(bf16[4,512,128]{2,1,0:T(8,128)(2,1)S(1)} %collective-permute-done.29), channel_id=1, source_target_pairs={{0,1},{1,2},{2,3},{3,0},{4,5},{5,6},{6,7},{7,4},{8,9},{9,10},{10,1... | collective-permute-start | bytes 1572872 | tf_op jit(solution)/shard_map/layer_grad/ppermute | solution.py:61
  225.9 40.3 %collective-permute-start.36 = (f32[1792,256]{1,0:T(8,128)}, f32[1792,256]{1,0:T(8,128)}, u32[]{:S(2)}, u32[]{:S(2)}) collective-permute-start(f32[1792,256]{1,0:T(8,128)} %fusion.12), channel_id=1, source_target_pairs={{0,8},{8,0},{16,24},{24,16},{32,40},{40,32},{48,56},{56,48},{64,72... | collective-permute-start | bytes 5505032 | tf_op jit(solution)/shard_map/down_grad/ppermute | solution.py:57
  225.9 46.1 %collective-permute-start.37 = (bf16[1792,256]{1,0:T(8,128)(2,1)}, bf16[1792,256]{1,0:T(8,128)(2,1)S(1)}, u32[]{:S(2)}, u32[]{:S(2)}) collective-permute-start(bf16[1792,256]{1,0:T(8,128)(2,1)} %fusion), channel_id=1, source_target_pairs={{0,16},{8,24},{16,0},{24,8},{32,48},{40,56},{48,32},{56,40},{64,80... | collective-permute-start | bytes 2752520 | tf_op jit(solution)/shard_map/down_grad/ppermute | solution.py:53
  228.0 18.1 %collective-permute-start.34 = (bf16[4,512,128]{2,1,0:T(8,128)(2,1)S(1)}, bf16[4,512,128]{2,1,0:T(8,128)(2,1)S(1)}, u32[]{:S(2)}, u32[]{:S(2)}) collective-permute-start(bf16[4,512,128]{2,1,0:T(8,128)(2,1)S(1)} %collective-permute-done.31), channel_id=1, source_target_pairs={{0,1},{1,2},{2,3},{3,0},{4,5},{5,6},{6,7},{7,4},{8,9},{9,10},{10,1... | collective-permute-start | bytes 1572872 | tf_op jit(solution)/shard_map/layer_grad/ppermute | solution.py:61
  233.4 12.8 %collective-permute-start.35 = (bf16[4,512,128]{2,1,0:T(8,128)(2,1)S(1)}, bf16[4,512,128]{2,1,0:T(8,128)(2,1)S(1)}, u32[]{:S(2)}, u32[]{:S(2)}) collective-permute-start(bf16[4,512,128]{2,1,0:T(8,128)(2,1)S(1)} %collective-permute-done.32), channel_id=1, source_target_pairs={{0,3},{1,0},{2,1},{3,2},{4,7},{5,4},{6,5},{7,6},{8,11},{9,8},{10,9... | collective-permute-start | bytes 1572872 | tf_op jit(solution)/shard_map/layer_grad/ppermute | solution.py:61
  (7 other events, 48.0 us)

commit v4 on v3

v4 whole, which is shorter than its diff:
```python
import functools
import jax
import jax.numpy as jnp
from jax import lax
from jax.experimental import pallas as pl
from jax.experimental.pallas import tpu as pltpu
from jax.sharding import PartitionSpec as P

SEQ = 128
NX, NZH, NCORE, NZL, NY = 4, 2, 2, 2, 4
GRAD_STEPS = 7
KEYS = ((0, 0), (1, 0), (0, 1), (0, 3), (0, 2), (1, 1), (1, 3), (1, 2))

score_scale = 20.0
loss_scale = 8192.0
eps_norm = 1e-05
eps_embed = 1e-06
highest = lax.Precision.HIGHEST
f32 = jnp.float32
bf16 = jnp.bfloat16
MIB = 1024 * 1024
QUICK = pl.CostEstimate(flops=1024, bytes_accessed=1024, transcendentals=0)


def dp_route(dx, dz, dc):
    pairs = []
    for x in range(NX):
        for z in range(NZH):
            for c in range(NCORE):
                to = (((x + dx) % NX) * NZH + (z + dz) % NZH) * NCORE + (c + dc) % NCORE
                pairs.append(((x * NZH + z) * NCORE + c, to))
    return pairs


def tensor_route(dz, dy):
    pairs = []
    for z in range(NZL):
        for y in range(NY):
            pairs.append((z * NY + y, ((z + dz) % NZL) * NY + (y + dy) % NY))
    return pairs


def swap_route(bit):
    size = NZH * NCORE
    return [(d, (d // size ^ bit) * size + d % size) for d in range(NX * size)]


def over_x(value, step):
    return lax.ppermute(value, "dp", dp_route(step, 0, 0))


def over_zh(value):
    return lax.ppermute(value, "dp", dp_route(0, 1, 0))


def over_core(value):
    return lax.ppermute(value, "dp", dp_route(0, 0, 1))


def over_y(value, step):
    return lax.ppermute(value, "tensor", tensor_route(0, step))


def over_zl(value):
    return lax.ppermute(value, "tensor", tensor_route(1, 0))


def gather_small(value, axis):
    n = lax.axis_size(axis)
    copies = jnp.broadcast_to(value[None], (n,) + value.shape)
    return lax.all_to_all(copies, axis, 0, 0)


def layer_dot_kernel(plan_ref, hidden_ref, weight_ref, *refs):
    *out_refs, total_ref = refs
    tile = 512

    @pl.when(pl.program_id(0) == 0)
    def _():
        for n in range(0, total_ref.shape[1], tile):
            total_ref[:, n : n + tile] = jnp.dot(
                hidden_ref[...], weight_ref[:, n : n + tile], preferred_element_type=f32
            )

    @pl.when(pl.program_id(0) == 1)
    def _():
        lanes = out_refs[0].shape[-1]
        flip = plan_ref[0] == 1
        for c, ref in enumerate(out_refs):
            for b in range(NX):
                start = pl.multiple_of((b * NY + plan_ref[1 + c]) * 2 * lanes, 2 * lanes)
                columns = pl.ds(start, 2 * lanes)
                pair = total_ref[:, columns] + jnp.dot(
                    hidden_ref[...], weight_ref[:, columns], preferred_element_type=f32
                )
                first, second = pair[:, :lanes], pair[:, lanes:]
                ref[0, b] = jnp.where(flip, second, first).astype(ref.dtype)
                ref[1, b] = jnp.where(flip, first, second).astype(ref.dtype)


def layer_dot(hidden, weight, columns, zl, group, dtypes):
    tokens, units = hidden.shape
    model_width = weight.shape[1]
    lanes = model_width // (NX * group)
    depth = units // 2
    out = pl.BlockSpec((2, NX, tokens, lanes), lambda k, s: (0, 0, 0, 0))
    return pl.pallas_call(
        layer_dot_kernel,
        grid_spec=pltpu.PrefetchScalarGridSpec(
            num_scalar_prefetch=1,
            grid=(2,),
            in_specs=[
                pl.BlockSpec((tokens, depth), lambda k, s: (0, k)),
                pl.BlockSpec((depth, model_width), lambda k, s: (k, 0)),
            ],
            out_specs=[out] * len(columns),
            scratch_shapes=[pltpu.VMEM((tokens, model_width), f32)],
        ),
        out_shape=[jax.ShapeDtypeStruct((2, NX, tokens, lanes), dtype) for dtype in dtypes],
        compiler_params=pltpu.CompilerParams(vmem_limit_bytes=56 * MIB),
        cost_estimate=pl.CostEstimate(
            flops=2 * tokens * units * model_width,
            bytes_accessed=2 * (tokens * units + units * model_width + tokens * model_width),
            transcendentals=0,
        ),
    )(jnp.stack([zl] + columns).astype(jnp.int32), hidden, weight)


def gram_kernel(plan_ref, mean_ref, gain_ref, strip_ref, out_ref):
    pooled = mean_ref[...] * gain_ref[...]
    gram = lax.dot_general(
        pooled, pooled, (((1,), (1,)), ((), ())), precision=highest, preferred_element_type=f32
    )
    out_ref[0] = jnp.concatenate([gram, jnp.zeros_like(gram)], axis=1)
    out_ref[1] = strip_ref[...]


def gram_part(means, gain, x):
    seqs, width = means.shape
    lanes = 2 * seqs
    return pl.pallas_call(
        gram_kernel,
        grid_spec=pltpu.PrefetchScalarGridSpec(
            num_scalar_prefetch=1,
            grid=(1,),
            in_specs=[
                pl.BlockSpec((seqs, width), lambda i, s: (0, 0)),
                pl.BlockSpec((1, width), lambda i, s: (0, 0)),
                pl.BlockSpec((seqs, lanes), lambda i, s: (0, s[0])),
            ],
            out_specs=pl.BlockSpec((2, seqs, lanes), lambda i, s: (0, 0, 0)),
        ),
        out_shape=jax.ShapeDtypeStruct((2, seqs, lanes), f32),
        compiler_params=pltpu.CompilerParams(vmem_limit_bytes=16 * MIB),
        cost_estimate=QUICK,
    )(x.astype(jnp.int32).reshape(1), means, gain, means)


def contrast_kernel(
    plan_ref, part_ref, same_ref, gain_block_ref, mean_ref, gain_ref, block_ref, block_gain_ref, own_ref, gain_grad_ref
):
    group = part_ref.shape[0]
    seqs = mean_ref.shape[0]
    rows = lax.broadcasted_iota(jnp.int32, (seqs, seqs), 0)
    cols = lax.broadcasted_iota(jnp.int32, (seqs, seqs), 1)
    gram = part_ref[0, 0]
    for r in range(1, group):
        gram += part_ref[r, 0]
    gram = gram[:, :seqs]
    diagonal = jnp.where(rows == cols, gram, 0.0)
    norm_col = jnp.sqrt(jnp.sum(diagonal, axis=1, keepdims=True) + eps_embed)
    norm_row = jnp.sqrt(jnp.sum(diagonal, axis=0, keepdims=True) + eps_embed)
    norms = norm_col * norm_row
    scores = score_scale * gram / norms
    query = rows % 2 == 0
    valid = query & (cols % 2 == 1) & (same_ref[...] > 0.5)
    weights = jnp.where(valid, jnp.exp(scores), 0.0)
    totals = jnp.sum(weights, axis=1, keepdims=True)
    soft = weights / jnp.where(totals > 0.0, totals, 1.0)
    target = jnp.where(query & (cols == rows + 1), 1.0, 0.0)
    d_score = loss_scale * (soft - target)
    both = d_score + d_score.T
    coef = jnp.sum(both * scores, axis=1, keepdims=True)
    mix = score_scale * both / norms - jnp.where(rows == cols, coef / (norm_col * norm_col), 0.0)
    mean, gain = mean_ref[...], gain_ref[...]
    d_pooled = jnp.dot(mix, mean * gain, precision=highest, preferred_element_type=f32)
    gain_grad_ref[...] = jnp.sum(d_pooled * mean, axis=0, keepdims=True)
    own_ref[...] = d_pooled * gain * (1.0 / SEQ)
    for place in range(group):
        part = part_ref[(place % NZL) * NY + place // NZL, 1]
        gain = gain_block_ref[0, place : place + 1, :]
        d_pooled = jnp.dot(mix, part * gain, precision=highest, preferred_element_type=f32)
        block_ref[place] = d_pooled * gain * (1.0 / SEQ)
        block_gain_ref[place : place + 1, :] = jnp.sum(d_pooled * part, axis=0, keepdims=True)


def contrast(parts, same, gain_blocks, means, gain, x):
    group, _, seqs, lanes = parts.shape
    width = means.shape[1]
    whole = lambda shape: pl.BlockSpec(shape, lambda i, s: (0,) * len(shape))
    return pl.pallas_call(
        contrast_kernel,
        grid_spec=pltpu.PrefetchScalarGridSpec(
            num_scalar_prefetch=1,
            grid=(1,),
            in_specs=[
                whole(parts.shape),
                whole(same.shape),
                pl.BlockSpec((1, group, lanes), lambda i, s: (s[0], 0, 0)),
                whole(means.shape),
                whole(gain.shape),
            ],
            out_specs=[whole((group, seqs, lanes)), whole((group, lanes)), whole((seqs, width)), whole((1, width))],
        ),
        out_shape=(
            jax.ShapeDtypeStruct((group, seqs, lanes), f32),
            jax.ShapeDtypeStruct((group, lanes), f32),
            jax.ShapeDtypeStruct((seqs, width), f32),
            jax.ShapeDtypeStruct((1, width), f32),
        ),
        compiler_params=pltpu.CompilerParams(vmem_limit_bytes=16 * MIB),
        cost_estimate=QUICK,
    )(x.astype(jnp.int32).reshape(1), parts, same, gain_blocks, means, gain)


def row_to_column(row):
    n = row.shape[1]
    eye = lax.broadcasted_iota(jnp.int32, (n, n), 0) == lax.broadcasted_iota(jnp.int32, (n, n), 1)
    return jnp.sum(jnp.where(eye, jnp.broadcast_to(row, (n, n)), 0.0), axis=1, keepdims=True)


def column_to_row(column):
    n = column.shape[0]
    eye = lax.broadcasted_iota(jnp.int32, (n, n), 0) == lax.broadcasted_iota(jnp.int32, (n, n), 1)
    return jnp.sum(jnp.where(eye, jnp.broadcast_to(column, (n, n)), 0.0), axis=0, keepdims=True)


def along_kernel(plan_ref, *refs):
    *layer_refs, scaled_ref, out_ref = refs
    tokens = layer_refs[0].shape[1]
    first = plan_ref[pl.program_id(0)]
    for s in range(tokens // SEQ):
        rows = slice(s * SEQ, (s + 1) * SEQ)
        along = None
        for i, ref in enumerate(layer_refs):
            scaled = scaled_ref[plan_ref[NX + i], pl.ds(first + s, 1), :]
            term = ref[0, rows, :].astype(f32) * scaled
            along = term if along is None else along + term
        out_ref[0, s : s + 1, :] = column_to_row(jnp.sum(along, axis=1, keepdims=True))


def along_part(strips, scaled, plan):
    _, tokens, lanes = strips[0].shape
    group = len(strips)
    seqs_here = tokens // SEQ
    return pl.pallas_call(
        along_kernel,
        grid_spec=pltpu.PrefetchScalarGridSpec(
            num_scalar_prefetch=1,
            grid=(NX,),
            in_specs=[pl.BlockSpec((1, tokens, lanes), lambda i, s: (i, 0, 0))] * group
            + [pl.BlockSpec(scaled.shape, lambda i, s: (0, 0, 0))],
            out_specs=pl.BlockSpec((1, seqs_here, SEQ), lambda i, s: (s[NX + 3 * group + i], 0, 0)),
        ),
        out_shape=jax.ShapeDtypeStruct((NX, seqs_here, SEQ), f32),
        compiler_params=pltpu.CompilerParams(vmem_limit_bytes=16 * MIB),
        cost_estimate=QUICK,
    )(plan, *strips, scaled)


def group_grad_kernel(plan_ref, *refs):
    *layer_refs, scaled_ref, sum_ref, low_ref, coef_ref, factor_ref = refs
    _, tokens, lanes = layer_refs[0].shape
    group = len(layer_refs)
    seqs_here = tokens // SEQ
    here = pl.program_id(0)
    first = plan_ref[here]

    @pl.when(here == 0)
    def _():
        for i in range(NX):
            position = plan_ref[NX + 3 * group + i]
            along, inverse = sum_ref[position], sum_ref[NX + position]
            coef = inverse * inverse * inverse * along / (NX * group * lanes)
            factor_ref[i, :seqs_here] = inverse
            factor_ref[i, seqs_here:] = coef
            if i == 0:
                coef_ref[...] = coef

    for s in range(seqs_here):
        rows = slice(s * SEQ, (s + 1) * SEQ)
        inverse = row_to_column(factor_ref[here, s : s + 1, :])
        coef = row_to_column(factor_ref[here, seqs_here + s : seqs_here + s + 1, :])
        for i, ref in enumerate(layer_refs):
            scaled = scaled_ref[plan_ref[NX + i], pl.ds(first + s, 1), :]
            low = inverse * scaled - ref[0, rows, :].astype(f32) * coef
            side = pl.ds(pl.multiple_of(plan_ref[NX + 2 * group + i], lanes), lanes)
            low_ref[plan_ref[NX + group + i], rows, side] = low.astype(bf16)


def group_grad(strips, scaled, sums, plan):
    _, tokens, lanes = strips[0].shape
    group = len(strips)
    quarter = group * lanes // 4
    seqs_here = tokens // SEQ
    return pl.pallas_call(
        group_grad_kernel,
        grid_spec=pltpu.PrefetchScalarGridSpec(
            num_scalar_prefetch=1,
            grid=(NX,),
            in_specs=[pl.BlockSpec((1, tokens, lanes), lambda i, s: (i, 0, 0))] * group
            + [pl.BlockSpec(scaled.shape, lambda i, s: (0, 0, 0))]
            + [pl.BlockSpec(sums.shape, lambda i, s: (0, 0, 0))],
            out_specs=[
                pl.BlockSpec((4, tokens, quarter), lambda i, s: (0, i, 0)),
                pl.BlockSpec((seqs_here, SEQ), lambda i, s: (0, 0)),
            ],
            scratch_shapes=[pltpu.VMEM((NX, 2 * seqs_here, SEQ), f32)],
        ),
        out_shape=(
            jax.ShapeDtypeStruct((4, NX * tokens, quarter), bf16),
            jax.ShapeDtypeStruct((seqs_here, SEQ), f32),
        ),
        compiler_params=pltpu.CompilerParams(vmem_limit_bytes=24 * MIB),
        cost_estimate=QUICK,
    )(plan, *strips, scaled, sums)


def hidden_grad_kernel(plan_ref, *refs):
    *refs, scaled_ref, block_gain_ref, inverse_ref, coef_ref, weight_ref, out_ref, resid_ref, gain_ref, low_ref = refs
    tokens = out_ref.shape[0]
    seqs_here = tokens // SEQ
    group = len(refs) // 2
    others, _, lanes = refs[0].shape
    width = resid_ref.shape[1]
    x, first = plan_ref[1], plan_ref[2]

    @pl.when(pl.program_id(0) == 0)
    def _():
        factors = [
            [jnp.broadcast_to(row_to_column(ref[s : s + 1, :]), (SEQ, lanes)) for ref in (inverse_ref, coef_ref)]
            for s in range(seqs_here)
        ]
        for i in range(group):
            place = plan_ref[3 + i]
            row_ref, strip_ref = refs[i], refs[group + i]
            for j in range(others + 1):
                block = lax.rem(x + j, others + 1)
                column = pl.ds(pl.multiple_of((block * group + place) * lanes, lanes), lanes)
                if j:
                    tail = row_ref[j - 1, tokens:, :].astype(f32)
                    tail = tail[:8] + tail[8:]
                    gain_ref[place, pl.ds(block, 1), :] = tail[seqs_here : seqs_here + 1]
                else:
                    gain_ref[place, pl.ds(block, 1), :] = block_gain_ref[pl.ds(place, 1), :]
                for s in range(seqs_here):
                    rows = slice(s * SEQ, (s + 1) * SEQ)
                    if j:
                        layer, scaled = row_ref[j - 1, rows, :], tail[s : s + 1]
                    else:
                        layer, scaled = strip_ref[0, rows, :], scaled_ref[place, pl.ds(first + s, 1), :]
                    inverse, coef = factors[s]
                    low_ref[rows, column] = (inverse * scaled - layer.astype(f32) * coef).astype(bf16)
        resid_ref[...] = low_ref[:, pl.ds(pl.multiple_of(plan_ref[0] * width, width), width)]

    out_ref[...] = lax.dot_general(
        low_ref[...], weight_ref[...], (((1,), (1,)), ((), ())), preferred_element_type=f32
    ).astype(out_ref.dtype)


def hidden_grad(rows, strips, scaled, block_gain, inverse, coef, weight, plan):
    others, height, lanes = rows[0].shape
    group = len(rows)
    seqs_here = inverse.shape[0]
    tokens = seqs_here * SEQ
    units, model_width = weight.shape
    chunk = units // GRAD_STEPS
    width = model_width // group
    whole = lambda shape: pl.BlockSpec(shape, lambda i, s: (0,) * len(shape))
    return pl.pallas_call(
        hidden_grad_kernel,
        grid_spec=pltpu.PrefetchScalarGridSpec(
            num_scalar_prefetch=1,
            grid=(GRAD_STEPS,),
            in_specs=[whole(rows[0].shape)] * group
            + [whole((1, tokens, lanes))] * group
            + [whole(v.shape) for v in (scaled, block_gain, inverse, coef)]
            + [pl.BlockSpec((chunk, model_width), lambda i, s: (i, 0))],
            out_specs=[
                pl.BlockSpec((tokens, chunk), lambda i, s: (0, i)),
                whole((tokens, width)),
                whole((group, others + 1, lanes)),
            ],
            scratch_shapes=[pltpu.VMEM((tokens, model_width), bf16)],
        ),
        out_shape=(
            jax.ShapeDtypeStruct((tokens, units), bf16),
            jax.ShapeDtypeStruct((tokens, width), bf16),
            jax.ShapeDtypeStruct((group, others + 1, lanes), f32),
        ),
        compiler_params=pltpu.CompilerParams(vmem_limit_bytes=56 * MIB),
        cost_estimate=QUICK,
    )(jnp.stack(plan).astype(jnp.int32), *rows, *strips, scaled, block_gain, inverse, coef, weight)


def tie(*values):
    return lax.optimization_barrier(values)


def gather_start(value):
    return {
        (0, 0): value,
        (1, 0): over_zl(value),
        (0, 1): over_y(value, -1),
        (0, 3): over_y(value, 1),
    }


def gather_next(got):
    got = dict(got)
    got[1, 1] = over_y(got[1, 0], -1)
    got[1, 3] = over_zl(got[0, 3])
    got[0, 2] = over_y(got[0, 3], 1)
    return got


def gather_last(got):
    got = dict(got)
    got[1, 2] = over_y(got[1, 1], -1)
    return got


def tie_gather(got, *values):
    keys = list(got)
    tied = tie(*got.values(), *values)
    return (dict(zip(keys, tied)),) + tuple(tied[len(keys) :])


def per_device(resid, hidden, down_weight, gain, domain_ids):
    tokens, units = hidden.shape
    model_width = down_weight.shape[1]
    group = lax.axis_size("tensor")
    shards = lax.axis_size("dp")
    width = model_width // group
    lanes = width // NX
    seqs_here = tokens // SEQ
    seqs = seqs_here * shards
    rank = lax.axis_index("tensor")
    zl, y = rank // NY, rank % NY
    place = y * NZL + zl
    shard = lax.axis_index("dp")
    x, zh, core = shard // (NZH * NCORE), (shard // NCORE) % NZH, shard % NCORE

    def place_of(part, step):
        return ((y + step) % NY) * NZL + (zl + part) % NZL

    with jax.named_scope("tables"):
        owner = jnp.repeat(domain_ids, seqs_here)
        same = (owner[:, None] == owner[None, :]).astype(f32)
        gain_blocks = gain.reshape(NX, group, lanes)
        gain_own = lax.dynamic_slice_in_dim(gain_blocks, place, 1, 1).reshape(1, width)
        peers = [((x + step) % NX) * (NZH * NCORE) + zh * NCORE + core for step in (0, -1, 1, 2)]
        places = [place_of(*key) for key in KEYS]
        plan = [p * seqs_here for p in peers] + places
        plan += [(p // 2) ^ (zh * NCORE + core) for p in places] + [p % 2 * lanes for p in places]
        plan += [(x + step) % NX for step in (0, -1, 1, 2)]
        plan = jnp.stack([jnp.asarray(v, jnp.int32) for v in plan])

    with jax.named_scope("hidden_exchange"):
        hidden_left = over_x(hidden, 1)
        hidden_right = over_x(hidden, -1)

    with jax.named_scope("resid_exchange"):
        pieces = resid.reshape(tokens, 2, NZL, lanes).transpose(2, 1, 0, 3)[:, None]
        pieces = jnp.broadcast_to(pieces, (NZL, NY // 2, 2, tokens, lanes))
        pieces = lax.all_to_all(pieces.reshape(group, tokens, lanes), "tensor", 0, 0)
        pieces = pieces.reshape(NX, 2, tokens, lanes)

    with jax.named_scope("layer_sum"):
        columns = [(y + step) % NY for step in (2, 1, 3, 0)]
        sums = layer_dot(hidden, down_weight, columns, zl, group, (bf16, bf16, bf16, f32))
        far, right, left, own, pieces = tie(*sums, pieces)
        from_left = over_y(far[0], 1)
        from_right = over_y(far[1], -1)
        from_left, from_right = tie(from_left, from_right)
        right0 = (right[0].astype(f32) + from_left.astype(f32)).astype(bf16)
        left1 = (left[1].astype(f32) + from_right.astype(f32)).astype(bf16)
        got_right = over_y(lax.dynamic_update_slice(right, right0[None], (0, 0, 0, 0)), 1)
        got_left = over_y(lax.dynamic_update_slice(left, left1[None], (1, 0, 0, 0)), -1)

    with jax.named_scope("hidden_exchange"):
        hidden_left, hidden_right, right0 = tie(hidden_left, hidden_right, right0)
        hidden_far = (
            over_x(hidden_left[: tokens // 2], 1),
            over_x(hidden_right[tokens // 2 :], -1),
        )
        got_right, got_left, *hidden_far = tie(got_right, got_left, *hidden_far)
        hidden_rows = jnp.concatenate([hidden, hidden_left, hidden_right] + hidden_far, axis=0)

    with jax.named_scope("layer_sum"):
        other_sum = own[1] + got_right[1].astype(f32) + got_left[1].astype(f32)
        from_zl = over_zl(other_sum.astype(bf16))
        from_zl, hidden_rows = tie(from_zl, hidden_rows)
        resid_strips = lax.dynamic_slice_in_dim(pieces, y // 2, 1, 1)[:, 0]
        layer = (
            own[0]
            + resid_strips.astype(f32)
            + got_right[0].astype(f32)
            + got_left[0].astype(f32)
            + from_zl.astype(f32)
        )

    with jax.named_scope("strip_exchange"):
        low_layer = layer.astype(bf16)
        strips_x = [lax.dynamic_slice_in_dim(low_layer, x, 1, 0)]
        for step in (1, -1, 2):
            strip = lax.dynamic_slice_in_dim(low_layer, (x + step) % NX, 1, 0)
            strips_x.append(over_x(strip, step))
        message = jnp.concatenate(strips_x, axis=0)

    with jax.named_scope("norm"):
        squares = jnp.sum(layer * layer, axis=(0, 2)).reshape(seqs_here, SEQ)
        squares = jnp.sum(gather_small(squares, "tensor"), axis=0)
        message, squares = tie(message, squares)
        got = gather_start(message)
        inverse = lax.rsqrt(squares / model_width + eps_norm)
        weighted = layer.reshape(NX, seqs_here, SEQ, lanes) * inverse[None, :, :, None]
        means = jnp.mean(weighted, axis=2).transpose(1, 0, 2).reshape(seqs_here, width)

    with jax.named_scope("contrast"):
        means_all = gather_small(means, "dp")
        got, means_all = tie_gather(got, means_all)
        got = gather_next(got)
        means_all = means_all.reshape(seqs, width)
        parts = gather_small(gram_part(means_all, gain_own, x), "tensor")
        got, parts, low_layer = tie_gather(got, parts, low_layer)
        got = gather_last(got)
        strips = [got[key] for key in KEYS]
        scaled, gain_grad_x, scaled_own, gain_grad = contrast(
            parts, same, gain_blocks, means_all, gain_own, x
        )

    with jax.named_scope("row_gather"):
        own_rows = lax.dynamic_slice_in_dim(scaled_own, shard * seqs_here, seqs_here, 0)
        own_rows = jnp.pad(jnp.concatenate([own_rows, gain_grad], axis=0), ((0, 8 - seqs_here - 1), (0, 0)))
        high = own_rows.astype(bf16)
        tail = jnp.concatenate([high, (own_rows - high.astype(f32)).astype(bf16)], axis=0)
        tail = tail.reshape(16, NX, lanes).transpose(1, 0, 2)
        blocks = jnp.concatenate([low_layer, tail], axis=1)
        blocks = jnp.concatenate([blocks, blocks], axis=0)
        rows = gather_start(lax.dynamic_slice_in_dim(blocks, x + 1, NX - 1, 0))

    with jax.named_scope("along"):
        own_inverse = jnp.where(jnp.arange(NX)[:, None, None] == x, inverse[None], 0.0)
        sums = jnp.concatenate([along_part(strips, scaled, plan), own_inverse], axis=0)
        sums = sums + lax.ppermute(sums, "dp", swap_route(1))
        sums = sums + lax.ppermute(sums, "dp", swap_route(2))
        rows, sums = tie_gather(rows, sums)
        rows = gather_next(rows)

    with jax.named_scope("down_grad"):
        low_x, coef = group_grad(strips, scaled, sums, plan)

        def down(low):
            return lax.dot_general(
                hidden_rows, low, (((0,), (0,)), ((), ())), preferred_element_type=f32
            )

        from_core = over_core(down(low_x[3]))
        summed = (down(low_x[2]) + from_core).astype(bf16)
        rows, summed, low0, low1 = tie_gather(rows, summed, low_x[0], low_x[1])
        rows = gather_last(rows)
        across = over_zh(summed)
        near = down(low0) + over_core(down(low1))

    with jax.named_scope("hidden_grad"):
        rows, near = tie_gather(rows, near)
        rows = [rows[key] for key in KEYS]
        grad_hidden, grad_resid, gain_grad = hidden_grad(
            rows, strips, scaled, gain_grad_x, inverse, coef, down_weight, [rank, x, shard * seqs_here] + places
        )
        grad_gain = lax.dynamic_slice(
            gain_grad, ((rank % 2) * 4, rank // 2, 0), (4, 1, lanes)
        ).reshape(width)

    with jax.named_scope("down_grad"):
        grad_down = near + across.astype(f32)

    return (grad_hidden, grad_resid, grad_down, grad_gain)


def solution(mesh):
    return jax.shard_map(
        per_device,
        mesh=mesh,
        in_specs=(P("dp", "tensor"), P("dp", "tensor"), P("tensor", None), P(), P()),
        out_specs=(P("dp", "tensor"), P("dp", "tensor"), P("tensor", "dp"), P("tensor")),
        check_vma=False,
    )
```

time: 275 us -> 240 us (0.87)
  starting transfers between devices: 77.9 us -> 59.5 us
  local copies, waits for them, and re-layouts: 38.9 us -> 22.7 us
  blocking collectives: 0 us -> 10.8 us
  Pallas kernels: 52.1 us -> 43 us
  matrix products: 17.8 us -> 14.6 us
    dynamic_update_slice x16 -> x1, local copies, waits for them, and re-layouts: 12.6 us -> 0.83 us  [per_device(): lax.dynamic_update_slice(right, right0[None], (0, 0, 0, 0))]
    all_to_all x4 -> x2, waiting for transfers between devices: 29.9 us -> 18.5 us  [gather_small(): return lax.all_to_all(copies, axis, 0, 0)]
    all_to_all x4 -> x2, starting transfers between devices: 22.4 us -> 11.1 us  [gather_small(): return lax.all_to_all(copies, axis, 0, 0)]
    ppermute x4 -> x2, starting transfers between devices: 12.9 us -> 1.89 us  [the longest x1 1.33 us: per_device(): sums = sums + lax.ppermute(sums, 'dp', swap_route(2))]
    all_to_all x0 -> x1, blocking collectives: none -> 10.8 us  [gather_small(): return lax.all_to_all(copies, axis, 0, 0)]
    ppermute x18 -> x14, waiting for transfers between devices: 26.1 us -> 35.7 us  [over_y(): return lax.ppermute(value, 'tensor', tensor_route(0, step))]
    pallas_call x5 -> x2, Pallas kernels: 42.1 us -> 32.9 us  [the longest x1 17.3 us: hidden_grad(): pl.pallas_call(hidden_grad_kernel, grid_spec=pltpu.PrefetchScalarGridSpec...]
    all_to_all x0 -> x1, starting transfers between devices: none -> 5.91 us  [per_device(): lax.all_to_all(pieces.reshape(group, tokens, lanes), 'tensor', 0, 0)]
  transfers between devices with their start and end apart: 42 -> 34, of which waited for: 16 -> 16; matrix products, arithmetic and copies ran while one was open for 20% -> 13% of each run, Pallas kernels for 15% -> 16%
where the time goes in v4:
time: 240 us; the launch traced here: 238 us
  waiting for transfers between devices  74.3 us (31%)
  starting transfers between devices  59.5 us (25%)
  Pallas kernels  43 us (18%)
  local copies, waits for them, and re-layouts  22.7 us (9%)
  matrix products  14.6 us (6%)
  other arithmetic  11.2 us (5%)
  blocking collectives  10.8 us (4%)
    ppermute x14, waiting for transfers between devices, over_y(): return lax.ppermute(value, 'tensor', tensor_route(0, step))  35.7 us
    ppermute x14, starting transfers between devices, over_y(): return lax.ppermute(value, 'tensor', tensor_route(0, step))  22.6 us
    all_to_all x2, waiting for transfers between devices, gather_small(): return lax.all_to_all(copies, axis, 0, 0)  18.5 us
    pallas_call x1, Pallas kernels, hidden_grad(): pl.pallas_call(hidden_grad_kernel, grid_spec=pltpu.PrefetchScalarGridSpec...  17.3 us
    pallas_call x1, Pallas kernels, layer_dot(): pl.pallas_call(layer_dot_kernel, grid_spec=pltpu.PrefetchScalarGridSpec(n...  15.6 us
    dot_general x4, matrix products, down(): lax.dot_general(hidden_rows, low, (((0,), (0,)), ((), ())), preferred_ele...  14.6 us
    all_to_all x2, starting transfers between devices, gather_small(): return lax.all_to_all(copies, axis, 0, 0)  11.1 us
    ppermute x7, starting transfers between devices, over_x(): return lax.ppermute(value, 'dp', dp_route(step, 0, 0))  11 us
  transfers between devices with their start and end apart: 34, of which 16 were waited for; matrix products, arithmetic and copies ran while one was open for 13% of the time, Pallas kernels for 16%

profile of v4, /device:TPU:0, one launch (start us, length us, event | category | flops | bytes accessed | tf_op | source)
XLA Modules:
  0.0 238.0 jit_solution(14874517189085624549)
XLA Ops:
  3.0 5.9 %all-to-all-start = ((bf16[8,512,128]{2,1,0:T(8,128)(2,1)}), bf16[8,512,128]{2,1,0:T(8,128)(2,1)S(1)}, u32[]{:S(2)}, u32[]{:S(2)}) async-start(bf16[8,512,128]{2,1,0:T(8,128)(2,1)} %bitcast.17), calls=%async_computation | async-start | bytes 2097152 | tf_op jit(solution)/shard_map/resid_exchange/all_to_all | solution.py:476
  8.9 1.5 collective-permute-start.4
  10.4 1.7 collective-permute-start.5
  12.8 15.6 %layer_sum.1 = (bf16[2,4,512,128]{3,2,1,0:T(8,128)(2,1)}, bf16[2,4,512,128]{3,2,1,0:T(8,128)(2,1)}, bf16[2,4,512,128]{3,2,1,0:T(8,128)(2,1)}, f32[2,4,512,128]{3,2,1,0:T(8,128)}) custom-call(s32[5]{0:T(128)} %stack.154.plan_ref, bf16[512,1792]{1,0:T(8,128)(2,1)} %hidden_ref.1, bf16[1792,4096]{1,0:T(8,128)(2,1)} %refs_20_.1), custom_call_target="tpu_custom_call" | custom-call | flops 7516192768 | bytes 20709376 | tf_op jit(solution)/shard_map/layer_sum/pallas_call | solution.py:107
  28.4 1.7 slice_bitcast_fusion.2
  30.1 2.1 collective-permute-start
  34.5 9.7 %collective-permute-done = bf16[4,512,128]{2,1,0:T(8,128)(2,1)S(1)} collective-permute-done((bf16[4,512,128]{2,1,0:T(8,128)(2,1)S(1)}, bf16[4,512,128]{2,1,0:T(8,128)(2,1)S(1)}, u32[]{:S(2)}, u32[]{:S(2)}) %collective-permute-start) | collective-permute-done | bytes 524320 | tf_op jit(solution)/shard_map/layer_sum/ppermute | solution.py:61
  45.3 2.8 %collective-permute-start.3 = (bf16[2,4,512,128]{3,2,1,0:T(8,128)(2,1)}, bf16[2,4,512,128]{3,2,1,0:T(8,128)(2,1)}, u32[]{:S(2)}, u32[]{:S(2)}) collective-permute-start(bf16[2,4,512,128]{3,2,1,0:T(8,128)(2,1)} %fusion.11), channel_id=1, source_target_pairs={{0,3},{1,0},{2,1},{3,2},{4,7},{5,4},{6,5},{7,6},{8,11},{9,8},{10,9... | collective-permute-start | bytes 3145736 | tf_op jit(solution)/shard_map/layer_sum/ppermute | solution.py:61
  50.1 1.8 collective-permute-done.4
  51.9 2.2 slice.53
  56.5 1.9 collective-permute-start.7
  58.3 1.8 constant_dynamic-update-slice_fusion.4
  60.1 1.6 constant_dynamic-update-slice_fusion.3
  61.7 7.2 %collective-permute-done.3 = bf16[2,4,512,128]{3,2,1,0:T(8,128)(2,1)} collective-permute-done((bf16[2,4,512,128]{3,2,1,0:T(8,128)(2,1)}, bf16[2,4,512,128]{3,2,1,0:T(8,128)(2,1)}, u32[]{:S(2)}, u32[]{:S(2)}) %collective-permute-start.3) | collective-permute-done | bytes 1048608 | tf_op jit(solution)/shard_map/layer_sum/ppermute | solution.py:61
  68.9 5.4 %collective-permute-done.2 = bf16[2,4,512,128]{3,2,1,0:T(8,128)(2,1)} collective-permute-done((bf16[2,4,512,128]{3,2,1,0:T(8,128)(2,1)}, bf16[2,4,512,128]{3,2,1,0:T(8,128)(2,1)}, u32[]{:S(2)}, u32[]{:S(2)}) %collective-permute-start.2) | collective-permute-done | bytes 1048608 | tf_op jit(solution)/shard_map/layer_sum/ppermute | solution.py:61
  74.3 2.2 collective-permute-done.6
  77.1 1.4 fusion.9
  78.5 1.5 collective-permute-start.8
  81.5 8.3 %collective-permute-done.8 = bf16[4,512,128]{2,1,0:T(8,128)(2,1)S(1)} collective-permute-done((bf16[4,512,128]{2,1,0:T(8,128)(2,1)S(1)}, bf16[4,512,128]{2,1,0:T(8,128)(2,1)S(1)}, u32[]{:S(2)}, u32[]{:S(2)}) %collective-permute-start.8) | collective-permute-done | bytes 524320 | tf_op jit(solution)/shard_map/layer_sum/ppermute | solution.py:65
  89.8 1.6 multiply_reduce_fusion.1
  91.6 3.6 %collective-permute-start.10 = (bf16[1,512,128]{2,1,0:T(8,128)(2,1)S(1)}, bf16[1,512,128]{2,1,0:T(8,128)(2,1)S(1)}, u32[]{:S(2)}, u32[]{:S(2)}) collective-permute-start(bf16[1,512,128]{2,1,0:T(8,128)(2,1)S(1)} %get-tuple-element.148), channel_id=1, source_target_pairs={{0,96},{8,104},{16,112},{24,120},{32,0},{40,8},{48,16},{56,24},{64... | collective-permute-start | bytes 393224 | tf_op jit(solution)/shard_map/strip_exchange/ppermute | solution.py:49
  96.1 10.8 %all_to_all.20 = f32[8,4,128]{2,1,0:T(4,128)S(1)} all-to-all(f32[8,4,128]{2,1,0:T(4,128)S(1)} %broadcast_in_dim.62), channel_id=1, replica_groups=mesh['dp'=16,'tensor'=8] {'tensor'}, dimensions={0} | all-to-all | bytes 32768 | tf_op jit(solution)/shard_map/norm/all_to_all | solution.py:71
  110.6 7.0 %all-to-all-start.2 = ((f32[16,4,512]{2,1,0:T(4,128)}), f32[16,4,512]{2,1,0:T(4,128)S(1)}, u32[]{:S(2)}, u32[]{:S(2)}) async-start(f32[16,4,512]{2,1,0:T(4,128)} %broadcast_in_dim.64), calls=%async_computation.2 | async-start | bytes 262144 | tf_op jit(solution)/shard_map/contrast/all_to_all | solution.py:71
  117.6 8.0 %all-to-all-done.2 = f32[16,4,512]{2,1,0:T(4,128)S(1)} async-done(((f32[16,4,512]{2,1,0:T(4,128)}), f32[16,4,512]{2,1,0:T(4,128)S(1)}, u32[]{:S(2)}, u32[]{:S(2)}) %all-to-all-start.2) | async-done | bytes 131104 | tf_op jit(solution)/shard_map/contrast/all_to_all | solution.py:71
  127.3 2.5 %collective-permute-start.15 = (bf16[4,512,128]{2,1,0:T(8,128)(2,1)S(1)}, bf16[4,512,128]{2,1,0:T(8,128)(2,1)}, u32[]{:S(2)}, u32[]{:S(2)}) collective-permute-start(bf16[4,512,128]{2,1,0:T(8,128)(2,1)S(1)} %collective-permute-done.12.refs_1_.refs_9_), channel_id=1, source_target_pairs={{0,3},{1,0},{2,1},{3,2},{4,7},{5,4},{6,5},{7,6},{8,11},{9,8},{10,9... | collective-permute-start | bytes 1572872 | tf_op jit(solution)/shard_map/contrast/ppermute | solution.py:61
  131.0 4.1 %all-to-all-start.3 = ((f32[8,2,64,128]{3,2,1,0:T(8,128)}), f32[8,2,64,128]{3,2,1,0:T(8,128)}, u32[]{:S(2)}, u32[]{:S(2)}) async-start(f32[8,2,64,128]{3,2,1,0:T(8,128)} %broadcast_in_dim.65), calls=%async_computation.3 | async-start | bytes 1048576 | tf_op jit(solution)/shard_map/contrast/all_to_all | solution.py:71
  137.3 10.5 %all-to-all-done.3.part_ref = f32[8,2,64,128]{3,2,1,0:T(8,128)} async-done(((f32[8,2,64,128]{3,2,1,0:T(8,128)}), f32[8,2,64,128]{3,2,1,0:T(8,128)}, u32[]{:S(2)}, u32[]{:S(2)}) %all-to-all-start.3) | async-done | bytes 524320 | tf_op jit(solution)/shard_map/contrast/all_to_all | solution.py:71
  147.8 2.4 %collective-permute-start.21 = (bf16[4,512,128]{2,1,0:T(8,128)(2,1)}, bf16[4,512,128]{2,1,0:T(8,128)(2,1)S(1)}, u32[]{:S(2)}, u32[]{:S(2)}) collective-permute-start(bf16[4,512,128]{2,1,0:T(8,128)(2,1)} %collective-permute-done.15.refs_5_.refs_13_), channel_id=1, source_target_pairs={{0,3},{1,0},{2,1},{3,2},{4,7},{5,4},{6,5},{7,6},{8,11},{9,8},{10,9... | collective-permute-start | bytes 1572872 | tf_op jit(solution)/shard_map/contrast/ppermute | solution.py:61
  151.7 1.8 contrast.3
  153.6 2.3 fusion.13.refs_0_
  157.3 2.0 collective-permute-start.20
  159.3 3.6 %collective-permute-done.21.refs_7_.refs_15_ = bf16[4,512,128]{2,1,0:T(8,128)(2,1)S(1)} collective-permute-done((bf16[4,512,128]{2,1,0:T(8,128)(2,1)}, bf16[4,512,128]{2,1,0:T(8,128)(2,1)S(1)}, u32[]{:S(2)}, u32[]{:S(2)}) %collective-permute-start.21) | collective-permute-done | bytes 524320 | tf_op jit(solution)/shard_map/contrast/ppermute | solution.py:61
  163.6 3.7 %along.1 = f32[4,4,128]{2,1,0:T(4,128)S(1)} custom-call(s32[32]{0:T(128)S(1)} %copy-done.12, bf16[4,512,128]{2,1,0:T(8,128)(2,1)S(1)} %pad_maximum_fusion.refs_0_.refs_8_, bf16[4,512,128]{2,1,0:T(8,128)(2,1)S(1)} %collective-permute-done.12.refs_1_.refs_9_, bf16[4,512,128]{2,1,0:T(8,128)(2,1)S(1)} %collective-permute-done.13.refs_2_.refs_10_, ...), custom_call_target="tpu_custom_call" | custom-call | flops 1024 | bytes 1024 | tf_op jit(solution)/shard_map/along/pallas_call | solution.py:256
  167.9 3.3 %collective-permute-done.22 = f32[8,4,128]{2,1,0:T(4,128)S(1)} collective-permute-done((f32[8,4,128]{2,1,0:T(4,128)S(1)}, f32[8,4,128]{2,1,0:T(4,128)S(1)}, u32[]{:S(2)}, u32[]{:S(2)}) %collective-permute-start.22) | collective-permute-done | bytes 16416 | tf_op jit(solution)/shard_map/along/ppermute | solution.py:556
  172.5 4.0 %collective-permute-done.23 = f32[8,4,128]{2,1,0:T(4,128)S(1)} collective-permute-done((f32[8,4,128]{2,1,0:T(4,128)S(1)}, f32[8,4,128]{2,1,0:T(4,128)S(1)}, u32[]{:S(2)}, u32[]{:S(2)}) %collective-permute-start.23) | collective-permute-done | bytes 16416 | tf_op jit(solution)/shard_map/along/ppermute | solution.py:557
  177.4 4.2 %down_grad.1 = (bf16[4,2048,256]{2,1,0:T(8,128)(2,1)S(1)}, f32[4,128]{1,0:T(4,128)S(1)}) custom-call(s32[32]{0:T(128)S(1)} %copy-done.13, bf16[4,512,128]{2,1,0:T(8,128)(2,1)S(1)} %pad_maximum_fusion.refs_0_.refs_8_, bf16[4,512,128]{2,1,0:T(8,128)(2,1)S(1)} %collective-permute-done.12.refs_1_.refs_9_, ...), custom_call_target="tpu_custom_call" | custom-call | flops 1024 | bytes 1024 | tf_op jit(solution)/shard_map/down_grad/pallas_call | solution.py:306
  181.7 2.2 fusion.4
  184.1 1.4 collective-permute-start.25
  185.5 1.6 collective-permute-start.26
  187.1 2.1 collective-permute-start.24
  189.3 3.2 %fusion = bf16[1792,256]{1,0:T(8,128)(2,1)} fusion(f32[1792,256]{1,0:T(8,128)S(1)} %collective-permute-done.27, bf16[2048,1792]{1,0:T(8,128)(2,1)S(1)} %copy-done.22, bf16[4,2048,256]{2,1,0:T(8,128)(2,1)S(1)} %get-tuple-element.115), kind=kOutput, calls=%fused_computation.2 | convolution fusion | flops 1879965696 | bytes 11141120 | tf_op jit(solution)/shard_map/down_grad/dot_general | solution.py:565
  192.5 5.6 %collective-permute-done.24.refs_5_ = bf16[3,528,128]{2,1,0:T(8,128)(2,1)} collective-permute-done((bf16[3,528,128]{2,1,0:T(8,128)(2,1)S(1)}, bf16[3,528,128]{2,1,0:T(8,128)(2,1)}, u32[]{:S(2)}, u32[]{:S(2)}) %collective-permute-start.24) | collective-permute-done | bytes 405536 | tf_op jit(solution)/shard_map/along/ppermute | solution.py:61
  198.6 3.5 %fusion.19 = f32[1792,256]{1,0:T(8,128)} fusion(bf16[2048,1792]{1,0:T(8,128)(2,1)S(1)} %copy-done.22, bf16[2048,256]{1,0:T(8,128)(2,1)S(1)} %get-tuple-element.124), kind=kOutput, calls=%fused_computation.62 | convolution fusion | flops 1879048192 | bytes 10223616 | tf_op jit(solution)/shard_map/down_grad/dot_general | solution.py:565
  203.7 3.2 %collective-permute-start.28 = (bf16[3,528,128]{2,1,0:T(8,128)(2,1)}, bf16[3,528,128]{2,1,0:T(8,128)(2,1)S(1)}, u32[]{:S(2)}, u32[]{:S(2)}) collective-permute-start(bf16[3,528,128]{2,1,0:T(8,128)(2,1)} %collective-permute-done.24.refs_5_), channel_id=1, source_target_pairs={{0,3},{1,0},{2,1},{3,2},{4,7},{5,4},{6,5},{7,6},{8,11},{9,8},{10,9... | collective-permute-start | bytes 1216520 | tf_op jit(solution)/shard_map/down_grad/ppermute | solution.py:61
  206.8 5.7 %convolution_add_fusion = f32[1792,256]{1,0:T(8,128)S(1)} fusion(f32[1792,256]{1,0:T(8,128)} %collective-permute-done.29, bf16[2048,1792]{1,0:T(8,128)(2,1)} %copy-done.21, bf16[2048,256]{1,0:T(8,128)(2,1)S(1)} %get-tuple-element.123), kind=kOutput, calls=%fused_computation | convolution fusion | flops 1879506944 | bytes 12058624 | tf_op jit(solution)/shard_map/down_grad/dot_general | solution.py:565
  212.5 3.6 %collective-permute-done.28.refs_7_ = bf16[3,528,128]{2,1,0:T(8,128)(2,1)S(1)} collective-permute-done((bf16[3,528,128]{2,1,0:T(8,128)(2,1)}, bf16[3,528,128]{2,1,0:T(8,128)(2,1)S(1)}, u32[]{:S(2)}, u32[]{:S(2)}) %collective-permute-start.28) | collective-permute-done | bytes 405536 | tf_op jit(solution)/shard_map/down_grad/ppermute | solution.py:61
  216.8 17.3 %hidden_grad.1 = (bf16[512,1792]{1,0:T(8,128)(2,1)}, bf16[512,512]{1,0:T(8,128)(2,1)}, f32[8,4,128]{2,1,0:T(4,128)}) custom-call(s32[11]{0:T(128)} %stack.148.plan_ref, bf16[3,528,128]{2,1,0:T(8,128)(2,1)} %copy-done.20, bf16[3,528,128]{2,1,0:T(8,128)(2,1)} %copy-done.23, bf16[3,528,128]{2,1,0:T(8,128)(2,1)} %copy-done.24, bf16[3,528,128]{2,1,0:T(8,128)(2,1)} %copy-done.25, ...), custom_call_target="tpu_custom_call" | custom-call | flops 1024 | bytes 1024 | tf_op jit(solution)/shard_map/hidden_grad/pallas_call | solution.py:380
  235.4 2.6 %convert_add_fusion = f32[1792,256]{1,0:T(8,128)} fusion(f32[1792,256]{1,0:T(8,128)S(1)} %convolution_add_fusion, bf16[1792,256]{1,0:T(8,128)(2,1)} %collective-permute-done.30), kind=kLoop, calls=%fused_computation.3 | loop fusion | flops 917504 | bytes 4587520 | tf_op jit(solution)/shard_map/down_grad/add | solution.py:587
  (141 shorter events, 32.6 us)
Async XLA Ops:
  3.0 25.4 %all-to-all-start = ((bf16[8,512,128]{2,1,0:T(8,128)(2,1)}), bf16[8,512,128]{2,1,0:T(8,128)(2,1)S(1)}, u32[]{:S(2)}, u32[]{:S(2)}) async-start(bf16[8,512,128]{2,1,0:T(8,128)(2,1)} %bitcast.17), calls=%async_computation | async-start | bytes 2097152 | tf_op jit(solution)/shard_map/resid_exchange/all_to_all | solution.py:476
  8.9 43.0 %collective-permute-start.4 = (bf16[512,1792]{1,0:T(8,128)(2,1)}, bf16[512,1792]{1,0:T(8,128)(2,1)}, u32[]{:S(2)}, u32[]{:S(2)}) collective-permute-start(bf16[512,1792]{1,0:T(8,128)(2,1)} %hidden_ref.1), channel_id=1, source_target_pairs={{0,32},{8,40},{16,48},{24,56},{32,64},{40,72},{48,80},{56,88},{64,... | collective-permute-start | bytes 5505032 | tf_op jit(solution)/shard_map/hidden_exchange/ppermute | solution.py:49
  10.4 41.5 %collective-permute-start.5 = (bf16[512,1792]{1,0:T(8,128)(2,1)}, bf16[512,1792]{1,0:T(8,128)(2,1)S(1)}, u32[]{:S(2)}, u32[]{:S(2)}) collective-permute-start(bf16[512,1792]{1,0:T(8,128)(2,1)} %hidden_ref.1), channel_id=1, source_target_pairs={{0,96},{8,104},{16,112},{24,120},{32,0},{40,8},{48,16},{56,24},{64... | collective-permute-start | bytes 5505032 | tf_op jit(solution)/shard_map/hidden_exchange/ppermute | solution.py:49
  28.4 25.7 %copy-start.17 = (bf16[8,512,128]{2,1,0:T(8,128)(2,1)}, bf16[8,512,128]{2,1,0:T(8,128)(2,1)S(1)}, u32[]{:S(2)}) copy-start(bf16[8,512,128]{2,1,0:T(8,128)(2,1)S(1)} %all-to-all-done) | copy-start | bytes 3145732
  30.1 14.1 %collective-permute-start = (bf16[4,512,128]{2,1,0:T(8,128)(2,1)S(1)}, bf16[4,512,128]{2,1,0:T(8,128)(2,1)S(1)}, u32[]{:S(2)}, u32[]{:S(2)}) collective-permute-start(bf16[4,512,128]{2,1,0:T(8,128)(2,1)S(1)} %get-tuple-element.145), channel_id=1, source_target_pairs={{0,1},{1,2},{2,3},{3,0},{4,5},{5,6},{6,7},{7,4},{8,9},{9,10},{10,1... | collective-permute-start | bytes 1572872 | tf_op jit(solution)/shard_map/layer_sum/ppermute | solution.py:61
  32.1 12.3 %collective-permute-start.1 = (bf16[4,512,128]{2,1,0:T(8,128)(2,1)S(1)}, bf16[4,512,128]{2,1,0:T(8,128)(2,1)S(1)}, u32[]{:S(2)}, u32[]{:S(2)}) collective-permute-start(bf16[4,512,128]{2,1,0:T(8,128)(2,1)S(1)} %get-tuple-element.144), channel_id=1, source_target_pairs={{0,3},{1,0},{2,1},{3,2},{4,7},{5,4},{6,5},{7,6},{8,11},{9,8},{10,9... | collective-permute-start | bytes 1572872 | tf_op jit(solution)/shard_map/layer_sum/ppermute | solution.py:61
  45.3 23.6 %collective-permute-start.3 = (bf16[2,4,512,128]{3,2,1,0:T(8,128)(2,1)}, bf16[2,4,512,128]{3,2,1,0:T(8,128)(2,1)}, u32[]{:S(2)}, u32[]{:S(2)}) collective-permute-start(bf16[2,4,512,128]{3,2,1,0:T(8,128)(2,1)} %fusion.11), channel_id=1, source_target_pairs={{0,3},{1,0},{2,1},{3,2},{4,7},{5,4},{6,5},{7,6},{8,11},{9,8},{10,9... | collective-permute-start | bytes 3145736 | tf_op jit(solution)/shard_map/layer_sum/ppermute | solution.py:61
  50.1 24.2 %collective-permute-start.2 = (bf16[2,4,512,128]{3,2,1,0:T(8,128)(2,1)}, bf16[2,4,512,128]{3,2,1,0:T(8,128)(2,1)}, u32[]{:S(2)}, u32[]{:S(2)}) collective-permute-start(bf16[2,4,512,128]{3,2,1,0:T(8,128)(2,1)} %bitcast_dynamic-update-slice_fusion), channel_id=1, source_target_pairs={{0,1},{1,2},{2,3},{3,0},{4,5},{5,6},{6,7},{7,4},{8,9},{9,10},{10,1... | collective-permute-start | bytes 3145736 | tf_op jit(solution)/shard_map/layer_sum/ppermute | solution.py:61
  54.1 22.4 %collective-permute-start.6 = (bf16[256,1792]{1,0:T(8,128)(2,1)}, bf16[256,1792]{1,0:T(8,128)(2,1)}, u32[]{:S(2)}, u32[]{:S(2)}) collective-permute-start(bf16[256,1792]{1,0:T(8,128)(2,1)} %slice.53), channel_id=1, source_target_pairs={{0,32},{8,40},{16,48},{24,56},{32,64},{40,72},{48,80},{56,88},{64,... | collective-permute-start | bytes 2752520 | tf_op jit(solution)/shard_map/hidden_exchange/ppermute | solution.py:49
  56.5 20.6 %collective-permute-start.7 = (bf16[256,1792]{1,0:T(8,128)(2,1)}, bf16[256,1792]{1,0:T(8,128)(2,1)S(1)}, u32[]{:S(2)}, u32[]{:S(2)}) collective-permute-start(bf16[256,1792]{1,0:T(8,128)(2,1)} %slice.54), channel_id=1, source_target_pairs={{0,96},{8,104},{16,112},{24,120},{32,0},{40,8},{48,16},{56,24},{64... | collective-permute-start | bytes 2752520 | tf_op jit(solution)/shard_map/hidden_exchange/ppermute | solution.py:49
  78.5 11.3 %collective-permute-start.8 = (bf16[4,512,128]{2,1,0:T(8,128)(2,1)S(1)}, bf16[4,512,128]{2,1,0:T(8,128)(2,1)S(1)}, u32[]{:S(2)}, u32[]{:S(2)}) collective-permute-start(bf16[4,512,128]{2,1,0:T(8,128)(2,1)S(1)} %fusion.9), channel_id=1, source_target_pairs={{0,4},{1,5},{2,6},{3,7},{4,0},{5,1},{6,2},{7,3},{8,12},{9,13},{10,... | collective-permute-start | bytes 1572872 | tf_op jit(solution)/shard_map/layer_sum/ppermute | solution.py:65
  81.5 48.3 %copy-start.9 = (f32[4096]{0:T(1024)S(1)}, f32[4096]{0:T(1024)}, u32[]{:S(2)}) copy-start(f32[4096]{0:T(1024)} %param.8) | copy-start | bytes 49156
  91.4 44.0 %copy-start.30 = (s32[16]{0:T(128)S(1)}, s32[16]{0:T(128)}, u32[]{:S(2)}) copy-start(s32[16]{0:T(128)} %param.9) | copy-start | bytes 196
  91.6 15.4 %collective-permute-start.10 = (bf16[1,512,128]{2,1,0:T(8,128)(2,1)S(1)}, bf16[1,512,128]{2,1,0:T(8,128)(2,1)S(1)}, u32[]{:S(2)}, u32[]{:S(2)}) collective-permute-start(bf16[1,512,128]{2,1,0:T(8,128)(2,1)S(1)} %get-tuple-element.148), channel_id=1, source_target_pairs={{0,96},{8,104},{16,112},{24,120},{32,0},{40,8},{48,16},{56,24},{64... | collective-permute-start | bytes 393224 | tf_op jit(solution)/shard_map/strip_exchange/ppermute | solution.py:49
  95.2 11.8 %collective-permute-start.11 = (bf16[1,512,128]{2,1,0:T(8,128)(2,1)S(1)}, bf16[1,512,128]{2,1,0:T(8,128)(2,1)S(1)}, u32[]{:S(2)}, u32[]{:S(2)}) collective-permute-start(bf16[1,512,128]{2,1,0:T(8,128)(2,1)S(1)} %get-tuple-element.147), channel_id=1, source_target_pairs={{0,64},{8,72},{16,80},{24,88},{32,96},{40,104},{48,112},{56,120},{... | collective-permute-start | bytes 393224 | tf_op jit(solution)/shard_map/strip_exchange/ppermute | solution.py:49
  95.2 11.8 %collective-permute-start.9 = (bf16[1,512,128]{2,1,0:T(8,128)(2,1)S(1)}, bf16[1,512,128]{2,1,0:T(8,128)(2,1)S(1)}, u32[]{:S(2)}, u32[]{:S(2)}) collective-permute-start(bf16[1,512,128]{2,1,0:T(8,128)(2,1)S(1)} %get-tuple-element.149), channel_id=1, source_target_pairs={{0,32},{8,40},{16,48},{24,56},{32,64},{40,72},{48,80},{56,88},{64,... | collective-permute-start | bytes 393224 | tf_op jit(solution)/shard_map/strip_exchange/ppermute | solution.py:49
  107.1 70.3 %copy-start = (bf16[4,512,128]{2,1,0:T(8,128)(2,1)}, bf16[4,512,128]{2,1,0:T(8,128)(2,1)S(1)}, u32[]{:S(2)}) copy-start(bf16[4,512,128]{2,1,0:T(8,128)(2,1)S(1)} %pad_maximum_fusion.refs_0_.refs_8_) | copy-start | bytes 1572868
  107.1 18.5 %collective-permute-start.12 = (bf16[4,512,128]{2,1,0:T(8,128)(2,1)S(1)}, bf16[4,512,128]{2,1,0:T(8,128)(2,1)S(1)}, u32[]{:S(2)}, u32[]{:S(2)}) collective-permute-start(bf16[4,512,128]{2,1,0:T(8,128)(2,1)S(1)} %pad_maximum_fusion.refs_0_.refs_8_), channel_id=1, source_target_pairs={{0,4},{1,5},{2,6},{3,7},{4,0},{5,1},{6,2},{7,3},{8,12},{9,13},{10,... | collective-permute-start | bytes 1572872 | tf_op jit(solution)/shard_map/norm/ppermute | solution.py:65
  107.8 17.8 %collective-permute-start.13 = (bf16[4,512,128]{2,1,0:T(8,128)(2,1)S(1)}, bf16[4,512,128]{2,1,0:T(8,128)(2,1)S(1)}, u32[]{:S(2)}, u32[]{:S(2)}) collective-permute-start(bf16[4,512,128]{2,1,0:T(8,128)(2,1)S(1)} %pad_maximum_fusion.refs_0_.refs_8_), channel_id=1, source_target_pairs={{0,3},{1,0},{2,1},{3,2},{4,7},{5,4},{6,5},{7,6},{8,11},{9,8},{10,9... | collective-permute-start | bytes 1572872 | tf_op jit(solution)/shard_map/norm/ppermute | solution.py:61
  109.0 16.6 %collective-permute-start.14 = (bf16[4,512,128]{2,1,0:T(8,128)(2,1)S(1)}, bf16[4,512,128]{2,1,0:T(8,128)(2,1)S(1)}, u32[]{:S(2)}, u32[]{:S(2)}) collective-permute-start(bf16[4,512,128]{2,1,0:T(8,128)(2,1)S(1)} %pad_maximum_fusion.refs_0_.refs_8_), channel_id=1, source_target_pairs={{0,1},{1,2},{2,3},{3,0},{4,5},{5,6},{6,7},{7,4},{8,9},{9,10},{10,1... | collective-permute-start | bytes 1572872 | tf_op jit(solution)/shard_map/norm/ppermute | solution.py:61
  109.8 57.5 %copy-start.29 = (f32[4,128]{1,0:T(4,128)}, f32[4,128]{1,0:T(4,128)S(1)}, u32[]{:S(2)}) copy-start(f32[4,128]{1,0:T(4,128)S(1)} %add_rsqrt_fusion.refs_18_) | copy-start | bytes 6148
  110.6 14.9 %all-to-all-start.2 = ((f32[16,4,512]{2,1,0:T(4,128)}), f32[16,4,512]{2,1,0:T(4,128)S(1)}, u32[]{:S(2)}, u32[]{:S(2)}) async-start(f32[16,4,512]{2,1,0:T(4,128)} %broadcast_in_dim.64), calls=%async_computation.2 | async-start | bytes 262144 | tf_op jit(solution)/shard_map/contrast/all_to_all | solution.py:71
  125.6 51.8 %copy-start.1 = (bf16[4,512,128]{2,1,0:T(8,128)(2,1)}, bf16[4,512,128]{2,1,0:T(8,128)(2,1)S(1)}, u32[]{:S(2)}) copy-start(bf16[4,512,128]{2,1,0:T(8,128)(2,1)S(1)} %collective-permute-done.12.refs_1_.refs_9_) | copy-start | bytes 1572868
  125.6 51.8 %copy-start.2 = (bf16[4,512,128]{2,1,0:T(8,128)(2,1)}, bf16[4,512,128]{2,1,0:T(8,128)(2,1)S(1)}, u32[]{:S(2)}) copy-start(bf16[4,512,128]{2,1,0:T(8,128)(2,1)S(1)} %collective-permute-done.13.refs_2_.refs_10_) | copy-start | bytes 1572868
  125.6 51.8 %copy-start.3 = (bf16[4,512,128]{2,1,0:T(8,128)(2,1)}, bf16[4,512,128]{2,1,0:T(8,128)(2,1)S(1)}, u32[]{:S(2)}) copy-start(bf16[4,512,128]{2,1,0:T(8,128)(2,1)S(1)} %collective-permute-done.14.refs_3_.refs_11_) | copy-start | bytes 1572868
  125.6 22.2 %collective-permute-start.16 = (bf16[4,512,128]{2,1,0:T(8,128)(2,1)S(1)}, bf16[4,512,128]{2,1,0:T(8,128)(2,1)S(1)}, u32[]{:S(2)}, u32[]{:S(2)}) collective-permute-start(bf16[4,512,128]{2,1,0:T(8,128)(2,1)S(1)} %collective-permute-done.14.refs_3_.refs_11_), channel_id=1, source_target_pairs={{0,4},{1,5},{2,6},{3,7},{4,0},{5,1},{6,2},{7,3},{8,12},{9,13},{10,... | collective-permute-start | bytes 1572872 | tf_op jit(solution)/shard_map/contrast/ppermute | solution.py:65
  126.6 21.2 %collective-permute-start.17 = (bf16[4,512,128]{2,1,0:T(8,128)(2,1)S(1)}, bf16[4,512,128]{2,1,0:T(8,128)(2,1)S(1)}, u32[]{:S(2)}, u32[]{:S(2)}) collective-permute-start(bf16[4,512,128]{2,1,0:T(8,128)(2,1)S(1)} %collective-permute-done.14.refs_3_.refs_11_), channel_id=1, source_target_pairs={{0,1},{1,2},{2,3},{3,0},{4,5},{5,6},{6,7},{7,4},{8,9},{9,10},{10,1... | collective-permute-start | bytes 1572872 | tf_op jit(solution)/shard_map/contrast/ppermute | solution.py:61
  127.3 20.4 %collective-permute-start.15 = (bf16[4,512,128]{2,1,0:T(8,128)(2,1)S(1)}, bf16[4,512,128]{2,1,0:T(8,128)(2,1)}, u32[]{:S(2)}, u32[]{:S(2)}) collective-permute-start(bf16[4,512,128]{2,1,0:T(8,128)(2,1)S(1)} %collective-permute-done.12.refs_1_.refs_9_), channel_id=1, source_target_pairs={{0,3},{1,0},{2,1},{3,2},{4,7},{5,4},{6,5},{7,6},{8,11},{9,8},{10,9... | collective-permute-start | bytes 1572872 | tf_op jit(solution)/shard_map/contrast/ppermute | solution.py:61
  131.0 16.8 %all-to-all-start.3 = ((f32[8,2,64,128]{3,2,1,0:T(8,128)}), f32[8,2,64,128]{3,2,1,0:T(8,128)}, u32[]{:S(2)}, u32[]{:S(2)}) async-start(f32[8,2,64,128]{3,2,1,0:T(8,128)} %broadcast_in_dim.65), calls=%async_computation.3 | async-start | bytes 1048576 | tf_op jit(solution)/shard_map/contrast/all_to_all | solution.py:71
  147.8 33.9 %copy-start.4 = (bf16[4,512,128]{2,1,0:T(8,128)(2,1)}, bf16[4,512,128]{2,1,0:T(8,128)(2,1)S(1)}, u32[]{:S(2)}) copy-start(bf16[4,512,128]{2,1,0:T(8,128)(2,1)S(1)} %collective-permute-done.16.refs_6_.refs_14_) | copy-start | bytes 1572868
  147.8 33.9 %copy-start.5 = (bf16[4,512,128]{2,1,0:T(8,128)(2,1)}, bf16[4,512,128]{2,1,0:T(8,128)(2,1)S(1)}, u32[]{:S(2)}) copy-start(bf16[4,512,128]{2,1,0:T(8,128)(2,1)S(1)} %collective-permute-done.17.refs_4_.refs_12_) | copy-start | bytes 1572868
  147.8 15.1 %collective-permute-start.21 = (bf16[4,512,128]{2,1,0:T(8,128)(2,1)}, bf16[4,512,128]{2,1,0:T(8,128)(2,1)S(1)}, u32[]{:S(2)}, u32[]{:S(2)}) collective-permute-start(bf16[4,512,128]{2,1,0:T(8,128)(2,1)} %collective-permute-done.15.refs_5_.refs_13_), channel_id=1, source_target_pairs={{0,3},{1,0},{2,1},{3,2},{4,7},{5,4},{6,5},{7,6},{8,11},{9,8},{10,9... | collective-permute-start | bytes 1572872 | tf_op jit(solution)/shard_map/contrast/ppermute | solution.py:61
  151.7 25.7 %copy-start.13 = (s32[32]{0:T(128)S(1)}, s32[32]{0:T(128)}, u32[]{:S(2)}) copy-start(s32[32]{0:T(128)} %stack.179.plan_ref) | copy-start | bytes 388
  153.5 23.0 %copy-start.14 = (f32[8,128]{1,0:T(8,128)}, f32[8,128]{1,0:T(8,128)S(1)}, u32[]{:S(2)}) copy-start(f32[8,128]{1,0:T(8,128)S(1)} %get-tuple-element.133.refs_17_) | copy-start | bytes 12292
  153.6 28.1 %copy-start.7 = (f32[8,64,128]{2,1,0:T(8,128)}, f32[8,64,128]{2,1,0:T(8,128)S(1)}, u32[]{:S(2)}) copy-start(f32[8,64,128]{2,1,0:T(8,128)S(1)} %get-tuple-element.108.refs_8_.refs_16_) | copy-start | bytes 786436
  156.0 20.5 %copy-start.20 = (bf16[3,528,128]{2,1,0:T(8,128)(2,1)}, bf16[3,528,128]{2,1,0:T(8,128)(2,1)S(1)}, u32[]{:S(2)}) copy-start(bf16[3,528,128]{2,1,0:T(8,128)(2,1)S(1)} %fusion.13.refs_0_) | copy-start | bytes 1216516
  156.0 20.5 %collective-permute-start.18 = (bf16[3,528,128]{2,1,0:T(8,128)(2,1)S(1)}, bf16[3,528,128]{2,1,0:T(8,128)(2,1)S(1)}, u32[]{:S(2)}, u32[]{:S(2)}) collective-permute-start(bf16[3,528,128]{2,1,0:T(8,128)(2,1)S(1)} %fusion.13.refs_0_), channel_id=1, source_target_pairs={{0,4},{1,5},{2,6},{3,7},{4,0},{5,1},{6,2},{7,3},{8,12},{9,13},{10,... | collective-permute-start | bytes 1216520 | tf_op jit(solution)/shard_map/row_gather/ppermute | solution.py:65
  157.2 19.3 %collective-permute-start.19 = (bf16[3,528,128]{2,1,0:T(8,128)(2,1)S(1)}, bf16[3,528,128]{2,1,0:T(8,128)(2,1)S(1)}, u32[]{:S(2)}, u32[]{:S(2)}) collective-permute-start(bf16[3,528,128]{2,1,0:T(8,128)(2,1)S(1)} %fusion.13.refs_0_), channel_id=1, source_target_pairs={{0,3},{1,0},{2,1},{3,2},{4,7},{5,4},{6,5},{7,6},{8,11},{9,8},{10,9... | collective-permute-start | bytes 1216520 | tf_op jit(solution)/shard_map/row_gather/ppermute | solution.py:61
  157.3 20.1 %collective-permute-start.20 = (bf16[3,528,128]{2,1,0:T(8,128)(2,1)S(1)}, bf16[3,528,128]{2,1,0:T(8,128)(2,1)S(1)}, u32[]{:S(2)}, u32[]{:S(2)}) collective-permute-start(bf16[3,528,128]{2,1,0:T(8,128)(2,1)S(1)} %fusion.13.refs_0_), channel_id=1, source_target_pairs={{0,1},{1,2},{2,3},{3,0},{4,5},{5,6},{6,7},{7,4},{8,9},{9,10},{10,1... | collective-permute-start | bytes 1216520 | tf_op jit(solution)/shard_map/row_gather/ppermute | solution.py:61
  167.3 3.8 %collective-permute-start.22 = (f32[8,4,128]{2,1,0:T(4,128)S(1)}, f32[8,4,128]{2,1,0:T(4,128)S(1)}, u32[]{:S(2)}, u32[]{:S(2)}) collective-permute-start(f32[8,4,128]{2,1,0:T(4,128)S(1)} %pad_maximum_fusion.1), channel_id=1, source_target_pairs={{0,32},{8,40},{16,48},{24,56},{32,0},{40,8},{48,16},{56,24},{64,96... | collective-permute-start | bytes 49160 | tf_op jit(solution)/shard_map/along/ppermute | solution.py:556
  171.2 5.3 %collective-permute-start.23 = (f32[8,4,128]{2,1,0:T(4,128)S(1)}, f32[8,4,128]{2,1,0:T(4,128)S(1)}, u32[]{:S(2)}, u32[]{:S(2)}) collective-permute-start(f32[8,4,128]{2,1,0:T(4,128)S(1)} %fusion.17), channel_id=1, source_target_pairs={{0,64},{8,72},{16,80},{24,88},{32,96},{40,104},{48,112},{56,120},{... | collective-permute-start | bytes 49160 | tf_op jit(solution)/shard_map/along/ppermute | solution.py:557
  184.0 5.3 %collective-permute-start.27 = (f32[1792,256]{1,0:T(8,128)S(1)}, f32[1792,256]{1,0:T(8,128)S(1)}, u32[]{:S(2)}, u32[]{:S(2)}) collective-permute-start(f32[1792,256]{1,0:T(8,128)S(1)} %fusion.4), channel_id=1, source_target_pairs={{0,8},{8,0},{16,24},{24,16},{32,40},{40,32},{48,56},{56,48},{64,72... | collective-permute-start | bytes 5505032 | tf_op jit(solution)/shard_map/down_grad/ppermute | solution.py:57
  184.1 14.0 %collective-permute-start.25 = (bf16[3,528,128]{2,1,0:T(8,128)(2,1)S(1)}, bf16[3,528,128]{2,1,0:T(8,128)(2,1)S(1)}, u32[]{:S(2)}, u32[]{:S(2)}) collective-permute-start(bf16[3,528,128]{2,1,0:T(8,128)(2,1)S(1)} %collective-permute-done.20.refs_3_), channel_id=1, source_target_pairs={{0,4},{1,5},{2,6},{3,7},{4,0},{5,1},{6,2},{7,3},{8,12},{9,13},{10,... | collective-permute-start | bytes 1216520 | tf_op jit(solution)/shard_map/along/ppermute | solution.py:65
  185.5 13.0 %collective-permute-start.26 = (bf16[3,528,128]{2,1,0:T(8,128)(2,1)S(1)}, bf16[3,528,128]{2,1,0:T(8,128)(2,1)S(1)}, u32[]{:S(2)}, u32[]{:S(2)}) collective-permute-start(bf16[3,528,128]{2,1,0:T(8,128)(2,1)S(1)} %collective-permute-done.20.refs_3_), channel_id=1, source_target_pairs={{0,1},{1,2},{2,3},{3,0},{4,5},{5,6},{6,7},{7,4},{8,9},{9,10},{10,1... | collective-permute-start | bytes 1216520 | tf_op jit(solution)/shard_map/along/ppermute | solution.py:61
  187.1 11.0 %collective-permute-start.24 = (bf16[3,528,128]{2,1,0:T(8,128)(2,1)S(1)}, bf16[3,528,128]{2,1,0:T(8,128)(2,1)}, u32[]{:S(2)}, u32[]{:S(2)}) collective-permute-start(bf16[3,528,128]{2,1,0:T(8,128)(2,1)S(1)} %collective-permute-done.18.refs_1_), channel_id=1, source_target_pairs={{0,3},{1,0},{2,1},{3,2},{4,7},{5,4},{6,5},{7,6},{8,11},{9,8},{10,9... | collective-permute-start | bytes 1216520 | tf_op jit(solution)/shard_map/along/ppermute | solution.py:61
  202.0 4.8 %collective-permute-start.29 = (f32[1792,256]{1,0:T(8,128)}, f32[1792,256]{1,0:T(8,128)}, u32[]{:S(2)}, u32[]{:S(2)}) collective-permute-start(f32[1792,256]{1,0:T(8,128)} %fusion.19), channel_id=1, source_target_pairs={{0,8},{8,0},{16,24},{24,16},{32,40},{40,32},{48,56},{56,48},{64,72... | collective-permute-start | bytes 5505032 | tf_op jit(solution)/shard_map/down_grad/ppermute | solution.py:57
  202.0 33.4 %collective-permute-start.30 = (bf16[1792,256]{1,0:T(8,128)(2,1)}, bf16[1792,256]{1,0:T(8,128)(2,1)}, u32[]{:S(2)}, u32[]{:S(2)}) collective-permute-start(bf16[1792,256]{1,0:T(8,128)(2,1)} %fusion), channel_id=1, source_target_pairs={{0,16},{8,24},{16,0},{24,8},{32,48},{40,56},{48,32},{56,40},{64,80... | collective-permute-start | bytes 2752520 | tf_op jit(solution)/shard_map/down_grad/ppermute | solution.py:53
  203.7 12.4 %collective-permute-start.28 = (bf16[3,528,128]{2,1,0:T(8,128)(2,1)}, bf16[3,528,128]{2,1,0:T(8,128)(2,1)S(1)}, u32[]{:S(2)}, u32[]{:S(2)}) collective-permute-start(bf16[3,528,128]{2,1,0:T(8,128)(2,1)} %collective-permute-done.24.refs_5_), channel_id=1, source_target_pairs={{0,3},{1,0},{2,1},{3,2},{4,7},{5,4},{6,5},{7,6},{8,11},{9,8},{10,9... | collective-permute-start | bytes 1216520 | tf_op jit(solution)/shard_map/down_grad/ppermute | solution.py:61
  (17 other events, 142.3 us)

commit v5 on v4

--- a/solution.py
+++ b/solution.py
@@ -73,50 +73,38 @@
 
 def layer_dot_kernel(plan_ref, hidden_ref, weight_ref, *refs):
     *out_refs, total_ref = refs
-    tile = 512
-
-    @pl.when(pl.program_id(0) == 0)
-    def _():
-        for n in range(0, total_ref.shape[1], tile):
-            total_ref[:, n : n + tile] = jnp.dot(
-                hidden_ref[...], weight_ref[:, n : n + tile], preferred_element_type=f32
-            )
-
-    @pl.when(pl.program_id(0) == 1)
-    def _():
-        lanes = out_refs[0].shape[-1]
-        flip = plan_ref[0] == 1
-        for c, ref in enumerate(out_refs):
-            for b in range(NX):
-                start = pl.multiple_of((b * NY + plan_ref[1 + c]) * 2 * lanes, 2 * lanes)
-                columns = pl.ds(start, 2 * lanes)
-                pair = total_ref[:, columns] + jnp.dot(
-                    hidden_ref[...], weight_ref[:, columns], preferred_element_type=f32
-                )
-                first, second = pair[:, :lanes], pair[:, lanes:]
-                ref[0, b] = jnp.where(flip, second, first).astype(ref.dtype)
-                ref[1, b] = jnp.where(flip, first, second).astype(ref.dtype)
+    lanes = out_refs[0].shape[-1]
+    flip = plan_ref[0] == 1
+    total_ref[...] = jnp.dot(hidden_ref[...], weight_ref[...], preferred_element_type=f32)
+    for c in range(len(out_refs) // 2):
+        same_ref, other_ref = out_refs[2 * c : 2 * c + 2]
+        start = pl.multiple_of(plan_ref[1 + c] * 2 * lanes, 2 * lanes)
+        pair = total_ref[:, pl.ds(start, 2 * lanes)]
+        first, second = pair[:, :lanes], pair[:, lanes:]
+        same_ref[0] = jnp.where(flip, second, first).astype(same_ref.dtype)
+        other_ref[0] = jnp.where(flip, first, second).astype(other_ref.dtype)
 
 
 def layer_dot(hidden, weight, columns, zl, group, dtypes):
     tokens, units = hidden.shape
     model_width = weight.shape[1]
     lanes = model_width // (NX * group)
-    depth = units // 2
-    out = pl.BlockSpec((2, NX, tokens, lanes), lambda k, s: (0, 0, 0, 0))
+    out = pl.BlockSpec((1, tokens, lanes), lambda b, s: (b, 0, 0))
     return pl.pallas_call(
         layer_dot_kernel,
         grid_spec=pltpu.PrefetchScalarGridSpec(
             num_scalar_prefetch=1,
-            grid=(2,),
+            grid=(NX,),
             in_specs=[
-                pl.BlockSpec((tokens, depth), lambda k, s: (0, k)),
-                pl.BlockSpec((depth, model_width), lambda k, s: (k, 0)),
+                pl.BlockSpec((tokens, units), lambda b, s: (0, 0)),
+                pl.BlockSpec((units, group * lanes), lambda b, s: (0, b)),
             ],
-            out_specs=[out] * len(columns),
-            scratch_shapes=[pltpu.VMEM((tokens, model_width), f32)],
-        ),
-        out_shape=[jax.ShapeDtypeStruct((2, NX, tokens, lanes), dtype) for dtype in dtypes],
+            out_specs=[out] * (2 * len(columns)),
+            scratch_shapes=[pltpu.VMEM((tokens, group * lanes), f32)],
+        ),
+        out_shape=[
+            jax.ShapeDtypeStruct((NX, tokens, lanes), dtype) for dtype in dtypes for _ in range(2)
+        ],
         compiler_params=pltpu.CompilerParams(vmem_limit_bytes=56 * MIB),
         cost_estimate=pl.CostEstimate(
             flops=2 * tokens * units * model_width,
@@ -327,7 +315,9 @@
 
 
 def hidden_grad_kernel(plan_ref, *refs):
-    *refs, scaled_ref, block_gain_ref, inverse_ref, coef_ref, weight_ref, out_ref, resid_ref, gain_ref, low_ref = refs
+    refs, outs = refs[:-5], refs[-5:]
+    out_ref, resid_ref, gain_ref, low_ref, gains_ref = outs
+    *refs, scaled_ref, block_gain_ref, inverse_ref, coef_ref, weight_ref = refs
     tokens = out_ref.shape[0]
     seqs_here = tokens // SEQ
     group = len(refs) // 2
@@ -350,9 +340,9 @@
                 if j:
                     tail = row_ref[j - 1, tokens:, :].astype(f32)
                     tail = tail[:8] + tail[8:]
-                    gain_ref[place, pl.ds(block, 1), :] = tail[seqs_here : seqs_here + 1]
+                    gains_ref[place, pl.ds(block, 1), :] = tail[seqs_here : seqs_here + 1]
                 else:
-                    gain_ref[place, pl.ds(block, 1), :] = block_gain_ref[pl.ds(place, 1), :]
+                    gains_ref[place, pl.ds(block, 1), :] = block_gain_ref[pl.ds(place, 1), :]
                 for s in range(seqs_here):
                     rows = slice(s * SEQ, (s + 1) * SEQ)
                     if j:
@@ -361,6 +351,9 @@
                         layer, scaled = strip_ref[0, rows, :], scaled_ref[place, pl.ds(first + s, 1), :]
                     inverse, coef = factors[s]
                     low_ref[rows, column] = (inverse * scaled - layer.astype(f32) * coef).astype(bf16)
+        first_place = plan_ref[0] % 2 * (group // 2)
+        for j in range(group // 2):
+            gain_ref[j : j + 1, :] = gains_ref[first_place + j, pl.ds(plan_ref[0] // 2, 1), :]
         resid_ref[...] = low_ref[:, pl.ds(pl.multiple_of(plan_ref[0] * width, width), width)]
 
     out_ref[...] = lax.dot_general(
@@ -389,14 +382,17 @@
             out_specs=[
                 pl.BlockSpec((tokens, chunk), lambda i, s: (0, i)),
                 whole((tokens, width)),
-                whole((group, others + 1, lanes)),
+                whole((group // 2, lanes)),
             ],
-            scratch_shapes=[pltpu.VMEM((tokens, model_width), bf16)],
+            scratch_shapes=[
+                pltpu.VMEM((tokens, model_width), bf16),
+                pltpu.VMEM((group, others + 1, lanes), f32),
+            ],
         ),
         out_shape=(
             jax.ShapeDtypeStruct((tokens, units), bf16),
             jax.ShapeDtypeStruct((tokens, width), bf16),
-            jax.ShapeDtypeStruct((group, others + 1, lanes), f32),
+            jax.ShapeDtypeStruct((group // 2, lanes), f32),
         ),
         compiler_params=pltpu.CompilerParams(vmem_limit_bytes=56 * MIB),
         cost_estimate=QUICK,
@@ -477,38 +473,33 @@
         pieces = pieces.reshape(NX, 2, tokens, lanes)
 
     with jax.named_scope("layer_sum"):
-        columns = [(y + step) % NY for step in (2, 1, 3, 0)]
-        sums = layer_dot(hidden, down_weight, columns, zl, group, (bf16, bf16, bf16, f32))
-        far, right, left, own, pieces = tie(*sums, pieces)
-        from_left = over_y(far[0], 1)
-        from_right = over_y(far[1], -1)
-        from_left, from_right = tie(from_left, from_right)
-        right0 = (right[0].astype(f32) + from_left.astype(f32)).astype(bf16)
-        left1 = (left[1].astype(f32) + from_right.astype(f32)).astype(bf16)
-        got_right = over_y(lax.dynamic_update_slice(right, right0[None], (0, 0, 0, 0)), 1)
-        got_left = over_y(lax.dynamic_update_slice(left, left1[None], (1, 0, 0, 0)), -1)
-
-    with jax.named_scope("hidden_exchange"):
-        hidden_left, hidden_right, right0 = tie(hidden_left, hidden_right, right0)
+        def dot_for(steps, dtypes):
+            columns = [(y + step) % NY for step in steps]
+            return layer_dot(hidden, down_weight, columns, zl, group, dtypes)
+
+        *sums, pieces = tie(*dot_for((2, 1, 3, 0), (bf16, bf16, bf16, f32)), pieces)
+        term = dict(zip([(part, step) for step in (2, 1, 3, 0) for part in (0, 1)], sums))
+
+        def add(*values):
+            return sum(value.astype(f32) for value in values)
+
+        from_12 = over_y(term[1, 2], -1)
+        from_11 = over_y(term[1, 1], 1)
+        from_12, from_11, hidden_left, hidden_right = tie(from_12, from_11, hidden_left, hidden_right)
         hidden_far = (
             over_x(hidden_left[: tokens // 2], 1),
             over_x(hidden_right[tokens // 2 :], -1),
         )
-        got_right, got_left, *hidden_far = tie(got_right, got_left, *hidden_far)
-        hidden_rows = jnp.concatenate([hidden, hidden_left, hidden_right] + hidden_far, axis=0)
-
-    with jax.named_scope("layer_sum"):
-        other_sum = own[1] + got_right[1].astype(f32) + got_left[1].astype(f32)
-        from_zl = over_zl(other_sum.astype(bf16))
-        from_zl, hidden_rows = tie(from_zl, hidden_rows)
+        from_13 = over_zl(add(term[1, 3], from_12).astype(bf16))
+        from_02 = over_y(term[0, 2], -1)
+        from_01 = over_y(term[0, 1], 1)
+        own_other = add(term[1, 0], from_11).astype(bf16)
+        from_13, from_02 = tie(from_13, from_02)
+        from_03 = over_y(add(term[0, 3], from_13, from_02).astype(bf16), -1)
+        from_10 = over_zl(own_other)
+        from_03, from_10, from_01, *hidden_far = tie(from_03, from_10, from_01, *hidden_far)
         resid_strips = lax.dynamic_slice_in_dim(pieces, y // 2, 1, 1)[:, 0]
-        layer = (
-            own[0]
-            + resid_strips.astype(f32)
-            + got_right[0].astype(f32)
-            + got_left[0].astype(f32)
-            + from_zl.astype(f32)
-        )
+        layer = add(term[0, 0], resid_strips, from_01, from_03, from_10)
 
     with jax.named_scope("strip_exchange"):
         low_layer = layer.astype(bf16)
@@ -522,6 +513,7 @@
         squares = jnp.sum(layer * layer, axis=(0, 2)).reshape(seqs_here, SEQ)
         squares = jnp.sum(gather_small(squares, "tensor"), axis=0)
         message, squares = tie(message, squares)
+        hidden_rows = jnp.concatenate([hidden, hidden_left, hidden_right] + hidden_far, axis=0)
         got = gather_start(message)
         inverse = lax.rsqrt(squares / model_width + eps_norm)
         weighted = layer.reshape(NX, seqs_here, SEQ, lanes) * inverse[None, :, :, None]
@@ -533,7 +525,7 @@
         got = gather_next(got)
         means_all = means_all.reshape(seqs, width)
         parts = gather_small(gram_part(means_all, gain_own, x), "tensor")
-        got, parts, low_layer = tie_gather(got, parts, low_layer)
+        got, parts, low_layer, hidden_rows = tie_gather(got, parts, low_layer, hidden_rows)
         got = gather_last(got)
         strips = [got[key] for key in KEYS]
         scaled, gain_grad_x, scaled_own, gain_grad = contrast(
@@ -543,8 +535,8 @@
     with jax.named_scope("row_gather"):
         own_rows = lax.dynamic_slice_in_dim(scaled_own, shard * seqs_here, seqs_here, 0)
         own_rows = jnp.pad(jnp.concatenate([own_rows, gain_grad], axis=0), ((0, 8 - seqs_here - 1), (0, 0)))
-        high = own_rows.astype(bf16)
-        tail = jnp.concatenate([high, (own_rows - high.astype(f32)).astype(bf16)], axis=0)
+        high = lax.reduce_precision(own_rows, exponent_bits=8, mantissa_bits=7)
+        tail = jnp.concatenate([high, own_rows - high], axis=0).astype(bf16)
         tail = tail.reshape(16, NX, lanes).transpose(1, 0, 2)
         blocks = jnp.concatenate([low_layer, tail], axis=1)
         blocks = jnp.concatenate([blocks, blocks], axis=0)
@@ -554,12 +546,14 @@
         own_inverse = jnp.where(jnp.arange(NX)[:, None, None] == x, inverse[None], 0.0)
         sums = jnp.concatenate([along_part(strips, scaled, plan), own_inverse], axis=0)
         sums = sums + lax.ppermute(sums, "dp", swap_route(1))
-        sums = sums + lax.ppermute(sums, "dp", swap_route(2))
         rows, sums = tie_gather(rows, sums)
         rows = gather_next(rows)
+        sums = sums + lax.ppermute(sums, "dp", swap_route(2))
 
     with jax.named_scope("down_grad"):
         low_x, coef = group_grad(strips, scaled, sums, plan)
+        rows, low_x = tie_gather(rows, low_x)
+        rows = gather_last(rows)
 
         def down(low):
             return lax.dot_general(
@@ -568,10 +562,10 @@
 
         from_core = over_core(down(low_x[3]))
         summed = (down(low_x[2]) + from_core).astype(bf16)
-        rows, summed, low0, low1 = tie_gather(rows, summed, low_x[0], low_x[1])
-        rows = gather_last(rows)
+        summed, low0, low1 = tie(summed, low_x[0], low_x[1])
         across = over_zh(summed)
-        near = down(low0) + over_core(down(low1))
+        near1 = down(low1)
+        near = down(low0) + over_core(near1)
 
     with jax.named_scope("hidden_grad"):
         rows, near = tie_gather(rows, near)
@@ -579,11 +573,10 @@
         grad_hidden, grad_resid, gain_grad = hidden_grad(
             rows, strips, scaled, gain_grad_x, inverse, coef, down_weight, [rank, x, shard * seqs_here] + places
         )
-        grad_gain = lax.dynamic_slice(
-            gain_grad, ((rank % 2) * 4, rank // 2, 0), (4, 1, lanes)
-        ).reshape(width)
+        grad_gain = gain_grad.reshape(width)
 
     with jax.named_scope("down_grad"):
+        across, grad_hidden = tie(across, grad_hidden)
         grad_down = near + across.astype(f32)
 
     return (grad_hidden, grad_resid, grad_down, grad_gain)

time: 240 us -> 226 us (0.942)
  waiting for transfers between devices: 74.3 us -> 59.5 us
  blocking collectives: 10.8 us -> 0 us
  starting transfers between devices: 59.5 us -> 67.6 us
  local copies, waits for them, and re-layouts: 22.7 us -> 28.9 us
    ppermute x14 -> x15, waiting for transfers between devices: 35.7 us -> 17.2 us  [over_y(): return lax.ppermute(value, 'tensor', tensor_route(0, step))]
    all_to_all x1 -> x0, blocking collectives: 10.8 us -> none  [gather_small(): return lax.all_to_all(copies, axis, 0, 0)]
    unnamed x66 -> x74, local copies, waits for them, and re-layouts: 8.47 us -> 16.7 us
    all_to_all x2 -> x3, starting transfers between devices: 11.1 us -> 16.2 us  [gather_small(): return lax.all_to_all(copies, axis, 0, 0)]
    ppermute x14 -> x15, starting transfers between devices: 22.6 us -> 26.5 us  [over_y(): return lax.ppermute(value, 'tensor', tensor_route(0, step))]
    ppermute x2, waiting for transfers between devices: 0.01 us -> 3.63 us  [over_core(): return lax.ppermute(value, 'dp', dp_route(0, 0, 1))]
    ppermute x7, waiting for transfers between devices: 4.62 us -> 7.49 us  [over_x(): return lax.ppermute(value, 'dp', dp_route(step, 0, 0))]
    all_to_all x2 -> x3, waiting for transfers between devices: 18.5 us -> 16.2 us  [gather_small(): return lax.all_to_all(copies, axis, 0, 0)]
  transfers between devices with their start and end apart: 34 -> 37, of which waited for: 16 -> 17; matrix products, arithmetic and copies ran while one was open for 13% -> 15% of each run, Pallas kernels for 16% -> 18%
where the time goes in v5:
time: 226 us; the launch traced here: 225 us
  starting transfers between devices  67.6 us (30%)
  waiting for transfers between devices  59.5 us (26%)
  Pallas kernels  40.7 us (18%)
  local copies, waits for them, and re-layouts  28.9 us (13%)
  matrix products  16.9 us (7%)
  other arithmetic  9.7 us (4%)
    ppermute x15, starting transfers between devices, over_y(): return lax.ppermute(value, 'tensor', tensor_route(0, step))  26.5 us
    pallas_call x1, Pallas kernels, hidden_grad(): pl.pallas_call(hidden_grad_kernel, grid_spec=pltpu.PrefetchScalarGridSpec...  17.3 us
    ppermute x15, waiting for transfers between devices, over_y(): return lax.ppermute(value, 'tensor', tensor_route(0, step))  17.2 us
    dot_general x4, matrix products, down(): lax.dot_general(hidden_rows, low, (((0,), (0,)), ((), ())), preferred_ele...  16.9 us
    unnamed x74, local copies, waits for them, and re-layouts  16.7 us
    all_to_all x3, starting transfers between devices, gather_small(): return lax.all_to_all(copies, axis, 0, 0)  16.2 us
    all_to_all x3, waiting for transfers between devices, gather_small(): return lax.all_to_all(copies, axis, 0, 0)  16.2 us
    pallas_call x1, Pallas kernels, layer_dot(): pl.pallas_call(layer_dot_kernel, grid_spec=pltpu.PrefetchScalarGridSpec(n...  13.4 us
  transfers between devices with their start and end apart: 37, of which 17 were waited for; matrix products, arithmetic and copies ran while one was open for 15% of the time, Pallas kernels for 18%

profile of v5, /device:TPU:0, one launch (start us, length us, event | category | flops | bytes accessed | tf_op | source)
XLA Modules:
  0.0 224.5 jit_solution(8605564203013946936)
XLA Ops:
  0.6 1.6 collective-permute-start.2
  2.3 1.7 collective-permute-start.3
  6.3 5.9 %all-to-all-start = ((bf16[8,512,128]{2,1,0:T(8,128)(2,1)}), bf16[8,512,128]{2,1,0:T(8,128)(2,1)S(1)}, u32[]{:S(2)}, u32[]{:S(2)}) async-start(bf16[8,512,128]{2,1,0:T(8,128)(2,1)} %bitcast.6), calls=%async_computation | async-start | bytes 2097152 | tf_op jit(solution)/shard_map/resid_exchange/all_to_all | solution.py:472
  12.8 13.4 %layer_sum.1 = (bf16[4,512,128]{2,1,0:T(8,128)(2,1)}, bf16[4,512,128]{2,1,0:T(8,128)(2,1)}, bf16[4,512,128]{2,1,0:T(8,128)(2,1)}, bf16[4,512,128]{2,1,0:T(8,128)...) custom-call(s32[5]{0:T(128)} %stack.140.plan_ref, ...), custom_call_target="tpu_custom_call" | custom-call | flops 7516192768 | bytes 20709376 | tf_op jit(solution)/shard_map/layer_sum/pallas_call | solution.py:93
  27.3 2.2 collective-permute-start
  29.5 3.2 %collective-permute-start.5 = (bf16[4,512,128]{2,1,0:T(8,128)(2,1)}, bf16[4,512,128]{2,1,0:T(8,128)(2,1)S(1)}, u32[]{:S(2)}, u32[]{:S(2)}) collective-permute-start(bf16[4,512,128]{2,1,0:T(8,128)(2,1)} %get-tuple-element.100), channel_id=1, source_target_pairs={{0,3},{1,0},{2,1},{3,2},{4,7},{5,4},{6,5},{7,6},{8,11},{9,8},{10,9... | collective-permute-start | bytes 1572872 | tf_op jit(solution)/shard_map/layer_sum/ppermute | solution.py:61
  32.8 9.6 %collective-permute-done = bf16[4,512,128]{2,1,0:T(8,128)(2,1)S(1)} collective-permute-done((bf16[4,512,128]{2,1,0:T(8,128)(2,1)}, bf16[4,512,128]{2,1,0:T(8,128)(2,1)S(1)}, u32[]{:S(2)}, u32[]{:S(2)}) %collective-permute-start) | collective-permute-done | bytes 524320 | tf_op jit(solution)/shard_map/layer_sum/ppermute | solution.py:61
  44.0 1.6 add_convert_fusion.2
  45.6 2.1 collective-permute-start.4
  47.7 1.6 collective-permute-start.8
  50.2 2.8 %collective-permute-start.10 = (bf16[256,1792]{1,0:T(8,128)(2,1)}, bf16[256,1792]{1,0:T(8,128)(2,1)}, u32[]{:S(2)}, u32[]{:S(2)}) collective-permute-start(bf16[256,1792]{1,0:T(8,128)(2,1)} %slice.19), channel_id=1, source_target_pairs={{0,96},{8,104},{16,112},{24,120},{32,0},{40,8},{48,16},{56,24},{64... | collective-permute-start | bytes 2752520 | tf_op jit(solution)/shard_map/layer_sum/ppermute | solution.py:49
  53.1 2.2 slice.18
  55.5 5.0 %collective-permute-done.4 = bf16[4,512,128]{2,1,0:T(8,128)(2,1)S(1)} collective-permute-done((bf16[4,512,128]{2,1,0:T(8,128)(2,1)S(1)}, bf16[4,512,128]{2,1,0:T(8,128)(2,1)S(1)}, u32[]{:S(2)}, u32[]{:S(2)}) %collective-permute-start.4) | collective-permute-done | bytes 524320 | tf_op jit(solution)/shard_map/layer_sum/ppermute | solution.py:65
  61.5 3.1 %collective-permute-start.6 = (bf16[4,512,128]{2,1,0:T(8,128)(2,1)}, bf16[4,512,128]{2,1,0:T(8,128)(2,1)}, u32[]{:S(2)}, u32[]{:S(2)}) collective-permute-start(bf16[4,512,128]{2,1,0:T(8,128)(2,1)} %add_convert_fusion.1), channel_id=1, source_target_pairs={{0,3},{1,0},{2,1},{3,2},{4,7},{5,4},{6,5},{7,6},{8,11},{9,8},{10,9... | collective-permute-start | bytes 1572872 | tf_op jit(solution)/shard_map/layer_sum/ppermute | solution.py:61
  65.5 2.9 %constant_dynamic-update-slice_fusion.4 = bf16[2048,1792]{1,0:T(8,128)(2,1)} fusion(bf16[512,1792]{1,0:T(8,128)(2,1)} %hidden_ref.1), kind=kLoop, calls=%fused_computation.40 | loop fusion | bytes 3670016
  68.4 1.7 collective-permute-done.7
  71.2 5.6 %collective-permute-done.9 = bf16[256,1792]{1,0:T(8,128)(2,1)} collective-permute-done((bf16[256,1792]{1,0:T(8,128)(2,1)}, bf16[256,1792]{1,0:T(8,128)(2,1)}, u32[]{:S(2)}, u32[]{:S(2)}) %collective-permute-start.9) | collective-permute-done | bytes 917536 | tf_op jit(solution)/shard_map/layer_sum/ppermute | solution.py:49
  76.8 2.1 multiply_reduce_fusion.1
  79.9 3.2 %collective-permute-start.12 = (bf16[1,512,128]{2,1,0:T(8,128)(2,1)S(1)}, bf16[1,512,128]{2,1,0:T(8,128)(2,1)S(1)}, u32[]{:S(2)}, u32[]{:S(2)}) collective-permute-start(bf16[1,512,128]{2,1,0:T(8,128)(2,1)S(1)} %get-tuple-element.172), channel_id=1, source_target_pairs={{0,96},{8,104},{16,112},{24,120},{32,0},{40,8},{48,16},{56,24},{64... | collective-permute-start | bytes 393224 | tf_op jit(solution)/shard_map/strip_exchange/ppermute | solution.py:49
  83.8 4.2 %all-to-all-start.1 = ((f32[8,4,128]{2,1,0:T(4,128)}), f32[8,4,128]{2,1,0:T(4,128)S(1)}, u32[]{:S(2)}, u32[]{:S(2)}) async-start(f32[8,4,128]{2,1,0:T(4,128)} %broadcast_in_dim.54), calls=%async_computation.1 | async-start | bytes 32768 | tf_op jit(solution)/shard_map/norm/all_to_all | solution.py:71
  88.6 5.6 %all-to-all-done.1 = f32[8,4,128]{2,1,0:T(4,128)S(1)} async-done(((f32[8,4,128]{2,1,0:T(4,128)}), f32[8,4,128]{2,1,0:T(4,128)S(1)}, u32[]{:S(2)}, u32[]{:S(2)}) %all-to-all-start.1) | async-done | bytes 16416 | tf_op jit(solution)/shard_map/norm/all_to_all | solution.py:71
  97.9 7.9 %all-to-all-start.2 = ((f32[16,4,512]{2,1,0:T(4,128)}), f32[16,4,512]{2,1,0:T(4,128)S(1)}, u32[]{:S(2)}, u32[]{:S(2)}) async-start(f32[16,4,512]{2,1,0:T(4,128)} %broadcast_in_dim.56), calls=%async_computation.2 | async-start | bytes 262144 | tf_op jit(solution)/shard_map/contrast/all_to_all | solution.py:71
  105.8 2.9 %constant_dynamic-update-slice_fusion.3 = bf16[2048,1792]{1,0:T(8,128)(2,1)} fusion(bf16[2048,1792]{1,0:T(8,128)(2,1)} %constant_dynamic-update-slice_fusion.4, bf16[512,1792]{1,0:T(8,128)(2,1)} %collective-permute-done.2), kind=kLoop, calls=%fused_computation.39 | loop fusion | bytes 3670016
  108.7 5.1 %all-to-all-done.2 = f32[16,4,512]{2,1,0:T(4,128)S(1)} async-done(((f32[16,4,512]{2,1,0:T(4,128)}), f32[16,4,512]{2,1,0:T(4,128)S(1)}, u32[]{:S(2)}, u32[]{:S(2)}) %all-to-all-start.2) | async-done | bytes 131104 | tf_op jit(solution)/shard_map/contrast/all_to_all | solution.py:71
  115.5 2.5 %collective-permute-start.17 = (bf16[4,512,128]{2,1,0:T(8,128)(2,1)S(1)}, bf16[4,512,128]{2,1,0:T(8,128)(2,1)}, u32[]{:S(2)}, u32[]{:S(2)}) collective-permute-start(bf16[4,512,128]{2,1,0:T(8,128)(2,1)S(1)} %collective-permute-done.14.refs_1_.refs_9_), channel_id=1, source_target_pairs={{0,3},{1,0},{2,1},{3,2},{4,7},{5,4},{6,5},{7,6},{8,11},{9,8},{10,9... | collective-permute-start | bytes 1572872 | tf_op jit(solution)/shard_map/contrast/ppermute | solution.py:61
  118.0 2.9 %constant_dynamic-update-slice_fusion.2 = bf16[2048,1792]{1,0:T(8,128)(2,1)} fusion(bf16[2048,1792]{1,0:T(8,128)(2,1)} %constant_dynamic-update-slice_fusion.3, bf16[512,1792]{1,0:T(8,128)(2,1)} %copy-done.17), kind=kLoop, calls=%fused_computation.38 | loop fusion | bytes 3670016
  122.1 4.1 %all-to-all-start.3 = ((f32[8,2,64,128]{3,2,1,0:T(8,128)}), f32[8,2,64,128]{3,2,1,0:T(8,128)}, u32[]{:S(2)}, u32[]{:S(2)}) async-start(f32[8,2,64,128]{3,2,1,0:T(8,128)} %broadcast_in_dim.57), calls=%async_computation.3 | async-start | bytes 1048576 | tf_op jit(solution)/shard_map/contrast/all_to_all | solution.py:71
  126.2 2.2 constant_dynamic-update-slice_fusion.1
  128.4 2.2 constant_dynamic-update-slice_fusion
  130.6 5.4 %all-to-all-done.3.part_ref = f32[8,2,64,128]{3,2,1,0:T(8,128)} async-done(((f32[8,2,64,128]{3,2,1,0:T(8,128)}), f32[8,2,64,128]{3,2,1,0:T(8,128)}, u32[]{:S(2)}, u32[]{:S(2)}) %all-to-all-start.3) | async-done | bytes 524320 | tf_op jit(solution)/shard_map/contrast/all_to_all | solution.py:71
  136.1 2.3 %collective-permute-start.23 = (bf16[4,512,128]{2,1,0:T(8,128)(2,1)}, bf16[4,512,128]{2,1,0:T(8,128)(2,1)S(1)}, u32[]{:S(2)}, u32[]{:S(2)}) collective-permute-start(bf16[4,512,128]{2,1,0:T(8,128)(2,1)} %collective-permute-done.17.refs_5_.refs_13_), channel_id=1, source_target_pairs={{0,3},{1,0},{2,1},{3,2},{4,7},{5,4},{6,5},{7,6},{8,11},{9,8},{10,9... | collective-permute-start | bytes 1572872 | tf_op jit(solution)/shard_map/contrast/ppermute | solution.py:61
  139.8 1.9 contrast.3
  141.8 2.4 %fusion.10.refs_0_ = bf16[3,528,128]{2,1,0:T(8,128)(2,1)S(1)} fusion(s32[]{:T(128)S(6)} %select_n.212, bf16[4,512,128]{2,1,0:T(8,128)(2,1)} %copy-done.16, bf16[4,16,128]{2,1,0:T(8,128)(2,1)S(1)} %maximum_bitcast_fusion), kind=kLoop, calls=%fused_computation.26 | loop fusion | flops 1622016 | bytes 946180 | tf_op jit(solution)/shard_map/row_gather/concatenate | solution.py:542
  145.4 2.0 collective-permute-start.22
  147.5 3.7 %collective-permute-done.23.refs_7_.refs_15_ = bf16[4,512,128]{2,1,0:T(8,128)(2,1)S(1)} collective-permute-done((bf16[4,512,128]{2,1,0:T(8,128)(2,1)}, bf16[4,512,128]{2,1,0:T(8,128)(2,1)S(1)}, u32[]{:S(2)}, u32[]{:S(2)}) %collective-permute-start.23) | collective-permute-done | bytes 524320 | tf_op jit(solution)/shard_map/contrast/ppermute | solution.py:61
  151.8 3.3 %along.1 = f32[4,4,128]{2,1,0:T(4,128)S(1)} custom-call(s32[32]{0:T(128)S(1)} %copy-done.12, bf16[4,512,128]{2,1,0:T(8,128)(2,1)S(1)} %pad_maximum_fusion.refs_0_.refs_8_, bf16[4,512,128]{2,1,0:T(8,128)(2,1)S(1)} %collective-permute-done.14.refs_1_.refs_9_, bf16[4,512,128]{2,1,0:T(8,128)(2,1)S(1)} %collective-permute-done.15.refs_2_.refs_10_, ...), custom_call_target="tpu_custom_call" | custom-call | flops 1024 | bytes 1024 | tf_op jit(solution)/shard_map/along/pallas_call | solution.py:244
  155.7 3.2 %collective-permute-done.24 = f32[8,4,128]{2,1,0:T(4,128)S(1)} collective-permute-done((f32[8,4,128]{2,1,0:T(4,128)S(1)}, f32[8,4,128]{2,1,0:T(4,128)S(1)}, u32[]{:S(2)}, u32[]{:S(2)}) %collective-permute-start.24) | collective-permute-done | bytes 16416 | tf_op jit(solution)/shard_map/along/ppermute | solution.py:548
  159.1 3.5 %collective-permute-start.25 = (bf16[3,528,128]{2,1,0:T(8,128)(2,1)S(1)}, bf16[3,528,128]{2,1,0:T(8,128)(2,1)S(1)}, u32[]{:S(2)}, u32[]{:S(2)}) collective-permute-start(bf16[3,528,128]{2,1,0:T(8,128)(2,1)S(1)} %collective-permute-done.20.refs_1_), channel_id=1, source_target_pairs={{0,3},{1,0},{2,1},{3,2},{4,7},{5,4},{6,5},{7,6},{8,11},{9,8},{10,9... | collective-permute-start | bytes 1216520 | tf_op jit(solution)/shard_map/along/ppermute | solution.py:61
  165.0 4.0 %collective-permute-done.28 = f32[8,4,128]{2,1,0:T(4,128)S(1)} collective-permute-done((f32[8,4,128]{2,1,0:T(4,128)S(1)}, f32[8,4,128]{2,1,0:T(4,128)S(1)}, u32[]{:S(2)}, u32[]{:S(2)}) %collective-permute-start.28) | collective-permute-done | bytes 16416 | tf_op jit(solution)/shard_map/along/ppermute | solution.py:551
  169.7 4.6 %down_grad.1 = (bf16[4,2048,256]{2,1,0:T(8,128)(2,1)S(1)}, f32[4,128]{1,0:T(4,128)S(1)}) custom-call(s32[32]{0:T(128)S(1)} %copy-done.13, bf16[4,512,128]{2,1,0:T(8,128)(2,1)S(1)} %pad_maximum_fusion.refs_0_.refs_8_, bf16[4,512,128]{2,1,0:T(8,128)(2,1)S(1)} %collective-permute-done.14.refs_1_.refs_9_, ...), custom_call_target="tpu_custom_call" | custom-call | flops 1024 | bytes 1024 | tf_op jit(solution)/shard_map/down_grad/pallas_call | solution.py:294
  176.0 5.5 %fusion.4 = f32[1792,256]{1,0:T(8,128)S(1)} fusion(bf16[2048,1792]{1,0:T(8,128)(2,1)} %constant_dynamic-update-slice_fusion, bf16[4,2048,256]{2,1,0:T(8,128)(2,1)S(1)} %get-tuple-element.139), kind=kOutput, calls=%fused_computation.12 | convolution fusion | flops 1879048192 | bytes 10223616 | tf_op jit(solution)/shard_map/down_grad/dot_general | solution.py:559
  181.9 3.6 %collective-permute-done.29 = f32[1792,256]{1,0:T(8,128)S(1)} collective-permute-done((f32[1792,256]{1,0:T(8,128)S(1)}, f32[1792,256]{1,0:T(8,128)S(1)}, u32[]{:S(2)}, u32[]{:S(2)}) %collective-permute-start.29) | collective-permute-done | bytes 1835040 | tf_op jit(solution)/shard_map/down_grad/ppermute | solution.py:57
  185.5 2.2 fusion
  187.8 3.4 %fusion.18 = f32[1792,256]{1,0:T(8,128)} fusion(bf16[2048,1792]{1,0:T(8,128)(2,1)S(1)} %bitcast.85, bf16[2048,256]{1,0:T(8,128)(2,1)S(1)} %get-tuple-element.149), kind=kOutput, calls=%fused_computation.55 | convolution fusion | flops 1879048192 | bytes 10223616 | tf_op jit(solution)/shard_map/down_grad/dot_general | solution.py:559
  193.0 3.2 %collective-permute-start.31 = (bf16[3,528,128]{2,1,0:T(8,128)(2,1)S(1)}, bf16[3,528,128]{2,1,0:T(8,128)(2,1)S(1)}, u32[]{:S(2)}, u32[]{:S(2)}) collective-permute-start(bf16[3,528,128]{2,1,0:T(8,128)(2,1)S(1)} %copy-done.27), channel_id=1, source_target_pairs={{0,3},{1,0},{2,1},{3,2},{4,7},{5,4},{6,5},{7,6},{8,11},{9,8},{10,9... | collective-permute-start | bytes 1216520 | tf_op jit(solution)/shard_map/down_grad/ppermute | solution.py:61
  196.2 5.8 %convolution_add_fusion = f32[1792,256]{1,0:T(8,128)S(1)} fusion(f32[1792,256]{1,0:T(8,128)} %collective-permute-done.32, bf16[2048,1792]{1,0:T(8,128)(2,1)} %constant_dynamic-update-slice_fusion, bf16[2048,256]{1,0:T(8,128)(2,1)S(1)} %get-tuple-element.148), kind=kOutput, calls=%fused_computation | convolution fusion | flops 1879506944 | bytes 12058624 | tf_op jit(solution)/shard_map/down_grad/dot_general | solution.py:559
  202.0 3.1 %collective-permute-done.31.refs_7_ = bf16[3,528,128]{2,1,0:T(8,128)(2,1)S(1)} collective-permute-done((bf16[3,528,128]{2,1,0:T(8,128)(2,1)S(1)}, bf16[3,528,128]{2,1,0:T(8,128)(2,1)S(1)}, u32[]{:S(2)}, u32[]{:S(2)}) %collective-permute-start.31) | collective-permute-done | bytes 405536 | tf_op jit(solution)/shard_map/down_grad/ppermute | solution.py:61
  205.8 17.3 %hidden_grad.1 = (bf16[512,1792]{1,0:T(8,128)(2,1)}, bf16[512,512]{1,0:T(8,128)(2,1)}, f32[4,128]{1,0:T(4,128)}) custom-call(s32[11]{0:T(128)} %stack.176.plan_ref, bf16[3,528,128]{2,1,0:T(8,128)(2,1)} %copy-done.20, bf16[3,528,128]{2,1,0:T(8,128)(2,1)} %copy-done.23, bf16[3,528,128]{2,1,0:T(8,128)(2,1)} %copy-done.24, bf16[3,528,128]{2,1,0:T(8,128)(2,1)} %copy-done.25, ...), custom_call_target="tpu_custom_call" | custom-call | flops 1024 | bytes 1024 | tf_op jit(solution)/shard_map/hidden_grad/pallas_call | solution.py:373
  (150 shorter events, 31.8 us)
Async XLA Ops:
  0.6 43.2 %collective-permute-start.2 = (bf16[512,1792]{1,0:T(8,128)(2,1)}, bf16[512,1792]{1,0:T(8,128)(2,1)}, u32[]{:S(2)}, u32[]{:S(2)}) collective-permute-start(bf16[512,1792]{1,0:T(8,128)(2,1)} %hidden_ref.1), channel_id=1, source_target_pairs={{0,32},{8,40},{16,48},{24,56},{32,64},{40,72},{48,80},{56,88},{64,... | collective-permute-start | bytes 5505032 | tf_op jit(solution)/shard_map/hidden_exchange/ppermute | solution.py:49
  2.3 41.7 %collective-permute-start.3 = (bf16[512,1792]{1,0:T(8,128)(2,1)}, bf16[512,1792]{1,0:T(8,128)(2,1)S(1)}, u32[]{:S(2)}, u32[]{:S(2)}) collective-permute-start(bf16[512,1792]{1,0:T(8,128)(2,1)} %hidden_ref.1), channel_id=1, source_target_pairs={{0,96},{8,104},{16,112},{24,120},{32,0},{40,8},{48,16},{56,24},{64... | collective-permute-start | bytes 5505032 | tf_op jit(solution)/shard_map/hidden_exchange/ppermute | solution.py:49
  6.3 21.0 %all-to-all-start = ((bf16[8,512,128]{2,1,0:T(8,128)(2,1)}), bf16[8,512,128]{2,1,0:T(8,128)(2,1)S(1)}, u32[]{:S(2)}, u32[]{:S(2)}) async-start(bf16[8,512,128]{2,1,0:T(8,128)(2,1)} %bitcast.6), calls=%async_computation | async-start | bytes 2097152 | tf_op jit(solution)/shard_map/resid_exchange/all_to_all | solution.py:472
  27.3 34.2 %copy-start.18 = (bf16[8,512,128]{2,1,0:T(8,128)(2,1)}, bf16[8,512,128]{2,1,0:T(8,128)(2,1)S(1)}, u32[]{:S(2)}) copy-start(bf16[8,512,128]{2,1,0:T(8,128)(2,1)S(1)} %all-to-all-done) | copy-start | bytes 3145732
  27.3 33.2 %copy-start.22 = (bf16[4,512,128]{2,1,0:T(8,128)(2,1)S(1)}, bf16[4,512,128]{2,1,0:T(8,128)(2,1)}, u32[]{:S(2)}) copy-start(bf16[4,512,128]{2,1,0:T(8,128)(2,1)} %get-tuple-element.95) | copy-start | bytes 1572868
  27.3 15.0 %collective-permute-start = (bf16[4,512,128]{2,1,0:T(8,128)(2,1)}, bf16[4,512,128]{2,1,0:T(8,128)(2,1)S(1)}, u32[]{:S(2)}, u32[]{:S(2)}) collective-permute-start(bf16[4,512,128]{2,1,0:T(8,128)(2,1)} %get-tuple-element.97), channel_id=1, source_target_pairs={{0,3},{1,0},{2,1},{3,2},{4,7},{5,4},{6,5},{7,6},{8,11},{9,8},{10,9... | collective-permute-start | bytes 1572872 | tf_op jit(solution)/shard_map/layer_sum/ppermute | solution.py:61
  29.5 13.7 %collective-permute-start.1 = (bf16[4,512,128]{2,1,0:T(8,128)(2,1)}, bf16[4,512,128]{2,1,0:T(8,128)(2,1)S(1)}, u32[]{:S(2)}, u32[]{:S(2)}) collective-permute-start(bf16[4,512,128]{2,1,0:T(8,128)(2,1)} %get-tuple-element.98), channel_id=1, source_target_pairs={{0,1},{1,2},{2,3},{3,0},{4,5},{5,6},{6,7},{7,4},{8,9},{9,10},{10,1... | collective-permute-start | bytes 1572872 | tf_op jit(solution)/shard_map/layer_sum/ppermute | solution.py:61
  29.5 25.8 %collective-permute-start.5 = (bf16[4,512,128]{2,1,0:T(8,128)(2,1)}, bf16[4,512,128]{2,1,0:T(8,128)(2,1)S(1)}, u32[]{:S(2)}, u32[]{:S(2)}) collective-permute-start(bf16[4,512,128]{2,1,0:T(8,128)(2,1)} %get-tuple-element.100), channel_id=1, source_target_pairs={{0,3},{1,0},{2,1},{3,2},{4,7},{5,4},{6,5},{7,6},{8,11},{9,8},{10,9... | collective-permute-start | bytes 1572872 | tf_op jit(solution)/shard_map/layer_sum/ppermute | solution.py:61
  45.6 14.9 %collective-permute-start.4 = (bf16[4,512,128]{2,1,0:T(8,128)(2,1)S(1)}, bf16[4,512,128]{2,1,0:T(8,128)(2,1)S(1)}, u32[]{:S(2)}, u32[]{:S(2)}) collective-permute-start(bf16[4,512,128]{2,1,0:T(8,128)(2,1)S(1)} %add_convert_fusion.2), channel_id=1, source_target_pairs={{0,4},{1,5},{2,6},{3,7},{4,0},{5,1},{6,2},{7,3},{8,12},{9,13},{10,... | collective-permute-start | bytes 1572872 | tf_op jit(solution)/shard_map/layer_sum/ppermute | solution.py:65
  47.7 20.7 %collective-permute-start.8 = (bf16[4,512,128]{2,1,0:T(8,128)(2,1)}, bf16[4,512,128]{2,1,0:T(8,128)(2,1)}, u32[]{:S(2)}, u32[]{:S(2)}) collective-permute-start(bf16[4,512,128]{2,1,0:T(8,128)(2,1)} %get-tuple-element.105), channel_id=1, source_target_pairs={{0,1},{1,2},{2,3},{3,0},{4,5},{5,6},{6,7},{7,4},{8,9},{9,10},{10,1... | collective-permute-start | bytes 1572872 | tf_op jit(solution)/shard_map/layer_sum/ppermute | solution.py:61
  50.2 21.0 %collective-permute-start.10 = (bf16[256,1792]{1,0:T(8,128)(2,1)}, bf16[256,1792]{1,0:T(8,128)(2,1)}, u32[]{:S(2)}, u32[]{:S(2)}) collective-permute-start(bf16[256,1792]{1,0:T(8,128)(2,1)} %slice.19), channel_id=1, source_target_pairs={{0,96},{8,104},{16,112},{24,120},{32,0},{40,8},{48,16},{56,24},{64... | collective-permute-start | bytes 2752520 | tf_op jit(solution)/shard_map/layer_sum/ppermute | solution.py:49
  55.2 21.6 %collective-permute-start.9 = (bf16[256,1792]{1,0:T(8,128)(2,1)}, bf16[256,1792]{1,0:T(8,128)(2,1)}, u32[]{:S(2)}, u32[]{:S(2)}) collective-permute-start(bf16[256,1792]{1,0:T(8,128)(2,1)} %slice.18), channel_id=1, source_target_pairs={{0,32},{8,40},{16,48},{24,56},{32,64},{40,72},{48,80},{56,88},{64,... | collective-permute-start | bytes 2752520 | tf_op jit(solution)/shard_map/layer_sum/ppermute | solution.py:49
  55.3 14.7 %collective-permute-start.7 = (bf16[4,512,128]{2,1,0:T(8,128)(2,1)S(1)}, bf16[4,512,128]{2,1,0:T(8,128)(2,1)}, u32[]{:S(2)}, u32[]{:S(2)}) collective-permute-start(bf16[4,512,128]{2,1,0:T(8,128)(2,1)S(1)} %add_convert_fusion), channel_id=1, source_target_pairs={{0,4},{1,5},{2,6},{3,7},{4,0},{5,1},{6,2},{7,3},{8,12},{9,13},{10,... | collective-permute-start | bytes 1572872 | tf_op jit(solution)/shard_map/layer_sum/ppermute | solution.py:65
  61.5 15.3 %collective-permute-start.6 = (bf16[4,512,128]{2,1,0:T(8,128)(2,1)}, bf16[4,512,128]{2,1,0:T(8,128)(2,1)}, u32[]{:S(2)}, u32[]{:S(2)}) collective-permute-start(bf16[4,512,128]{2,1,0:T(8,128)(2,1)} %add_convert_fusion.1), channel_id=1, source_target_pairs={{0,3},{1,0},{2,1},{3,2},{4,7},{5,4},{6,5},{7,6},{8,11},{9,8},{10,9... | collective-permute-start | bytes 1572872 | tf_op jit(solution)/shard_map/layer_sum/ppermute | solution.py:61
  79.9 14.4 %collective-permute-start.11 = (bf16[1,512,128]{2,1,0:T(8,128)(2,1)S(1)}, bf16[1,512,128]{2,1,0:T(8,128)(2,1)S(1)}, u32[]{:S(2)}, u32[]{:S(2)}) collective-permute-start(bf16[1,512,128]{2,1,0:T(8,128)(2,1)S(1)} %get-tuple-element.173), channel_id=1, source_target_pairs={{0,32},{8,40},{16,48},{24,56},{32,64},{40,72},{48,80},{56,88},{64,... | collective-permute-start | bytes 393224 | tf_op jit(solution)/shard_map/strip_exchange/ppermute | solution.py:49
  79.9 14.3 %collective-permute-start.12 = (bf16[1,512,128]{2,1,0:T(8,128)(2,1)S(1)}, bf16[1,512,128]{2,1,0:T(8,128)(2,1)S(1)}, u32[]{:S(2)}, u32[]{:S(2)}) collective-permute-start(bf16[1,512,128]{2,1,0:T(8,128)(2,1)S(1)} %get-tuple-element.172), channel_id=1, source_target_pairs={{0,96},{8,104},{16,112},{24,120},{32,0},{40,8},{48,16},{56,24},{64... | collective-permute-start | bytes 393224 | tf_op jit(solution)/shard_map/strip_exchange/ppermute | solution.py:49
  83.2 11.1 %collective-permute-start.13 = (bf16[1,512,128]{2,1,0:T(8,128)(2,1)S(1)}, bf16[1,512,128]{2,1,0:T(8,128)(2,1)S(1)}, u32[]{:S(2)}, u32[]{:S(2)}) collective-permute-start(bf16[1,512,128]{2,1,0:T(8,128)(2,1)S(1)} %get-tuple-element.171), channel_id=1, source_target_pairs={{0,64},{8,72},{16,80},{24,88},{32,96},{40,104},{48,112},{56,120},{... | collective-permute-start | bytes 393224 | tf_op jit(solution)/shard_map/strip_exchange/ppermute | solution.py:49
  83.2 37.7 %copy-start.10 = (f32[1,512]{1,0:T(1,128)}, f32[1,512]{1,0:T(1,128)S(1)}, u32[]{:S(2)}) copy-start(f32[1,512]{1,0:T(1,128)S(1)} %fusion.15.gain_ref) | copy-start | bytes 6148
  83.8 10.4 %all-to-all-start.1 = ((f32[8,4,128]{2,1,0:T(4,128)}), f32[8,4,128]{2,1,0:T(4,128)S(1)}, u32[]{:S(2)}, u32[]{:S(2)}) async-start(f32[8,4,128]{2,1,0:T(4,128)} %broadcast_in_dim.54), calls=%async_computation.1 | async-start | bytes 32768 | tf_op jit(solution)/shard_map/norm/all_to_all | solution.py:71
  94.4 74.7 %copy-start = (bf16[4,512,128]{2,1,0:T(8,128)(2,1)}, bf16[4,512,128]{2,1,0:T(8,128)(2,1)S(1)}, u32[]{:S(2)}) copy-start(bf16[4,512,128]{2,1,0:T(8,128)(2,1)S(1)} %pad_maximum_fusion.refs_0_.refs_8_) | copy-start | bytes 1572868
  94.4 19.4 %collective-permute-start.14 = (bf16[4,512,128]{2,1,0:T(8,128)(2,1)S(1)}, bf16[4,512,128]{2,1,0:T(8,128)(2,1)S(1)}, u32[]{:S(2)}, u32[]{:S(2)}) collective-permute-start(bf16[4,512,128]{2,1,0:T(8,128)(2,1)S(1)} %pad_maximum_fusion.refs_0_.refs_8_), channel_id=1, source_target_pairs={{0,4},{1,5},{2,6},{3,7},{4,0},{5,1},{6,2},{7,3},{8,12},{9,13},{10,... | collective-permute-start | bytes 1572872 | tf_op jit(solution)/shard_map/norm/ppermute | solution.py:65
  95.0 18.7 %collective-permute-start.15 = (bf16[4,512,128]{2,1,0:T(8,128)(2,1)S(1)}, bf16[4,512,128]{2,1,0:T(8,128)(2,1)S(1)}, u32[]{:S(2)}, u32[]{:S(2)}) collective-permute-start(bf16[4,512,128]{2,1,0:T(8,128)(2,1)S(1)} %pad_maximum_fusion.refs_0_.refs_8_), channel_id=1, source_target_pairs={{0,3},{1,0},{2,1},{3,2},{4,7},{5,4},{6,5},{7,6},{8,11},{9,8},{10,9... | collective-permute-start | bytes 1572872 | tf_op jit(solution)/shard_map/norm/ppermute | solution.py:61
  96.3 17.5 %collective-permute-start.16 = (bf16[4,512,128]{2,1,0:T(8,128)(2,1)S(1)}, bf16[4,512,128]{2,1,0:T(8,128)(2,1)S(1)}, u32[]{:S(2)}, u32[]{:S(2)}) collective-permute-start(bf16[4,512,128]{2,1,0:T(8,128)(2,1)S(1)} %pad_maximum_fusion.refs_0_.refs_8_), channel_id=1, source_target_pairs={{0,1},{1,2},{2,3},{3,0},{4,5},{5,6},{6,7},{7,4},{8,9},{9,10},{10,1... | collective-permute-start | bytes 1572872 | tf_op jit(solution)/shard_map/norm/ppermute | solution.py:61
  97.1 50.4 %copy-start.31 = (f32[4,128]{1,0:T(4,128)}, f32[4,128]{1,0:T(4,128)S(1)}, u32[]{:S(2)}) copy-start(f32[4,128]{1,0:T(4,128)S(1)} %add_rsqrt_fusion.refs_18_) | copy-start | bytes 6148
  97.9 15.9 %all-to-all-start.2 = ((f32[16,4,512]{2,1,0:T(4,128)}), f32[16,4,512]{2,1,0:T(4,128)S(1)}, u32[]{:S(2)}, u32[]{:S(2)}) async-start(f32[16,4,512]{2,1,0:T(4,128)} %broadcast_in_dim.56), calls=%async_computation.2 | async-start | bytes 262144 | tf_op jit(solution)/shard_map/contrast/all_to_all | solution.py:71
  113.8 55.3 %copy-start.1 = (bf16[4,512,128]{2,1,0:T(8,128)(2,1)}, bf16[4,512,128]{2,1,0:T(8,128)(2,1)S(1)}, u32[]{:S(2)}) copy-start(bf16[4,512,128]{2,1,0:T(8,128)(2,1)S(1)} %collective-permute-done.14.refs_1_.refs_9_) | copy-start | bytes 1572868
  113.8 55.3 %copy-start.2 = (bf16[4,512,128]{2,1,0:T(8,128)(2,1)}, bf16[4,512,128]{2,1,0:T(8,128)(2,1)S(1)}, u32[]{:S(2)}) copy-start(bf16[4,512,128]{2,1,0:T(8,128)(2,1)S(1)} %collective-permute-done.15.refs_2_.refs_10_) | copy-start | bytes 1572868
  113.8 55.3 %copy-start.3 = (bf16[4,512,128]{2,1,0:T(8,128)(2,1)}, bf16[4,512,128]{2,1,0:T(8,128)(2,1)S(1)}, u32[]{:S(2)}) copy-start(bf16[4,512,128]{2,1,0:T(8,128)(2,1)S(1)} %collective-permute-done.16.refs_3_.refs_11_) | copy-start | bytes 1572868
  113.8 22.2 %collective-permute-start.18 = (bf16[4,512,128]{2,1,0:T(8,128)(2,1)S(1)}, bf16[4,512,128]{2,1,0:T(8,128)(2,1)S(1)}, u32[]{:S(2)}, u32[]{:S(2)}) collective-permute-start(bf16[4,512,128]{2,1,0:T(8,128)(2,1)S(1)} %collective-permute-done.16.refs_3_.refs_11_), channel_id=1, source_target_pairs={{0,4},{1,5},{2,6},{3,7},{4,0},{5,1},{6,2},{7,3},{8,12},{9,13},{10,... | collective-permute-start | bytes 1572872 | tf_op jit(solution)/shard_map/contrast/ppermute | solution.py:65
  114.7 21.3 %collective-permute-start.19 = (bf16[4,512,128]{2,1,0:T(8,128)(2,1)S(1)}, bf16[4,512,128]{2,1,0:T(8,128)(2,1)S(1)}, u32[]{:S(2)}, u32[]{:S(2)}) collective-permute-start(bf16[4,512,128]{2,1,0:T(8,128)(2,1)S(1)} %collective-permute-done.16.refs_3_.refs_11_), channel_id=1, source_target_pairs={{0,1},{1,2},{2,3},{3,0},{4,5},{5,6},{6,7},{7,4},{8,9},{9,10},{10,1... | collective-permute-start | bytes 1572872 | tf_op jit(solution)/shard_map/contrast/ppermute | solution.py:61
  115.5 20.6 %collective-permute-start.17 = (bf16[4,512,128]{2,1,0:T(8,128)(2,1)S(1)}, bf16[4,512,128]{2,1,0:T(8,128)(2,1)}, u32[]{:S(2)}, u32[]{:S(2)}) collective-permute-start(bf16[4,512,128]{2,1,0:T(8,128)(2,1)S(1)} %collective-permute-done.14.refs_1_.refs_9_), channel_id=1, source_target_pairs={{0,3},{1,0},{2,1},{3,2},{4,7},{5,4},{6,5},{7,6},{8,11},{9,8},{10,9... | collective-permute-start | bytes 1572872 | tf_op jit(solution)/shard_map/contrast/ppermute | solution.py:61
  122.1 14.0 %all-to-all-start.3 = ((f32[8,2,64,128]{3,2,1,0:T(8,128)}), f32[8,2,64,128]{3,2,1,0:T(8,128)}, u32[]{:S(2)}, u32[]{:S(2)}) async-start(f32[8,2,64,128]{3,2,1,0:T(8,128)} %broadcast_in_dim.57), calls=%async_computation.3 | async-start | bytes 1048576 | tf_op jit(solution)/shard_map/contrast/all_to_all | solution.py:71
  136.0 38.2 %copy-start.4 = (bf16[4,512,128]{2,1,0:T(8,128)(2,1)}, bf16[4,512,128]{2,1,0:T(8,128)(2,1)S(1)}, u32[]{:S(2)}) copy-start(bf16[4,512,128]{2,1,0:T(8,128)(2,1)S(1)} %collective-permute-done.18.refs_6_.refs_14_) | copy-start | bytes 1572868
  136.1 38.2 %copy-start.5 = (bf16[4,512,128]{2,1,0:T(8,128)(2,1)}, bf16[4,512,128]{2,1,0:T(8,128)(2,1)S(1)}, u32[]{:S(2)}) copy-start(bf16[4,512,128]{2,1,0:T(8,128)(2,1)S(1)} %collective-permute-done.19.refs_4_.refs_12_) | copy-start | bytes 1572868
  136.1 15.1 %collective-permute-start.23 = (bf16[4,512,128]{2,1,0:T(8,128)(2,1)}, bf16[4,512,128]{2,1,0:T(8,128)(2,1)S(1)}, u32[]{:S(2)}, u32[]{:S(2)}) collective-permute-start(bf16[4,512,128]{2,1,0:T(8,128)(2,1)} %collective-permute-done.17.refs_5_.refs_13_), channel_id=1, source_target_pairs={{0,3},{1,0},{2,1},{3,2},{4,7},{5,4},{6,5},{7,6},{8,11},{9,8},{10,9... | collective-permute-start | bytes 1572872 | tf_op jit(solution)/shard_map/contrast/ppermute | solution.py:61
  141.7 32.5 %copy-start.7 = (f32[8,64,128]{2,1,0:T(8,128)}, f32[8,64,128]{2,1,0:T(8,128)S(1)}, u32[]{:S(2)}) copy-start(f32[8,64,128]{2,1,0:T(8,128)S(1)} %get-tuple-element.132.refs_8_.refs_16_) | copy-start | bytes 786436
  144.2 14.8 %collective-permute-start.20 = (bf16[3,528,128]{2,1,0:T(8,128)(2,1)S(1)}, bf16[3,528,128]{2,1,0:T(8,128)(2,1)S(1)}, u32[]{:S(2)}, u32[]{:S(2)}) collective-permute-start(bf16[3,528,128]{2,1,0:T(8,128)(2,1)S(1)} %fusion.10.refs_0_), channel_id=1, source_target_pairs={{0,4},{1,5},{2,6},{3,7},{4,0},{5,1},{6,2},{7,3},{8,12},{9,13},{10,... | collective-permute-start | bytes 1216520 | tf_op jit(solution)/shard_map/row_gather/ppermute | solution.py:65
  145.4 13.6 %collective-permute-start.21 = (bf16[3,528,128]{2,1,0:T(8,128)(2,1)S(1)}, bf16[3,528,128]{2,1,0:T(8,128)(2,1)S(1)}, u32[]{:S(2)}, u32[]{:S(2)}) collective-permute-start(bf16[3,528,128]{2,1,0:T(8,128)(2,1)S(1)} %fusion.10.refs_0_), channel_id=1, source_target_pairs={{0,3},{1,0},{2,1},{3,2},{4,7},{5,4},{6,5},{7,6},{8,11},{9,8},{10,9... | collective-permute-start | bytes 1216520 | tf_op jit(solution)/shard_map/row_gather/ppermute | solution.py:61
  145.4 13.6 %collective-permute-start.22 = (bf16[3,528,128]{2,1,0:T(8,128)(2,1)S(1)}, bf16[3,528,128]{2,1,0:T(8,128)(2,1)S(1)}, u32[]{:S(2)}, u32[]{:S(2)}) collective-permute-start(bf16[3,528,128]{2,1,0:T(8,128)(2,1)S(1)} %fusion.10.refs_0_), channel_id=1, source_target_pairs={{0,1},{1,2},{2,3},{3,0},{4,5},{5,6},{6,7},{7,4},{8,9},{9,10},{10,1... | collective-permute-start | bytes 1216520 | tf_op jit(solution)/shard_map/row_gather/ppermute | solution.py:61
  155.2 3.8 %collective-permute-start.24 = (f32[8,4,128]{2,1,0:T(4,128)S(1)}, f32[8,4,128]{2,1,0:T(4,128)S(1)}, u32[]{:S(2)}, u32[]{:S(2)}) collective-permute-start(f32[8,4,128]{2,1,0:T(4,128)S(1)} %pad_maximum_fusion.1), channel_id=1, source_target_pairs={{0,32},{8,40},{16,48},{24,56},{32,0},{40,8},{48,16},{56,24},{64,96... | collective-permute-start | bytes 49160 | tf_op jit(solution)/shard_map/along/ppermute | solution.py:548
  159.1 15.2 %collective-permute-start.25 = (bf16[3,528,128]{2,1,0:T(8,128)(2,1)S(1)}, bf16[3,528,128]{2,1,0:T(8,128)(2,1)S(1)}, u32[]{:S(2)}, u32[]{:S(2)}) collective-permute-start(bf16[3,528,128]{2,1,0:T(8,128)(2,1)S(1)} %collective-permute-done.20.refs_1_), channel_id=1, source_target_pairs={{0,3},{1,0},{2,1},{3,2},{4,7},{5,4},{6,5},{7,6},{8,11},{9,8},{10,9... | collective-permute-start | bytes 1216520 | tf_op jit(solution)/shard_map/along/ppermute | solution.py:61
  162.6 11.7 %collective-permute-start.26 = (bf16[3,528,128]{2,1,0:T(8,128)(2,1)S(1)}, bf16[3,528,128]{2,1,0:T(8,128)(2,1)S(1)}, u32[]{:S(2)}, u32[]{:S(2)}) collective-permute-start(bf16[3,528,128]{2,1,0:T(8,128)(2,1)S(1)} %collective-permute-done.22.refs_3_), channel_id=1, source_target_pairs={{0,4},{1,5},{2,6},{3,7},{4,0},{5,1},{6,2},{7,3},{8,12},{9,13},{10,... | collective-permute-start | bytes 1216520 | tf_op jit(solution)/shard_map/along/ppermute | solution.py:65
  163.8 10.6 %collective-permute-start.27 = (bf16[3,528,128]{2,1,0:T(8,128)(2,1)S(1)}, bf16[3,528,128]{2,1,0:T(8,128)(2,1)S(1)}, u32[]{:S(2)}, u32[]{:S(2)}) collective-permute-start(bf16[3,528,128]{2,1,0:T(8,128)(2,1)S(1)} %collective-permute-done.22.refs_3_), channel_id=1, source_target_pairs={{0,1},{1,2},{2,3},{3,0},{4,5},{5,6},{6,7},{7,4},{8,9},{9,10},{10,1... | collective-permute-start | bytes 1216520 | tf_op jit(solution)/shard_map/along/ppermute | solution.py:61
  163.8 5.2 %collective-permute-start.28 = (f32[8,4,128]{2,1,0:T(4,128)S(1)}, f32[8,4,128]{2,1,0:T(4,128)S(1)}, u32[]{:S(2)}, u32[]{:S(2)}) collective-permute-start(f32[8,4,128]{2,1,0:T(4,128)S(1)} %fusion.16), channel_id=1, source_target_pairs={{0,64},{8,72},{16,80},{24,88},{32,96},{40,104},{48,112},{56,120},{... | collective-permute-start | bytes 49160 | tf_op jit(solution)/shard_map/along/ppermute | solution.py:551
  181.5 4.1 %collective-permute-start.29 = (f32[1792,256]{1,0:T(8,128)S(1)}, f32[1792,256]{1,0:T(8,128)S(1)}, u32[]{:S(2)}, u32[]{:S(2)}) collective-permute-start(f32[1792,256]{1,0:T(8,128)S(1)} %fusion.4), channel_id=1, source_target_pairs={{0,8},{8,0},{16,24},{24,16},{32,40},{40,32},{48,56},{56,48},{64,72... | collective-permute-start | bytes 5505032 | tf_op jit(solution)/shard_map/down_grad/ppermute | solution.py:57
  191.2 5.0 %collective-permute-start.32 = (f32[1792,256]{1,0:T(8,128)}, f32[1792,256]{1,0:T(8,128)}, u32[]{:S(2)}, u32[]{:S(2)}) collective-permute-start(f32[1792,256]{1,0:T(8,128)} %fusion.18), channel_id=1, source_target_pairs={{0,8},{8,0},{16,24},{24,16},{32,40},{40,32},{48,56},{56,48},{64,72... | collective-permute-start | bytes 5505032 | tf_op jit(solution)/shard_map/down_grad/ppermute | solution.py:57
  191.3 31.8 %collective-permute-start.30 = (bf16[1792,256]{1,0:T(8,128)(2,1)S(1)}, bf16[1792,256]{1,0:T(8,128)(2,1)S(1)}, u32[]{:S(2)}, u32[]{:S(2)}) collective-permute-start(bf16[1792,256]{1,0:T(8,128)(2,1)S(1)} %fusion), channel_id=1, source_target_pairs={{0,16},{8,24},{16,0},{24,8},{32,48},{40,56},{48,32},{56,40},{64,80... | collective-permute-start | bytes 2752520 | tf_op jit(solution)/shard_map/down_grad/ppermute | solution.py:53
  193.0 12.1 %collective-permute-start.31 = (bf16[3,528,128]{2,1,0:T(8,128)(2,1)S(1)}, bf16[3,528,128]{2,1,0:T(8,128)(2,1)S(1)}, u32[]{:S(2)}, u32[]{:S(2)}) collective-permute-start(bf16[3,528,128]{2,1,0:T(8,128)(2,1)S(1)} %copy-done.27), channel_id=1, source_target_pairs={{0,3},{1,0},{2,1},{3,2},{4,7},{5,4},{6,5},{7,6},{8,11},{9,8},{10,9... | collective-permute-start | bytes 1216520 | tf_op jit(solution)/shard_map/down_grad/ppermute | solution.py:61
  (24 other events, 241.0 us)

commit v6 on v5

--- a/solution.py
+++ b/solution.py
@@ -114,13 +114,25 @@
     )(jnp.stack([zl] + columns).astype(jnp.int32), hidden, weight)
 
 
+def pair_picks(seqs):
+    rows = lax.broadcasted_iota(jnp.int32, (seqs // 2, seqs), 0)
+    cols = lax.broadcasted_iota(jnp.int32, (seqs // 2, seqs), 1)
+    return (cols == 2 * rows).astype(f32), (cols == 2 * rows + 1).astype(f32)
+
+
+def exact_dot(left, right, contract):
+    return lax.dot_general(left, right, (contract, ((), ())), precision=highest, preferred_element_type=f32)
+
+
 def gram_kernel(plan_ref, mean_ref, gain_ref, strip_ref, out_ref):
+    seqs, width = mean_ref.shape
     pooled = mean_ref[...] * gain_ref[...]
-    gram = lax.dot_general(
-        pooled, pooled, (((1,), (1,)), ((), ())), precision=highest, preferred_element_type=f32
-    )
-    out_ref[0] = jnp.concatenate([gram, jnp.zeros_like(gram)], axis=1)
-    out_ref[1] = strip_ref[...]
+    queries, passages = [exact_dot(pick, pooled, ((1,), (0,))) for pick in pair_picks(seqs)]
+    dots = exact_dot(queries, passages, ((1,), (1,)))
+    squares = exact_dot(jnp.ones((8, width), f32), pooled * pooled, ((1,), (1,)))
+    out_ref[:seqs, :] = strip_ref[...]
+    out_ref[seqs : seqs + 8, :] = jnp.concatenate([dots[8 * i : 8 * i + 8] for i in range(4)], axis=1)
+    out_ref[seqs + 8 :, :] = jnp.concatenate([squares, jnp.zeros_like(squares)], axis=1)
 
 
 def gram_part(means, gain, x):
@@ -136,9 +148,9 @@
                 pl.BlockSpec((1, width), lambda i, s: (0, 0)),
                 pl.BlockSpec((seqs, lanes), lambda i, s: (0, s[0])),
             ],
-            out_specs=pl.BlockSpec((2, seqs, lanes), lambda i, s: (0, 0, 0)),
-        ),
-        out_shape=jax.ShapeDtypeStruct((2, seqs, lanes), f32),
+            out_specs=pl.BlockSpec((seqs + 16, lanes), lambda i, s: (0, 0)),
+        ),
+        out_shape=jax.ShapeDtypeStruct((seqs + 16, lanes), f32),
         compiler_params=pltpu.CompilerParams(vmem_limit_bytes=16 * MIB),
         cost_estimate=QUICK,
     )(x.astype(jnp.int32).reshape(1), means, gain, means)
@@ -151,13 +163,16 @@
     seqs = mean_ref.shape[0]
     rows = lax.broadcasted_iota(jnp.int32, (seqs, seqs), 0)
     cols = lax.broadcasted_iota(jnp.int32, (seqs, seqs), 1)
-    gram = part_ref[0, 0]
+    total = part_ref[0, seqs:, :]
     for r in range(1, group):
-        gram += part_ref[r, 0]
-    gram = gram[:, :seqs]
-    diagonal = jnp.where(rows == cols, gram, 0.0)
-    norm_col = jnp.sqrt(jnp.sum(diagonal, axis=1, keepdims=True) + eps_embed)
-    norm_row = jnp.sqrt(jnp.sum(diagonal, axis=0, keepdims=True) + eps_embed)
+        total += part_ref[r, seqs:, :]
+    half = seqs // 2
+    dots = jnp.concatenate([total[:8, half * i : half * (i + 1)] for i in range(4)], axis=0)
+    pick_query, pick_passage = pair_picks(seqs)
+    gram = exact_dot(pick_query, exact_dot(dots, pick_passage, ((1,), (0,))), ((0,), (0,)))
+    gram = gram + gram.T
+    norm_row = jnp.sqrt(total[8:9, :seqs] + eps_embed)
+    norm_col = row_to_column(norm_row)
     norms = norm_col * norm_row
     scores = score_scale * gram / norms
     query = rows % 2 == 0
@@ -175,7 +190,7 @@
     gain_grad_ref[...] = jnp.sum(d_pooled * mean, axis=0, keepdims=True)
     own_ref[...] = d_pooled * gain * (1.0 / SEQ)
     for place in range(group):
-        part = part_ref[(place % NZL) * NY + place // NZL, 1]
+        part = part_ref[(place % NZL) * NY + place // NZL, :seqs, :]
         gain = gain_block_ref[0, place : place + 1, :]
         d_pooled = jnp.dot(mix, part * gain, precision=highest, preferred_element_type=f32)
         block_ref[place] = d_pooled * gain * (1.0 / SEQ)
@@ -183,8 +198,8 @@
 
 
 def contrast(parts, same, gain_blocks, means, gain, x):
-    group, _, seqs, lanes = parts.shape
-    width = means.shape[1]
+    group, _, lanes = parts.shape
+    seqs, width = means.shape
     whole = lambda shape: pl.BlockSpec(shape, lambda i, s: (0,) * len(shape))
     return pl.pallas_call(
         contrast_kernel,
@@ -223,31 +238,55 @@
     return jnp.sum(jnp.where(eye, jnp.broadcast_to(column, (n, n)), 0.0), axis=0, keepdims=True)
 
 
+def strip_reader(refs):
+    *refs, last = refs
+    first_half = pl.program_id(0) < NX // 2
+
+    def read(i, rows):
+        value = refs[i][0, rows, :]
+        if i == len(refs) - 1:
+            value = jnp.where(first_half, value, last[0, rows, :])
+        return value.astype(f32)
+
+    return read
+
+
+def strip_specs(strips):
+    _, tokens, lanes = strips[0].shape
+    half = NX // 2
+    block = (1, tokens, lanes)
+    return [pl.BlockSpec(block, lambda i, s: (i, 0, 0))] * (len(strips) - 2) + [
+        pl.BlockSpec(block, lambda i, s: (jnp.minimum(i, half - 1), 0, 0)),
+        pl.BlockSpec(block, lambda i, s: (jnp.maximum(i - half, 0), 0, 0)),
+    ]
+
+
 def along_kernel(plan_ref, *refs):
     *layer_refs, scaled_ref, out_ref = refs
     tokens = layer_refs[0].shape[1]
+    group = len(layer_refs) - 1
+    read = strip_reader(layer_refs)
     first = plan_ref[pl.program_id(0)]
     for s in range(tokens // SEQ):
         rows = slice(s * SEQ, (s + 1) * SEQ)
         along = None
-        for i, ref in enumerate(layer_refs):
+        for i in range(group):
             scaled = scaled_ref[plan_ref[NX + i], pl.ds(first + s, 1), :]
-            term = ref[0, rows, :].astype(f32) * scaled
+            term = read(i, rows) * scaled
             along = term if along is None else along + term
         out_ref[0, s : s + 1, :] = column_to_row(jnp.sum(along, axis=1, keepdims=True))
 
 
 def along_part(strips, scaled, plan):
     _, tokens, lanes = strips[0].shape
-    group = len(strips)
+    group = len(strips) - 1
     seqs_here = tokens // SEQ
     return pl.pallas_call(
         along_kernel,
         grid_spec=pltpu.PrefetchScalarGridSpec(
             num_scalar_prefetch=1,
             grid=(NX,),
-            in_specs=[pl.BlockSpec((1, tokens, lanes), lambda i, s: (i, 0, 0))] * group
-            + [pl.BlockSpec(scaled.shape, lambda i, s: (0, 0, 0))],
+            in_specs=strip_specs(strips) + [pl.BlockSpec(scaled.shape, lambda i, s: (0, 0, 0))],
             out_specs=pl.BlockSpec((1, seqs_here, SEQ), lambda i, s: (s[NX + 3 * group + i], 0, 0)),
         ),
         out_shape=jax.ShapeDtypeStruct((NX, seqs_here, SEQ), f32),
@@ -259,7 +298,8 @@
 def group_grad_kernel(plan_ref, *refs):
     *layer_refs, scaled_ref, sum_ref, low_ref, coef_ref, factor_ref = refs
     _, tokens, lanes = layer_refs[0].shape
-    group = len(layer_refs)
+    group = len(layer_refs) - 1
+    read = strip_reader(layer_refs)
     seqs_here = tokens // SEQ
     here = pl.program_id(0)
     first = plan_ref[here]
@@ -279,16 +319,16 @@
         rows = slice(s * SEQ, (s + 1) * SEQ)
         inverse = row_to_column(factor_ref[here, s : s + 1, :])
         coef = row_to_column(factor_ref[here, seqs_here + s : seqs_here + s + 1, :])
-        for i, ref in enumerate(layer_refs):
+        for i in range(group):
             scaled = scaled_ref[plan_ref[NX + i], pl.ds(first + s, 1), :]
-            low = inverse * scaled - ref[0, rows, :].astype(f32) * coef
+            low = inverse * scaled - read(i, rows) * coef
             side = pl.ds(pl.multiple_of(plan_ref[NX + 2 * group + i], lanes), lanes)
             low_ref[plan_ref[NX + group + i], rows, side] = low.astype(bf16)
 
 
 def group_grad(strips, scaled, sums, plan):
     _, tokens, lanes = strips[0].shape
-    group = len(strips)
+    group = len(strips) - 1
     quarter = group * lanes // 4
     seqs_here = tokens // SEQ
     return pl.pallas_call(
@@ -296,7 +336,7 @@
         grid_spec=pltpu.PrefetchScalarGridSpec(
             num_scalar_prefetch=1,
             grid=(NX,),
-            in_specs=[pl.BlockSpec((1, tokens, lanes), lambda i, s: (i, 0, 0))] * group
+            in_specs=strip_specs(strips)
             + [pl.BlockSpec(scaled.shape, lambda i, s: (0, 0, 0))]
             + [pl.BlockSpec(sums.shape, lambda i, s: (0, 0, 0))],
             out_specs=[
@@ -321,6 +361,7 @@
     tokens = out_ref.shape[0]
     seqs_here = tokens // SEQ
     group = len(refs) // 2
+    row_refs, rest_ref, strip_refs = refs[:group], refs[group], refs[group + 1 :]
     others, _, lanes = refs[0].shape
     width = resid_ref.shape[1]
     x, first = plan_ref[1], plan_ref[2]
@@ -333,19 +374,24 @@
         ]
         for i in range(group):
             place = plan_ref[3 + i]
-            row_ref, strip_ref = refs[i], refs[group + i]
+            row_ref, strip_ref = row_refs[i], strip_refs[i]
+            last = i == group - 1
+            tail_ref, tail_start = (rest_ref, tokens // 2) if last else (row_ref, tokens)
             for j in range(others + 1):
                 block = lax.rem(x + j, others + 1)
                 column = pl.ds(pl.multiple_of((block * group + place) * lanes, lanes), lanes)
                 if j:
-                    tail = row_ref[j - 1, tokens:, :].astype(f32)
+                    tail = tail_ref[j - 1, tail_start:, :].astype(f32)
                     tail = tail[:8] + tail[8:]
                     gains_ref[place, pl.ds(block, 1), :] = tail[seqs_here : seqs_here + 1]
                 else:
                     gains_ref[place, pl.ds(block, 1), :] = block_gain_ref[pl.ds(place, 1), :]
                 for s in range(seqs_here):
                     rows = slice(s * SEQ, (s + 1) * SEQ)
-                    if j:
+                    if j and last and 2 * s >= seqs_here:
+                        rest = slice(rows.start - tokens // 2, rows.stop - tokens // 2)
+                        layer, scaled = rest_ref[j - 1, rest, :], tail[s : s + 1]
+                    elif j:
                         layer, scaled = row_ref[j - 1, rows, :], tail[s : s + 1]
                     else:
                         layer, scaled = strip_ref[0, rows, :], scaled_ref[place, pl.ds(first + s, 1), :]
@@ -363,7 +409,7 @@
 
 def hidden_grad(rows, strips, scaled, block_gain, inverse, coef, weight, plan):
     others, height, lanes = rows[0].shape
-    group = len(rows)
+    group = len(strips)
     seqs_here = inverse.shape[0]
     tokens = seqs_here * SEQ
     units, model_width = weight.shape
@@ -375,7 +421,7 @@
         grid_spec=pltpu.PrefetchScalarGridSpec(
             num_scalar_prefetch=1,
             grid=(GRAD_STEPS,),
-            in_specs=[whole(rows[0].shape)] * group
+            in_specs=[whole(row.shape) for row in rows]
             + [whole((1, tokens, lanes))] * group
             + [whole(v.shape) for v in (scaled, block_gain, inverse, coef)]
             + [pl.BlockSpec((chunk, model_width), lambda i, s: (i, 0))],
@@ -420,9 +466,10 @@
     return got
 
 
-def gather_last(got):
+def gather_last(got, cut):
     got = dict(got)
-    got[1, 2] = over_y(got[1, 1], -1)
+    got[1, 2] = over_y(got[1, 1][:, :cut], -1)
+    got["rest"] = over_y(got[1, 3][:, cut:], 1)
     return got
 
 
@@ -465,6 +512,7 @@
     with jax.named_scope("hidden_exchange"):
         hidden_left = over_x(hidden, 1)
         hidden_right = over_x(hidden, -1)
+        hidden_far = over_x(hidden, 2)
 
     with jax.named_scope("resid_exchange"):
         pieces = resid.reshape(tokens, 2, NZL, lanes).transpose(2, 1, 0, 3)[:, None]
@@ -485,19 +533,15 @@
 
         from_12 = over_y(term[1, 2], -1)
         from_11 = over_y(term[1, 1], 1)
+        from_02 = over_y(term[0, 2], 1)
         from_12, from_11, hidden_left, hidden_right = tie(from_12, from_11, hidden_left, hidden_right)
-        hidden_far = (
-            over_x(hidden_left[: tokens // 2], 1),
-            over_x(hidden_right[tokens // 2 :], -1),
-        )
         from_13 = over_zl(add(term[1, 3], from_12).astype(bf16))
-        from_02 = over_y(term[0, 2], -1)
-        from_01 = over_y(term[0, 1], 1)
         own_other = add(term[1, 0], from_11).astype(bf16)
         from_13, from_02 = tie(from_13, from_02)
-        from_03 = over_y(add(term[0, 3], from_13, from_02).astype(bf16), -1)
+        from_03 = over_y(add(term[0, 3], from_13).astype(bf16), -1)
+        from_01 = over_y(add(term[0, 1], from_02).astype(bf16), 1)
         from_10 = over_zl(own_other)
-        from_03, from_10, from_01, *hidden_far = tie(from_03, from_10, from_01, *hidden_far)
+        from_03, from_10, from_01 = tie(from_03, from_10, from_01)
         resid_strips = lax.dynamic_slice_in_dim(pieces, y // 2, 1, 1)[:, 0]
         layer = add(term[0, 0], resid_strips, from_01, from_03, from_10)
 
@@ -512,8 +556,8 @@
     with jax.named_scope("norm"):
         squares = jnp.sum(layer * layer, axis=(0, 2)).reshape(seqs_here, SEQ)
         squares = jnp.sum(gather_small(squares, "tensor"), axis=0)
-        message, squares = tie(message, squares)
-        hidden_rows = jnp.concatenate([hidden, hidden_left, hidden_right] + hidden_far, axis=0)
+        message, squares, hidden_far = tie(message, squares, hidden_far)
+        hidden_rows = jnp.concatenate([hidden, hidden_left, hidden_right, hidden_far], axis=0)
         got = gather_start(message)
         inverse = lax.rsqrt(squares / model_width + eps_norm)
         weighted = layer.reshape(NX, seqs_here, SEQ, lanes) * inverse[None, :, :, None]
@@ -526,8 +570,9 @@
         means_all = means_all.reshape(seqs, width)
         parts = gather_small(gram_part(means_all, gain_own, x), "tensor")
         got, parts, low_layer, hidden_rows = tie_gather(got, parts, low_layer, hidden_rows)
-        got = gather_last(got)
-        strips = [got[key] for key in KEYS]
+        half = NX // 2
+        got[1, 2] = over_y(got[1, 1][:half], -1)
+        strips = [got[key] for key in KEYS] + [over_y(got[1, 3][half:], 1)]
         scaled, gain_grad_x, scaled_own, gain_grad = contrast(
             parts, same, gain_blocks, means_all, gain_own, x
         )
@@ -553,25 +598,27 @@
     with jax.named_scope("down_grad"):
         low_x, coef = group_grad(strips, scaled, sums, plan)
         rows, low_x = tie_gather(rows, low_x)
-        rows = gather_last(rows)
+        rows = gather_last(rows, tokens // 2)
 
         def down(low):
             return lax.dot_general(
                 hidden_rows, low, (((0,), (0,)), ((), ())), preferred_element_type=f32
             )
 
-        from_core = over_core(down(low_x[3]))
-        summed = (down(low_x[2]) + from_core).astype(bf16)
-        summed, low0, low1 = tie(summed, low_x[0], low_x[1])
+        part3, low_x = tie(down(low_x[3]), low_x)
+        part1, low_x = tie(down(low_x[1]), low_x)
+        from_core = over_core(part3), over_core(part1)
+        summed = (down(low_x[2]) + from_core[0]).astype(bf16)
+        summed, low0 = tie(summed, low_x[0])
         across = over_zh(summed)
-        near1 = down(low1)
-        near = down(low0) + over_core(near1)
+        rows, low0 = tie_gather(rows, low0)
+        near = down(low0) + from_core[1]
 
     with jax.named_scope("hidden_grad"):
         rows, near = tie_gather(rows, near)
-        rows = [rows[key] for key in KEYS]
+        rows = [rows[key] for key in KEYS + ("rest",)]
         grad_hidden, grad_resid, gain_grad = hidden_grad(
-            rows, strips, scaled, gain_grad_x, inverse, coef, down_weight, [rank, x, shard * seqs_here] + places
+            rows, strips[:group], scaled, gain_grad_x, inverse, coef, down_weight, [rank, x, shard * seqs_here] + places
         )
         grad_gain = gain_grad.reshape(width)
 

time: 226 us -> 215 us (0.951)
  local copies, waits for them, and re-layouts: 28.9 us -> 9.77 us
  other arithmetic: 9.7 us -> 23.8 us
  starting transfers between devices: 67.6 us -> 62.8 us
  matrix products: 16.9 us -> 14.5 us
    unnamed x74 -> x62, local copies, waits for them, and re-layouts: 16.7 us -> 2.95 us
    concatenate x0 -> x1, other arithmetic: none -> 11 us  [per_device(): jnp.concatenate([hidden, hidden_left, hidden_right, hidden_far], axis=0)]
    ppermute x15 -> x17, waiting for transfers between devices: 17.2 us -> 27 us  [over_y(): return lax.ppermute(value, 'tensor', tensor_route(0, step))]
    ppermute x7 -> x6, waiting for transfers between devices: 7.49 us -> 0.46 us  [over_x(): return lax.ppermute(value, 'dp', dp_route(step, 0, 0))]
    ppermute x15 -> x17, starting transfers between devices: 26.5 us -> 22.1 us  [over_y(): return lax.ppermute(value, 'tensor', tensor_route(0, step))]
    ppermute x6, waiting for transfers between devices: 6.63 us -> 11 us  [over_zl(): return lax.ppermute(value, 'tensor', tensor_route(1, 0))]
    ppermute x2, waiting for transfers between devices: 3.63 us -> 0.01 us  [over_core(): return lax.ppermute(value, 'dp', dp_route(0, 0, 1))]
    all_to_all x3, waiting for transfers between devices: 16.2 us -> 12.9 us  [gather_small(): return lax.all_to_all(copies, axis, 0, 0)]
  transfers between devices with their start and end apart: 37 -> 38, of which waited for: 17 -> 16; matrix products, arithmetic and copies ran while one was open for 15% -> 19% of each run, Pallas kernels for 18% -> 19%
where the time goes in v6:
time: 215 us; the launch traced here: 214 us
  starting transfers between devices  62.8 us (29%)
  waiting for transfers between devices  59.9 us (28%)
  Pallas kernels  41.4 us (19%)
  other arithmetic  23.8 us (11%)
  matrix products  14.5 us (7%)
  local copies, waits for them, and re-layouts  9.77 us (5%)
    ppermute x17, waiting for transfers between devices, over_y(): return lax.ppermute(value, 'tensor', tensor_route(0, step))  27 us
    ppermute x17, starting transfers between devices, over_y(): return lax.ppermute(value, 'tensor', tensor_route(0, step))  22.1 us
    pallas_call x1, Pallas kernels, hidden_grad(): pl.pallas_call(hidden_grad_kernel, grid_spec=pltpu.PrefetchScalarGridSpec...  17.3 us
    dot_general x4, matrix products, down(): lax.dot_general(hidden_rows, low, (((0,), (0,)), ((), ())), preferred_ele...  14.5 us
    all_to_all x3, starting transfers between devices, gather_small(): return lax.all_to_all(copies, axis, 0, 0)  14.4 us
    pallas_call x1, Pallas kernels, layer_dot(): pl.pallas_call(layer_dot_kernel, grid_spec=pltpu.PrefetchScalarGridSpec(n...  13.4 us
    all_to_all x3, waiting for transfers between devices, gather_small(): return lax.all_to_all(copies, axis, 0, 0)  12.9 us
    concatenate x1, other arithmetic, per_device(): jnp.concatenate([hidden, hidden_left, hidden_right, hidden_far], axis=0)  11 us
  transfers between devices with their start and end apart: 38, of which 16 were waited for; matrix products, arithmetic and copies ran while one was open for 19% of the time, Pallas kernels for 19%

profile of v6, /device:TPU:0, one launch (start us, length us, event | category | flops | bytes accessed | tf_op | source)
XLA Modules:
  0.0 214.1 jit_solution(4926295290693451787)
XLA Ops:
  0.6 1.6 collective-permute-start.2
  2.3 1.7 collective-permute-start.3
  3.9 1.2 reshape.60
  6.3 5.9 %all-to-all-start = ((bf16[8,512,128]{2,1,0:T(8,128)(2,1)}), bf16[8,512,128]{2,1,0:T(8,128)(2,1)S(1)}, u32[]{:S(2)}, u32[]{:S(2)}) async-start(bf16[8,512,128]{2,1,0:T(8,128)(2,1)} %bitcast.6), calls=%async_computation | async-start | bytes 2097152 | tf_op jit(solution)/shard_map/resid_exchange/all_to_all | solution.py:520
  12.9 13.4 %layer_sum.1 = (bf16[4,512,128]{2,1,0:T(8,128)(2,1)}, bf16[4,512,128]{2,1,0:T(8,128)(2,1)}, bf16[4,512,128]{2,1,0:T(8,128)(2,1)}, bf16[4,512,128]{2,1,0:T(8,128)...) custom-call(s32[5]{0:T(128)} %stack.140.plan_ref, ...), custom_call_target="tpu_custom_call" | custom-call | flops 7516192768 | bytes 20709376 | tf_op jit(solution)/shard_map/layer_sum/pallas_call | solution.py:93
  27.3 2.2 %collective-permute-start = (bf16[4,512,128]{2,1,0:T(8,128)(2,1)}, bf16[4,512,128]{2,1,0:T(8,128)(2,1)S(1)}, u32[]{:S(2)}, u32[]{:S(2)}) collective-permute-start(bf16[4,512,128]{2,1,0:T(8,128)(2,1)} %get-tuple-element.110), channel_id=1, source_target_pairs={{0,3},{1,0},{2,1},{3,2},{4,7},{5,4},{6,5},{7,6},{8,11},{9,8},{10,9... | collective-permute-start | bytes 1572872 | tf_op jit(solution)/shard_map/layer_sum/ppermute | solution.py:61
  30.4 10.7 %collective-permute-done = bf16[4,512,128]{2,1,0:T(8,128)(2,1)S(1)} collective-permute-done((bf16[4,512,128]{2,1,0:T(8,128)(2,1)}, bf16[4,512,128]{2,1,0:T(8,128)(2,1)S(1)}, u32[]{:S(2)}, u32[]{:S(2)}) %collective-permute-start) | collective-permute-done | bytes 524320 | tf_op jit(solution)/shard_map/layer_sum/ppermute | solution.py:61
  41.0 4.8 %collective-permute-done.1 = bf16[4,512,128]{2,1,0:T(8,128)(2,1)S(1)} collective-permute-done((bf16[4,512,128]{2,1,0:T(8,128)(2,1)}, bf16[4,512,128]{2,1,0:T(8,128)(2,1)S(1)}, u32[]{:S(2)}, u32[]{:S(2)}) %collective-permute-start.1) | collective-permute-done | bytes 524320 | tf_op jit(solution)/shard_map/layer_sum/ppermute | solution.py:61
  45.9 1.6 add_convert_fusion.3
  47.4 1.5 collective-permute-start.4
  49.0 1.8 collective-permute-start.12
  50.8 2.1 add_convert_fusion.1
  54.5 7.9 %collective-permute-done.4 = bf16[4,512,128]{2,1,0:T(8,128)(2,1)S(1)} collective-permute-done((bf16[4,512,128]{2,1,0:T(8,128)(2,1)S(1)}, bf16[4,512,128]{2,1,0:T(8,128)(2,1)S(1)}, u32[]{:S(2)}, u32[]{:S(2)}) %collective-permute-start.4) | collective-permute-done | bytes 524320 | tf_op jit(solution)/shard_map/layer_sum/ppermute | solution.py:65
  62.4 1.2 add_convert_fusion.2
  63.5 1.3 collective-permute-start.6
  66.8 3.1 %collective-permute-done.7 = bf16[4,512,128]{2,1,0:T(8,128)(2,1)} collective-permute-done((bf16[4,512,128]{2,1,0:T(8,128)(2,1)}, bf16[4,512,128]{2,1,0:T(8,128)(2,1)}, u32[]{:S(2)}, u32[]{:S(2)}) %collective-permute-start.7) | collective-permute-done | bytes 524320 | tf_op jit(solution)/shard_map/layer_sum/ppermute | solution.py:65
  69.9 3.0 %collective-permute-done.6 = bf16[4,512,128]{2,1,0:T(8,128)(2,1)} collective-permute-done((bf16[4,512,128]{2,1,0:T(8,128)(2,1)S(1)}, bf16[4,512,128]{2,1,0:T(8,128)(2,1)}, u32[]{:S(2)}, u32[]{:S(2)}) %collective-permute-start.6) | collective-permute-done | bytes 524320 | tf_op jit(solution)/shard_map/layer_sum/ppermute | solution.py:61
  72.9 4.1 %collective-permute-done.8 = bf16[4,512,128]{2,1,0:T(8,128)(2,1)} collective-permute-done((bf16[4,512,128]{2,1,0:T(8,128)(2,1)}, bf16[4,512,128]{2,1,0:T(8,128)(2,1)}, u32[]{:S(2)}, u32[]{:S(2)}) %collective-permute-start.8) | collective-permute-done | bytes 524320 | tf_op jit(solution)/shard_map/layer_sum/ppermute | solution.py:61
  77.0 2.1 multiply_reduce_fusion.1
  80.1 2.1 collective-permute-start.11
  82.2 1.4 collective-permute-start.10
  85.5 3.3 %all-to-all-start.1 = ((f32[8,4,128]{2,1,0:T(4,128)}), f32[8,4,128]{2,1,0:T(4,128)S(1)}, u32[]{:S(2)}, u32[]{:S(2)}) async-start(f32[8,4,128]{2,1,0:T(4,128)} %broadcast_in_dim.54), calls=%async_computation.1 | async-start | bytes 32768 | tf_op jit(solution)/shard_map/norm/all_to_all | solution.py:71
  88.9 6.0 %all-to-all-done.1 = f32[8,4,128]{2,1,0:T(4,128)S(1)} async-done(((f32[8,4,128]{2,1,0:T(4,128)}), f32[8,4,128]{2,1,0:T(4,128)S(1)}, u32[]{:S(2)}, u32[]{:S(2)}) %all-to-all-start.1) | async-done | bytes 16416 | tf_op jit(solution)/shard_map/norm/all_to_all | solution.py:71
  96.0 3.0 %collective-permute-start.14 = (bf16[4,512,128]{2,1,0:T(8,128)(2,1)S(1)}, bf16[4,512,128]{2,1,0:T(8,128)(2,1)S(1)}, u32[]{:S(2)}, u32[]{:S(2)}) collective-permute-start(bf16[4,512,128]{2,1,0:T(8,128)(2,1)S(1)} %pad_maximum_fusion.1.refs_0_.refs_9_), channel_id=1, source_target_pairs={{0,3},{1,0},{2,1},{3,2},{4,7},{5,4},{6,5},{7,6},{8,11},{9,8},{10,9... | collective-permute-start | bytes 1572872 | tf_op jit(solution)/shard_map/norm/ppermute | solution.py:61
  99.9 6.8 %all-to-all-start.2 = ((f32[16,4,512]{2,1,0:T(4,128)}), f32[16,4,512]{2,1,0:T(4,128)S(1)}, u32[]{:S(2)}, u32[]{:S(2)}) async-start(f32[16,4,512]{2,1,0:T(4,128)} %broadcast_in_dim.56), calls=%async_computation.2 | async-start | bytes 262144 | tf_op jit(solution)/shard_map/contrast/all_to_all | solution.py:71
  107.7 6.9 %all-to-all-done.2 = f32[16,4,512]{2,1,0:T(4,128)S(1)} async-done(((f32[16,4,512]{2,1,0:T(4,128)}), f32[16,4,512]{2,1,0:T(4,128)S(1)}, u32[]{:S(2)}, u32[]{:S(2)}) %all-to-all-start.2) | async-done | bytes 131104 | tf_op jit(solution)/shard_map/contrast/all_to_all | solution.py:71
  116.4 2.7 %collective-permute-start.16 = (bf16[4,512,128]{2,1,0:T(8,128)(2,1)S(1)}, bf16[4,512,128]{2,1,0:T(8,128)(2,1)S(1)}, u32[]{:S(2)}, u32[]{:S(2)}) collective-permute-start(bf16[4,512,128]{2,1,0:T(8,128)(2,1)S(1)} %collective-permute-done.13.refs_1_.refs_10_), channel_id=1, source_target_pairs={{0,3},{1,0},{2,1},{3,2},{4,7},{5,4},{6,5},{7,6},{8,11},{9,8},{10,9... | collective-permute-start | bytes 1572872 | tf_op jit(solution)/shard_map/contrast/ppermute | solution.py:61
  120.4 4.3 %all-to-all-start.3 = ((f32[8,80,128]{2,1,0:T(8,128)}), f32[8,80,128]{2,1,0:T(8,128)}, u32[]{:S(2)}, u32[]{:S(2)}) async-start(f32[8,80,128]{2,1,0:T(8,128)} %broadcast_in_dim.57), calls=%async_computation.3 | async-start | bytes 655360 | tf_op jit(solution)/shard_map/contrast/all_to_all | solution.py:71
  124.6 11.0 %pad_maximum_fusion = bf16[2048,1792]{1,0:T(8,128)(2,1)} fusion(bf16[512,1792]{1,0:T(8,128)(2,1)} %collective-permute-done.12, bf16[512,1792]{1,0:T(8,128)(2,1)} %collective-permute-done.3, bf16[512,1792]{1,0:T(8,128)(2,1)} %copy-done.18, bf16[512,1792]{1,0:T(8,128)(2,1)} %hidden_ref.1), kind=kLoop, calls=%fused_computation | loop fusion | flops 29360128 | bytes 14680064 | tf_op jit(solution)/shard_map/norm/concatenate | solution.py:560
  135.8 3.0 %collective-permute-start.22 = (bf16[2,512,128]{2,1,0:T(8,128)(2,1)S(1)}, bf16[2,512,128]{2,1,0:T(8,128)(2,1)S(1)}, u32[]{:S(2)}, u32[]{:S(2)}) collective-permute-start(bf16[2,512,128]{2,1,0:T(8,128)(2,1)S(1)} %slice.24), channel_id=1, source_target_pairs={{0,3},{1,0},{2,1},{3,2},{4,7},{5,4},{6,5},{7,6},{8,11},{9,8},{10,9... | collective-permute-start | bytes 786440 | tf_op jit(solution)/shard_map/contrast/ppermute | solution.py:61
  140.3 2.2 %contrast.3 = (f32[8,64,128]{2,1,0:T(8,128)S(1)}, f32[8,128]{1,0:T(8,128)S(1)}, f32[64,512]{1,0:T(8,128)S(1)}, f32[1,512]{1,0:T(1,128)S(1)}) custom-call(s32[1]{0:T(128)} %bitcast.13.plan_ref, f32[8,80,128]{2,1,0:T(8,128)} %all-to-all-done.3.part_ref, f32[64,64]{1,0:T(8,128)S(1)} %copy-done.8, f32[4,8,128]{2,1,0:T(8,128)S(1)} %bitcast.81, ...), custom_call_target="tpu_custom_call" | custom-call | flops 1024 | bytes 1024 | tf_op jit(solution)/shard_map/contrast/pallas_call | solution.py:204
  142.5 2.4 %fusion.13.refs_0_ = bf16[3,528,128]{2,1,0:T(8,128)(2,1)S(1)} fusion(s32[]{:T(128)S(6)} %select_n.212, bf16[4,512,128]{2,1,0:T(8,128)(2,1)} %copy-done.17, bf16[4,16,128]{2,1,0:T(8,128)(2,1)S(1)} %maximum_bitcast_fusion), kind=kLoop, calls=%fused_computation.30 | loop fusion | flops 1622016 | bytes 946180 | tf_op jit(solution)/shard_map/row_gather/concatenate | solution.py:587
  144.9 1.6 collective-permute-start.19
  146.5 3.2 %collective-permute-start.20 = (bf16[3,528,128]{2,1,0:T(8,128)(2,1)S(1)}, bf16[3,528,128]{2,1,0:T(8,128)(2,1)S(1)}, u32[]{:S(2)}, u32[]{:S(2)}) collective-permute-start(bf16[3,528,128]{2,1,0:T(8,128)(2,1)S(1)} %fusion.13.refs_0_), channel_id=1, source_target_pairs={{0,3},{1,0},{2,1},{3,2},{4,7},{5,4},{6,5},{7,6},{8,11},{9,8},{10,9... | collective-permute-start | bytes 1216520 | tf_op jit(solution)/shard_map/row_gather/ppermute | solution.py:61
  150.4 3.8 %along.1 = f32[4,4,128]{2,1,0:T(4,128)S(1)} custom-call(s32[32]{0:T(128)S(1)} %copy-done.12, bf16[4,512,128]{2,1,0:T(8,128)(2,1)S(1)} %pad_maximum_fusion.1.refs_0_.refs_9_, bf16[4,512,128]{2,1,0:T(8,128)(2,1)S(1)} %collective-permute-done.13.refs_1_.refs_10_, bf16[4,512,128]{2,1,0:T(8,128)(2,1)S(1)} %collective-permute-done.14.refs_2_.refs_11_, ...), custom_call_target="tpu_custom_call" | custom-call | flops 1024 | bytes 1024 | tf_op jit(solution)/shard_map/along/pallas_call | solution.py:284
  154.6 3.5 %collective-permute-done.24 = f32[8,4,128]{2,1,0:T(4,128)S(1)} collective-permute-done((f32[8,4,128]{2,1,0:T(4,128)S(1)}, f32[8,4,128]{2,1,0:T(4,128)S(1)}, u32[]{:S(2)}, u32[]{:S(2)}) %collective-permute-start.24) | collective-permute-done | bytes 16416 | tf_op jit(solution)/shard_map/along/ppermute | solution.py:593
  158.1 2.3 %collective-permute-done.21.refs_3_ = bf16[3,528,128]{2,1,0:T(8,128)(2,1)S(1)} collective-permute-done((bf16[3,528,128]{2,1,0:T(8,128)(2,1)S(1)}, bf16[3,528,128]{2,1,0:T(8,128)(2,1)S(1)}, u32[]{:S(2)}, u32[]{:S(2)}) %collective-permute-start.21) | collective-permute-done | bytes 405536 | tf_op jit(solution)/shard_map/row_gather/ppermute | solution.py:61
  162.9 1.3 collective-permute-start.28
  164.2 4.0 %collective-permute-done.28 = f32[8,4,128]{2,1,0:T(4,128)S(1)} collective-permute-done((f32[8,4,128]{2,1,0:T(4,128)S(1)}, f32[8,4,128]{2,1,0:T(4,128)S(1)}, u32[]{:S(2)}, u32[]{:S(2)}) %collective-permute-start.28) | collective-permute-done | bytes 16416 | tf_op jit(solution)/shard_map/along/ppermute | solution.py:596
  168.2 4.3 %down_grad.1 = (bf16[4,2048,256]{2,1,0:T(8,128)(2,1)S(1)}, f32[4,128]{1,0:T(4,128)S(1)}) custom-call(s32[32]{0:T(128)S(1)} %copy-done.13, bf16[4,512,128]{2,1,0:T(8,128)(2,1)S(1)} %pad_maximum_fusion.1.refs_0_.refs_9_, bf16[4,512,128]{2,1,0:T(8,128)(2,1)S(1)} %collective-permute-done.13.refs_1_.refs_10_, ...), custom_call_target="tpu_custom_call" | custom-call | flops 1024 | bytes 1024 | tf_op jit(solution)/shard_map/down_grad/pallas_call | solution.py:334
  172.7 2.2 %fusion.7 = f32[1792,256]{1,0:T(8,128)S(1)} fusion(bf16[2048,1792]{1,0:T(8,128)(2,1)S(1)} %copy-done.16, bf16[4,2048,256]{2,1,0:T(8,128)(2,1)S(1)} %get-tuple-element.153), kind=kOutput, calls=%fused_computation.16 | convolution fusion | flops 1879048192 | bytes 10223616 | tf_op jit(solution)/shard_map/down_grad/dot_general | solution.py:604
  175.2 3.4 %fusion.5 = f32[1792,256]{1,0:T(8,128)} fusion(bf16[2048,1792]{1,0:T(8,128)(2,1)S(1)} %copy-done.16, bf16[4,2048,256]{2,1,0:T(8,128)(2,1)S(1)} %get-tuple-element.153), kind=kOutput, calls=%fused_computation.14 | convolution fusion | flops 1879048192 | bytes 10223616 | tf_op jit(solution)/shard_map/down_grad/dot_general | solution.py:604
  179.1 2.3 %collective-permute-start.31 = (bf16[3,256,128]{2,1,0:T(8,128)(2,1)S(1)}, bf16[3,256,128]{2,1,0:T(8,128)(2,1)S(1)}, u32[]{:S(2)}, u32[]{:S(2)}) collective-permute-start(bf16[3,256,128]{2,1,0:T(8,128)(2,1)S(1)} %slice.30), channel_id=1, source_target_pairs={{0,3},{1,0},{2,1},{3,2},{4,7},{5,4},{6,5},{7,6},{8,11},{9,8},{10,9... | collective-permute-start | bytes 589832 | tf_op jit(solution)/shard_map/down_grad/ppermute | solution.py:61
  181.6 3.2 %fusion = bf16[1792,256]{1,0:T(8,128)(2,1)} fusion(f32[1792,256]{1,0:T(8,128)S(1)} %collective-permute-done.29, bf16[2048,1792]{1,0:T(8,128)(2,1)S(1)} %copy-done.16, bf16[4,2048,256]{2,1,0:T(8,128)(2,1)S(1)} %get-tuple-element.153), kind=kOutput, calls=%fused_computation.3 | convolution fusion | flops 1879965696 | bytes 11141120 | tf_op jit(solution)/shard_map/down_grad/dot_general | solution.py:604
  184.8 2.9 %collective-permute-start.30 = (bf16[1792,256]{1,0:T(8,128)(2,1)}, bf16[1792,256]{1,0:T(8,128)(2,1)S(1)}, u32[]{:S(2)}, u32[]{:S(2)}) collective-permute-start(bf16[1792,256]{1,0:T(8,128)(2,1)} %fusion), channel_id=1, source_target_pairs={{0,16},{8,24},{16,0},{24,8},{32,48},{40,56},{48,32},{56,40},{64,80... | collective-permute-start | bytes 2752520 | tf_op jit(solution)/shard_map/down_grad/ppermute | solution.py:53
  189.5 5.8 %convolution_add_fusion = f32[1792,256]{1,0:T(8,128)S(1)} fusion(f32[1792,256]{1,0:T(8,128)} %collective-permute-done.33, bf16[2048,1792]{1,0:T(8,128)(2,1)} %pad_maximum_fusion, bf16[2048,256]{1,0:T(8,128)(2,1)S(1)} %slice_bitcast_fusion), kind=kOutput, calls=%fused_computation.1 | convolution fusion | flops 1879506944 | bytes 12058624 | tf_op jit(solution)/shard_map/down_grad/dot_general | solution.py:604
  195.4 17.3 %hidden_grad.1 = (bf16[512,1792]{1,0:T(8,128)(2,1)}, bf16[512,512]{1,0:T(8,128)(2,1)}, f32[4,128]{1,0:T(4,128)}) custom-call(s32[11]{0:T(128)} %stack.176.plan_ref, bf16[3,528,128]{2,1,0:T(8,128)(2,1)} %copy-done.19, bf16[3,528,128]{2,1,0:T(8,128)(2,1)} %copy-done.23, bf16[3,528,128]{2,1,0:T(8,128)(2,1)} %copy-done.24, bf16[3,528,128]{2,1,0:T(8,128)(2,1)} %copy-done.25, ...), custom_call_target="tpu_custom_call" | custom-call | flops 1024 | bytes 1024 | tf_op jit(solution)/shard_map/hidden_grad/pallas_call | solution.py:419
  212.6 1.4 convert_add_fusion
  (142 shorter events, 23.7 us)
Async XLA Ops:
  0.6 45.2 %collective-permute-start.2 = (bf16[512,1792]{1,0:T(8,128)(2,1)}, bf16[512,1792]{1,0:T(8,128)(2,1)S(1)}, u32[]{:S(2)}, u32[]{:S(2)}) collective-permute-start(bf16[512,1792]{1,0:T(8,128)(2,1)} %hidden_ref.1), channel_id=1, source_target_pairs={{0,32},{8,40},{16,48},{24,56},{32,64},{40,72},{48,80},{56,88},{64,... | collective-permute-start | bytes 5505032 | tf_op jit(solution)/shard_map/hidden_exchange/ppermute | solution.py:49
  2.3 43.6 %collective-permute-start.3 = (bf16[512,1792]{1,0:T(8,128)(2,1)}, bf16[512,1792]{1,0:T(8,128)(2,1)}, u32[]{:S(2)}, u32[]{:S(2)}) collective-permute-start(bf16[512,1792]{1,0:T(8,128)(2,1)} %hidden_ref.1), channel_id=1, source_target_pairs={{0,96},{8,104},{16,112},{24,120},{32,0},{40,8},{48,16},{56,24},{64... | collective-permute-start | bytes 5505032 | tf_op jit(solution)/shard_map/hidden_exchange/ppermute | solution.py:49
  6.3 21.0 %all-to-all-start = ((bf16[8,512,128]{2,1,0:T(8,128)(2,1)}), bf16[8,512,128]{2,1,0:T(8,128)(2,1)S(1)}, u32[]{:S(2)}, u32[]{:S(2)}) async-start(bf16[8,512,128]{2,1,0:T(8,128)(2,1)} %bitcast.6), calls=%async_computation | async-start | bytes 2097152 | tf_op jit(solution)/shard_map/resid_exchange/all_to_all | solution.py:520
  26.2 40.3 %copy-start.30 = (s32[16]{0:T(128)S(1)}, s32[16]{0:T(128)}, u32[]{:S(2)}) copy-start(s32[16]{0:T(128)} %param.9) | copy-start | bytes 196
  27.3 37.5 %copy-start.22 = (bf16[4,512,128]{2,1,0:T(8,128)(2,1)S(1)}, bf16[4,512,128]{2,1,0:T(8,128)(2,1)}, u32[]{:S(2)}) copy-start(bf16[4,512,128]{2,1,0:T(8,128)(2,1)} %get-tuple-element.117) | copy-start | bytes 1572868
  27.3 13.7 %collective-permute-start = (bf16[4,512,128]{2,1,0:T(8,128)(2,1)}, bf16[4,512,128]{2,1,0:T(8,128)(2,1)S(1)}, u32[]{:S(2)}, u32[]{:S(2)}) collective-permute-start(bf16[4,512,128]{2,1,0:T(8,128)(2,1)} %get-tuple-element.110), channel_id=1, source_target_pairs={{0,3},{1,0},{2,1},{3,2},{4,7},{5,4},{6,5},{7,6},{8,11},{9,8},{10,9... | collective-permute-start | bytes 1572872 | tf_op jit(solution)/shard_map/layer_sum/ppermute | solution.py:61
  29.6 16.3 %collective-permute-start.1 = (bf16[4,512,128]{2,1,0:T(8,128)(2,1)}, bf16[4,512,128]{2,1,0:T(8,128)(2,1)S(1)}, u32[]{:S(2)}, u32[]{:S(2)}) collective-permute-start(bf16[4,512,128]{2,1,0:T(8,128)(2,1)} %get-tuple-element.111), channel_id=1, source_target_pairs={{0,1},{1,2},{2,3},{3,0},{4,5},{5,6},{6,7},{7,4},{8,9},{9,10},{10,1... | collective-permute-start | bytes 1572872 | tf_op jit(solution)/shard_map/layer_sum/ppermute | solution.py:61
  29.6 24.9 %collective-permute-start.5 = (bf16[4,512,128]{2,1,0:T(8,128)(2,1)}, bf16[4,512,128]{2,1,0:T(8,128)(2,1)S(1)}, u32[]{:S(2)}, u32[]{:S(2)}) collective-permute-start(bf16[4,512,128]{2,1,0:T(8,128)(2,1)} %get-tuple-element.113), channel_id=1, source_target_pairs={{0,1},{1,2},{2,3},{3,0},{4,5},{5,6},{6,7},{7,4},{8,9},{9,10},{10,1... | collective-permute-start | bytes 1572872 | tf_op jit(solution)/shard_map/layer_sum/ppermute | solution.py:61
  47.4 14.9 %collective-permute-start.4 = (bf16[4,512,128]{2,1,0:T(8,128)(2,1)S(1)}, bf16[4,512,128]{2,1,0:T(8,128)(2,1)S(1)}, u32[]{:S(2)}, u32[]{:S(2)}) collective-permute-start(bf16[4,512,128]{2,1,0:T(8,128)(2,1)S(1)} %add_convert_fusion.3), channel_id=1, source_target_pairs={{0,4},{1,5},{2,6},{3,7},{4,0},{5,1},{6,2},{7,3},{8,12},{9,13},{10,... | collective-permute-start | bytes 1572872 | tf_op jit(solution)/shard_map/layer_sum/ppermute | solution.py:65
  49.0 46.5 %collective-permute-start.12 = (bf16[512,1792]{1,0:T(8,128)(2,1)}, bf16[512,1792]{1,0:T(8,128)(2,1)}, u32[]{:S(2)}, u32[]{:S(2)}) collective-permute-start(bf16[512,1792]{1,0:T(8,128)(2,1)} %hidden_ref.1), channel_id=1, source_target_pairs={{0,64},{8,72},{16,80},{24,88},{32,96},{40,104},{48,112},{56,120},{... | collective-permute-start | bytes 5505032 | tf_op jit(solution)/shard_map/hidden_exchange/ppermute | solution.py:49
  52.9 17.0 %collective-permute-start.7 = (bf16[4,512,128]{2,1,0:T(8,128)(2,1)}, bf16[4,512,128]{2,1,0:T(8,128)(2,1)}, u32[]{:S(2)}, u32[]{:S(2)}) collective-permute-start(bf16[4,512,128]{2,1,0:T(8,128)(2,1)} %add_convert_fusion.1), channel_id=1, source_target_pairs={{0,4},{1,5},{2,6},{3,7},{4,0},{5,1},{6,2},{7,3},{8,12},{9,13},{10,... | collective-permute-start | bytes 1572872 | tf_op jit(solution)/shard_map/layer_sum/ppermute | solution.py:65
  63.5 9.4 %collective-permute-start.6 = (bf16[4,512,128]{2,1,0:T(8,128)(2,1)S(1)}, bf16[4,512,128]{2,1,0:T(8,128)(2,1)}, u32[]{:S(2)}, u32[]{:S(2)}) collective-permute-start(bf16[4,512,128]{2,1,0:T(8,128)(2,1)S(1)} %add_convert_fusion.2), channel_id=1, source_target_pairs={{0,3},{1,0},{2,1},{3,2},{4,7},{5,4},{6,5},{7,6},{8,11},{9,8},{10,9... | collective-permute-start | bytes 1572872 | tf_op jit(solution)/shard_map/layer_sum/ppermute | solution.py:61
  65.8 11.3 %collective-permute-start.8 = (bf16[4,512,128]{2,1,0:T(8,128)(2,1)}, bf16[4,512,128]{2,1,0:T(8,128)(2,1)}, u32[]{:S(2)}, u32[]{:S(2)}) collective-permute-start(bf16[4,512,128]{2,1,0:T(8,128)(2,1)} %add_convert_fusion), channel_id=1, source_target_pairs={{0,1},{1,2},{2,3},{3,0},{4,5},{5,6},{6,7},{7,4},{8,9},{9,10},{10,1... | collective-permute-start | bytes 1572872 | tf_op jit(solution)/shard_map/layer_sum/ppermute | solution.py:61
  66.8 41.0 %copy-start.9 = (f32[4096]{0:T(1024)S(1)}, f32[4096]{0:T(1024)}, u32[]{:S(2)}) copy-start(f32[4096]{0:T(1024)} %param.8) | copy-start | bytes 49156
  80.1 14.9 %collective-permute-start.11 = (bf16[1,512,128]{2,1,0:T(8,128)(2,1)S(1)}, bf16[1,512,128]{2,1,0:T(8,128)(2,1)S(1)}, u32[]{:S(2)}, u32[]{:S(2)}) collective-permute-start(bf16[1,512,128]{2,1,0:T(8,128)(2,1)S(1)} %get-tuple-element.195), channel_id=1, source_target_pairs={{0,64},{8,72},{16,80},{24,88},{32,96},{40,104},{48,112},{56,120},{... | collective-permute-start | bytes 393224 | tf_op jit(solution)/shard_map/strip_exchange/ppermute | solution.py:49
  82.2 13.0 %collective-permute-start.10 = (bf16[1,512,128]{2,1,0:T(8,128)(2,1)S(1)}, bf16[1,512,128]{2,1,0:T(8,128)(2,1)S(1)}, u32[]{:S(2)}, u32[]{:S(2)}) collective-permute-start(bf16[1,512,128]{2,1,0:T(8,128)(2,1)S(1)} %get-tuple-element.196), channel_id=1, source_target_pairs={{0,96},{8,104},{16,112},{24,120},{32,0},{40,8},{48,16},{56,24},{64... | collective-permute-start | bytes 393224 | tf_op jit(solution)/shard_map/strip_exchange/ppermute | solution.py:49
  83.5 11.9 %collective-permute-start.9 = (bf16[1,512,128]{2,1,0:T(8,128)(2,1)S(1)}, bf16[1,512,128]{2,1,0:T(8,128)(2,1)S(1)}, u32[]{:S(2)}, u32[]{:S(2)}) collective-permute-start(bf16[1,512,128]{2,1,0:T(8,128)(2,1)S(1)} %get-tuple-element.197), channel_id=1, source_target_pairs={{0,32},{8,40},{16,48},{24,56},{32,64},{40,72},{48,80},{56,88},{64,... | collective-permute-start | bytes 393224 | tf_op jit(solution)/shard_map/strip_exchange/ppermute | solution.py:49
  85.5 9.5 %all-to-all-start.1 = ((f32[8,4,128]{2,1,0:T(4,128)}), f32[8,4,128]{2,1,0:T(4,128)S(1)}, u32[]{:S(2)}, u32[]{:S(2)}) async-start(f32[8,4,128]{2,1,0:T(4,128)} %broadcast_in_dim.54), calls=%async_computation.1 | async-start | bytes 32768 | tf_op jit(solution)/shard_map/norm/all_to_all | solution.py:71
  95.5 72.7 %copy-start = (bf16[4,512,128]{2,1,0:T(8,128)(2,1)}, bf16[4,512,128]{2,1,0:T(8,128)(2,1)S(1)}, u32[]{:S(2)}) copy-start(bf16[4,512,128]{2,1,0:T(8,128)(2,1)S(1)} %pad_maximum_fusion.1.refs_0_.refs_9_) | copy-start | bytes 1572868
  95.5 19.1 %collective-permute-start.13 = (bf16[4,512,128]{2,1,0:T(8,128)(2,1)S(1)}, bf16[4,512,128]{2,1,0:T(8,128)(2,1)S(1)}, u32[]{:S(2)}, u32[]{:S(2)}) collective-permute-start(bf16[4,512,128]{2,1,0:T(8,128)(2,1)S(1)} %pad_maximum_fusion.1.refs_0_.refs_9_), channel_id=1, source_target_pairs={{0,4},{1,5},{2,6},{3,7},{4,0},{5,1},{6,2},{7,3},{8,12},{9,13},{10,... | collective-permute-start | bytes 1572872 | tf_op jit(solution)/shard_map/norm/ppermute | solution.py:65
  96.0 18.7 %collective-permute-start.14 = (bf16[4,512,128]{2,1,0:T(8,128)(2,1)S(1)}, bf16[4,512,128]{2,1,0:T(8,128)(2,1)S(1)}, u32[]{:S(2)}, u32[]{:S(2)}) collective-permute-start(bf16[4,512,128]{2,1,0:T(8,128)(2,1)S(1)} %pad_maximum_fusion.1.refs_0_.refs_9_), channel_id=1, source_target_pairs={{0,3},{1,0},{2,1},{3,2},{4,7},{5,4},{6,5},{7,6},{8,11},{9,8},{10,9... | collective-permute-start | bytes 1572872 | tf_op jit(solution)/shard_map/norm/ppermute | solution.py:61
  99.0 15.7 %collective-permute-start.15 = (bf16[4,512,128]{2,1,0:T(8,128)(2,1)S(1)}, bf16[4,512,128]{2,1,0:T(8,128)(2,1)S(1)}, u32[]{:S(2)}, u32[]{:S(2)}) collective-permute-start(bf16[4,512,128]{2,1,0:T(8,128)(2,1)S(1)} %pad_maximum_fusion.1.refs_0_.refs_9_), channel_id=1, source_target_pairs={{0,1},{1,2},{2,3},{3,0},{4,5},{5,6},{6,7},{7,4},{8,9},{9,10},{10,1... | collective-permute-start | bytes 1572872 | tf_op jit(solution)/shard_map/norm/ppermute | solution.py:61
  99.0 50.7 %copy-start.29 = (f32[4,128]{1,0:T(4,128)}, f32[4,128]{1,0:T(4,128)S(1)}, u32[]{:S(2)}) copy-start(f32[4,128]{1,0:T(4,128)S(1)} %add_rsqrt_fusion.refs_19_) | copy-start | bytes 6148
  99.9 14.8 %all-to-all-start.2 = ((f32[16,4,512]{2,1,0:T(4,128)}), f32[16,4,512]{2,1,0:T(4,128)S(1)}, u32[]{:S(2)}, u32[]{:S(2)}) async-start(f32[16,4,512]{2,1,0:T(4,128)} %broadcast_in_dim.56), calls=%async_computation.2 | async-start | bytes 262144 | tf_op jit(solution)/shard_map/contrast/all_to_all | solution.py:71
  114.6 53.6 %copy-start.3 = (bf16[4,512,128]{2,1,0:T(8,128)(2,1)}, bf16[4,512,128]{2,1,0:T(8,128)(2,1)S(1)}, u32[]{:S(2)}) copy-start(bf16[4,512,128]{2,1,0:T(8,128)(2,1)S(1)} %collective-permute-done.13.refs_1_.refs_10_) | copy-start | bytes 1572868
  114.7 53.6 %copy-start.4 = (bf16[4,512,128]{2,1,0:T(8,128)(2,1)}, bf16[4,512,128]{2,1,0:T(8,128)(2,1)S(1)}, u32[]{:S(2)}) copy-start(bf16[4,512,128]{2,1,0:T(8,128)(2,1)S(1)} %collective-permute-done.14.refs_2_.refs_11_) | copy-start | bytes 1572868
  114.7 53.6 %copy-start.5 = (bf16[4,512,128]{2,1,0:T(8,128)(2,1)}, bf16[4,512,128]{2,1,0:T(8,128)(2,1)S(1)}, u32[]{:S(2)}) copy-start(bf16[4,512,128]{2,1,0:T(8,128)(2,1)S(1)} %collective-permute-done.15.refs_3_.refs_12_) | copy-start | bytes 1572868
  114.7 21.0 %collective-permute-start.17 = (bf16[4,512,128]{2,1,0:T(8,128)(2,1)S(1)}, bf16[4,512,128]{2,1,0:T(8,128)(2,1)S(1)}, u32[]{:S(2)}, u32[]{:S(2)}) collective-permute-start(bf16[4,512,128]{2,1,0:T(8,128)(2,1)S(1)} %collective-permute-done.15.refs_3_.refs_12_), channel_id=1, source_target_pairs={{0,4},{1,5},{2,6},{3,7},{4,0},{5,1},{6,2},{7,3},{8,12},{9,13},{10,... | collective-permute-start | bytes 1572872 | tf_op jit(solution)/shard_map/contrast/ppermute | solution.py:65
  115.8 19.9 %collective-permute-start.18 = (bf16[4,512,128]{2,1,0:T(8,128)(2,1)S(1)}, bf16[4,512,128]{2,1,0:T(8,128)(2,1)}, u32[]{:S(2)}, u32[]{:S(2)}) collective-permute-start(bf16[4,512,128]{2,1,0:T(8,128)(2,1)S(1)} %collective-permute-done.15.refs_3_.refs_12_), channel_id=1, source_target_pairs={{0,1},{1,2},{2,3},{3,0},{4,5},{5,6},{6,7},{7,4},{8,9},{9,10},{10,1... | collective-permute-start | bytes 1572872 | tf_op jit(solution)/shard_map/contrast/ppermute | solution.py:61
  116.4 19.3 %collective-permute-start.16 = (bf16[4,512,128]{2,1,0:T(8,128)(2,1)S(1)}, bf16[4,512,128]{2,1,0:T(8,128)(2,1)S(1)}, u32[]{:S(2)}, u32[]{:S(2)}) collective-permute-start(bf16[4,512,128]{2,1,0:T(8,128)(2,1)S(1)} %collective-permute-done.13.refs_1_.refs_10_), channel_id=1, source_target_pairs={{0,3},{1,0},{2,1},{3,2},{4,7},{5,4},{6,5},{7,6},{8,11},{9,8},{10,9... | collective-permute-start | bytes 1572872 | tf_op jit(solution)/shard_map/contrast/ppermute | solution.py:61
  120.4 15.3 %all-to-all-start.3 = ((f32[8,80,128]{2,1,0:T(8,128)}), f32[8,80,128]{2,1,0:T(8,128)}, u32[]{:S(2)}, u32[]{:S(2)}) async-start(f32[8,80,128]{2,1,0:T(8,128)} %broadcast_in_dim.57), calls=%async_computation.3 | async-start | bytes 655360 | tf_op jit(solution)/shard_map/contrast/all_to_all | solution.py:71
  135.7 36.9 %copy-start.2 = (bf16[4,512,128]{2,1,0:T(8,128)(2,1)}, bf16[4,512,128]{2,1,0:T(8,128)(2,1)S(1)}, u32[]{:S(2)}) copy-start(bf16[4,512,128]{2,1,0:T(8,128)(2,1)S(1)} %collective-permute-done.16.refs_5_.refs_14_) | copy-start | bytes 1572868
  135.7 36.8 %copy-start.1 = (bf16[4,512,128]{2,1,0:T(8,128)(2,1)}, bf16[4,512,128]{2,1,0:T(8,128)(2,1)S(1)}, u32[]{:S(2)}) copy-start(bf16[4,512,128]{2,1,0:T(8,128)(2,1)S(1)} %collective-permute-done.17.refs_6_.refs_15_) | copy-start | bytes 1572868
  135.8 14.0 %collective-permute-start.22 = (bf16[2,512,128]{2,1,0:T(8,128)(2,1)S(1)}, bf16[2,512,128]{2,1,0:T(8,128)(2,1)S(1)}, u32[]{:S(2)}, u32[]{:S(2)}) collective-permute-start(bf16[2,512,128]{2,1,0:T(8,128)(2,1)S(1)} %slice.24), channel_id=1, source_target_pairs={{0,3},{1,0},{2,1},{3,2},{4,7},{5,4},{6,5},{7,6},{8,11},{9,8},{10,9... | collective-permute-start | bytes 786440 | tf_op jit(solution)/shard_map/contrast/ppermute | solution.py:61
  138.8 11.0 %collective-permute-start.23 = (bf16[2,512,128]{2,1,0:T(8,128)(2,1)S(1)}, bf16[2,512,128]{2,1,0:T(8,128)(2,1)S(1)}, u32[]{:S(2)}, u32[]{:S(2)}) collective-permute-start(bf16[2,512,128]{2,1,0:T(8,128)(2,1)S(1)} %slice.25), channel_id=1, source_target_pairs={{0,1},{1,2},{2,3},{3,0},{4,5},{5,6},{6,7},{7,4},{8,9},{9,10},{10,1... | collective-permute-start | bytes 786440 | tf_op jit(solution)/shard_map/contrast/ppermute | solution.py:61
  144.9 13.1 %collective-permute-start.19 = (bf16[3,528,128]{2,1,0:T(8,128)(2,1)S(1)}, bf16[3,528,128]{2,1,0:T(8,128)(2,1)S(1)}, u32[]{:S(2)}, u32[]{:S(2)}) collective-permute-start(bf16[3,528,128]{2,1,0:T(8,128)(2,1)S(1)} %fusion.13.refs_0_), channel_id=1, source_target_pairs={{0,4},{1,5},{2,6},{3,7},{4,0},{5,1},{6,2},{7,3},{8,12},{9,13},{10,... | collective-permute-start | bytes 1216520 | tf_op jit(solution)/shard_map/row_gather/ppermute | solution.py:65
  146.5 11.6 %collective-permute-start.20 = (bf16[3,528,128]{2,1,0:T(8,128)(2,1)S(1)}, bf16[3,528,128]{2,1,0:T(8,128)(2,1)S(1)}, u32[]{:S(2)}, u32[]{:S(2)}) collective-permute-start(bf16[3,528,128]{2,1,0:T(8,128)(2,1)S(1)} %fusion.13.refs_0_), channel_id=1, source_target_pairs={{0,3},{1,0},{2,1},{3,2},{4,7},{5,4},{6,5},{7,6},{8,11},{9,8},{10,9... | collective-permute-start | bytes 1216520 | tf_op jit(solution)/shard_map/row_gather/ppermute | solution.py:61
  149.7 10.7 %collective-permute-start.21 = (bf16[3,528,128]{2,1,0:T(8,128)(2,1)S(1)}, bf16[3,528,128]{2,1,0:T(8,128)(2,1)S(1)}, u32[]{:S(2)}, u32[]{:S(2)}) collective-permute-start(bf16[3,528,128]{2,1,0:T(8,128)(2,1)S(1)} %fusion.13.refs_0_), channel_id=1, source_target_pairs={{0,1},{1,2},{2,3},{3,0},{4,5},{5,6},{6,7},{7,4},{8,9},{9,10},{10,1... | collective-permute-start | bytes 1216520 | tf_op jit(solution)/shard_map/row_gather/ppermute | solution.py:61
  154.2 3.8 %collective-permute-start.24 = (f32[8,4,128]{2,1,0:T(4,128)S(1)}, f32[8,4,128]{2,1,0:T(4,128)S(1)}, u32[]{:S(2)}, u32[]{:S(2)}) collective-permute-start(f32[8,4,128]{2,1,0:T(4,128)S(1)} %pad_maximum_fusion.2), channel_id=1, source_target_pairs={{0,32},{8,40},{16,48},{24,56},{32,0},{40,8},{48,16},{56,24},{64,96... | collective-permute-start | bytes 49160 | tf_op jit(solution)/shard_map/along/ppermute | solution.py:593
  160.4 12.2 %collective-permute-start.25 = (bf16[3,528,128]{2,1,0:T(8,128)(2,1)S(1)}, bf16[3,528,128]{2,1,0:T(8,128)(2,1)S(1)}, u32[]{:S(2)}, u32[]{:S(2)}) collective-permute-start(bf16[3,528,128]{2,1,0:T(8,128)(2,1)S(1)} %collective-permute-done.19.refs_1_), channel_id=1, source_target_pairs={{0,3},{1,0},{2,1},{3,2},{4,7},{5,4},{6,5},{7,6},{8,11},{9,8},{10,9... | collective-permute-start | bytes 1216520 | tf_op jit(solution)/shard_map/along/ppermute | solution.py:61
  161.4 11.2 %collective-permute-start.26 = (bf16[3,528,128]{2,1,0:T(8,128)(2,1)S(1)}, bf16[3,528,128]{2,1,0:T(8,128)(2,1)S(1)}, u32[]{:S(2)}, u32[]{:S(2)}) collective-permute-start(bf16[3,528,128]{2,1,0:T(8,128)(2,1)S(1)} %collective-permute-done.21.refs_3_), channel_id=1, source_target_pairs={{0,4},{1,5},{2,6},{3,7},{4,0},{5,1},{6,2},{7,3},{8,12},{9,13},{10,... | collective-permute-start | bytes 1216520 | tf_op jit(solution)/shard_map/along/ppermute | solution.py:65
  162.0 10.7 %collective-permute-start.27 = (bf16[3,528,128]{2,1,0:T(8,128)(2,1)S(1)}, bf16[3,528,128]{2,1,0:T(8,128)(2,1)S(1)}, u32[]{:S(2)}, u32[]{:S(2)}) collective-permute-start(bf16[3,528,128]{2,1,0:T(8,128)(2,1)S(1)} %collective-permute-done.21.refs_3_), channel_id=1, source_target_pairs={{0,1},{1,2},{2,3},{3,0},{4,5},{5,6},{6,7},{7,4},{8,9},{9,10},{10,1... | collective-permute-start | bytes 1216520 | tf_op jit(solution)/shard_map/along/ppermute | solution.py:61
  162.9 5.2 %collective-permute-start.28 = (f32[8,4,128]{2,1,0:T(4,128)S(1)}, f32[8,4,128]{2,1,0:T(4,128)S(1)}, u32[]{:S(2)}, u32[]{:S(2)}) collective-permute-start(f32[8,4,128]{2,1,0:T(4,128)S(1)} %fusion.19), channel_id=1, source_target_pairs={{0,64},{8,72},{16,80},{24,88},{32,96},{40,104},{48,112},{56,120},{... | collective-permute-start | bytes 49160 | tf_op jit(solution)/shard_map/along/ppermute | solution.py:596
  174.9 6.7 %collective-permute-start.29 = (f32[1792,256]{1,0:T(8,128)S(1)}, f32[1792,256]{1,0:T(8,128)S(1)}, u32[]{:S(2)}, u32[]{:S(2)}) collective-permute-start(f32[1792,256]{1,0:T(8,128)S(1)} %fusion.7), channel_id=1, source_target_pairs={{0,8},{8,0},{16,24},{24,16},{32,40},{40,32},{48,56},{56,48},{64,72... | collective-permute-start | bytes 5505032 | tf_op jit(solution)/shard_map/down_grad/ppermute | solution.py:57
  178.6 11.0 %collective-permute-start.33 = (f32[1792,256]{1,0:T(8,128)}, f32[1792,256]{1,0:T(8,128)}, u32[]{:S(2)}, u32[]{:S(2)}) collective-permute-start(f32[1792,256]{1,0:T(8,128)} %fusion.5), channel_id=1, source_target_pairs={{0,8},{8,0},{16,24},{24,16},{32,40},{40,32},{48,56},{56,48},{64,72... | collective-permute-start | bytes 5505032 | tf_op jit(solution)/shard_map/down_grad/ppermute | solution.py:57
  179.1 9.3 %collective-permute-start.31 = (bf16[3,256,128]{2,1,0:T(8,128)(2,1)S(1)}, bf16[3,256,128]{2,1,0:T(8,128)(2,1)S(1)}, u32[]{:S(2)}, u32[]{:S(2)}) collective-permute-start(bf16[3,256,128]{2,1,0:T(8,128)(2,1)S(1)} %slice.30), channel_id=1, source_target_pairs={{0,3},{1,0},{2,1},{3,2},{4,7},{5,4},{6,5},{7,6},{8,11},{9,8},{10,9... | collective-permute-start | bytes 589832 | tf_op jit(solution)/shard_map/down_grad/ppermute | solution.py:61
  181.5 8.1 %collective-permute-start.32 = (bf16[3,272,128]{2,1,0:T(8,128)(2,1)S(1)}, bf16[3,272,128]{2,1,0:T(8,128)(2,1)S(1)}, u32[]{:S(2)}, u32[]{:S(2)}) collective-permute-start(bf16[3,272,128]{2,1,0:T(8,128)(2,1)S(1)} %slice.31), channel_id=1, source_target_pairs={{0,1},{1,2},{2,3},{3,0},{4,5},{5,6},{6,7},{7,4},{8,9},{9,10},{10,1... | collective-permute-start | bytes 626696 | tf_op jit(solution)/shard_map/down_grad/ppermute | solution.py:61
  184.8 27.9 %collective-permute-start.30 = (bf16[1792,256]{1,0:T(8,128)(2,1)}, bf16[1792,256]{1,0:T(8,128)(2,1)S(1)}, u32[]{:S(2)}, u32[]{:S(2)}) collective-permute-start(bf16[1792,256]{1,0:T(8,128)(2,1)} %fusion), channel_id=1, source_target_pairs={{0,16},{8,24},{16,0},{24,8},{32,48},{40,56},{48,32},{56,40},{64,80... | collective-permute-start | bytes 2752520 | tf_op jit(solution)/shard_map/down_grad/ppermute | solution.py:53
  (21 other events, 284.4 us)

commit v7 on v6

--- a/solution.py
+++ b/solution.py
@@ -364,7 +364,7 @@
     row_refs, rest_ref, strip_refs = refs[:group], refs[group], refs[group + 1 :]
     others, _, lanes = refs[0].shape
     width = resid_ref.shape[1]
-    x, first = plan_ref[1], plan_ref[2]
+    rank, x, first = [plan_ref[2 * NX + 3 * group + i] for i in range(3)]
 
     @pl.when(pl.program_id(0) == 0)
     def _():
@@ -373,7 +373,7 @@
             for s in range(seqs_here)
         ]
         for i in range(group):
-            place = plan_ref[3 + i]
+            place = plan_ref[NX + i]
             row_ref, strip_ref = row_refs[i], strip_refs[i]
             last = i == group - 1
             tail_ref, tail_start = (rest_ref, tokens // 2) if last else (row_ref, tokens)
@@ -397,10 +397,10 @@
                         layer, scaled = strip_ref[0, rows, :], scaled_ref[place, pl.ds(first + s, 1), :]
                     inverse, coef = factors[s]
                     low_ref[rows, column] = (inverse * scaled - layer.astype(f32) * coef).astype(bf16)
-        first_place = plan_ref[0] % 2 * (group // 2)
+        first_place = rank % 2 * (group // 2)
         for j in range(group // 2):
-            gain_ref[j : j + 1, :] = gains_ref[first_place + j, pl.ds(plan_ref[0] // 2, 1), :]
-        resid_ref[...] = low_ref[:, pl.ds(pl.multiple_of(plan_ref[0] * width, width), width)]
+            gain_ref[j : j + 1, :] = gains_ref[first_place + j, pl.ds(rank // 2, 1), :]
+        resid_ref[...] = low_ref[:, pl.ds(pl.multiple_of(rank * width, width), width)]
 
     out_ref[...] = lax.dot_general(
         low_ref[...], weight_ref[...], (((1,), (1,)), ((), ())), preferred_element_type=f32
@@ -442,7 +442,7 @@
         ),
         compiler_params=pltpu.CompilerParams(vmem_limit_bytes=56 * MIB),
         cost_estimate=QUICK,
-    )(jnp.stack(plan).astype(jnp.int32), *rows, *strips, scaled, block_gain, inverse, coef, weight)
+    )(plan, *rows, *strips, scaled, block_gain, inverse, coef, weight)
 
 
 def tie(*values):
@@ -507,6 +507,7 @@
         plan = [p * seqs_here for p in peers] + places
         plan += [(p // 2) ^ (zh * NCORE + core) for p in places] + [p % 2 * lanes for p in places]
         plan += [(x + step) % NX for step in (0, -1, 1, 2)]
+        plan += [rank, x, shard * seqs_here]
         plan = jnp.stack([jnp.asarray(v, jnp.int32) for v in plan])
 
     with jax.named_scope("hidden_exchange"):
@@ -569,7 +570,10 @@
         got = gather_next(got)
         means_all = means_all.reshape(seqs, width)
         parts = gather_small(gram_part(means_all, gain_own, x), "tensor")
-        got, parts, low_layer, hidden_rows = tie_gather(got, parts, low_layer, hidden_rows)
+        row_blocks = jnp.concatenate([low_layer, low_layer], axis=0)
+        row_blocks = lax.dynamic_slice_in_dim(row_blocks, x + 1, NX - 1, 0)
+        row_blocks = jnp.pad(row_blocks, ((0, 0), (0, 16), (0, 0)))
+        got, parts, row_blocks, hidden_rows = tie_gather(got, parts, row_blocks, hidden_rows)
         half = NX // 2
         got[1, 2] = over_y(got[1, 1][:half], -1)
         strips = [got[key] for key in KEYS] + [over_y(got[1, 3][half:], 1)]
@@ -583,9 +587,8 @@
         high = lax.reduce_precision(own_rows, exponent_bits=8, mantissa_bits=7)
         tail = jnp.concatenate([high, own_rows - high], axis=0).astype(bf16)
         tail = tail.reshape(16, NX, lanes).transpose(1, 0, 2)
-        blocks = jnp.concatenate([low_layer, tail], axis=1)
-        blocks = jnp.concatenate([blocks, blocks], axis=0)
-        rows = gather_start(lax.dynamic_slice_in_dim(blocks, x + 1, NX - 1, 0))
+        tail = lax.dynamic_slice_in_dim(jnp.concatenate([tail, tail], axis=0), x + 1, NX - 1, 0)
+        rows = gather_start(lax.dynamic_update_slice(row_blocks, tail, (0, tokens, 0)))
 
     with jax.named_scope("along"):
         own_inverse = jnp.where(jnp.arange(NX)[:, None, None] == x, inverse[None], 0.0)
@@ -618,7 +621,7 @@
         rows, near = tie_gather(rows, near)
         rows = [rows[key] for key in KEYS + ("rest",)]
         grad_hidden, grad_resid, gain_grad = hidden_grad(
-            rows, strips[:group], scaled, gain_grad_x, inverse, coef, down_weight, [rank, x, shard * seqs_here] + places
+            rows, strips[:group], scaled, gain_grad_x, inverse, coef, down_weight, plan
         )
         grad_gain = gain_grad.reshape(width)
 

time: 215 us -> 207 us (0.963)
  matrix products: 14.5 us -> 8.76 us
  waiting for transfers between devices: 59.9 us -> 63.3 us
  local copies, waits for them, and re-layouts: 9.77 us -> 7.08 us
  other arithmetic: 23.8 us -> 21.5 us
    dot_general x4, matrix products: 14.5 us -> 8.76 us  [down(): lax.dot_general(hidden_rows, low, (((0,), (0,)), ((), ())), preferred_ele...]
    ppermute x17, waiting for transfers between devices: 27 us -> 29.3 us  [over_y(): return lax.ppermute(value, 'tensor', tensor_route(0, step))]
    unnamed x62 -> x50, local copies, waits for them, and re-layouts: 2.95 us -> 0.69 us
    ppermute x6, waiting for transfers between devices: 0.46 us -> 2.62 us  [over_x(): return lax.ppermute(value, 'dp', dp_route(step, 0, 0))]
  transfers between devices with their start and end apart: 38 -> 38, of which waited for: 16 -> 18; matrix products, arithmetic and copies ran while one was open for 19% -> 16% of each run, Pallas kernels for 19% -> 20%
where the time goes in v7:
time: 207 us; the launch traced here: 206 us
  waiting for transfers between devices  63.3 us (31%)
  starting transfers between devices  62.5 us (30%)
  Pallas kernels  41.3 us (20%)
  other arithmetic  21.5 us (10%)
  matrix products  8.76 us (4%)
  local copies, waits for them, and re-layouts  7.08 us (3%)
    ppermute x17, waiting for transfers between devices, over_y(): return lax.ppermute(value, 'tensor', tensor_route(0, step))  29.3 us
    ppermute x17, starting transfers between devices, over_y(): return lax.ppermute(value, 'tensor', tensor_route(0, step))  22 us
    pallas_call x1, Pallas kernels, hidden_grad(): pl.pallas_call(hidden_grad_kernel, grid_spec=pltpu.PrefetchScalarGridSpec...  17.3 us
    all_to_all x3, starting transfers between devices, gather_small(): return lax.all_to_all(copies, axis, 0, 0)  14.7 us
    pallas_call x1, Pallas kernels, layer_dot(): pl.pallas_call(layer_dot_kernel, grid_spec=pltpu.PrefetchScalarGridSpec(n...  13.4 us
    all_to_all x3, waiting for transfers between devices, gather_small(): return lax.all_to_all(copies, axis, 0, 0)  11.6 us
    ppermute x6, waiting for transfers between devices, over_zl(): return lax.ppermute(value, 'tensor', tensor_route(1, 0))  11.4 us
    concatenate x1, other arithmetic, per_device(): jnp.concatenate([hidden, hidden_left, hidden_right, hidden_far], axis=0)  11 us
  transfers between devices with their start and end apart: 38, of which 18 were waited for; matrix products, arithmetic and copies ran while one was open for 16% of the time, Pallas kernels for 20%

profile of v7, /device:TPU:0, one launch (start us, length us, event | category | flops | bytes accessed | tf_op | source)
XLA Modules:
  0.0 206.1 jit_solution(18017695841282885948)
XLA Ops:
  0.6 1.6 collective-permute-start.2
  2.3 1.7 collective-permute-start.3
  6.3 5.9 %all-to-all-start = ((bf16[8,512,128]{2,1,0:T(8,128)(2,1)}), bf16[8,512,128]{2,1,0:T(8,128)(2,1)S(1)}, u32[]{:S(2)}, u32[]{:S(2)}) async-start(bf16[8,512,128]{2,1,0:T(8,128)(2,1)} %bitcast.6), calls=%async_computation | async-start | bytes 2097152 | tf_op jit(solution)/shard_map/resid_exchange/all_to_all | solution.py:521
  12.9 13.4 %layer_sum.1 = (bf16[4,512,128]{2,1,0:T(8,128)(2,1)}, bf16[4,512,128]{2,1,0:T(8,128)(2,1)}, bf16[4,512,128]{2,1,0:T(8,128)(2,1)}, bf16[4,512,128]{2,1,0:T(8,128)...) custom-call(s32[5]{0:T(128)} %stack.129.plan_ref, ...), custom_call_target="tpu_custom_call" | custom-call | flops 7516192768 | bytes 20709376 | tf_op jit(solution)/shard_map/layer_sum/pallas_call | solution.py:93
  27.4 2.2 %collective-permute-start = (bf16[4,512,128]{2,1,0:T(8,128)(2,1)}, bf16[4,512,128]{2,1,0:T(8,128)(2,1)S(1)}, u32[]{:S(2)}, u32[]{:S(2)}) collective-permute-start(bf16[4,512,128]{2,1,0:T(8,128)(2,1)} %get-tuple-element.110), channel_id=1, source_target_pairs={{0,3},{1,0},{2,1},{3,2},{4,7},{5,4},{6,5},{7,6},{8,11},{9,8},{10,9... | collective-permute-start | bytes 1572872 | tf_op jit(solution)/shard_map/layer_sum/ppermute | solution.py:61
  30.4 10.7 %collective-permute-done = bf16[4,512,128]{2,1,0:T(8,128)(2,1)S(1)} collective-permute-done((bf16[4,512,128]{2,1,0:T(8,128)(2,1)}, bf16[4,512,128]{2,1,0:T(8,128)(2,1)S(1)}, u32[]{:S(2)}, u32[]{:S(2)}) %collective-permute-start) | collective-permute-done | bytes 524320 | tf_op jit(solution)/shard_map/layer_sum/ppermute | solution.py:61
  41.1 4.8 %collective-permute-done.1 = bf16[4,512,128]{2,1,0:T(8,128)(2,1)S(1)} collective-permute-done((bf16[4,512,128]{2,1,0:T(8,128)(2,1)}, bf16[4,512,128]{2,1,0:T(8,128)(2,1)S(1)}, u32[]{:S(2)}, u32[]{:S(2)}) %collective-permute-start.1) | collective-permute-done | bytes 524320 | tf_op jit(solution)/shard_map/layer_sum/ppermute | solution.py:61
  47.0 1.5 collective-permute-start.4
  48.6 1.8 collective-permute-start.12
  50.4 2.1 %add_convert_fusion.1 = bf16[4,512,128]{2,1,0:T(8,128)(2,1)} fusion(f32[4,512,128]{2,1,0:T(8,128)} %get-tuple-element.115, bf16[4,512,128]{2,1,0:T(8,128)(2,1)S(1)} %collective-permute-done.1), kind=kLoop, calls=%fused_computation.23 | loop fusion | flops 786432 | bytes 2097152 | tf_op jit(solution)/shard_map/layer_sum/convert_element_type | solution.py:540
  53.1 1.4 collective-permute-done.5
  54.5 7.5 %collective-permute-done.4 = bf16[4,512,128]{2,1,0:T(8,128)(2,1)S(1)} collective-permute-done((bf16[4,512,128]{2,1,0:T(8,128)(2,1)S(1)}, bf16[4,512,128]{2,1,0:T(8,128)(2,1)S(1)}, u32[]{:S(2)}, u32[]{:S(2)}) %collective-permute-start.4) | collective-permute-done | bytes 524320 | tf_op jit(solution)/shard_map/layer_sum/ppermute | solution.py:65
  63.2 1.3 collective-permute-start.6
  65.8 3.9 %collective-permute-done.7 = bf16[4,512,128]{2,1,0:T(8,128)(2,1)} collective-permute-done((bf16[4,512,128]{2,1,0:T(8,128)(2,1)}, bf16[4,512,128]{2,1,0:T(8,128)(2,1)}, u32[]{:S(2)}, u32[]{:S(2)}) %collective-permute-start.7) | collective-permute-done | bytes 524320 | tf_op jit(solution)/shard_map/layer_sum/ppermute | solution.py:65
  69.6 2.9 %collective-permute-done.6 = bf16[4,512,128]{2,1,0:T(8,128)(2,1)} collective-permute-done((bf16[4,512,128]{2,1,0:T(8,128)(2,1)S(1)}, bf16[4,512,128]{2,1,0:T(8,128)(2,1)}, u32[]{:S(2)}, u32[]{:S(2)}) %collective-permute-start.6) | collective-permute-done | bytes 524320 | tf_op jit(solution)/shard_map/layer_sum/ppermute | solution.py:61
  72.5 3.4 %collective-permute-done.8 = bf16[4,512,128]{2,1,0:T(8,128)(2,1)} collective-permute-done((bf16[4,512,128]{2,1,0:T(8,128)(2,1)S(1)}, bf16[4,512,128]{2,1,0:T(8,128)(2,1)}, u32[]{:S(2)}, u32[]{:S(2)}) %collective-permute-start.8) | collective-permute-done | bytes 524320 | tf_op jit(solution)/shard_map/layer_sum/ppermute | solution.py:61
  76.0 2.1 %multiply_reduce_fusion.1 = (f32[512]{0:T(512)S(1)}, f32[4,512,128]{2,1,0:T(8,128)S(1)}) fusion(bf16[4,512,128]{2,1,0:T(8,128)(2,1)} %collective-permute-done.7, bf16[4,512,128]{2,1,0:T(8,128)(2,1)} %collective-permute-done.6, bf16[4,512,128]{2,1,0:T(8,128)(2,1)} %collective-permute-done.8, f32[4,512,128]{2,1,0:T(8,128)} %get-tuple-element.106, ...), kind=kLoop, calls=%fused_computation.21 | loop fusion | flops 2620928 | bytes 4196356 | tf_op jit(solution)/shard_map/norm/reduce_sum | solution.py:558
  78.2 2.2 %collective-permute-start.11 = (bf16[1,512,128]{2,1,0:T(8,128)(2,1)S(1)}, bf16[1,512,128]{2,1,0:T(8,128)(2,1)S(1)}, u32[]{:S(2)}, u32[]{:S(2)}) collective-permute-start(bf16[1,512,128]{2,1,0:T(8,128)(2,1)S(1)} %get-tuple-element.195), channel_id=1, source_target_pairs={{0,64},{8,72},{16,80},{24,88},{32,96},{40,104},{48,112},{56,120},{... | collective-permute-start | bytes 393224 | tf_op jit(solution)/shard_map/strip_exchange/ppermute | solution.py:49
  80.4 1.4 collective-permute-start.10
  83.1 3.3 %all-to-all-start.1 = ((f32[8,4,128]{2,1,0:T(4,128)}), f32[8,4,128]{2,1,0:T(4,128)S(1)}, u32[]{:S(2)}, u32[]{:S(2)}) async-start(f32[8,4,128]{2,1,0:T(4,128)} %broadcast_in_dim.54), calls=%async_computation.1 | async-start | bytes 32768 | tf_op jit(solution)/shard_map/norm/all_to_all | solution.py:71
  86.9 5.7 %all-to-all-done.1 = f32[8,4,128]{2,1,0:T(4,128)S(1)} async-done(((f32[8,4,128]{2,1,0:T(4,128)}), f32[8,4,128]{2,1,0:T(4,128)S(1)}, u32[]{:S(2)}, u32[]{:S(2)}) %all-to-all-start.1) | async-done | bytes 16416 | tf_op jit(solution)/shard_map/norm/all_to_all | solution.py:71
  92.6 1.3 collective-permute-done.11
  93.9 1.3 collective-permute-done.10
  95.7 3.0 %collective-permute-start.14 = (bf16[4,512,128]{2,1,0:T(8,128)(2,1)S(1)}, bf16[4,512,128]{2,1,0:T(8,128)(2,1)S(1)}, u32[]{:S(2)}, u32[]{:S(2)}) collective-permute-start(bf16[4,512,128]{2,1,0:T(8,128)(2,1)S(1)} %pad_maximum_fusion.1.refs_0_.refs_9_), channel_id=1, source_target_pairs={{0,3},{1,0},{2,1},{3,2},{4,7},{5,4},{6,5},{7,6},{8,11},{9,8},{10,9... | collective-permute-start | bytes 1572872 | tf_op jit(solution)/shard_map/norm/ppermute | solution.py:61
  99.6 7.1 %all-to-all-start.2 = ((f32[16,4,512]{2,1,0:T(4,128)}), f32[16,4,512]{2,1,0:T(4,128)S(1)}, u32[]{:S(2)}, u32[]{:S(2)}) async-start(f32[16,4,512]{2,1,0:T(4,128)} %broadcast_in_dim.56), calls=%async_computation.2 | async-start | bytes 262144 | tf_op jit(solution)/shard_map/contrast/all_to_all | solution.py:71
  108.8 5.9 %all-to-all-done.2 = f32[16,4,512]{2,1,0:T(4,128)S(1)} async-done(((f32[16,4,512]{2,1,0:T(4,128)}), f32[16,4,512]{2,1,0:T(4,128)S(1)}, u32[]{:S(2)}, u32[]{:S(2)}) %all-to-all-start.2) | async-done | bytes 131104 | tf_op jit(solution)/shard_map/contrast/all_to_all | solution.py:71
  116.4 2.7 %collective-permute-start.16 = (bf16[4,512,128]{2,1,0:T(8,128)(2,1)S(1)}, bf16[4,512,128]{2,1,0:T(8,128)(2,1)S(1)}, u32[]{:S(2)}, u32[]{:S(2)}) collective-permute-start(bf16[4,512,128]{2,1,0:T(8,128)(2,1)S(1)} %collective-permute-done.13.refs_1_.refs_10_), channel_id=1, source_target_pairs={{0,3},{1,0},{2,1},{3,2},{4,7},{5,4},{6,5},{7,6},{8,11},{9,8},{10,9... | collective-permute-start | bytes 1572872 | tf_op jit(solution)/shard_map/contrast/ppermute | solution.py:61
  120.4 4.3 %all-to-all-start.3 = ((f32[8,80,128]{2,1,0:T(8,128)}), f32[8,80,128]{2,1,0:T(8,128)}, u32[]{:S(2)}, u32[]{:S(2)}) async-start(f32[8,80,128]{2,1,0:T(8,128)} %broadcast_in_dim.57), calls=%async_computation.3 | async-start | bytes 655360 | tf_op jit(solution)/shard_map/contrast/all_to_all | solution.py:71
  124.7 11.0 %pad_maximum_fusion = bf16[2048,1792]{1,0:T(8,128)(2,1)} fusion(bf16[512,1792]{1,0:T(8,128)(2,1)} %collective-permute-done.12, bf16[512,1792]{1,0:T(8,128)(2,1)} %collective-permute-done.3, bf16[512,1792]{1,0:T(8,128)(2,1)} %collective-permute-done.2, bf16[512,1792]{1,0:T(8,128)(2,1)} %hidden_ref.1), kind=kLoop, calls=%fused_computation | loop fusion | flops 29360128 | bytes 14680064 | tf_op jit(solution)/shard_map/norm/concatenate | solution.py:561
  135.8 3.0 %collective-permute-start.22 = (bf16[2,512,128]{2,1,0:T(8,128)(2,1)S(1)}, bf16[2,512,128]{2,1,0:T(8,128)(2,1)S(1)}, u32[]{:S(2)}, u32[]{:S(2)}) collective-permute-start(bf16[2,512,128]{2,1,0:T(8,128)(2,1)S(1)} %slice.24), channel_id=1, source_target_pairs={{0,3},{1,0},{2,1},{3,2},{4,7},{5,4},{6,5},{7,6},{8,11},{9,8},{10,9... | collective-permute-start | bytes 786440 | tf_op jit(solution)/shard_map/contrast/ppermute | solution.py:61
  138.9 2.2 %contrast.3 = (f32[8,64,128]{2,1,0:T(8,128)S(1)}, f32[8,128]{1,0:T(8,128)S(1)}, f32[64,512]{1,0:T(8,128)S(1)}, f32[1,512]{1,0:T(1,128)S(1)}) custom-call(s32[1]{0:T(128)} %bitcast.13.plan_ref, f32[8,80,128]{2,1,0:T(8,128)} %all-to-all-done.3.part_ref, f32[64,64]{1,0:T(8,128)S(1)} %compare_convert_fusion.same_ref, f32[4,8,128]{2,1,0:T(8,128)S(1)} %bitcast.81, ...), custom_call_target="tpu_custom_call" | custom-call | flops 1024 | bytes 1024 | tf_op jit(solution)/shard_map/contrast/pallas_call | solution.py:204
  142.3 1.5 collective-permute-start.19
  143.8 3.2 %collective-permute-start.20 = (bf16[3,528,128]{2,1,0:T(8,128)(2,1)}, bf16[3,528,128]{2,1,0:T(8,128)(2,1)S(1)}, u32[]{:S(2)}, u32[]{:S(2)}) collective-permute-start(bf16[3,528,128]{2,1,0:T(8,128)(2,1)} %fusion.15.refs_0_), channel_id=1, source_target_pairs={{0,3},{1,0},{2,1},{3,2},{4,7},{5,4},{6,5},{7,6},{8,11},{9,8},{10,9... | collective-permute-start | bytes 1216520 | tf_op jit(solution)/shard_map/row_gather/ppermute | solution.py:61
  147.3 3.8 %along.1 = f32[4,4,128]{2,1,0:T(4,128)S(1)} custom-call(s32[35]{0:T(128)S(1)} %stack.164.plan_ref, bf16[4,512,128]{2,1,0:T(8,128)(2,1)S(1)} %pad_maximum_fusion.1.refs_0_.refs_9_, bf16[4,512,128]{2,1,0:T(8,128)(2,1)S(1)} %collective-permute-done.13.refs_1_.refs_10_, bf16[4,512,128]{2,1,0:T(8,128)(2,1)S(1)} %collective-permute-done.14.refs_2_.refs_11_, ...), custom_call_target="tpu_custom_call" | custom-call | flops 1024 | bytes 1024 | tf_op jit(solution)/shard_map/along/pallas_call | solution.py:284
  151.6 3.3 %collective-permute-done.24 = f32[8,4,128]{2,1,0:T(4,128)S(1)} collective-permute-done((f32[8,4,128]{2,1,0:T(4,128)S(1)}, f32[8,4,128]{2,1,0:T(4,128)S(1)}, u32[]{:S(2)}, u32[]{:S(2)}) %collective-permute-start.24) | collective-permute-done | bytes 16416 | tf_op jit(solution)/shard_map/along/ppermute | solution.py:596
  154.9 3.0 %collective-permute-done.21.refs_3_ = bf16[3,528,128]{2,1,0:T(8,128)(2,1)S(1)} collective-permute-done((bf16[3,528,128]{2,1,0:T(8,128)(2,1)}, bf16[3,528,128]{2,1,0:T(8,128)(2,1)S(1)}, u32[]{:S(2)}, u32[]{:S(2)}) %collective-permute-start.21) | collective-permute-done | bytes 405536 | tf_op jit(solution)/shard_map/row_gather/ppermute | solution.py:61
  158.8 1.7 collective-permute-start.27
  161.7 4.0 %collective-permute-done.28 = f32[8,4,128]{2,1,0:T(4,128)S(1)} collective-permute-done((f32[8,4,128]{2,1,0:T(4,128)S(1)}, f32[8,4,128]{2,1,0:T(4,128)S(1)}, u32[]{:S(2)}, u32[]{:S(2)}) %collective-permute-start.28) | collective-permute-done | bytes 16416 | tf_op jit(solution)/shard_map/along/ppermute | solution.py:599
  165.8 4.2 %down_grad.1 = (bf16[4,2048,256]{2,1,0:T(8,128)(2,1)S(1)}, f32[4,128]{1,0:T(4,128)S(1)}) custom-call(s32[35]{0:T(128)S(1)} %stack.164.plan_ref, bf16[4,512,128]{2,1,0:T(8,128)(2,1)S(1)} %pad_maximum_fusion.1.refs_0_.refs_9_, bf16[4,512,128]{2,1,0:T(8,128)(2,1)S(1)} %collective-permute-done.13.refs_1_.refs_10_, ...), custom_call_target="tpu_custom_call" | custom-call | flops 1024 | bytes 1024 | tf_op jit(solution)/shard_map/down_grad/pallas_call | solution.py:334
  170.1 2.2 %fusion.7 = f32[1792,256]{1,0:T(8,128)S(1)} fusion(bf16[2048,1792]{1,0:T(8,128)(2,1)S(1)} %copy-done.12, bf16[4,2048,256]{2,1,0:T(8,128)(2,1)S(1)} %get-tuple-element.153), kind=kOutput, calls=%fused_computation.14 | convolution fusion | flops 1879048192 | bytes 10223616 | tf_op jit(solution)/shard_map/down_grad/dot_general | solution.py:607
  172.4 2.2 %fusion.5 = f32[1792,256]{1,0:T(8,128)S(1)} fusion(bf16[2048,1792]{1,0:T(8,128)(2,1)S(1)} %copy-done.12, bf16[4,2048,256]{2,1,0:T(8,128)(2,1)S(1)} %get-tuple-element.153), kind=kOutput, calls=%fused_computation.12 | convolution fusion | flops 1879048192 | bytes 10223616 | tf_op jit(solution)/shard_map/down_grad/dot_general | solution.py:607
  175.4 1.6 collective-permute-start.31
  177.7 2.2 %fusion = bf16[1792,256]{1,0:T(8,128)(2,1)S(1)} fusion(f32[1792,256]{1,0:T(8,128)S(1)} %collective-permute-done.29, bf16[2048,1792]{1,0:T(8,128)(2,1)S(1)} %copy-done.12, bf16[4,2048,256]{2,1,0:T(8,128)(2,1)S(1)} %get-tuple-element.153), kind=kOutput, calls=%fused_computation.3 | convolution fusion | flops 1879965696 | bytes 11141120 | tf_op jit(solution)/shard_map/down_grad/dot_general | solution.py:607
  179.9 2.3 %collective-permute-start.30 = (bf16[1792,256]{1,0:T(8,128)(2,1)S(1)}, bf16[1792,256]{1,0:T(8,128)(2,1)S(1)}, u32[]{:S(2)}, u32[]{:S(2)}) collective-permute-start(bf16[1792,256]{1,0:T(8,128)(2,1)S(1)} %fusion), channel_id=1, source_target_pairs={{0,16},{8,24},{16,0},{24,8},{32,48},{40,56},{48,32},{56,40},{64,80... | collective-permute-start | bytes 2752520 | tf_op jit(solution)/shard_map/down_grad/ppermute | solution.py:53
  182.3 2.8 %collective-permute-done.32.refs_8_ = bf16[3,272,128]{2,1,0:T(8,128)(2,1)S(1)} collective-permute-done((bf16[3,272,128]{2,1,0:T(8,128)(2,1)S(1)}, bf16[3,272,128]{2,1,0:T(8,128)(2,1)S(1)}, u32[]{:S(2)}, u32[]{:S(2)}) %collective-permute-start.32) | collective-permute-done | bytes 208928 | tf_op jit(solution)/shard_map/down_grad/ppermute | solution.py:61
  185.2 2.2 %convolution_add_fusion = f32[1792,256]{1,0:T(8,128)S(1)} fusion(f32[1792,256]{1,0:T(8,128)S(1)} %collective-permute-done.33, bf16[2048,1792]{1,0:T(8,128)(2,1)S(1)} %copy-done.12, bf16[2048,256]{1,0:T(8,128)(2,1)S(1)} %slice_bitcast_fusion), kind=kOutput, calls=%fused_computation.1 | convolution fusion | flops 1879506944 | bytes 12058624 | tf_op jit(solution)/shard_map/down_grad/dot_general | solution.py:607
  187.4 17.3 %hidden_grad.1 = (bf16[512,1792]{1,0:T(8,128)(2,1)}, bf16[512,512]{1,0:T(8,128)(2,1)}, f32[4,128]{1,0:T(4,128)}) custom-call(s32[35]{0:T(128)} %copy-done.9, bf16[3,528,128]{2,1,0:T(8,128)(2,1)} %fusion.15.refs_0_, bf16[3,528,128]{2,1,0:T(8,128)(2,1)} %copy-done.17, bf16[3,528,128]{2,1,0:T(8,128)(2,1)} %copy-done.18, bf16[3,528,128]{2,1,0:T(8,128)(2,1)} %copy-done.19, ...), custom_call_target="tpu_custom_call" | custom-call | flops 1024 | bytes 1024 | tf_op jit(solution)/shard_map/hidden_grad/pallas_call | solution.py:419
  204.7 1.4 convert_add_fusion
  (131 shorter events, 23.0 us)
Async XLA Ops:
  0.6 45.2 %collective-permute-start.2 = (bf16[512,1792]{1,0:T(8,128)(2,1)}, bf16[512,1792]{1,0:T(8,128)(2,1)}, u32[]{:S(2)}, u32[]{:S(2)}) collective-permute-start(bf16[512,1792]{1,0:T(8,128)(2,1)} %hidden_ref.1), channel_id=1, source_target_pairs={{0,32},{8,40},{16,48},{24,56},{32,64},{40,72},{48,80},{56,88},{64,... | collective-permute-start | bytes 5505032 | tf_op jit(solution)/shard_map/hidden_exchange/ppermute | solution.py:49
  2.3 43.6 %collective-permute-start.3 = (bf16[512,1792]{1,0:T(8,128)(2,1)}, bf16[512,1792]{1,0:T(8,128)(2,1)}, u32[]{:S(2)}, u32[]{:S(2)}) collective-permute-start(bf16[512,1792]{1,0:T(8,128)(2,1)} %hidden_ref.1), channel_id=1, source_target_pairs={{0,96},{8,104},{16,112},{24,120},{32,0},{40,8},{48,16},{56,24},{64... | collective-permute-start | bytes 5505032 | tf_op jit(solution)/shard_map/hidden_exchange/ppermute | solution.py:49
  6.3 21.0 %all-to-all-start = ((bf16[8,512,128]{2,1,0:T(8,128)(2,1)}), bf16[8,512,128]{2,1,0:T(8,128)(2,1)S(1)}, u32[]{:S(2)}, u32[]{:S(2)}) async-start(bf16[8,512,128]{2,1,0:T(8,128)(2,1)} %bitcast.6), calls=%async_computation | async-start | bytes 2097152 | tf_op jit(solution)/shard_map/resid_exchange/all_to_all | solution.py:521
  26.2 38.2 %copy-start.16 = (bf16[4,512,128]{2,1,0:T(8,128)(2,1)S(1)}, bf16[4,512,128]{2,1,0:T(8,128)(2,1)}, u32[]{:S(2)}) copy-start(bf16[4,512,128]{2,1,0:T(8,128)(2,1)} %get-tuple-element.117) | copy-start | bytes 1572868
  26.2 39.3 %copy-start.24 = (s32[16]{0:T(128)S(1)}, s32[16]{0:T(128)}, u32[]{:S(2)}) copy-start(s32[16]{0:T(128)} %param.9) | copy-start | bytes 196
  27.4 13.7 %collective-permute-start = (bf16[4,512,128]{2,1,0:T(8,128)(2,1)}, bf16[4,512,128]{2,1,0:T(8,128)(2,1)S(1)}, u32[]{:S(2)}, u32[]{:S(2)}) collective-permute-start(bf16[4,512,128]{2,1,0:T(8,128)(2,1)} %get-tuple-element.110), channel_id=1, source_target_pairs={{0,3},{1,0},{2,1},{3,2},{4,7},{5,4},{6,5},{7,6},{8,11},{9,8},{10,9... | collective-permute-start | bytes 1572872 | tf_op jit(solution)/shard_map/layer_sum/ppermute | solution.py:61
  29.6 16.3 %collective-permute-start.1 = (bf16[4,512,128]{2,1,0:T(8,128)(2,1)}, bf16[4,512,128]{2,1,0:T(8,128)(2,1)S(1)}, u32[]{:S(2)}, u32[]{:S(2)}) collective-permute-start(bf16[4,512,128]{2,1,0:T(8,128)(2,1)} %get-tuple-element.111), channel_id=1, source_target_pairs={{0,1},{1,2},{2,3},{3,0},{4,5},{5,6},{6,7},{7,4},{8,9},{9,10},{10,1... | collective-permute-start | bytes 1572872 | tf_op jit(solution)/shard_map/layer_sum/ppermute | solution.py:61
  29.6 24.9 %collective-permute-start.5 = (bf16[4,512,128]{2,1,0:T(8,128)(2,1)}, bf16[4,512,128]{2,1,0:T(8,128)(2,1)S(1)}, u32[]{:S(2)}, u32[]{:S(2)}) collective-permute-start(bf16[4,512,128]{2,1,0:T(8,128)(2,1)} %get-tuple-element.113), channel_id=1, source_target_pairs={{0,1},{1,2},{2,3},{3,0},{4,5},{5,6},{6,7},{7,4},{8,9},{9,10},{10,1... | collective-permute-start | bytes 1572872 | tf_op jit(solution)/shard_map/layer_sum/ppermute | solution.py:61
  47.0 14.9 %collective-permute-start.4 = (bf16[4,512,128]{2,1,0:T(8,128)(2,1)S(1)}, bf16[4,512,128]{2,1,0:T(8,128)(2,1)S(1)}, u32[]{:S(2)}, u32[]{:S(2)}) collective-permute-start(bf16[4,512,128]{2,1,0:T(8,128)(2,1)S(1)} %add_convert_fusion.3), channel_id=1, source_target_pairs={{0,4},{1,5},{2,6},{3,7},{4,0},{5,1},{6,2},{7,3},{8,12},{9,13},{10,... | collective-permute-start | bytes 1572872 | tf_op jit(solution)/shard_map/layer_sum/ppermute | solution.py:65
  48.6 46.7 %collective-permute-start.12 = (bf16[512,1792]{1,0:T(8,128)(2,1)}, bf16[512,1792]{1,0:T(8,128)(2,1)}, u32[]{:S(2)}, u32[]{:S(2)}) collective-permute-start(bf16[512,1792]{1,0:T(8,128)(2,1)} %hidden_ref.1), channel_id=1, source_target_pairs={{0,64},{8,72},{16,80},{24,88},{32,96},{40,104},{48,112},{56,120},{... | collective-permute-start | bytes 5505032 | tf_op jit(solution)/shard_map/hidden_exchange/ppermute | solution.py:49
  52.5 17.1 %collective-permute-start.7 = (bf16[4,512,128]{2,1,0:T(8,128)(2,1)}, bf16[4,512,128]{2,1,0:T(8,128)(2,1)}, u32[]{:S(2)}, u32[]{:S(2)}) collective-permute-start(bf16[4,512,128]{2,1,0:T(8,128)(2,1)} %add_convert_fusion.1), channel_id=1, source_target_pairs={{0,4},{1,5},{2,6},{3,7},{4,0},{5,1},{6,2},{7,3},{8,12},{9,13},{10,... | collective-permute-start | bytes 1572872 | tf_op jit(solution)/shard_map/layer_sum/ppermute | solution.py:65
  63.2 9.4 %collective-permute-start.6 = (bf16[4,512,128]{2,1,0:T(8,128)(2,1)S(1)}, bf16[4,512,128]{2,1,0:T(8,128)(2,1)}, u32[]{:S(2)}, u32[]{:S(2)}) collective-permute-start(bf16[4,512,128]{2,1,0:T(8,128)(2,1)S(1)} %add_convert_fusion.2), channel_id=1, source_target_pairs={{0,3},{1,0},{2,1},{3,2},{4,7},{5,4},{6,5},{7,6},{8,11},{9,8},{10,9... | collective-permute-start | bytes 1572872 | tf_op jit(solution)/shard_map/layer_sum/ppermute | solution.py:61
  64.6 11.4 %collective-permute-start.8 = (bf16[4,512,128]{2,1,0:T(8,128)(2,1)S(1)}, bf16[4,512,128]{2,1,0:T(8,128)(2,1)}, u32[]{:S(2)}, u32[]{:S(2)}) collective-permute-start(bf16[4,512,128]{2,1,0:T(8,128)(2,1)S(1)} %add_convert_fusion), channel_id=1, source_target_pairs={{0,1},{1,2},{2,3},{3,0},{4,5},{5,6},{6,7},{7,4},{8,9},{9,10},{10,1... | collective-permute-start | bytes 1572872 | tf_op jit(solution)/shard_map/layer_sum/ppermute | solution.py:61
  78.2 15.6 %collective-permute-start.11 = (bf16[1,512,128]{2,1,0:T(8,128)(2,1)S(1)}, bf16[1,512,128]{2,1,0:T(8,128)(2,1)S(1)}, u32[]{:S(2)}, u32[]{:S(2)}) collective-permute-start(bf16[1,512,128]{2,1,0:T(8,128)(2,1)S(1)} %get-tuple-element.195), channel_id=1, source_target_pairs={{0,64},{8,72},{16,80},{24,88},{32,96},{40,104},{48,112},{56,120},{... | collective-permute-start | bytes 393224 | tf_op jit(solution)/shard_map/strip_exchange/ppermute | solution.py:49
  80.4 14.8 %collective-permute-start.10 = (bf16[1,512,128]{2,1,0:T(8,128)(2,1)S(1)}, bf16[1,512,128]{2,1,0:T(8,128)(2,1)S(1)}, u32[]{:S(2)}, u32[]{:S(2)}) collective-permute-start(bf16[1,512,128]{2,1,0:T(8,128)(2,1)S(1)} %get-tuple-element.196), channel_id=1, source_target_pairs={{0,96},{8,104},{16,112},{24,120},{32,0},{40,8},{48,16},{56,24},{64... | collective-permute-start | bytes 393224 | tf_op jit(solution)/shard_map/strip_exchange/ppermute | solution.py:49
  81.8 13.3 %collective-permute-start.9 = (bf16[1,512,128]{2,1,0:T(8,128)(2,1)S(1)}, bf16[1,512,128]{2,1,0:T(8,128)(2,1)S(1)}, u32[]{:S(2)}, u32[]{:S(2)}) collective-permute-start(bf16[1,512,128]{2,1,0:T(8,128)(2,1)S(1)} %get-tuple-element.197), channel_id=1, source_target_pairs={{0,32},{8,40},{16,48},{24,56},{32,64},{40,72},{48,80},{56,88},{64,... | collective-permute-start | bytes 393224 | tf_op jit(solution)/shard_map/strip_exchange/ppermute | solution.py:49
  83.1 9.5 %all-to-all-start.1 = ((f32[8,4,128]{2,1,0:T(4,128)}), f32[8,4,128]{2,1,0:T(4,128)S(1)}, u32[]{:S(2)}, u32[]{:S(2)}) async-start(f32[8,4,128]{2,1,0:T(4,128)} %broadcast_in_dim.54), calls=%async_computation.1 | async-start | bytes 32768 | tf_op jit(solution)/shard_map/norm/all_to_all | solution.py:71
  95.3 70.4 %copy-start = (bf16[4,512,128]{2,1,0:T(8,128)(2,1)}, bf16[4,512,128]{2,1,0:T(8,128)(2,1)S(1)}, u32[]{:S(2)}) copy-start(bf16[4,512,128]{2,1,0:T(8,128)(2,1)S(1)} %pad_maximum_fusion.1.refs_0_.refs_9_) | copy-start | bytes 1572868
  95.3 19.4 %collective-permute-start.13 = (bf16[4,512,128]{2,1,0:T(8,128)(2,1)S(1)}, bf16[4,512,128]{2,1,0:T(8,128)(2,1)S(1)}, u32[]{:S(2)}, u32[]{:S(2)}) collective-permute-start(bf16[4,512,128]{2,1,0:T(8,128)(2,1)S(1)} %pad_maximum_fusion.1.refs_0_.refs_9_), channel_id=1, source_target_pairs={{0,4},{1,5},{2,6},{3,7},{4,0},{5,1},{6,2},{7,3},{8,12},{9,13},{10,... | collective-permute-start | bytes 1572872 | tf_op jit(solution)/shard_map/norm/ppermute | solution.py:65
  95.7 18.9 %collective-permute-start.14 = (bf16[4,512,128]{2,1,0:T(8,128)(2,1)S(1)}, bf16[4,512,128]{2,1,0:T(8,128)(2,1)S(1)}, u32[]{:S(2)}, u32[]{:S(2)}) collective-permute-start(bf16[4,512,128]{2,1,0:T(8,128)(2,1)S(1)} %pad_maximum_fusion.1.refs_0_.refs_9_), channel_id=1, source_target_pairs={{0,3},{1,0},{2,1},{3,2},{4,7},{5,4},{6,5},{7,6},{8,11},{9,8},{10,9... | collective-permute-start | bytes 1572872 | tf_op jit(solution)/shard_map/norm/ppermute | solution.py:61
  98.8 15.9 %collective-permute-start.15 = (bf16[4,512,128]{2,1,0:T(8,128)(2,1)S(1)}, bf16[4,512,128]{2,1,0:T(8,128)(2,1)S(1)}, u32[]{:S(2)}, u32[]{:S(2)}) collective-permute-start(bf16[4,512,128]{2,1,0:T(8,128)(2,1)S(1)} %pad_maximum_fusion.1.refs_0_.refs_9_), channel_id=1, source_target_pairs={{0,1},{1,2},{2,3},{3,0},{4,5},{5,6},{6,7},{7,4},{8,9},{9,10},{10,1... | collective-permute-start | bytes 1572872 | tf_op jit(solution)/shard_map/norm/ppermute | solution.py:61
  98.8 48.3 %copy-start.23 = (f32[4,128]{1,0:T(4,128)}, f32[4,128]{1,0:T(4,128)S(1)}, u32[]{:S(2)}) copy-start(f32[4,128]{1,0:T(4,128)S(1)} %add_rsqrt_fusion.refs_19_) | copy-start | bytes 6148
  99.6 15.0 %all-to-all-start.2 = ((f32[16,4,512]{2,1,0:T(4,128)}), f32[16,4,512]{2,1,0:T(4,128)S(1)}, u32[]{:S(2)}, u32[]{:S(2)}) async-start(f32[16,4,512]{2,1,0:T(4,128)} %broadcast_in_dim.56), calls=%async_computation.2 | async-start | bytes 262144 | tf_op jit(solution)/shard_map/contrast/all_to_all | solution.py:71
  106.8 58.9 %copy-start.9 = (s32[35]{0:T(128)}, s32[35]{0:T(128)S(1)}, u32[]{:S(2)}) copy-start(s32[35]{0:T(128)S(1)} %stack.164.plan_ref) | copy-start | bytes 424
  114.7 51.1 %copy-start.3 = (bf16[4,512,128]{2,1,0:T(8,128)(2,1)}, bf16[4,512,128]{2,1,0:T(8,128)(2,1)S(1)}, u32[]{:S(2)}) copy-start(bf16[4,512,128]{2,1,0:T(8,128)(2,1)S(1)} %collective-permute-done.13.refs_1_.refs_10_) | copy-start | bytes 1572868
  114.7 51.1 %copy-start.4 = (bf16[4,512,128]{2,1,0:T(8,128)(2,1)}, bf16[4,512,128]{2,1,0:T(8,128)(2,1)S(1)}, u32[]{:S(2)}) copy-start(bf16[4,512,128]{2,1,0:T(8,128)(2,1)S(1)} %collective-permute-done.14.refs_2_.refs_11_) | copy-start | bytes 1572868
  114.7 51.1 %copy-start.5 = (bf16[4,512,128]{2,1,0:T(8,128)(2,1)}, bf16[4,512,128]{2,1,0:T(8,128)(2,1)S(1)}, u32[]{:S(2)}) copy-start(bf16[4,512,128]{2,1,0:T(8,128)(2,1)S(1)} %collective-permute-done.15.refs_3_.refs_12_) | copy-start | bytes 1572868
  114.7 21.0 %collective-permute-start.17 = (bf16[4,512,128]{2,1,0:T(8,128)(2,1)S(1)}, bf16[4,512,128]{2,1,0:T(8,128)(2,1)S(1)}, u32[]{:S(2)}, u32[]{:S(2)}) collective-permute-start(bf16[4,512,128]{2,1,0:T(8,128)(2,1)S(1)} %collective-permute-done.15.refs_3_.refs_12_), channel_id=1, source_target_pairs={{0,4},{1,5},{2,6},{3,7},{4,0},{5,1},{6,2},{7,3},{8,12},{9,13},{10,... | collective-permute-start | bytes 1572872 | tf_op jit(solution)/shard_map/contrast/ppermute | solution.py:65
  115.8 19.9 %collective-permute-start.18 = (bf16[4,512,128]{2,1,0:T(8,128)(2,1)S(1)}, bf16[4,512,128]{2,1,0:T(8,128)(2,1)}, u32[]{:S(2)}, u32[]{:S(2)}) collective-permute-start(bf16[4,512,128]{2,1,0:T(8,128)(2,1)S(1)} %collective-permute-done.15.refs_3_.refs_12_), channel_id=1, source_target_pairs={{0,1},{1,2},{2,3},{3,0},{4,5},{5,6},{6,7},{7,4},{8,9},{9,10},{10,1... | collective-permute-start | bytes 1572872 | tf_op jit(solution)/shard_map/contrast/ppermute | solution.py:61
  116.4 19.3 %collective-permute-start.16 = (bf16[4,512,128]{2,1,0:T(8,128)(2,1)S(1)}, bf16[4,512,128]{2,1,0:T(8,128)(2,1)S(1)}, u32[]{:S(2)}, u32[]{:S(2)}) collective-permute-start(bf16[4,512,128]{2,1,0:T(8,128)(2,1)S(1)} %collective-permute-done.13.refs_1_.refs_10_), channel_id=1, source_target_pairs={{0,3},{1,0},{2,1},{3,2},{4,7},{5,4},{6,5},{7,6},{8,11},{9,8},{10,9... | collective-permute-start | bytes 1572872 | tf_op jit(solution)/shard_map/contrast/ppermute | solution.py:61
  120.4 15.2 %all-to-all-start.3 = ((f32[8,80,128]{2,1,0:T(8,128)}), f32[8,80,128]{2,1,0:T(8,128)}, u32[]{:S(2)}, u32[]{:S(2)}) async-start(f32[8,80,128]{2,1,0:T(8,128)} %broadcast_in_dim.57), calls=%async_computation.3 | async-start | bytes 655360 | tf_op jit(solution)/shard_map/contrast/all_to_all | solution.py:71
  135.7 34.3 %copy-start.2 = (bf16[4,512,128]{2,1,0:T(8,128)(2,1)}, bf16[4,512,128]{2,1,0:T(8,128)(2,1)S(1)}, u32[]{:S(2)}) copy-start(bf16[4,512,128]{2,1,0:T(8,128)(2,1)S(1)} %collective-permute-done.16.refs_5_.refs_14_) | copy-start | bytes 1572868
  135.7 34.3 %copy-start.1 = (bf16[4,512,128]{2,1,0:T(8,128)(2,1)}, bf16[4,512,128]{2,1,0:T(8,128)(2,1)S(1)}, u32[]{:S(2)}) copy-start(bf16[4,512,128]{2,1,0:T(8,128)(2,1)S(1)} %collective-permute-done.17.refs_6_.refs_15_) | copy-start | bytes 1572868
  135.8 11.3 %collective-permute-start.22 = (bf16[2,512,128]{2,1,0:T(8,128)(2,1)S(1)}, bf16[2,512,128]{2,1,0:T(8,128)(2,1)S(1)}, u32[]{:S(2)}, u32[]{:S(2)}) collective-permute-start(bf16[2,512,128]{2,1,0:T(8,128)(2,1)S(1)} %slice.24), channel_id=1, source_target_pairs={{0,3},{1,0},{2,1},{3,2},{4,7},{5,4},{6,5},{7,6},{8,11},{9,8},{10,9... | collective-permute-start | bytes 786440 | tf_op jit(solution)/shard_map/contrast/ppermute | solution.py:61
  138.8 8.5 %collective-permute-start.23 = (bf16[2,512,128]{2,1,0:T(8,128)(2,1)S(1)}, bf16[2,512,128]{2,1,0:T(8,128)(2,1)S(1)}, u32[]{:S(2)}, u32[]{:S(2)}) collective-permute-start(bf16[2,512,128]{2,1,0:T(8,128)(2,1)S(1)} %slice.25), channel_id=1, source_target_pairs={{0,1},{1,2},{2,3},{3,0},{4,5},{5,6},{6,7},{7,4},{8,9},{9,10},{10,1... | collective-permute-start | bytes 786440 | tf_op jit(solution)/shard_map/contrast/ppermute | solution.py:61
  142.3 12.6 %collective-permute-start.19 = (bf16[3,528,128]{2,1,0:T(8,128)(2,1)}, bf16[3,528,128]{2,1,0:T(8,128)(2,1)S(1)}, u32[]{:S(2)}, u32[]{:S(2)}) collective-permute-start(bf16[3,528,128]{2,1,0:T(8,128)(2,1)} %fusion.15.refs_0_), channel_id=1, source_target_pairs={{0,4},{1,5},{2,6},{3,7},{4,0},{5,1},{6,2},{7,3},{8,12},{9,13},{10,... | collective-permute-start | bytes 1216520 | tf_op jit(solution)/shard_map/row_gather/ppermute | solution.py:65
  143.8 11.1 %collective-permute-start.20 = (bf16[3,528,128]{2,1,0:T(8,128)(2,1)}, bf16[3,528,128]{2,1,0:T(8,128)(2,1)S(1)}, u32[]{:S(2)}, u32[]{:S(2)}) collective-permute-start(bf16[3,528,128]{2,1,0:T(8,128)(2,1)} %fusion.15.refs_0_), channel_id=1, source_target_pairs={{0,3},{1,0},{2,1},{3,2},{4,7},{5,4},{6,5},{7,6},{8,11},{9,8},{10,9... | collective-permute-start | bytes 1216520 | tf_op jit(solution)/shard_map/row_gather/ppermute | solution.py:61
  147.0 10.9 %collective-permute-start.21 = (bf16[3,528,128]{2,1,0:T(8,128)(2,1)}, bf16[3,528,128]{2,1,0:T(8,128)(2,1)S(1)}, u32[]{:S(2)}, u32[]{:S(2)}) collective-permute-start(bf16[3,528,128]{2,1,0:T(8,128)(2,1)} %fusion.15.refs_0_), channel_id=1, source_target_pairs={{0,1},{1,2},{2,3},{3,0},{4,5},{5,6},{6,7},{7,4},{8,9},{9,10},{10,1... | collective-permute-start | bytes 1216520 | tf_op jit(solution)/shard_map/row_gather/ppermute | solution.py:61
  151.1 3.8 %collective-permute-start.24 = (f32[8,4,128]{2,1,0:T(4,128)S(1)}, f32[8,4,128]{2,1,0:T(4,128)S(1)}, u32[]{:S(2)}, u32[]{:S(2)}) collective-permute-start(f32[8,4,128]{2,1,0:T(4,128)S(1)} %pad_maximum_fusion.2), channel_id=1, source_target_pairs={{0,32},{8,40},{16,48},{24,56},{32,0},{40,8},{48,16},{56,24},{64,96... | collective-permute-start | bytes 49160 | tf_op jit(solution)/shard_map/along/ppermute | solution.py:596
  157.9 12.2 %collective-permute-start.25 = (bf16[3,528,128]{2,1,0:T(8,128)(2,1)S(1)}, bf16[3,528,128]{2,1,0:T(8,128)(2,1)S(1)}, u32[]{:S(2)}, u32[]{:S(2)}) collective-permute-start(bf16[3,528,128]{2,1,0:T(8,128)(2,1)S(1)} %collective-permute-done.19.refs_1_), channel_id=1, source_target_pairs={{0,3},{1,0},{2,1},{3,2},{4,7},{5,4},{6,5},{7,6},{8,11},{9,8},{10,9... | collective-permute-start | bytes 1216520 | tf_op jit(solution)/shard_map/along/ppermute | solution.py:61
  158.2 11.8 %collective-permute-start.26 = (bf16[3,528,128]{2,1,0:T(8,128)(2,1)S(1)}, bf16[3,528,128]{2,1,0:T(8,128)(2,1)S(1)}, u32[]{:S(2)}, u32[]{:S(2)}) collective-permute-start(bf16[3,528,128]{2,1,0:T(8,128)(2,1)S(1)} %collective-permute-done.21.refs_3_), channel_id=1, source_target_pairs={{0,4},{1,5},{2,6},{3,7},{4,0},{5,1},{6,2},{7,3},{8,12},{9,13},{10,... | collective-permute-start | bytes 1216520 | tf_op jit(solution)/shard_map/along/ppermute | solution.py:65
  158.8 11.3 %collective-permute-start.27 = (bf16[3,528,128]{2,1,0:T(8,128)(2,1)S(1)}, bf16[3,528,128]{2,1,0:T(8,128)(2,1)S(1)}, u32[]{:S(2)}, u32[]{:S(2)}) collective-permute-start(bf16[3,528,128]{2,1,0:T(8,128)(2,1)S(1)} %collective-permute-done.21.refs_3_), channel_id=1, source_target_pairs={{0,1},{1,2},{2,3},{3,0},{4,5},{5,6},{6,7},{7,4},{8,9},{9,10},{10,1... | collective-permute-start | bytes 1216520 | tf_op jit(solution)/shard_map/along/ppermute | solution.py:61
  160.5 5.2 %collective-permute-start.28 = (f32[8,4,128]{2,1,0:T(4,128)S(1)}, f32[8,4,128]{2,1,0:T(4,128)S(1)}, u32[]{:S(2)}, u32[]{:S(2)}) collective-permute-start(f32[8,4,128]{2,1,0:T(4,128)S(1)} %fusion.19), channel_id=1, source_target_pairs={{0,64},{8,72},{16,80},{24,88},{32,96},{40,104},{48,112},{56,120},{... | collective-permute-start | bytes 49160 | tf_op jit(solution)/shard_map/along/ppermute | solution.py:599
  172.4 5.3 %collective-permute-start.29 = (f32[1792,256]{1,0:T(8,128)S(1)}, f32[1792,256]{1,0:T(8,128)S(1)}, u32[]{:S(2)}, u32[]{:S(2)}) collective-permute-start(f32[1792,256]{1,0:T(8,128)S(1)} %fusion.7), channel_id=1, source_target_pairs={{0,8},{8,0},{16,24},{24,16},{32,40},{40,32},{48,56},{56,48},{64,72... | collective-permute-start | bytes 5505032 | tf_op jit(solution)/shard_map/down_grad/ppermute | solution.py:57
  174.6 10.6 %collective-permute-start.33 = (f32[1792,256]{1,0:T(8,128)S(1)}, f32[1792,256]{1,0:T(8,128)S(1)}, u32[]{:S(2)}, u32[]{:S(2)}) collective-permute-start(f32[1792,256]{1,0:T(8,128)S(1)} %fusion.5), channel_id=1, source_target_pairs={{0,8},{8,0},{16,24},{24,16},{32,40},{40,32},{48,56},{56,48},{64,72... | collective-permute-start | bytes 5505032 | tf_op jit(solution)/shard_map/down_grad/ppermute | solution.py:57
  175.4 6.9 %collective-permute-start.31 = (bf16[3,256,128]{2,1,0:T(8,128)(2,1)S(1)}, bf16[3,256,128]{2,1,0:T(8,128)(2,1)S(1)}, u32[]{:S(2)}, u32[]{:S(2)}) collective-permute-start(bf16[3,256,128]{2,1,0:T(8,128)(2,1)S(1)} %slice.30), channel_id=1, source_target_pairs={{0,3},{1,0},{2,1},{3,2},{4,7},{5,4},{6,5},{7,6},{8,11},{9,8},{10,9... | collective-permute-start | bytes 589832 | tf_op jit(solution)/shard_map/down_grad/ppermute | solution.py:61
  177.1 8.1 %collective-permute-start.32 = (bf16[3,272,128]{2,1,0:T(8,128)(2,1)S(1)}, bf16[3,272,128]{2,1,0:T(8,128)(2,1)S(1)}, u32[]{:S(2)}, u32[]{:S(2)}) collective-permute-start(bf16[3,272,128]{2,1,0:T(8,128)(2,1)S(1)} %slice.31), channel_id=1, source_target_pairs={{0,1},{1,2},{2,3},{3,0},{4,5},{5,6},{6,7},{7,4},{8,9},{9,10},{10,1... | collective-permute-start | bytes 626696 | tf_op jit(solution)/shard_map/down_grad/ppermute | solution.py:61
  179.9 24.8 %collective-permute-start.30 = (bf16[1792,256]{1,0:T(8,128)(2,1)S(1)}, bf16[1792,256]{1,0:T(8,128)(2,1)S(1)}, u32[]{:S(2)}, u32[]{:S(2)}) collective-permute-start(bf16[1792,256]{1,0:T(8,128)(2,1)S(1)} %fusion), channel_id=1, source_target_pairs={{0,16},{8,24},{16,0},{24,8},{32,48},{40,56},{48,32},{56,40},{64,80... | collective-permute-start | bytes 2752520 | tf_op jit(solution)/shard_map/down_grad/ppermute | solution.py:53
  (15 other events, 184.5 us)

commit v8 on v7

--- a/solution.py
+++ b/solution.py
@@ -122,6 +122,23 @@
 
 def exact_dot(left, right, contract):
     return lax.dot_general(left, right, (contract, ((), ())), precision=highest, preferred_element_type=f32)
+
+
+def cut_kernel(slab_ref, out_ref):
+    lanes = out_ref.shape[-1]
+    for r in range(out_ref.shape[0]):
+        j = r % NY % 2 * 2 + r // NY
+        out_ref[r] = slab_ref[:, j * lanes : (j + 1) * lanes]
+
+
+def cut_strips(slab, group):
+    tokens, width = slab.shape
+    return pl.pallas_call(
+        cut_kernel,
+        out_shape=jax.ShapeDtypeStruct((group, tokens, width // NX), slab.dtype),
+        compiler_params=pltpu.CompilerParams(vmem_limit_bytes=16 * MIB),
+        cost_estimate=QUICK,
+    )(slab)
 
 
 def gram_kernel(plan_ref, mean_ref, gain_ref, strip_ref, out_ref):
@@ -516,9 +533,7 @@
         hidden_far = over_x(hidden, 2)
 
     with jax.named_scope("resid_exchange"):
-        pieces = resid.reshape(tokens, 2, NZL, lanes).transpose(2, 1, 0, 3)[:, None]
-        pieces = jnp.broadcast_to(pieces, (NZL, NY // 2, 2, tokens, lanes))
-        pieces = lax.all_to_all(pieces.reshape(group, tokens, lanes), "tensor", 0, 0)
+        pieces = lax.all_to_all(cut_strips(resid, group), "tensor", 0, 0)
         pieces = pieces.reshape(NX, 2, tokens, lanes)
 
     with jax.named_scope("layer_sum"):

time: 207 us -> 207 us (level)
  transfers between devices with their start and end apart: 38 -> 38, of which waited for: 18 -> 18; matrix products, arithmetic and copies ran while one was open for 16% -> 15% of each run, Pallas kernels for 20% -> 21%
where the time goes in v8:
time: 207 us; the launch traced here: 206 us
  waiting for transfers between devices  63.5 us (31%)
  starting transfers between devices  62.5 us (30%)
  Pallas kernels  42.5 us (21%)
  other arithmetic  21.5 us (10%)
  matrix products  8.76 us (4%)
  local copies, waits for them, and re-layouts  5.74 us (3%)
    ppermute x17, waiting for transfers between devices, over_y(): return lax.ppermute(value, 'tensor', tensor_route(0, step))  29.3 us
    ppermute x17, starting transfers between devices, over_y(): return lax.ppermute(value, 'tensor', tensor_route(0, step))  22 us
    pallas_call x1, Pallas kernels, hidden_grad(): pl.pallas_call(hidden_grad_kernel, grid_spec=pltpu.PrefetchScalarGridSpec...  17.3 us
    all_to_all x3, starting transfers between devices, gather_small(): return lax.all_to_all(copies, axis, 0, 0)  14.6 us
    pallas_call x1, Pallas kernels, layer_dot(): pl.pallas_call(layer_dot_kernel, grid_spec=pltpu.PrefetchScalarGridSpec(n...  13.4 us
    ppermute x6, waiting for transfers between devices, over_zl(): return lax.ppermute(value, 'tensor', tensor_route(1, 0))  11.6 us
    all_to_all x3, waiting for transfers between devices, gather_small(): return lax.all_to_all(copies, axis, 0, 0)  11.5 us
    concatenate x1, other arithmetic, per_device(): jnp.concatenate([hidden, hidden_left, hidden_right, hidden_far], axis=0)  11 us
  transfers between devices with their start and end apart: 38, of which 18 were waited for; matrix products, arithmetic and copies ran while one was open for 15% of the time, Pallas kernels for 21%

profile of v8, /device:TPU:0, one launch (start us, length us, event | category | flops | bytes accessed | tf_op | source)
XLA Modules:
  0.0 206.2 jit_solution(14623260098984891791)
XLA Ops:
  0.6 1.6 collective-permute-start.2
  2.3 1.7 collective-permute-start.3
  6.1 5.9 %all-to-all-start = ((bf16[8,512,128]{2,1,0:T(8,128)(2,1)}), bf16[8,512,128]{2,1,0:T(8,128)(2,1)S(1)}, u32[]{:S(2)}, u32[]{:S(2)}) async-start(bf16[8,512,128]{2,1,0:T(8,128)(2,1)} %resid_exchange.1), calls=%async_computation | async-start | bytes 2097152 | tf_op jit(solution)/shard_map/resid_exchange/all_to_all | solution.py:536
  12.6 13.4 %layer_sum.1 = (bf16[4,512,128]{2,1,0:T(8,128)(2,1)}, bf16[4,512,128]{2,1,0:T(8,128)(2,1)}, bf16[4,512,128]{2,1,0:T(8,128)(2,1)}, bf16[4,512,128]{2,1,0:T(8,128)...) custom-call(s32[5]{0:T(128)} %stack.129.plan_ref, ...), custom_call_target="tpu_custom_call" | custom-call | flops 7516192768 | bytes 20709376 | tf_op jit(solution)/shard_map/layer_sum/pallas_call | solution.py:93
  27.2 2.2 %collective-permute-start = (bf16[4,512,128]{2,1,0:T(8,128)(2,1)}, bf16[4,512,128]{2,1,0:T(8,128)(2,1)S(1)}, u32[]{:S(2)}, u32[]{:S(2)}) collective-permute-start(bf16[4,512,128]{2,1,0:T(8,128)(2,1)} %get-tuple-element.110), channel_id=1, source_target_pairs={{0,3},{1,0},{2,1},{3,2},{4,7},{5,4},{6,5},{7,6},{8,11},{9,8},{10,9... | collective-permute-start | bytes 1572872 | tf_op jit(solution)/shard_map/layer_sum/ppermute | solution.py:61
  30.2 10.7 %collective-permute-done = bf16[4,512,128]{2,1,0:T(8,128)(2,1)S(1)} collective-permute-done((bf16[4,512,128]{2,1,0:T(8,128)(2,1)}, bf16[4,512,128]{2,1,0:T(8,128)(2,1)S(1)}, u32[]{:S(2)}, u32[]{:S(2)}) %collective-permute-start) | collective-permute-done | bytes 524320 | tf_op jit(solution)/shard_map/layer_sum/ppermute | solution.py:61
  40.9 4.8 %collective-permute-done.1 = bf16[4,512,128]{2,1,0:T(8,128)(2,1)S(1)} collective-permute-done((bf16[4,512,128]{2,1,0:T(8,128)(2,1)}, bf16[4,512,128]{2,1,0:T(8,128)(2,1)S(1)}, u32[]{:S(2)}, u32[]{:S(2)}) %collective-permute-start.1) | collective-permute-done | bytes 524320 | tf_op jit(solution)/shard_map/layer_sum/ppermute | solution.py:61
  46.8 1.5 collective-permute-start.4
  48.4 1.8 collective-permute-start.12
  50.2 2.1 %add_convert_fusion.1 = bf16[4,512,128]{2,1,0:T(8,128)(2,1)} fusion(f32[4,512,128]{2,1,0:T(8,128)} %get-tuple-element.115, bf16[4,512,128]{2,1,0:T(8,128)(2,1)S(1)} %collective-permute-done.1), kind=kLoop, calls=%fused_computation.23 | loop fusion | flops 786432 | bytes 2097152 | tf_op jit(solution)/shard_map/layer_sum/convert_element_type | solution.py:555
  52.9 1.4 collective-permute-done.5
  54.3 7.5 %collective-permute-done.4 = bf16[4,512,128]{2,1,0:T(8,128)(2,1)S(1)} collective-permute-done((bf16[4,512,128]{2,1,0:T(8,128)(2,1)S(1)}, bf16[4,512,128]{2,1,0:T(8,128)(2,1)S(1)}, u32[]{:S(2)}, u32[]{:S(2)}) %collective-permute-start.4) | collective-permute-done | bytes 524320 | tf_op jit(solution)/shard_map/layer_sum/ppermute | solution.py:65
  63.0 1.5 collective-permute-start.6
  65.5 4.1 %collective-permute-done.7 = bf16[4,512,128]{2,1,0:T(8,128)(2,1)} collective-permute-done((bf16[4,512,128]{2,1,0:T(8,128)(2,1)}, bf16[4,512,128]{2,1,0:T(8,128)(2,1)}, u32[]{:S(2)}, u32[]{:S(2)}) %collective-permute-start.7) | collective-permute-done | bytes 524320 | tf_op jit(solution)/shard_map/layer_sum/ppermute | solution.py:65
  69.6 2.7 %collective-permute-done.6 = bf16[4,512,128]{2,1,0:T(8,128)(2,1)} collective-permute-done((bf16[4,512,128]{2,1,0:T(8,128)(2,1)S(1)}, bf16[4,512,128]{2,1,0:T(8,128)(2,1)}, u32[]{:S(2)}, u32[]{:S(2)}) %collective-permute-start.6) | collective-permute-done | bytes 524320 | tf_op jit(solution)/shard_map/layer_sum/ppermute | solution.py:61
  72.3 3.7 %collective-permute-done.8 = bf16[4,512,128]{2,1,0:T(8,128)(2,1)} collective-permute-done((bf16[4,512,128]{2,1,0:T(8,128)(2,1)S(1)}, bf16[4,512,128]{2,1,0:T(8,128)(2,1)}, u32[]{:S(2)}, u32[]{:S(2)}) %collective-permute-start.8) | collective-permute-done | bytes 524320 | tf_op jit(solution)/shard_map/layer_sum/ppermute | solution.py:61
  76.0 2.1 %multiply_reduce_fusion.1 = (f32[512]{0:T(512)S(1)}, f32[4,512,128]{2,1,0:T(8,128)S(1)}) fusion(bf16[4,512,128]{2,1,0:T(8,128)(2,1)} %collective-permute-done.7, bf16[4,512,128]{2,1,0:T(8,128)(2,1)} %collective-permute-done.6, bf16[4,512,128]{2,1,0:T(8,128)(2,1)} %collective-permute-done.8, f32[4,512,128]{2,1,0:T(8,128)} %get-tuple-element.106, ...), kind=kLoop, calls=%fused_computation.21 | loop fusion | flops 2620928 | bytes 4196356 | tf_op jit(solution)/shard_map/norm/reduce_sum | solution.py:573
  78.2 2.2 %collective-permute-start.11 = (bf16[1,512,128]{2,1,0:T(8,128)(2,1)S(1)}, bf16[1,512,128]{2,1,0:T(8,128)(2,1)S(1)}, u32[]{:S(2)}, u32[]{:S(2)}) collective-permute-start(bf16[1,512,128]{2,1,0:T(8,128)(2,1)S(1)} %get-tuple-element.195), channel_id=1, source_target_pairs={{0,64},{8,72},{16,80},{24,88},{32,96},{40,104},{48,112},{56,120},{... | collective-permute-start | bytes 393224 | tf_op jit(solution)/shard_map/strip_exchange/ppermute | solution.py:49
  80.4 1.4 collective-permute-start.10
  83.1 3.3 %all-to-all-start.1 = ((f32[8,4,128]{2,1,0:T(4,128)}), f32[8,4,128]{2,1,0:T(4,128)S(1)}, u32[]{:S(2)}, u32[]{:S(2)}) async-start(f32[8,4,128]{2,1,0:T(4,128)} %broadcast_in_dim.47), calls=%async_computation.1 | async-start | bytes 32768 | tf_op jit(solution)/shard_map/norm/all_to_all | solution.py:71
  86.9 5.7 %all-to-all-done.1 = f32[8,4,128]{2,1,0:T(4,128)S(1)} async-done(((f32[8,4,128]{2,1,0:T(4,128)}), f32[8,4,128]{2,1,0:T(4,128)S(1)}, u32[]{:S(2)}, u32[]{:S(2)}) %all-to-all-start.1) | async-done | bytes 16416 | tf_op jit(solution)/shard_map/norm/all_to_all | solution.py:71
  92.6 1.3 collective-permute-done.11
  93.9 1.3 collective-permute-done.10
  95.7 3.0 %collective-permute-start.14 = (bf16[4,512,128]{2,1,0:T(8,128)(2,1)S(1)}, bf16[4,512,128]{2,1,0:T(8,128)(2,1)S(1)}, u32[]{:S(2)}, u32[]{:S(2)}) collective-permute-start(bf16[4,512,128]{2,1,0:T(8,128)(2,1)S(1)} %pad_maximum_fusion.1.refs_0_.refs_9_), channel_id=1, source_target_pairs={{0,3},{1,0},{2,1},{3,2},{4,7},{5,4},{6,5},{7,6},{8,11},{9,8},{10,9... | collective-permute-start | bytes 1572872 | tf_op jit(solution)/shard_map/norm/ppermute | solution.py:61
  99.6 7.1 %all-to-all-start.2 = ((f32[16,4,512]{2,1,0:T(4,128)}), f32[16,4,512]{2,1,0:T(4,128)S(1)}, u32[]{:S(2)}, u32[]{:S(2)}) async-start(f32[16,4,512]{2,1,0:T(4,128)} %broadcast_in_dim.49), calls=%async_computation.2 | async-start | bytes 262144 | tf_op jit(solution)/shard_map/contrast/all_to_all | solution.py:71
  108.8 5.9 %all-to-all-done.2 = f32[16,4,512]{2,1,0:T(4,128)S(1)} async-done(((f32[16,4,512]{2,1,0:T(4,128)}), f32[16,4,512]{2,1,0:T(4,128)S(1)}, u32[]{:S(2)}, u32[]{:S(2)}) %all-to-all-start.2) | async-done | bytes 131104 | tf_op jit(solution)/shard_map/contrast/all_to_all | solution.py:71
  116.4 2.7 %collective-permute-start.16 = (bf16[4,512,128]{2,1,0:T(8,128)(2,1)S(1)}, bf16[4,512,128]{2,1,0:T(8,128)(2,1)S(1)}, u32[]{:S(2)}, u32[]{:S(2)}) collective-permute-start(bf16[4,512,128]{2,1,0:T(8,128)(2,1)S(1)} %collective-permute-done.13.refs_1_.refs_10_), channel_id=1, source_target_pairs={{0,3},{1,0},{2,1},{3,2},{4,7},{5,4},{6,5},{7,6},{8,11},{9,8},{10,9... | collective-permute-start | bytes 1572872 | tf_op jit(solution)/shard_map/contrast/ppermute | solution.py:61
  120.4 4.2 %all-to-all-start.3 = ((f32[8,80,128]{2,1,0:T(8,128)}), f32[8,80,128]{2,1,0:T(8,128)}, u32[]{:S(2)}, u32[]{:S(2)}) async-start(f32[8,80,128]{2,1,0:T(8,128)} %broadcast_in_dim.50), calls=%async_computation.3 | async-start | bytes 655360 | tf_op jit(solution)/shard_map/contrast/all_to_all | solution.py:71
  124.7 11.0 %pad_maximum_fusion = bf16[2048,1792]{1,0:T(8,128)(2,1)} fusion(bf16[512,1792]{1,0:T(8,128)(2,1)} %collective-permute-done.12, bf16[512,1792]{1,0:T(8,128)(2,1)} %collective-permute-done.3, bf16[512,1792]{1,0:T(8,128)(2,1)} %collective-permute-done.2, bf16[512,1792]{1,0:T(8,128)(2,1)} %hidden_ref.1), kind=kLoop, calls=%fused_computation | loop fusion | flops 29360128 | bytes 14680064 | tf_op jit(solution)/shard_map/norm/concatenate | solution.py:576
  135.8 3.0 %collective-permute-start.22 = (bf16[2,512,128]{2,1,0:T(8,128)(2,1)S(1)}, bf16[2,512,128]{2,1,0:T(8,128)(2,1)S(1)}, u32[]{:S(2)}, u32[]{:S(2)}) collective-permute-start(bf16[2,512,128]{2,1,0:T(8,128)(2,1)S(1)} %slice.24), channel_id=1, source_target_pairs={{0,3},{1,0},{2,1},{3,2},{4,7},{5,4},{6,5},{7,6},{8,11},{9,8},{10,9... | collective-permute-start | bytes 786440 | tf_op jit(solution)/shard_map/contrast/ppermute | solution.py:61
  138.9 2.2 %contrast.3 = (f32[8,64,128]{2,1,0:T(8,128)S(1)}, f32[8,128]{1,0:T(8,128)S(1)}, f32[64,512]{1,0:T(8,128)S(1)}, f32[1,512]{1,0:T(1,128)S(1)}) custom-call(s32[1]{0:T(128)} %bitcast.11.plan_ref, f32[8,80,128]{2,1,0:T(8,128)} %all-to-all-done.3.part_ref, f32[64,64]{1,0:T(8,128)S(1)} %compare_convert_fusion.same_ref, f32[4,8,128]{2,1,0:T(8,128)S(1)} %bitcast.79, ...), custom_call_target="tpu_custom_call" | custom-call | flops 1024 | bytes 1024 | tf_op jit(solution)/shard_map/contrast/pallas_call | solution.py:221
  142.4 1.5 collective-permute-start.19
  143.9 3.2 %collective-permute-start.20 = (bf16[3,528,128]{2,1,0:T(8,128)(2,1)}, bf16[3,528,128]{2,1,0:T(8,128)(2,1)S(1)}, u32[]{:S(2)}, u32[]{:S(2)}) collective-permute-start(bf16[3,528,128]{2,1,0:T(8,128)(2,1)} %fusion.15.refs_0_), channel_id=1, source_target_pairs={{0,3},{1,0},{2,1},{3,2},{4,7},{5,4},{6,5},{7,6},{8,11},{9,8},{10,9... | collective-permute-start | bytes 1216520 | tf_op jit(solution)/shard_map/row_gather/ppermute | solution.py:61
  147.3 3.8 %along.1 = f32[4,4,128]{2,1,0:T(4,128)S(1)} custom-call(s32[35]{0:T(128)S(1)} %stack.164.plan_ref, bf16[4,512,128]{2,1,0:T(8,128)(2,1)S(1)} %pad_maximum_fusion.1.refs_0_.refs_9_, bf16[4,512,128]{2,1,0:T(8,128)(2,1)S(1)} %collective-permute-done.13.refs_1_.refs_10_, bf16[4,512,128]{2,1,0:T(8,128)(2,1)S(1)} %collective-permute-done.14.refs_2_.refs_11_, ...), custom_call_target="tpu_custom_call" | custom-call | flops 1024 | bytes 1024 | tf_op jit(solution)/shard_map/along/pallas_call | solution.py:301
  151.7 3.3 %collective-permute-done.24 = f32[8,4,128]{2,1,0:T(4,128)S(1)} collective-permute-done((f32[8,4,128]{2,1,0:T(4,128)S(1)}, f32[8,4,128]{2,1,0:T(4,128)S(1)}, u32[]{:S(2)}, u32[]{:S(2)}) %collective-permute-start.24) | collective-permute-done | bytes 16416 | tf_op jit(solution)/shard_map/along/ppermute | solution.py:611
  155.0 3.0 %collective-permute-done.21.refs_3_ = bf16[3,528,128]{2,1,0:T(8,128)(2,1)S(1)} collective-permute-done((bf16[3,528,128]{2,1,0:T(8,128)(2,1)}, bf16[3,528,128]{2,1,0:T(8,128)(2,1)S(1)}, u32[]{:S(2)}, u32[]{:S(2)}) %collective-permute-start.21) | collective-permute-done | bytes 405536 | tf_op jit(solution)/shard_map/row_gather/ppermute | solution.py:61
  158.9 1.7 collective-permute-start.27
  161.8 4.0 %collective-permute-done.28 = f32[8,4,128]{2,1,0:T(4,128)S(1)} collective-permute-done((f32[8,4,128]{2,1,0:T(4,128)S(1)}, f32[8,4,128]{2,1,0:T(4,128)S(1)}, u32[]{:S(2)}, u32[]{:S(2)}) %collective-permute-start.28) | collective-permute-done | bytes 16416 | tf_op jit(solution)/shard_map/along/ppermute | solution.py:614
  165.8 4.2 %down_grad.1 = (bf16[4,2048,256]{2,1,0:T(8,128)(2,1)S(1)}, f32[4,128]{1,0:T(4,128)S(1)}) custom-call(s32[35]{0:T(128)S(1)} %stack.164.plan_ref, bf16[4,512,128]{2,1,0:T(8,128)(2,1)S(1)} %pad_maximum_fusion.1.refs_0_.refs_9_, bf16[4,512,128]{2,1,0:T(8,128)(2,1)S(1)} %collective-permute-done.13.refs_1_.refs_10_, ...), custom_call_target="tpu_custom_call" | custom-call | flops 1024 | bytes 1024 | tf_op jit(solution)/shard_map/down_grad/pallas_call | solution.py:351
  170.2 2.2 %fusion.7 = f32[1792,256]{1,0:T(8,128)S(1)} fusion(bf16[2048,1792]{1,0:T(8,128)(2,1)S(1)} %copy-done.13, bf16[4,2048,256]{2,1,0:T(8,128)(2,1)S(1)} %get-tuple-element.153), kind=kOutput, calls=%fused_computation.14 | convolution fusion | flops 1879048192 | bytes 10223616 | tf_op jit(solution)/shard_map/down_grad/dot_general | solution.py:622
  172.5 2.2 %fusion.5 = f32[1792,256]{1,0:T(8,128)S(1)} fusion(bf16[2048,1792]{1,0:T(8,128)(2,1)S(1)} %copy-done.13, bf16[4,2048,256]{2,1,0:T(8,128)(2,1)S(1)} %get-tuple-element.153), kind=kOutput, calls=%fused_computation.12 | convolution fusion | flops 1879048192 | bytes 10223616 | tf_op jit(solution)/shard_map/down_grad/dot_general | solution.py:622
  175.5 1.6 collective-permute-start.31
  177.8 2.2 %fusion = bf16[1792,256]{1,0:T(8,128)(2,1)S(1)} fusion(f32[1792,256]{1,0:T(8,128)S(1)} %collective-permute-done.29, bf16[2048,1792]{1,0:T(8,128)(2,1)S(1)} %copy-done.13, bf16[4,2048,256]{2,1,0:T(8,128)(2,1)S(1)} %get-tuple-element.153), kind=kOutput, calls=%fused_computation.3 | convolution fusion | flops 1879965696 | bytes 11141120 | tf_op jit(solution)/shard_map/down_grad/dot_general | solution.py:622
  180.0 2.3 %collective-permute-start.30 = (bf16[1792,256]{1,0:T(8,128)(2,1)S(1)}, bf16[1792,256]{1,0:T(8,128)(2,1)S(1)}, u32[]{:S(2)}, u32[]{:S(2)}) collective-permute-start(bf16[1792,256]{1,0:T(8,128)(2,1)S(1)} %fusion), channel_id=1, source_target_pairs={{0,16},{8,24},{16,0},{24,8},{32,48},{40,56},{48,32},{56,40},{64,80... | collective-permute-start | bytes 2752520 | tf_op jit(solution)/shard_map/down_grad/ppermute | solution.py:53
  182.4 2.8 %collective-permute-done.32.refs_8_ = bf16[3,272,128]{2,1,0:T(8,128)(2,1)S(1)} collective-permute-done((bf16[3,272,128]{2,1,0:T(8,128)(2,1)S(1)}, bf16[3,272,128]{2,1,0:T(8,128)(2,1)S(1)}, u32[]{:S(2)}, u32[]{:S(2)}) %collective-permute-start.32) | collective-permute-done | bytes 208928 | tf_op jit(solution)/shard_map/down_grad/ppermute | solution.py:61
  185.3 2.2 %convolution_add_fusion = f32[1792,256]{1,0:T(8,128)S(1)} fusion(f32[1792,256]{1,0:T(8,128)S(1)} %collective-permute-done.33, bf16[2048,1792]{1,0:T(8,128)(2,1)S(1)} %copy-done.13, bf16[2048,256]{1,0:T(8,128)(2,1)S(1)} %slice_bitcast_fusion), kind=kOutput, calls=%fused_computation.1 | convolution fusion | flops 1879506944 | bytes 12058624 | tf_op jit(solution)/shard_map/down_grad/dot_general | solution.py:622
  187.5 17.3 %hidden_grad.1 = (bf16[512,1792]{1,0:T(8,128)(2,1)}, bf16[512,512]{1,0:T(8,128)(2,1)}, f32[4,128]{1,0:T(4,128)}) custom-call(s32[35]{0:T(128)} %copy-done.10, bf16[3,528,128]{2,1,0:T(8,128)(2,1)} %fusion.15.refs_0_, bf16[3,528,128]{2,1,0:T(8,128)(2,1)} %copy-done.18, bf16[3,528,128]{2,1,0:T(8,128)(2,1)} %copy-done.19, bf16[3,528,128]{2,1,0:T(8,128)(2,1)} %copy-done.20, ...), custom_call_target="tpu_custom_call" | custom-call | flops 1024 | bytes 1024 | tf_op jit(solution)/shard_map/hidden_grad/pallas_call | solution.py:436
  204.8 1.4 convert_add_fusion
  (131 shorter events, 22.6 us)
Async XLA Ops:
  0.6 45.0 %collective-permute-start.2 = (bf16[512,1792]{1,0:T(8,128)(2,1)}, bf16[512,1792]{1,0:T(8,128)(2,1)}, u32[]{:S(2)}, u32[]{:S(2)}) collective-permute-start(bf16[512,1792]{1,0:T(8,128)(2,1)} %hidden_ref.1), channel_id=1, source_target_pairs={{0,32},{8,40},{16,48},{24,56},{32,64},{40,72},{48,80},{56,88},{64,... | collective-permute-start | bytes 5505032 | tf_op jit(solution)/shard_map/hidden_exchange/ppermute | solution.py:49
  2.3 43.4 %collective-permute-start.3 = (bf16[512,1792]{1,0:T(8,128)(2,1)}, bf16[512,1792]{1,0:T(8,128)(2,1)}, u32[]{:S(2)}, u32[]{:S(2)}) collective-permute-start(bf16[512,1792]{1,0:T(8,128)(2,1)} %hidden_ref.1), channel_id=1, source_target_pairs={{0,96},{8,104},{16,112},{24,120},{32,0},{40,8},{48,16},{56,24},{64... | collective-permute-start | bytes 5505032 | tf_op jit(solution)/shard_map/hidden_exchange/ppermute | solution.py:49
  6.1 21.0 %all-to-all-start = ((bf16[8,512,128]{2,1,0:T(8,128)(2,1)}), bf16[8,512,128]{2,1,0:T(8,128)(2,1)S(1)}, u32[]{:S(2)}, u32[]{:S(2)}) async-start(bf16[8,512,128]{2,1,0:T(8,128)(2,1)} %resid_exchange.1), calls=%async_computation | async-start | bytes 2097152 | tf_op jit(solution)/shard_map/resid_exchange/all_to_all | solution.py:536
  26.0 38.4 %copy-start.17 = (bf16[4,512,128]{2,1,0:T(8,128)(2,1)S(1)}, bf16[4,512,128]{2,1,0:T(8,128)(2,1)}, u32[]{:S(2)}) copy-start(bf16[4,512,128]{2,1,0:T(8,128)(2,1)} %get-tuple-element.117) | copy-start | bytes 1572868
  26.0 39.2 %copy-start.25 = (s32[16]{0:T(128)S(1)}, s32[16]{0:T(128)}, u32[]{:S(2)}) copy-start(s32[16]{0:T(128)} %param.9) | copy-start | bytes 196
  27.2 13.7 %collective-permute-start = (bf16[4,512,128]{2,1,0:T(8,128)(2,1)}, bf16[4,512,128]{2,1,0:T(8,128)(2,1)S(1)}, u32[]{:S(2)}, u32[]{:S(2)}) collective-permute-start(bf16[4,512,128]{2,1,0:T(8,128)(2,1)} %get-tuple-element.110), channel_id=1, source_target_pairs={{0,3},{1,0},{2,1},{3,2},{4,7},{5,4},{6,5},{7,6},{8,11},{9,8},{10,9... | collective-permute-start | bytes 1572872 | tf_op jit(solution)/shard_map/layer_sum/ppermute | solution.py:61
  29.4 16.3 %collective-permute-start.1 = (bf16[4,512,128]{2,1,0:T(8,128)(2,1)}, bf16[4,512,128]{2,1,0:T(8,128)(2,1)S(1)}, u32[]{:S(2)}, u32[]{:S(2)}) collective-permute-start(bf16[4,512,128]{2,1,0:T(8,128)(2,1)} %get-tuple-element.111), channel_id=1, source_target_pairs={{0,1},{1,2},{2,3},{3,0},{4,5},{5,6},{6,7},{7,4},{8,9},{9,10},{10,1... | collective-permute-start | bytes 1572872 | tf_op jit(solution)/shard_map/layer_sum/ppermute | solution.py:61
  29.4 24.9 %collective-permute-start.5 = (bf16[4,512,128]{2,1,0:T(8,128)(2,1)}, bf16[4,512,128]{2,1,0:T(8,128)(2,1)S(1)}, u32[]{:S(2)}, u32[]{:S(2)}) collective-permute-start(bf16[4,512,128]{2,1,0:T(8,128)(2,1)} %get-tuple-element.113), channel_id=1, source_target_pairs={{0,1},{1,2},{2,3},{3,0},{4,5},{5,6},{6,7},{7,4},{8,9},{9,10},{10,1... | collective-permute-start | bytes 1572872 | tf_op jit(solution)/shard_map/layer_sum/ppermute | solution.py:61
  46.8 14.9 %collective-permute-start.4 = (bf16[4,512,128]{2,1,0:T(8,128)(2,1)S(1)}, bf16[4,512,128]{2,1,0:T(8,128)(2,1)S(1)}, u32[]{:S(2)}, u32[]{:S(2)}) collective-permute-start(bf16[4,512,128]{2,1,0:T(8,128)(2,1)S(1)} %add_convert_fusion.3), channel_id=1, source_target_pairs={{0,4},{1,5},{2,6},{3,7},{4,0},{5,1},{6,2},{7,3},{8,12},{9,13},{10,... | collective-permute-start | bytes 1572872 | tf_op jit(solution)/shard_map/layer_sum/ppermute | solution.py:65
  48.4 46.9 %collective-permute-start.12 = (bf16[512,1792]{1,0:T(8,128)(2,1)}, bf16[512,1792]{1,0:T(8,128)(2,1)}, u32[]{:S(2)}, u32[]{:S(2)}) collective-permute-start(bf16[512,1792]{1,0:T(8,128)(2,1)} %hidden_ref.1), channel_id=1, source_target_pairs={{0,64},{8,72},{16,80},{24,88},{32,96},{40,104},{48,112},{56,120},{... | collective-permute-start | bytes 5505032 | tf_op jit(solution)/shard_map/hidden_exchange/ppermute | solution.py:49
  52.3 17.3 %collective-permute-start.7 = (bf16[4,512,128]{2,1,0:T(8,128)(2,1)}, bf16[4,512,128]{2,1,0:T(8,128)(2,1)}, u32[]{:S(2)}, u32[]{:S(2)}) collective-permute-start(bf16[4,512,128]{2,1,0:T(8,128)(2,1)} %add_convert_fusion.1), channel_id=1, source_target_pairs={{0,4},{1,5},{2,6},{3,7},{4,0},{5,1},{6,2},{7,3},{8,12},{9,13},{10,... | collective-permute-start | bytes 1572872 | tf_op jit(solution)/shard_map/layer_sum/ppermute | solution.py:65
  63.0 9.4 %collective-permute-start.6 = (bf16[4,512,128]{2,1,0:T(8,128)(2,1)S(1)}, bf16[4,512,128]{2,1,0:T(8,128)(2,1)}, u32[]{:S(2)}, u32[]{:S(2)}) collective-permute-start(bf16[4,512,128]{2,1,0:T(8,128)(2,1)S(1)} %add_convert_fusion.2), channel_id=1, source_target_pairs={{0,3},{1,0},{2,1},{3,2},{4,7},{5,4},{6,5},{7,6},{8,11},{9,8},{10,9... | collective-permute-start | bytes 1572872 | tf_op jit(solution)/shard_map/layer_sum/ppermute | solution.py:61
  64.6 11.4 %collective-permute-start.8 = (bf16[4,512,128]{2,1,0:T(8,128)(2,1)S(1)}, bf16[4,512,128]{2,1,0:T(8,128)(2,1)}, u32[]{:S(2)}, u32[]{:S(2)}) collective-permute-start(bf16[4,512,128]{2,1,0:T(8,128)(2,1)S(1)} %add_convert_fusion), channel_id=1, source_target_pairs={{0,1},{1,2},{2,3},{3,0},{4,5},{5,6},{6,7},{7,4},{8,9},{9,10},{10,1... | collective-permute-start | bytes 1572872 | tf_op jit(solution)/shard_map/layer_sum/ppermute | solution.py:61
  78.2 15.6 %collective-permute-start.11 = (bf16[1,512,128]{2,1,0:T(8,128)(2,1)S(1)}, bf16[1,512,128]{2,1,0:T(8,128)(2,1)S(1)}, u32[]{:S(2)}, u32[]{:S(2)}) collective-permute-start(bf16[1,512,128]{2,1,0:T(8,128)(2,1)S(1)} %get-tuple-element.195), channel_id=1, source_target_pairs={{0,64},{8,72},{16,80},{24,88},{32,96},{40,104},{48,112},{56,120},{... | collective-permute-start | bytes 393224 | tf_op jit(solution)/shard_map/strip_exchange/ppermute | solution.py:49
  80.4 14.8 %collective-permute-start.10 = (bf16[1,512,128]{2,1,0:T(8,128)(2,1)S(1)}, bf16[1,512,128]{2,1,0:T(8,128)(2,1)S(1)}, u32[]{:S(2)}, u32[]{:S(2)}) collective-permute-start(bf16[1,512,128]{2,1,0:T(8,128)(2,1)S(1)} %get-tuple-element.196), channel_id=1, source_target_pairs={{0,96},{8,104},{16,112},{24,120},{32,0},{40,8},{48,16},{56,24},{64... | collective-permute-start | bytes 393224 | tf_op jit(solution)/shard_map/strip_exchange/ppermute | solution.py:49
  81.8 13.3 %collective-permute-start.9 = (bf16[1,512,128]{2,1,0:T(8,128)(2,1)S(1)}, bf16[1,512,128]{2,1,0:T(8,128)(2,1)S(1)}, u32[]{:S(2)}, u32[]{:S(2)}) collective-permute-start(bf16[1,512,128]{2,1,0:T(8,128)(2,1)S(1)} %get-tuple-element.197), channel_id=1, source_target_pairs={{0,32},{8,40},{16,48},{24,56},{32,64},{40,72},{48,80},{56,88},{64,... | collective-permute-start | bytes 393224 | tf_op jit(solution)/shard_map/strip_exchange/ppermute | solution.py:49
  83.1 9.5 %all-to-all-start.1 = ((f32[8,4,128]{2,1,0:T(4,128)}), f32[8,4,128]{2,1,0:T(4,128)S(1)}, u32[]{:S(2)}, u32[]{:S(2)}) async-start(f32[8,4,128]{2,1,0:T(4,128)} %broadcast_in_dim.47), calls=%async_computation.1 | async-start | bytes 32768 | tf_op jit(solution)/shard_map/norm/all_to_all | solution.py:71
  95.3 70.5 %copy-start = (bf16[4,512,128]{2,1,0:T(8,128)(2,1)}, bf16[4,512,128]{2,1,0:T(8,128)(2,1)S(1)}, u32[]{:S(2)}) copy-start(bf16[4,512,128]{2,1,0:T(8,128)(2,1)S(1)} %pad_maximum_fusion.1.refs_0_.refs_9_) | copy-start | bytes 1572868
  95.3 19.4 %collective-permute-start.13 = (bf16[4,512,128]{2,1,0:T(8,128)(2,1)S(1)}, bf16[4,512,128]{2,1,0:T(8,128)(2,1)S(1)}, u32[]{:S(2)}, u32[]{:S(2)}) collective-permute-start(bf16[4,512,128]{2,1,0:T(8,128)(2,1)S(1)} %pad_maximum_fusion.1.refs_0_.refs_9_), channel_id=1, source_target_pairs={{0,4},{1,5},{2,6},{3,7},{4,0},{5,1},{6,2},{7,3},{8,12},{9,13},{10,... | collective-permute-start | bytes 1572872 | tf_op jit(solution)/shard_map/norm/ppermute | solution.py:65
  95.7 18.9 %collective-permute-start.14 = (bf16[4,512,128]{2,1,0:T(8,128)(2,1)S(1)}, bf16[4,512,128]{2,1,0:T(8,128)(2,1)S(1)}, u32[]{:S(2)}, u32[]{:S(2)}) collective-permute-start(bf16[4,512,128]{2,1,0:T(8,128)(2,1)S(1)} %pad_maximum_fusion.1.refs_0_.refs_9_), channel_id=1, source_target_pairs={{0,3},{1,0},{2,1},{3,2},{4,7},{5,4},{6,5},{7,6},{8,11},{9,8},{10,9... | collective-permute-start | bytes 1572872 | tf_op jit(solution)/shard_map/norm/ppermute | solution.py:61
  98.8 15.9 %collective-permute-start.15 = (bf16[4,512,128]{2,1,0:T(8,128)(2,1)S(1)}, bf16[4,512,128]{2,1,0:T(8,128)(2,1)S(1)}, u32[]{:S(2)}, u32[]{:S(2)}) collective-permute-start(bf16[4,512,128]{2,1,0:T(8,128)(2,1)S(1)} %pad_maximum_fusion.1.refs_0_.refs_9_), channel_id=1, source_target_pairs={{0,1},{1,2},{2,3},{3,0},{4,5},{5,6},{6,7},{7,4},{8,9},{9,10},{10,1... | collective-permute-start | bytes 1572872 | tf_op jit(solution)/shard_map/norm/ppermute | solution.py:61
  98.8 48.3 %copy-start.24 = (f32[4,128]{1,0:T(4,128)}, f32[4,128]{1,0:T(4,128)S(1)}, u32[]{:S(2)}) copy-start(f32[4,128]{1,0:T(4,128)S(1)} %add_rsqrt_fusion.refs_19_) | copy-start | bytes 6148
  99.6 15.0 %all-to-all-start.2 = ((f32[16,4,512]{2,1,0:T(4,128)}), f32[16,4,512]{2,1,0:T(4,128)S(1)}, u32[]{:S(2)}, u32[]{:S(2)}) async-start(f32[16,4,512]{2,1,0:T(4,128)} %broadcast_in_dim.49), calls=%async_computation.2 | async-start | bytes 262144 | tf_op jit(solution)/shard_map/contrast/all_to_all | solution.py:71
  106.8 59.0 %copy-start.10 = (s32[35]{0:T(128)}, s32[35]{0:T(128)S(1)}, u32[]{:S(2)}) copy-start(s32[35]{0:T(128)S(1)} %stack.164.plan_ref) | copy-start | bytes 424
  114.7 51.1 %copy-start.3 = (bf16[4,512,128]{2,1,0:T(8,128)(2,1)}, bf16[4,512,128]{2,1,0:T(8,128)(2,1)S(1)}, u32[]{:S(2)}) copy-start(bf16[4,512,128]{2,1,0:T(8,128)(2,1)S(1)} %collective-permute-done.13.refs_1_.refs_10_) | copy-start | bytes 1572868
  114.7 51.1 %copy-start.4 = (bf16[4,512,128]{2,1,0:T(8,128)(2,1)}, bf16[4,512,128]{2,1,0:T(8,128)(2,1)S(1)}, u32[]{:S(2)}) copy-start(bf16[4,512,128]{2,1,0:T(8,128)(2,1)S(1)} %collective-permute-done.14.refs_2_.refs_11_) | copy-start | bytes 1572868
  114.7 51.1 %copy-start.5 = (bf16[4,512,128]{2,1,0:T(8,128)(2,1)}, bf16[4,512,128]{2,1,0:T(8,128)(2,1)S(1)}, u32[]{:S(2)}) copy-start(bf16[4,512,128]{2,1,0:T(8,128)(2,1)S(1)} %collective-permute-done.15.refs_3_.refs_12_) | copy-start | bytes 1572868
  114.7 21.1 %collective-permute-start.17 = (bf16[4,512,128]{2,1,0:T(8,128)(2,1)S(1)}, bf16[4,512,128]{2,1,0:T(8,128)(2,1)S(1)}, u32[]{:S(2)}, u32[]{:S(2)}) collective-permute-start(bf16[4,512,128]{2,1,0:T(8,128)(2,1)S(1)} %collective-permute-done.15.refs_3_.refs_12_), channel_id=1, source_target_pairs={{0,4},{1,5},{2,6},{3,7},{4,0},{5,1},{6,2},{7,3},{8,12},{9,13},{10,... | collective-permute-start | bytes 1572872 | tf_op jit(solution)/shard_map/contrast/ppermute | solution.py:65
  115.8 20.0 %collective-permute-start.18 = (bf16[4,512,128]{2,1,0:T(8,128)(2,1)S(1)}, bf16[4,512,128]{2,1,0:T(8,128)(2,1)}, u32[]{:S(2)}, u32[]{:S(2)}) collective-permute-start(bf16[4,512,128]{2,1,0:T(8,128)(2,1)S(1)} %collective-permute-done.15.refs_3_.refs_12_), channel_id=1, source_target_pairs={{0,1},{1,2},{2,3},{3,0},{4,5},{5,6},{6,7},{7,4},{8,9},{9,10},{10,1... | collective-permute-start | bytes 1572872 | tf_op jit(solution)/shard_map/contrast/ppermute | solution.py:61
  116.4 19.3 %collective-permute-start.16 = (bf16[4,512,128]{2,1,0:T(8,128)(2,1)S(1)}, bf16[4,512,128]{2,1,0:T(8,128)(2,1)S(1)}, u32[]{:S(2)}, u32[]{:S(2)}) collective-permute-start(bf16[4,512,128]{2,1,0:T(8,128)(2,1)S(1)} %collective-permute-done.13.refs_1_.refs_10_), channel_id=1, source_target_pairs={{0,3},{1,0},{2,1},{3,2},{4,7},{5,4},{6,5},{7,6},{8,11},{9,8},{10,9... | collective-permute-start | bytes 1572872 | tf_op jit(solution)/shard_map/contrast/ppermute | solution.py:61
  120.4 15.3 %all-to-all-start.3 = ((f32[8,80,128]{2,1,0:T(8,128)}), f32[8,80,128]{2,1,0:T(8,128)}, u32[]{:S(2)}, u32[]{:S(2)}) async-start(f32[8,80,128]{2,1,0:T(8,128)} %broadcast_in_dim.50), calls=%async_computation.3 | async-start | bytes 655360 | tf_op jit(solution)/shard_map/contrast/all_to_all | solution.py:71
  135.7 34.3 %copy-start.2 = (bf16[4,512,128]{2,1,0:T(8,128)(2,1)}, bf16[4,512,128]{2,1,0:T(8,128)(2,1)S(1)}, u32[]{:S(2)}) copy-start(bf16[4,512,128]{2,1,0:T(8,128)(2,1)S(1)} %collective-permute-done.16.refs_5_.refs_14_) | copy-start | bytes 1572868
  135.8 34.3 %copy-start.1 = (bf16[4,512,128]{2,1,0:T(8,128)(2,1)}, bf16[4,512,128]{2,1,0:T(8,128)(2,1)S(1)}, u32[]{:S(2)}) copy-start(bf16[4,512,128]{2,1,0:T(8,128)(2,1)S(1)} %collective-permute-done.17.refs_6_.refs_15_) | copy-start | bytes 1572868
  135.8 11.4 %collective-permute-start.22 = (bf16[2,512,128]{2,1,0:T(8,128)(2,1)S(1)}, bf16[2,512,128]{2,1,0:T(8,128)(2,1)S(1)}, u32[]{:S(2)}, u32[]{:S(2)}) collective-permute-start(bf16[2,512,128]{2,1,0:T(8,128)(2,1)S(1)} %slice.24), channel_id=1, source_target_pairs={{0,3},{1,0},{2,1},{3,2},{4,7},{5,4},{6,5},{7,6},{8,11},{9,8},{10,9... | collective-permute-start | bytes 786440 | tf_op jit(solution)/shard_map/contrast/ppermute | solution.py:61
  138.8 8.5 %collective-permute-start.23 = (bf16[2,512,128]{2,1,0:T(8,128)(2,1)S(1)}, bf16[2,512,128]{2,1,0:T(8,128)(2,1)S(1)}, u32[]{:S(2)}, u32[]{:S(2)}) collective-permute-start(bf16[2,512,128]{2,1,0:T(8,128)(2,1)S(1)} %slice.25), channel_id=1, source_target_pairs={{0,1},{1,2},{2,3},{3,0},{4,5},{5,6},{6,7},{7,4},{8,9},{9,10},{10,1... | collective-permute-start | bytes 786440 | tf_op jit(solution)/shard_map/contrast/ppermute | solution.py:61
  142.4 12.5 %collective-permute-start.19 = (bf16[3,528,128]{2,1,0:T(8,128)(2,1)}, bf16[3,528,128]{2,1,0:T(8,128)(2,1)S(1)}, u32[]{:S(2)}, u32[]{:S(2)}) collective-permute-start(bf16[3,528,128]{2,1,0:T(8,128)(2,1)} %fusion.15.refs_0_), channel_id=1, source_target_pairs={{0,4},{1,5},{2,6},{3,7},{4,0},{5,1},{6,2},{7,3},{8,12},{9,13},{10,... | collective-permute-start | bytes 1216520 | tf_op jit(solution)/shard_map/row_gather/ppermute | solution.py:65
  143.9 11.1 %collective-permute-start.20 = (bf16[3,528,128]{2,1,0:T(8,128)(2,1)}, bf16[3,528,128]{2,1,0:T(8,128)(2,1)S(1)}, u32[]{:S(2)}, u32[]{:S(2)}) collective-permute-start(bf16[3,528,128]{2,1,0:T(8,128)(2,1)} %fusion.15.refs_0_), channel_id=1, source_target_pairs={{0,3},{1,0},{2,1},{3,2},{4,7},{5,4},{6,5},{7,6},{8,11},{9,8},{10,9... | collective-permute-start | bytes 1216520 | tf_op jit(solution)/shard_map/row_gather/ppermute | solution.py:61
  147.1 10.9 %collective-permute-start.21 = (bf16[3,528,128]{2,1,0:T(8,128)(2,1)}, bf16[3,528,128]{2,1,0:T(8,128)(2,1)S(1)}, u32[]{:S(2)}, u32[]{:S(2)}) collective-permute-start(bf16[3,528,128]{2,1,0:T(8,128)(2,1)} %fusion.15.refs_0_), channel_id=1, source_target_pairs={{0,1},{1,2},{2,3},{3,0},{4,5},{5,6},{6,7},{7,4},{8,9},{9,10},{10,1... | collective-permute-start | bytes 1216520 | tf_op jit(solution)/shard_map/row_gather/ppermute | solution.py:61
  151.1 3.8 %collective-permute-start.24 = (f32[8,4,128]{2,1,0:T(4,128)S(1)}, f32[8,4,128]{2,1,0:T(4,128)S(1)}, u32[]{:S(2)}, u32[]{:S(2)}) collective-permute-start(f32[8,4,128]{2,1,0:T(4,128)S(1)} %pad_maximum_fusion.2), channel_id=1, source_target_pairs={{0,32},{8,40},{16,48},{24,56},{32,0},{40,8},{48,16},{56,24},{64,96... | collective-permute-start | bytes 49160 | tf_op jit(solution)/shard_map/along/ppermute | solution.py:611
  158.0 12.2 %collective-permute-start.25 = (bf16[3,528,128]{2,1,0:T(8,128)(2,1)S(1)}, bf16[3,528,128]{2,1,0:T(8,128)(2,1)S(1)}, u32[]{:S(2)}, u32[]{:S(2)}) collective-permute-start(bf16[3,528,128]{2,1,0:T(8,128)(2,1)S(1)} %collective-permute-done.19.refs_1_), channel_id=1, source_target_pairs={{0,3},{1,0},{2,1},{3,2},{4,7},{5,4},{6,5},{7,6},{8,11},{9,8},{10,9... | collective-permute-start | bytes 1216520 | tf_op jit(solution)/shard_map/along/ppermute | solution.py:61
  158.3 11.8 %collective-permute-start.26 = (bf16[3,528,128]{2,1,0:T(8,128)(2,1)S(1)}, bf16[3,528,128]{2,1,0:T(8,128)(2,1)S(1)}, u32[]{:S(2)}, u32[]{:S(2)}) collective-permute-start(bf16[3,528,128]{2,1,0:T(8,128)(2,1)S(1)} %collective-permute-done.21.refs_3_), channel_id=1, source_target_pairs={{0,4},{1,5},{2,6},{3,7},{4,0},{5,1},{6,2},{7,3},{8,12},{9,13},{10,... | collective-permute-start | bytes 1216520 | tf_op jit(solution)/shard_map/along/ppermute | solution.py:65
  158.9 11.3 %collective-permute-start.27 = (bf16[3,528,128]{2,1,0:T(8,128)(2,1)S(1)}, bf16[3,528,128]{2,1,0:T(8,128)(2,1)S(1)}, u32[]{:S(2)}, u32[]{:S(2)}) collective-permute-start(bf16[3,528,128]{2,1,0:T(8,128)(2,1)S(1)} %collective-permute-done.21.refs_3_), channel_id=1, source_target_pairs={{0,1},{1,2},{2,3},{3,0},{4,5},{5,6},{6,7},{7,4},{8,9},{9,10},{10,1... | collective-permute-start | bytes 1216520 | tf_op jit(solution)/shard_map/along/ppermute | solution.py:61
  160.5 5.2 %collective-permute-start.28 = (f32[8,4,128]{2,1,0:T(4,128)S(1)}, f32[8,4,128]{2,1,0:T(4,128)S(1)}, u32[]{:S(2)}, u32[]{:S(2)}) collective-permute-start(f32[8,4,128]{2,1,0:T(4,128)S(1)} %fusion.19), channel_id=1, source_target_pairs={{0,64},{8,72},{16,80},{24,88},{32,96},{40,104},{48,112},{56,120},{... | collective-permute-start | bytes 49160 | tf_op jit(solution)/shard_map/along/ppermute | solution.py:614
  172.4 5.3 %collective-permute-start.29 = (f32[1792,256]{1,0:T(8,128)S(1)}, f32[1792,256]{1,0:T(8,128)S(1)}, u32[]{:S(2)}, u32[]{:S(2)}) collective-permute-start(f32[1792,256]{1,0:T(8,128)S(1)} %fusion.7), channel_id=1, source_target_pairs={{0,8},{8,0},{16,24},{24,16},{32,40},{40,32},{48,56},{56,48},{64,72... | collective-permute-start | bytes 5505032 | tf_op jit(solution)/shard_map/down_grad/ppermute | solution.py:57
  174.7 10.6 %collective-permute-start.33 = (f32[1792,256]{1,0:T(8,128)S(1)}, f32[1792,256]{1,0:T(8,128)S(1)}, u32[]{:S(2)}, u32[]{:S(2)}) collective-permute-start(f32[1792,256]{1,0:T(8,128)S(1)} %fusion.5), channel_id=1, source_target_pairs={{0,8},{8,0},{16,24},{24,16},{32,40},{40,32},{48,56},{56,48},{64,72... | collective-permute-start | bytes 5505032 | tf_op jit(solution)/shard_map/down_grad/ppermute | solution.py:57
  175.5 6.9 %collective-permute-start.31 = (bf16[3,256,128]{2,1,0:T(8,128)(2,1)S(1)}, bf16[3,256,128]{2,1,0:T(8,128)(2,1)S(1)}, u32[]{:S(2)}, u32[]{:S(2)}) collective-permute-start(bf16[3,256,128]{2,1,0:T(8,128)(2,1)S(1)} %slice.30), channel_id=1, source_target_pairs={{0,3},{1,0},{2,1},{3,2},{4,7},{5,4},{6,5},{7,6},{8,11},{9,8},{10,9... | collective-permute-start | bytes 589832 | tf_op jit(solution)/shard_map/down_grad/ppermute | solution.py:61
  177.2 8.1 %collective-permute-start.32 = (bf16[3,272,128]{2,1,0:T(8,128)(2,1)S(1)}, bf16[3,272,128]{2,1,0:T(8,128)(2,1)S(1)}, u32[]{:S(2)}, u32[]{:S(2)}) collective-permute-start(bf16[3,272,128]{2,1,0:T(8,128)(2,1)S(1)} %slice.31), channel_id=1, source_target_pairs={{0,1},{1,2},{2,3},{3,0},{4,5},{5,6},{6,7},{7,4},{8,9},{9,10},{10,1... | collective-permute-start | bytes 626696 | tf_op jit(solution)/shard_map/down_grad/ppermute | solution.py:61
  180.0 24.8 %collective-permute-start.30 = (bf16[1792,256]{1,0:T(8,128)(2,1)S(1)}, bf16[1792,256]{1,0:T(8,128)(2,1)S(1)}, u32[]{:S(2)}, u32[]{:S(2)}) collective-permute-start(bf16[1792,256]{1,0:T(8,128)(2,1)S(1)} %fusion), channel_id=1, source_target_pairs={{0,16},{8,24},{16,0},{24,8},{32,48},{40,56},{48,32},{56,40},{64,80... | collective-permute-start | bytes 2752520 | tf_op jit(solution)/shard_map/down_grad/ppermute | solution.py:53
  (16 other events, 185.9 us)
